TPU v7x, 32 devices: a whole 2x2x4 slice. The times are simulated.
32 devices in a mesh: groups: 2 (over x), orb: 8 (over z, y), aux: 2 (over core).
Axes of the slice: x: 2, y: 2, z: 4, core: 2. Of those that a mesh axis runs over, the one named last changes fastest.
Arguments:
- blocks: bfloat16 [64, 576, 1024], P(('groups', 'orb'), None, 'aux'), parts along dimension 0, may hold values from -1.25 to 1.25
- virt_energy: bfloat16 [64, 576], P(('groups', 'orb')), parts along dimension 0, may hold values from 0.19921875 to 4
- occ_energy: float32 [64], P('groups'), parts along dimension 0, may hold values from -2 to -0.3
- owner_slot: int32 [64], P('groups'), parts along dimension 0, may hold values from 0 to 31, as said below
- pairs: int32 [512, 2], P(('groups', 'orb')), parts along dimension 0, may hold values from 0 to 31, as said below
- domains: int32 [512, 2, 512], P(('groups', 'orb')), parts along dimension 0, may hold values from 0 to 575, as said below
Outputs:
- amplitudes: bfloat16 [512, 512, 512], P(('groups', 'orb', 'aux')), parts along dimension 0
There are 2 independent parts, one for each index of `groups`. A program takes and returns all parts, laid end to end along the dimension named above; each array names one. Nothing has to cross between parts.
Inputs may be any that keep to these rules, and one draw needn't show every extreme that they name: A permutation: orbital o is stored in slot owner_slot[o] of blocks and virt_energy. `pairs`: rows 8 * k to 8 * k + 7 share their first orbital, the one in slot k, so each aligned block of 32 rows has first orbitals stored in that block's 4 slots. The second orbital differs from the first and no pair repeats. Within one aligned block of 32 rows, at most 2 distinct second orbitals lie in any one block of 4 slots, and in every aligned block exactly 2 lie in some block of slots. `domains`: each row of 512 positions is strictly increasing.
All inputs are finite; a program needn't handle non-finite values.
Results may differ from a plain program's by a relative error of at most 0.001.
Values may be sent and summed in bfloat16 or wider, within the bound.
No kernel may reach another device: no remote copies, remote signals or barrier semaphores. Data moves between devices by JAX's collectives and lax.ppermute only.
A program may use at most 192 MiB of HBM per device.

v0:
```python
import jax
import jax.numpy as jnp
from jax import lax
from jax.sharding import PartitionSpec as P

CAP = 2


def request_table(slot_list, occ_dev, orb_count, slot_cap):
    source = slot_list // occ_dev
    local_part = slot_list % occ_dev
    hit_table = (source[:, None, None] == jnp.arange(orb_count, dtype=jnp.int32)[None, :, None]) & (
        local_part[:, None, None] == jnp.arange(occ_dev, dtype=jnp.int32)[None, None, :]
    )
    wanted = jnp.any(hit_table, axis=0).astype(jnp.int32)
    rank_table = jnp.cumsum(wanted, axis=1) - 1
    mark_table = (
        (wanted[:, :, None] == 1)
        & (rank_table[:, :, None] == jnp.arange(slot_cap, dtype=jnp.int32)[None, None, :])
    ).astype(jnp.int32)
    request = (
        jnp.sum(mark_table * jnp.arange(occ_dev, dtype=jnp.int32)[None, :, None], axis=1)
        + jnp.sum(mark_table, axis=1)
        - 1
    )
    return (request, rank_table)


def pair_integrals(slot_one, slot_two, cols_one, cols_two, local_blocks, partner_blocks):
    block_one = lax.dynamic_index_in_dim(local_blocks, slot_one, 0, keepdims=False)
    block_two = lax.dynamic_index_in_dim(partner_blocks, slot_two, 0, keepdims=False)
    chosen_one = jnp.take(block_one, cols_one, axis=0)
    chosen_two = jnp.take(block_two, cols_two, axis=0)
    return lax.dot_general(
        chosen_one, chosen_two, (((1,), (1,)), ((), ())), preferred_element_type=jnp.float32
    )


def integral_rows(
    local_blocks,
    partner_blocks,
    local_index,
    partner_index,
    cols_first,
    cols_second,
    first_row,
    row_count,
):
    batch_size = 4

    def window(values):
        picked = lax.dynamic_slice_in_dim(values, first_row, row_count, 0)
        return picked.reshape((row_count // batch_size, batch_size) + values.shape[1:])

    pieces = (window(local_index), window(partner_index), window(cols_first), window(cols_second))

    def one_batch(batch_items):
        slots_one, slots_two, first_cols, second_cols = batch_items
        return jax.vmap(pair_integrals, in_axes=(0, 0, 0, 0, None, None))(
            slots_one, slots_two, first_cols, second_cols, local_blocks, partner_blocks
        )

    result = lax.map(one_batch, pieces)
    return result.reshape((row_count,) + result.shape[2:])


def domain_energy(stored_energy, slot_index, cols):
    rows = jnp.take(stored_energy, slot_index, axis=0)
    return jnp.take_along_axis(rows, cols, axis=1).astype(jnp.float32)


def per_device(blocks, virt_energy, occ_energy, owner_slot, pairs, domains):
    orb_count = lax.axis_size("orb")
    aux_count = lax.axis_size("aux")
    occ_dev = blocks.shape[0]
    pair_dev = pairs.shape[0]
    own_orb = lax.axis_index("orb")
    own_rows = pair_dev // aux_count
    first_row = lax.axis_index("aux") * own_rows

    def own_window(values):
        return lax.dynamic_slice_in_dim(values, first_row, own_rows, 0)

    slot_first = owner_slot[pairs[:, 0]]
    slot_second = owner_slot[pairs[:, 1]]
    local_index = slot_first - own_orb * occ_dev
    cols_first = domains[:, 0, :]
    cols_second = domains[:, 1, :]
    wanted_rows, rank_table = request_table(slot_second, occ_dev, orb_count, CAP)
    asked_rows = lax.all_to_all(wanted_rows, "orb", split_axis=0, concat_axis=0, tiled=True)
    send_index = jnp.maximum(asked_rows.reshape(-1), 0)
    send_blocks = jnp.take(blocks, send_index, axis=0)
    send_energy = jnp.take(virt_energy, send_index, axis=0)
    partner_blocks, partner_energy = (
        lax.all_to_all(send_blocks, "orb", split_axis=0, concat_axis=0, tiled=True),
        lax.all_to_all(send_energy, "orb", split_axis=0, concat_axis=0, tiled=True),
    )
    source_second = slot_second // occ_dev
    partner_index = source_second * CAP + rank_table[source_second, slot_second % occ_dev]
    whole_partner, whole_local = (
        lax.all_gather(partner_blocks, "aux", axis=2, tiled=True),
        lax.all_gather(blocks, "aux", axis=2, tiled=True),
    )
    integrals = integral_rows(
        whole_local,
        whole_partner,
        local_index,
        partner_index,
        cols_first,
        cols_second,
        first_row,
        own_rows,
    )
    own_partner = own_window(partner_index)
    energy_first = domain_energy(virt_energy, own_window(local_index), own_window(cols_first))
    energy_second = domain_energy(partner_energy, own_partner, own_window(cols_second))
    own_pairs = own_window(pairs)
    occ_shift = occ_energy[own_pairs[:, 0]] + occ_energy[own_pairs[:, 1]]
    denominator = energy_first[:, :, None] + energy_second[:, None, :] - occ_shift[:, None, None]
    return (-integrals / denominator).astype(jnp.bfloat16)


def solution(mesh):
    in_specs = (
        P(("groups", "orb"), None, "aux"),
        P(("groups", "orb"), None),
        P("groups"),
        P("groups"),
        P(("groups", "orb"), None),
        P(("groups", "orb"), None, None),
    )
    out_specs = P(("groups", "orb", "aux"), None, None)
    return jax.shard_map(
        per_device, mesh=mesh, in_specs=in_specs, out_specs=out_specs, check_vma=False
    )
```

profile of v0, /device:TPU:0, one launch (start us, length us, event | category | flops | bytes accessed | tf_op | source)
XLA Modules:
  0.0 848.1 jit_solution(8799605016974541770)
XLA Ops:
  6.5 0.8 fusion.22
  7.3 1.4 gather_fusion.5
  9.4 13.5 %all_to_all.23 = s32[8,1,2]{2,1,0:T(1,128)S(1)} all-to-all(s32[8,1,2]{2,1,0:T(1,128)S(1)} %copy.18), channel_id=1, replica_groups=mesh['groups'=2,'orb'=8,'aux'=2] {'orb'}, dimensions={0} | all-to-all | bytes 128 | tf_op jit(solution)/shard_map/all_to_all | solution.py:90
  23.1 6.7 gather_fusion.7
  29.8 8.3 broadcast_select_fusion
  38.1 5.0 all-to-all-start.1
  43.2 0.7 all-gather.3.cloned.1.call-update
  44.0 203.6 %all-to-all-done.1 = bf16[16,576,512]{2,1,0:T(8,128)(2,1)} async-done(((bf16[16,576,512]{2,1,0:T(8,128)(2,1)}), bf16[16,576,512]{2,1,0:T(8,128)(2,1)}, u32[]{:S(2)}, u32[]{:S(2)}) %all-to-all-start.1) | async-done | bytes 9437216 | tf_op jit(solution)/shard_map/all_to_all | solution.py:95
  247.6 0.6 copy-done.2
  248.2 0.7 gather_fusion.4
  249.1 0.7 gather_fusion.6
  250.1 0.7 gather_fusion.10
  250.7 0.7 gather_fusion.9
  251.5 0.5 broadcast.652
  252.0 0.8 fusion.31
  253.0 0.6 add.198
  253.6 0.6 gather_fusion.11
  254.2 0.6 gather_fusion.13
  254.9 0.6 all_to_all.17
  255.5 3.6 all-to-all-start.2
  259.2 69.7 %gather_fusion.12 = bf16[8192]{0:T(1024)(128)(2,1)S(1)} fusion(bf16[16,576]{1,0:T(8,128)(2,1)S(1)} %broadcast_select_fusion.2, s32[8192]{0:T(1024)S(1)} %bitcast.138), kind=kCustom, calls=%fused_computation.2.clone | custom fusion | bytes 98304 | tf_op jit(solution)/shard_map/jit(take_along_axis)/gather | solution.py:69
  329.0 0.6 fusion.18
  329.6 0.6 gather_fusion.8
  330.3 69.7 %gather_fusion.14 = bf16[8192]{0:T(1024)(128)(2,1)S(1)} fusion(bf16[16,576]{1,0:T(8,128)(2,1)S(1)} %broadcast_select_fusion.3, s32[8192]{0:T(1024)S(1)} %bitcast.137), kind=kCustom, calls=%fused_computation.7.clone | custom fusion | bytes 98304 | tf_op jit(solution)/shard_map/jit(take_along_axis)/gather | solution.py:69
  400.1 0.6 fusion.19
  400.7 427.8 %while.10 = (s32[]{:T(128)}, f32[4,4,512,512]{3,2,1,0:T(8,128)}, s32[4,4]{1,0:T(4,128)S(1)}, bf16[4,576,1024]{2,1,0:T(8,128)(2,1)}, s32[4,4,512]{2,1,0:T(4,128)S...) while((s32[]{:T(128)}, f32[4,4,512,512]{3,2,1,0:T(8,128)}, ...), condition=%wide.region_5.7_spmd, body=%wide.region_4.6_spmd.sunk | while | flops 2151731200 | bytes 48357652 | solution.py:63
  400.8 9.4 %gather_fusion = bf16[4,576,1024]{2,1,0:T(8,128)(2,1)} fusion(bf16[16,576,1024]{2,1,0:T(8,128)(2,1)} %get-tuple-element.186, s32[4]{0:T(128)S(1)} %get-tuple-element.156), kind=kCustom, calls=%fused_computation.5.clone.1 | custom fusion | bytes 9437232 | tf_op jit(solution)/shard_map/while/body/eval_jaxpr/vmap(jit(dynamic_index_in_dim))/gather | solution.py:31
  410.2 42.0 %gather_fusion.1 = bf16[2048,1024]{1,0:T(8,128)(2,1)} fusion(bf16[4,576,1024]{2,1,0:T(8,128)(2,1)} %gather_fusion, s32[2048]{0:T(1024)S(1)} %bitcast.136), kind=kCustom, calls=%fused_computation.3.clone.clone.1 | custom fusion | bytes 8404992 | tf_op jit(solution)/shard_map/while/body/eval_jaxpr/vmap(jit(_take))/gather | solution.py:33
  452.2 5.4 gather_fusion.2
  457.6 42.1 %gather_fusion.3 = bf16[2048,1024]{1,0:T(8,128)(2,1)} fusion(bf16[4,576,1024]{2,1,0:T(8,128)(2,1)} %gather_fusion.2, s32[2048]{0:T(1024)S(1)} %bitcast.135), kind=kCustom, calls=%fused_computation.clone.clone.1 | custom fusion | bytes 8404992 | tf_op jit(solution)/shard_map/while/body/eval_jaxpr/vmap(jit(_take))/gather | solution.py:32
  499.7 7.9 bitcast_dynamic-update-slice_fusion.2
  507.7 9.4 %gather_fusion = bf16[4,576,1024]{2,1,0:T(8,128)(2,1)} fusion(bf16[16,576,1024]{2,1,0:T(8,128)(2,1)} %get-tuple-element.186, s32[4]{0:T(128)S(1)} %get-tuple-element.156), kind=kCustom, calls=%fused_computation.5.clone.1 | custom fusion | bytes 9437232 | tf_op jit(solution)/shard_map/while/body/eval_jaxpr/vmap(jit(dynamic_index_in_dim))/gather | solution.py:31
  517.1 42.0 %gather_fusion.1 = bf16[2048,1024]{1,0:T(8,128)(2,1)} fusion(bf16[4,576,1024]{2,1,0:T(8,128)(2,1)} %gather_fusion, s32[2048]{0:T(1024)S(1)} %bitcast.136), kind=kCustom, calls=%fused_computation.3.clone.clone.1 | custom fusion | bytes 8404992 | tf_op jit(solution)/shard_map/while/body/eval_jaxpr/vmap(jit(_take))/gather | solution.py:33
  559.2 5.4 gather_fusion.2
  564.5 42.1 %gather_fusion.3 = bf16[2048,1024]{1,0:T(8,128)(2,1)} fusion(bf16[4,576,1024]{2,1,0:T(8,128)(2,1)} %gather_fusion.2, s32[2048]{0:T(1024)S(1)} %bitcast.135), kind=kCustom, calls=%fused_computation.clone.clone.1 | custom fusion | bytes 8404992 | tf_op jit(solution)/shard_map/while/body/eval_jaxpr/vmap(jit(_take))/gather | solution.py:32
  606.6 8.0 bitcast_dynamic-update-slice_fusion.2
  614.7 9.4 %gather_fusion = bf16[4,576,1024]{2,1,0:T(8,128)(2,1)} fusion(bf16[16,576,1024]{2,1,0:T(8,128)(2,1)} %get-tuple-element.186, s32[4]{0:T(128)S(1)} %get-tuple-element.156), kind=kCustom, calls=%fused_computation.5.clone.1 | custom fusion | bytes 9437232 | tf_op jit(solution)/shard_map/while/body/eval_jaxpr/vmap(jit(dynamic_index_in_dim))/gather | solution.py:31
  624.1 42.0 %gather_fusion.1 = bf16[2048,1024]{1,0:T(8,128)(2,1)} fusion(bf16[4,576,1024]{2,1,0:T(8,128)(2,1)} %gather_fusion, s32[2048]{0:T(1024)S(1)} %bitcast.136), kind=kCustom, calls=%fused_computation.3.clone.clone.1 | custom fusion | bytes 8404992 | tf_op jit(solution)/shard_map/while/body/eval_jaxpr/vmap(jit(_take))/gather | solution.py:33
  666.1 5.4 gather_fusion.2
  671.5 42.1 %gather_fusion.3 = bf16[2048,1024]{1,0:T(8,128)(2,1)} fusion(bf16[4,576,1024]{2,1,0:T(8,128)(2,1)} %gather_fusion.2, s32[2048]{0:T(1024)S(1)} %bitcast.135), kind=kCustom, calls=%fused_computation.clone.clone.1 | custom fusion | bytes 8404992 | tf_op jit(solution)/shard_map/while/body/eval_jaxpr/vmap(jit(_take))/gather | solution.py:32
  713.6 8.0 bitcast_dynamic-update-slice_fusion.2
  721.7 9.4 %gather_fusion = bf16[4,576,1024]{2,1,0:T(8,128)(2,1)} fusion(bf16[16,576,1024]{2,1,0:T(8,128)(2,1)} %get-tuple-element.186, s32[4]{0:T(128)S(1)} %get-tuple-element.156), kind=kCustom, calls=%fused_computation.5.clone.1 | custom fusion | bytes 9437232 | tf_op jit(solution)/shard_map/while/body/eval_jaxpr/vmap(jit(dynamic_index_in_dim))/gather | solution.py:31
  731.1 42.0 %gather_fusion.1 = bf16[2048,1024]{1,0:T(8,128)(2,1)} fusion(bf16[4,576,1024]{2,1,0:T(8,128)(2,1)} %gather_fusion, s32[2048]{0:T(1024)S(1)} %bitcast.136), kind=kCustom, calls=%fused_computation.3.clone.clone.1 | custom fusion | bytes 8404992 | tf_op jit(solution)/shard_map/while/body/eval_jaxpr/vmap(jit(_take))/gather | solution.py:33
  773.1 5.4 gather_fusion.2
  778.5 42.1 %gather_fusion.3 = bf16[2048,1024]{1,0:T(8,128)(2,1)} fusion(bf16[4,576,1024]{2,1,0:T(8,128)(2,1)} %gather_fusion.2, s32[2048]{0:T(1024)S(1)} %bitcast.135), kind=kCustom, calls=%fused_computation.clone.clone.1 | custom fusion | bytes 8404992 | tf_op jit(solution)/shard_map/while/body/eval_jaxpr/vmap(jit(_take))/gather | solution.py:32
  820.6 7.9 bitcast_dynamic-update-slice_fusion.2
  828.5 7.0 neg.6
  835.5 5.7 fusion.15
  (91 shorter events, 2.2 us)
Async XLA Ops:
  6.5 247.1 %copy-start = (bf16[4,576]{1,0:T(4,128)(2,1)S(1)}, bf16[4,576]{1,0:T(4,128)(2,1)}, u32[]{:S(2)}) copy-start(bf16[4,576]{1,0:T(4,128)(2,1)} %param.15) | copy-start | bytes 13828
  38.1 209.4 %all-to-all-start.1 = ((bf16[16,576,512]{2,1,0:T(8,128)(2,1)}), bf16[16,576,512]{2,1,0:T(8,128)(2,1)}, u32[]{:S(2)}, u32[]{:S(2)}) async-start(bf16[16,576,512]{2,1,0:T(8,128)(2,1)} %broadcast_select_fusion), calls=%async_computation.1 | async-start | bytes 18874368 | tf_op jit(solution)/shard_map/all_to_all | solution.py:95
  43.2 357.5 %all-gather.3.cloned.1.call-start = ((), (), s32[]{:S(2)}) async-start(), calls=%async_computation.3 | async-start | bytes 7077888 | tf_op jit(solution)/shard_map/all_gather | solution.py:102
  43.9 356.8 %all-gather.5.cloned.1.call-start = ((), (), s32[]{:S(2)}) async-start(), calls=%async_computation.4 | async-start | bytes 28311552 | tf_op jit(solution)/shard_map/all_gather | solution.py:101
  247.6 0.7 copy-start.2
  247.6 2.4 copy-start.7
  247.6 2.5 copy-start.3
  247.6 3.8 copy-start.6
  255.5 74.1 %all-to-all-start.2 = ((bf16[8,2,576]{2,1,0:T(2,128)(2,1)}), bf16[8,2,576]{2,1,0:T(2,128)(2,1)S(1)}, u32[]{:S(2)}, u32[]{:S(2)}) async-start(bf16[8,2,576]{2,1,0:T(2,128)(2,1)} %all_to_all.17), calls=%async_computation.2 | async-start | bytes 40960 | tf_op jit(solution)/shard_map/all_to_all | solution.py:96
  828.4 7.0 copy-start.4
  828.4 7.0 copy-start.5
  828.5 7.0 copy-start.8
  835.5 5.7 copy-start.1
Sparse Core Ops, SparseCore 0:
  45.6 15.8 all-gather.2
  247.7 32.9 all-gather.4
where the time goes:
time: 854 us; the launch traced here: 848 us
  local copies, waits for them, and re-layouts  551 us (65%)
  waiting for transfers between devices  204 us (24%)
  matrix products  31.7 us (4%)
  other arithmetic  24.8 us (3%)
  between operations  13.7 us (2%)
  blocking collectives  13.5 us (2%)
  starting transfers between devices  8.73 us (1%)
    all_to_all x1, waiting for transfers between devices, per_device(): lax.all_to_all(send_blocks, 'orb', split_axis=0, concat_axis=0, tiled=True)  204 us
    gather x4, local copies, waits for them, and re-layouts, pair_integrals(): chosen_one = jnp.take(block_one, cols_one, axis=0)  168 us
    gather x4, local copies, waits for them, and re-layouts, pair_integrals(): chosen_two = jnp.take(block_two, cols_two, axis=0)  168 us
    gather x4, local copies, waits for them, and re-layouts, domain_energy(): return jnp.take_along_axis(rows, cols, axis=1).astype(jnp.float32)  139 us
    gather x4, local copies, waits for them, and re-layouts, pair_integrals(): lax.dynamic_index_in_dim(partner_blocks, slot_two, 0, keepdims=False)  37.6 us
    dot_general x4, matrix products, pair_integrals(): lax.dot_general(chosen_one, chosen_two, (((1,), (1,)), ((), ())), preferr...  31.7 us
    gather x4, local copies, waits for them, and re-layouts, pair_integrals(): lax.dynamic_index_in_dim(local_blocks, slot_one, 0, keepdims=False)  21.5 us
  transfers between devices with their start and end apart: 4, of which 1 were waited for; matrix products, arithmetic and copies ran while one was open for 17% of the time, Pallas kernels for 0%

commit v1 on v0

v1 whole, which is shorter than its diff:
```python
import functools

import jax
import jax.numpy as jnp
from jax import lax
from jax.experimental import pallas as pl
from jax.experimental.pallas import tpu as pltpu
from jax.sharding import PartitionSpec as P

NT = (((1,), (1,)), ((), ()))


def windows(full, kept):
    slack = full - kept
    tile = 256 - slack if 0 <= slack <= 128 else kept
    found = []
    base = 0
    while base < kept:
        rows = min(tile, kept - base)
        found.append((base, rows, rows + slack))
        base += rows
    return found


def pair_kernel(
    call, wins, has_prev,
    meta_ref, shift_ref, dom_ref, ve1_ref, ve2_ref,
    own_ref, other_ref, a_own, a_other, b_own, b_other, *rest,
):
    if has_prev:
        rest = rest[1:]
    out_ref, first, second, side_a, side_b, e1_buf, out_buf, first_sem, second_sem, out_sem = rest
    pairs_here = out_ref.shape[0]
    kept = out_ref.shape[1]
    half = own_ref.shape[2]
    n_first = first.shape[0]
    lo = meta_ref[0, call]
    hi = meta_ref[0, call + 1]
    base_first = meta_ref[1, 0]

    def first_copies():
        out = []
        for k in range(n_first):
            out.append(pltpu.make_async_copy(
                own_ref.at[base_first + k], first.at[k, :, pl.ds(0, half)], first_sem.at[2 * k]))
            out.append(pltpu.make_async_copy(
                other_ref.at[base_first + k], first.at[k, :, pl.ds(half, half)], first_sem.at[2 * k + 1]))
        return out

    def fetch(i, slot):
        p = meta_ref[2, i]
        which = meta_ref[3, p]
        idx = meta_ref[4, p]

        def go(x_own, x_other):
            pltpu.make_async_copy(
                x_own.at[idx], second.at[slot, :, pl.ds(0, half)], second_sem.at[slot, 0]).start()
            pltpu.make_async_copy(
                x_other.at[idx], second.at[slot, :, pl.ds(half, half)], second_sem.at[slot, 1]).start()

        @pl.when(which == 0)
        def _():
            go(a_own, a_other)

        @pl.when(which == 1)
        def _():
            go(b_own, b_other)

    def await_fetch(slot):
        for k in range(2):
            pltpu.make_async_copy(
                a_own.at[0], second.at[slot, :, pl.ds(k * half, half)], second_sem.at[slot, k]).wait()

    def out_copy(p, slot):
        return pltpu.make_async_copy(out_buf.at[slot], out_ref.at[p], out_sem.at[slot])

    @pl.when(hi > lo)
    def _():
        for c in first_copies():
            c.start()
        fetch(lo, lax.rem(lo, 2))
        for c in first_copies():
            c.wait()

    lanes = lax.broadcasted_iota(jnp.int32, (kept, 128), 1)

    def step(i, carry):
        slot = lax.rem(i, 2)
        p = meta_ref[2, i]
        f = p // (pairs_here // n_first)

        @pl.when(i + 1 < hi)
        def _():
            fetch(i + 1, 1 - slot)

        def chosen(side):
            wanted = jnp.where(lanes == 2 * p + side, dom_ref[...], 0.0)
            return jnp.sum(wanted, axis=1, keepdims=True)

        cols1 = chosen(0)
        cols2 = chosen(1)
        for base, rows, span in wins:
            kk = lax.broadcasted_iota(jnp.int32, (rows, span), 1).astype(jnp.float32) + float(base)
            hit = cols1[base:base + rows] == kk
            ve = ve1_ref[p, :, base:base + span]
            e1 = jnp.sum(jnp.where(hit, ve, 0.0), axis=1, keepdims=True)
            e1_buf[base:base + rows, :] = jnp.broadcast_to(e1, (rows, 128))
            pick = jnp.where(hit, 1.0, 0.0).astype(jnp.bfloat16)
            got = jnp.dot(pick, first[f, base:base + span, :], preferred_element_type=jnp.float32)
            side_a[base:base + rows, :] = got.astype(jnp.bfloat16)
        await_fetch(slot)
        e2_parts = []
        for base, rows, span in wins:
            kk = lax.broadcasted_iota(jnp.int32, (rows, span), 1).astype(jnp.float32) + float(base)
            hit = cols2[base:base + rows] == kk
            pick = jnp.where(hit, 1.0, 0.0).astype(jnp.bfloat16)
            got = jnp.dot(pick, second[slot, base:base + span, :], preferred_element_type=jnp.float32)
            side_b[base:base + rows, :] = got.astype(jnp.bfloat16)
            ve = jnp.broadcast_to(ve2_ref[p, :, base:base + span], (8, span)).astype(jnp.bfloat16)
            e2_parts.append(
                lax.dot_general(ve, pick, NT, preferred_element_type=jnp.float32)[0:1])
        e2 = jnp.concatenate(e2_parts, axis=1)

        @pl.when(i >= lo + 2)
        def _():
            out_copy(p, slot).wait()

        shift = shift_ref[p]
        chunk = 256
        for r in range(0, kept, chunk):
            c = lax.dot_general(
                side_a[r:r + chunk, :], side_b[...], NT, preferred_element_type=jnp.float32)
            for col in range(0, kept, 128):
                den = e1_buf[r:r + chunk, :] + e2[:, col:col + 128] - shift
                inv = pl.reciprocal(den, approx=True)
                neg = inv * (den * inv - 2.0)
                out_buf[slot, r:r + chunk, col:col + 128] = (
                    c[:, col:col + 128] * neg).astype(jnp.bfloat16)
        out_copy(p, slot).start()
        return carry

    lax.fori_loop(lo, hi, step, 0)

    @pl.when(hi - lo >= 2)
    def _():
        out_copy(0, lax.rem(hi, 2)).wait()

    @pl.when(hi > lo)
    def _():
        out_copy(0, lax.rem(hi + 1, 2)).wait()


def run_pairs(call, expected, meta, shift, dom, ve1, ve2, own, other, col_arrays, opp_arrays, prev, n_first):
    pairs_here = ve1.shape[0]
    full, half = own.shape[1], own.shape[2]
    kept = dom.shape[0]
    wins = windows(full, kept)
    any_spec = pl.BlockSpec(memory_space=pl.ANY)
    smem = pl.BlockSpec(memory_space=pltpu.SMEM)
    vmem = pl.BlockSpec(memory_space=pltpu.VMEM)
    operands = [meta, shift, dom, ve1, ve2, own, other, *col_arrays, *opp_arrays]
    in_specs = [smem, smem, vmem, vmem, vmem] + [any_spec] * 6
    aliases = {}
    if prev is not None:
        aliases = {len(operands): 0}
        operands.append(prev)
        in_specs.append(any_spec)
    bf = jnp.bfloat16
    return pl.pallas_call(
        functools.partial(pair_kernel, call, wins, prev is not None),
        out_shape=jax.ShapeDtypeStruct((pairs_here, kept, kept), bf),
        in_specs=in_specs,
        out_specs=any_spec,
        scratch_shapes=[
            pltpu.VMEM((n_first, full, 2 * half), bf),
            pltpu.VMEM((2, full, 2 * half), bf),
            pltpu.VMEM((kept, 2 * half), bf),
            pltpu.VMEM((kept, 2 * half), bf),
            pltpu.VMEM((kept, 128), jnp.float32),
            pltpu.VMEM((2, kept, kept), bf),
            pltpu.SemaphoreType.DMA((2 * n_first,)),
            pltpu.SemaphoreType.DMA((2, 2)),
            pltpu.SemaphoreType.DMA((2,)),
        ],
        input_output_aliases=aliases,
        compiler_params=pltpu.CompilerParams(vmem_limit_bytes=40 * 1024 * 1024),
        cost_estimate=pl.CostEstimate(
            flops=int(expected * 4 * kept * kept * 2 * half * 2),
            bytes_accessed=int(expected * (full * half * 4 + kept * kept * 2)),
            transcendentals=0),
        name=f"pairs_{call}",
    )(*operands)


def picks(source, i0, i1):
    return [lax.dynamic_slice_in_dim(source, i0, 1, 0), lax.dynamic_slice_in_dim(source, i1, 1, 0)]


def per_device(blocks, virt_energy, occ_energy, owner_slot, pairs, domains):
    orb_count = lax.axis_size("orb")
    aux_count = lax.axis_size("aux")
    occ_dev, full, half = blocks.shape
    pair_dev = pairs.shape[0]
    kept = domains.shape[2]
    own_rows = pair_dev // aux_count
    n_first = occ_dev // aux_count
    core = lax.axis_index("aux")
    o = lax.axis_index("orb")
    z, y = o // 2, o % 2
    chain = orb_count // 2
    n_slots = orb_count * occ_dev

    def over(axis, perm, *arrays):
        got = [lax.ppermute(a, axis, perm) for a in arrays]
        return got if len(got) > 1 else got[0]

    swap_aux = [(0, 1), (1, 0)]
    swap_y = [(k, k ^ 1) for k in range(orb_count)]

    def down_perm(d):
        return [(k, k - 2) for k in range(2, orb_count) if k // 2 <= chain - d]

    def up_perm(d):
        return [(k, k + 2) for k in range(orb_count - 2) if k // 2 >= d - 1]

    downs, ups = [], []
    down, up = blocks, blocks
    for d in range(1, chain):
        down = over("orb", down_perm(d), down)
        up = over("orb", up_perm(d), up)
        downs.append(down)
        ups.append(up)
    local_other = over("aux", swap_aux, blocks)
    ve_all = lax.all_gather(virt_energy, "orb", axis=0, tiled=True)

    orbitals = jnp.arange(owner_slot.shape[0], dtype=jnp.int32)
    hit_second = pairs[:, 1][:, None] == orbitals[None, :]
    slot_second = jnp.sum(jnp.where(hit_second, owner_slot[None, :], 0), axis=1)
    slots = jnp.arange(n_slots, dtype=jnp.int32)
    wanted = jnp.any(slot_second[:, None] == slots[None, :], axis=0).reshape(orb_count, occ_dev)
    local = jnp.arange(occ_dev, dtype=jnp.int32)[None, :]
    want_lo = jnp.min(jnp.where(wanted, local, occ_dev - 1), axis=1)
    want_hi = jnp.max(jnp.where(wanted, local, 0), axis=1)
    want = jnp.stack([want_lo, want_hi])
    want_opp = over("orb", swap_y, want)

    first_row = core * own_rows
    own_second = lax.dynamic_slice_in_dim(slot_second, first_row, own_rows, 0)
    own_pairs = lax.dynamic_slice_in_dim(pairs, first_row, own_rows, 0)
    src = own_second // occ_dev
    part = own_second % occ_dev
    rank = jnp.any(
        (slot_second[None, :] // occ_dev == src[:, None]) & (slot_second[None, :] < own_second[:, None]),
        axis=1).astype(jnp.int32)
    src_z, src_y = src // 2, src % 2
    dist = jnp.abs(src_z - z)
    is_opp = (src_y != y).astype(jnp.int32)
    from_up = src_z < z
    both = 2 * dist <= chain - 1
    idx = jnp.where(
        dist == 0,
        jnp.where(is_opp == 1, rank, part),
        rank + jnp.where(both & from_up, 2, 0))
    rows = jnp.arange(own_rows, dtype=jnp.int32)
    before = (dist[None, :] < dist[:, None]) | ((dist[None, :] == dist[:, None]) & (rows[None, :] < rows[:, None]))
    place = jnp.sum(before.astype(jnp.int32), axis=1)
    order = jnp.sum(jnp.where(place[None, :] == rows[:, None], rows[None, :], 0), axis=1)
    bounds = jnp.sum((dist[None, :] < jnp.arange(chain + 1, dtype=jnp.int32)[:, None]).astype(jnp.int32), axis=1)
    width = max(own_rows, chain + 1)

    def padded(v):
        v = v.reshape(-1)
        return jnp.pad(v, (0, width - v.shape[0]))

    meta = jnp.stack([padded(bounds), padded(core * n_first), padded(order), padded(is_opp), padded(idx)])

    def occ(col):
        hit = own_pairs[:, col][:, None] == orbitals[None, :]
        return jnp.sum(jnp.where(hit, occ_energy[None, :], 0.0), axis=1)

    shift = occ(0) + occ(1)
    first_slot = o * occ_dev + core * n_first + rows // (own_rows // n_first)

    def energies(slot):
        hit = (slot[:, None] == slots[None, :]).astype(jnp.bfloat16)
        rows_of = jnp.dot(hit, ve_all, preferred_element_type=jnp.float32)
        return rows_of.reshape(own_rows, 1, full)

    ve1, ve2 = energies(first_slot), energies(own_second)
    dom = lax.dynamic_slice_in_dim(domains, first_row, own_rows, 0)
    dom = dom.reshape(2 * own_rows, kept).T.astype(jnp.float32)
    dom = jnp.pad(dom, ((0, 0), (0, 128 - 2 * own_rows)))

    def idx_of(table, row, source):
        return lax.dynamic_index_in_dim(table[row], jnp.clip(source, 0, orb_count - 1), 0, keepdims=False)

    def chosen(arrays, table, sources):
        got = []
        for a, s in zip(arrays, sources):
            got += picks(a, idx_of(table, 0, s), idx_of(table, 1, s))
        return jnp.concatenate(got, axis=0)

    y_own = over("orb", swap_y, chosen([blocks], want_opp, [o]))
    y_other = over("aux", swap_aux, y_own)
    out = run_pairs(
        0, own_rows / 4, meta, shift, dom, ve1, ve2, blocks, local_other,
        (blocks, local_other), (y_own, y_other), None, n_first)
    for d in range(1, chain):
        down, up = downs[d - 1], ups[d - 1]
        s_down, s_up = o + 2 * d, o - 2 * d
        if 2 * d <= chain - 1:
            mine = chosen([down, up], want, [s_down, s_up])
            theirs = chosen([down, up], want_opp, [s_down, s_up])
        else:
            is_down = z + d <= chain - 1
            s = jnp.where(is_down, s_down, s_up)
            mine = jnp.where(is_down, chosen([down], want, [s]), chosen([up], want, [s]))
            theirs = jnp.where(is_down, chosen([down], want_opp, [s]), chosen([up], want_opp, [s]))
        mine_other = over("aux", swap_aux, mine)
        opp_own = over("orb", swap_y, theirs)
        opp_other = over("aux", swap_aux, opp_own)
        out = run_pairs(
            d, own_rows / 4, meta, shift, dom, ve1, ve2, blocks, local_other,
            (mine, mine_other), (opp_own, opp_other), out, n_first)
    return out


def solution(mesh):
    in_specs = (
        P(("groups", "orb"), None, "aux"),
        P(("groups", "orb"), None),
        P("groups"),
        P("groups"),
        P(("groups", "orb"), None),
        P(("groups", "orb"), None, None),
    )
    out_specs = P(("groups", "orb", "aux"), None, None)
    return jax.shard_map(
        per_device, mesh=mesh, in_specs=in_specs, out_specs=out_specs, check_vma=False
    )
```

time: 854 us -> 310 us (0.36)
  local copies, waits for them, and re-layouts: 551 us -> 20 us
  waiting for transfers between devices: 204 us -> 103 us
  blocking collectives: 13.5 us -> 72.6 us
  Pallas kernels: 0 us -> 41.3 us
  matrix products: 31.7 us -> 0.38 us
  between operations: 13.7 us -> 34.3 us
  other arithmetic: 24.8 us -> 11.2 us
  starting transfers between devices: 8.73 us -> 21.7 us
    gather x29 -> x0, local copies, waits for them, and re-layouts: 548 us -> none  [the longest x4 168 us: pair_integrals(): chosen_one = jnp.take(block_one, cols_one, axis=0)]
    all_to_all x2 -> x0, waiting for transfers between devices: 204 us -> none  [the longest x1 204 us: per_device(): lax.all_to_all(send_blocks, 'orb', split_axis=0, concat_axis=0, tiled=True)]
    ppermute x0 -> x19, waiting for transfers between devices: none -> 103 us  [over(): got = [lax.ppermute(a, axis, perm) for a in arrays]]
    all_gather x0 -> x1, blocking collectives: none -> 72.6 us  [per_device(): ve_all = lax.all_gather(virt_energy, 'orb', axis=0, tiled=True)]
    pallas_call x0 -> x4, Pallas kernels: none -> 41.3 us  [run_pairs(): pl.pallas_call(functools.partial(pair_kernel, call, wins, prev is not Non...]
    dot_general x4 -> x2, matrix products: 31.7 us -> 0.38 us  [energies(): rows_of = jnp.dot(hit, ve_all, preferred_element_type=jnp.float32)]
    ppermute x0 -> x19, starting transfers between devices: none -> 21.7 us  [over(): got = [lax.ppermute(a, axis, perm) for a in arrays]]
    dynamic_slice x3 -> x10, local copies, waits for them, and re-layouts: 1.42 us -> 18.8 us  [the longest x7 16.7 us: picks(): lax.dynamic_slice_in_dim(source, i0, 1, 0)]
  transfers between devices with their start and end apart: 4 -> 19, of which waited for: 1 -> 6; matrix products, arithmetic and copies ran while one was open for 17% -> 10% of each run, Pallas kernels for 0% -> 9%
where the time goes in v1:
time: 310 us; the launch traced here: 305 us
  waiting for transfers between devices  103 us (33%)
  blocking collectives  72.6 us (23%)
  Pallas kernels  41.3 us (13%)
  between operations  34.3 us (11%)
  starting transfers between devices  21.7 us (7%)
  local copies, waits for them, and re-layouts  20 us (6%)
  other arithmetic  11.2 us (4%)
    ppermute x19, waiting for transfers between devices, over(): got = [lax.ppermute(a, axis, perm) for a in arrays]  103 us
    all_gather x1, blocking collectives, per_device(): ve_all = lax.all_gather(virt_energy, 'orb', axis=0, tiled=True)  72.6 us
    pallas_call x4, Pallas kernels, run_pairs(): pl.pallas_call(functools.partial(pair_kernel, call, wins, prev is not Non...  41.3 us
    ppermute x19, starting transfers between devices, over(): got = [lax.ppermute(a, axis, perm) for a in arrays]  21.7 us
    dynamic_slice x7, local copies, waits for them, and re-layouts, picks(): lax.dynamic_slice_in_dim(source, i0, 1, 0)  16.7 us
  transfers between devices with their start and end apart: 19, of which 6 were waited for; matrix products, arithmetic and copies ran while one was open for 10% of the time, Pallas kernels for 9%

profile of v1, /device:TPU:0, one launch (start us, length us, event | category | flops | bytes accessed | tf_op | source)
XLA Modules:
  0.0 304.6 jit_solution(9788482090957206612)
XLA Ops:
  0.0 6.4 %collective-permute-start.4 = (bf16[4,576,512]{2,1,0:T(8,128)(2,1)}, bf16[4,576,512]{2,1,0:T(8,128)(2,1)}, u32[]{:S(2)}, u32[]{:S(2)}) collective-permute-start(bf16[4,576,512]{2,1,0:T(8,128)(2,1)} %own_ref.7), channel_id=1, source_target_pairs={{0,4},{2,6},{4,8},{6,10},{8,12},{10,14},{1,5},{3,7},{5,9},{7,11},{... | collective-permute-start | bytes 7077896 | tf_op jit(solution)/shard_map/ppermute | solution.py:214
  6.4 1.3 collective-permute-start.1
  7.7 48.0 %collective-permute-done.4 = bf16[4,576,512]{2,1,0:T(8,128)(2,1)} collective-permute-done((bf16[4,576,512]{2,1,0:T(8,128)(2,1)}, bf16[4,576,512]{2,1,0:T(8,128)(2,1)}, u32[]{:S(2)}, u32[]{:S(2)}) %collective-permute-start.4) | collective-permute-done | bytes 2359328 | tf_op jit(solution)/shard_map/ppermute | solution.py:214
  55.7 2.1 collective-permute-start.5
  57.8 3.5 %collective-permute-done.1 = bf16[4,576,512]{2,1,0:T(8,128)(2,1)} collective-permute-done((bf16[4,576,512]{2,1,0:T(8,128)(2,1)}, bf16[4,576,512]{2,1,0:T(8,128)(2,1)}, u32[]{:S(2)}, u32[]{:S(2)}) %collective-permute-start.1) | collective-permute-done | bytes 2359328 | tf_op jit(solution)/shard_map/ppermute | solution.py:214
  61.3 1.3 collective-permute-start.2
  62.7 0.7 slice_bitcast_fusion.2
  63.4 0.8 select_reduce_fusion
  64.4 0.2 select_reduce_fusion.5
  64.6 1.6 collective-permute-start.8
  66.1 0.7 fusion.11
  74.4 0.8 constant_dynamic-slice_fusion.36
  75.2 0.7 constant_dynamic-slice_fusion.1
  83.6 2.6 constant_dynamic-slice_fusion.10
  86.2 2.8 constant_dynamic-slice_fusion.6
  89.0 1.7 pad_maximum_fusion.1
  90.7 0.5 collective-permute-start.15
  91.3 0.2 select_reduce_fusion.1
  91.5 2.1 collective-permute-start.6
  93.7 21.8 %collective-permute-done.2 = bf16[4,576,512]{2,1,0:T(8,128)(2,1)} collective-permute-done((bf16[4,576,512]{2,1,0:T(8,128)(2,1)}, bf16[4,576,512]{2,1,0:T(8,128)(2,1)}, u32[]{:S(2)}, u32[]{:S(2)}) %collective-permute-start.2) | collective-permute-done | bytes 2359328 | tf_op jit(solution)/shard_map/ppermute | solution.py:214
  115.4 1.3 collective-permute-start.3
  116.7 72.6 %all-gather = bf16[8,4,576]{2,1,0:T(4,128)(2,1)S(1)} all-gather(bf16[1,4,576]{2,1,0:T(4,128)(2,1)S(1)} %bitcast.42), channel_id=1, replica_groups=mesh['groups'=2,'orb'=8,'aux'=2] {'orb'}, dimensions={0}, use_global_device_ids=true | all-gather | bytes 41472 | tf_op jit(solution)/shard_map/all_gather | solution.py:234
  189.4 0.2 fusion.4
  189.6 0.2 fusion.3
  193.6 1.1 pad_maximum_fusion.2
  194.7 1.6 collective-permute-start.17
  204.1 0.2 and_reduce_fusion
  208.0 1.7 pad_maximum_fusion.a_own
  209.8 2.8 constant_dynamic-slice_fusion.17
  212.6 2.3 collective-permute-done.17.b_own
  214.9 0.5 collective-permute-start.16
  215.4 2.8 constant_dynamic-slice_fusion.20
  218.2 1.2 maximum_select_fusion.3
  219.4 1.5 collective-permute-start.12
  221.0 0.2 convert_reduce_fusion
  225.1 2.8 constant_dynamic-slice_fusion.27
  227.9 2.8 constant_dynamic-slice_fusion.30
  230.7 1.3 maximum_select_fusion.1
  231.9 0.8 collective-permute-start.9
  232.8 2.0 maximum_select_fusion.2.a_own
  234.9 13.7 %collective-permute-done.12.b_own = bf16[2,576,512]{2,1,0:T(8,128)(2,1)} collective-permute-done((bf16[2,576,512]{2,1,0:T(8,128)(2,1)}, bf16[2,576,512]{2,1,0:T(8,128)(2,1)}, u32[]{:S(2)}, u32[]{:S(2)}) %collective-permute-start.12) | collective-permute-done | bytes 1179680 | tf_op jit(solution)/shard_map/ppermute | solution.py:214
  248.6 10.1 %pairs_0.1.rest_0_ = bf16[16,512,512]{2,1,0:T(8,128)(2,1)} custom-call(s32[5,16]{1,0:T(8,128)S(1)} %stack.32.meta_ref, f32[16]{0:T(128)S(1)} %add.170.shift_ref, f32[512,128]{1,0:T(8,128)S(1)} %pad.14.dom_ref, f32[16,1,576]{2,1,0:T(1,128)S(1)} %reshape.93.ve1_ref, f32[16,1,576]{2,1,0:T(1,128)S(1)} %reshape.94.ve2_ref, bf16[4,576,512]{2,1,0:T(8,128)(2,1)S(1)} %copy-done.1, ...), custom_call_target="tpu_custom_call" | custom-call | flops 8589934592 | bytes 6815744 | tf_op jit(solution)/shard_map/pairs_0/pallas_call | solution.py:169
  258.8 0.2 maximum_select_fusion.a_own
  259.0 0.7 collective-permute-start.7
  259.7 13.7 %collective-permute-done.9.b_own = bf16[2,576,512]{2,1,0:T(8,128)(2,1)} collective-permute-done((bf16[2,576,512]{2,1,0:T(8,128)(2,1)}, bf16[2,576,512]{2,1,0:T(8,128)(2,1)}, u32[]{:S(2)}, u32[]{:S(2)}) %collective-permute-start.9) | collective-permute-done | bytes 1179680 | tf_op jit(solution)/shard_map/ppermute | solution.py:214
  273.4 10.1 %pairs_1.1.rest_0_ = bf16[16,512,512]{2,1,0:T(8,128)(2,1)} custom-call(s32[5,16]{1,0:T(8,128)S(1)} %stack.32.meta_ref, f32[16]{0:T(128)S(1)} %add.170.shift_ref, f32[512,128]{1,0:T(8,128)S(1)} %pad.14.dom_ref, f32[16,1,576]{2,1,0:T(1,128)S(1)} %reshape.93.ve1_ref, f32[16,1,576]{2,1,0:T(1,128)S(1)} %reshape.94.ve2_ref, ...), custom_call_target="tpu_custom_call", output_to_operand_aliasing={{}: (11, {})} | custom-call | flops 8589934592 | bytes 6815744 | tf_op jit(solution)/shard_map/pairs_1/pallas_call | solution.py:169
  283.6 6.6 %pairs_2.1.rest_0_ = bf16[16,512,512]{2,1,0:T(8,128)(2,1)} custom-call(s32[5,16]{1,0:T(8,128)S(1)} %stack.32.meta_ref, f32[16]{0:T(128)S(1)} %add.170.shift_ref, f32[512,128]{1,0:T(8,128)S(1)} %pad.14.dom_ref, f32[16,1,576]{2,1,0:T(1,128)S(1)} %reshape.93.ve1_ref, f32[16,1,576]{2,1,0:T(1,128)S(1)} %reshape.94.ve2_ref, ...), custom_call_target="tpu_custom_call", output_to_operand_aliasing={{}: (11, {})} | custom-call | flops 8589934592 | bytes 6815744 | tf_op jit(solution)/shard_map/pairs_2/pallas_call | solution.py:169
  290.2 14.4 %pairs_3.1 = bf16[16,512,512]{2,1,0:T(8,128)(2,1)} custom-call(s32[5,16]{1,0:T(8,128)S(1)} %stack.32.meta_ref, f32[16]{0:T(128)S(1)} %add.170.shift_ref, f32[512,128]{1,0:T(8,128)S(1)} %pad.14.dom_ref, f32[16,1,576]{2,1,0:T(1,128)S(1)} %reshape.93.ve1_ref, f32[16,1,576]{2,1,0:T(1,128)S(1)} %reshape.94.ve2_ref, ...), custom_call_target="tpu_custom_call", output_to_operand_aliasing={{}: (11, {})} | custom-call | flops 8589934592 | bytes 6815744 | tf_op jit(solution)/shard_map/pairs_3/pallas_call | solution.py:169
  (61 shorter events, 1.2 us)
Async XLA Ops:
  0.0 55.7 %collective-permute-start.4 = (bf16[4,576,512]{2,1,0:T(8,128)(2,1)}, bf16[4,576,512]{2,1,0:T(8,128)(2,1)}, u32[]{:S(2)}, u32[]{:S(2)}) collective-permute-start(bf16[4,576,512]{2,1,0:T(8,128)(2,1)} %own_ref.7), channel_id=1, source_target_pairs={{0,4},{2,6},{4,8},{6,10},{8,12},{10,14},{1,5},{3,7},{5,9},{7,11},{... | collective-permute-start | bytes 7077896 | tf_op jit(solution)/shard_map/ppermute | solution.py:214
  6.4 54.9 %collective-permute-start.1 = (bf16[4,576,512]{2,1,0:T(8,128)(2,1)}, bf16[4,576,512]{2,1,0:T(8,128)(2,1)}, u32[]{:S(2)}, u32[]{:S(2)}) collective-permute-start(bf16[4,576,512]{2,1,0:T(8,128)(2,1)} %own_ref.7), channel_id=1, source_target_pairs={{4,0},{6,2},{8,4},{10,6},{12,8},{14,10},{5,1},{7,3},{9,5},{11,7},{... | collective-permute-start | bytes 7077896 | tf_op jit(solution)/shard_map/ppermute | solution.py:214
  55.7 35.8 %collective-permute-start.5 = (bf16[4,576,512]{2,1,0:T(8,128)(2,1)}, bf16[4,576,512]{2,1,0:T(8,128)(2,1)}, u32[]{:S(2)}, u32[]{:S(2)}) collective-permute-start(bf16[4,576,512]{2,1,0:T(8,128)(2,1)} %collective-permute-done.4), channel_id=1, source_target_pairs={{4,8},{6,10},{8,12},{10,14},{5,9},{7,11},{9,13},{11,15},{20,24},{2... | collective-permute-start | bytes 7077896 | tf_op jit(solution)/shard_map/ppermute | solution.py:214
  61.3 54.1 %collective-permute-start.2 = (bf16[4,576,512]{2,1,0:T(8,128)(2,1)}, bf16[4,576,512]{2,1,0:T(8,128)(2,1)}, u32[]{:S(2)}, u32[]{:S(2)}) collective-permute-start(bf16[4,576,512]{2,1,0:T(8,128)(2,1)} %collective-permute-done.1), channel_id=1, source_target_pairs={{4,0},{6,2},{8,4},{10,6},{5,1},{7,3},{9,5},{11,7},{20,16},{22,18},... | collective-permute-start | bytes 7077896 | tf_op jit(solution)/shard_map/ppermute | solution.py:214
  62.6 169.3 %collective-permute-start = (bf16[4,576,512]{2,1,0:T(8,128)(2,1)}, bf16[4,576,512]{2,1,0:T(8,128)(2,1)}, u32[]{:S(2)}, u32[]{:S(2)}) collective-permute-start(bf16[4,576,512]{2,1,0:T(8,128)(2,1)} %own_ref.7), channel_id=1, source_target_pairs={{0,1},{1,0},{2,3},{3,2},{4,5},{5,4},{6,7},{7,6},{8,9},{9,8},{10,11... | collective-permute-start | bytes 7077896 | tf_op jit(solution)/shard_map/ppermute | solution.py:214
  64.6 10.6 %collective-permute-start.8 = (s32[2,8]{1,0:T(2,128)S(1)}, s32[2,8]{1,0:T(2,128)S(1)}, u32[]{:S(2)}, u32[]{:S(2)}) collective-permute-start(s32[2,8]{1,0:T(2,128)S(1)} %pad_add_fusion), channel_id=1, source_target_pairs={{0,2},{2,0},{4,6},{6,4},{8,10},{10,8},{12,14},{14,12},{1,3},{3,1},... | collective-permute-start | bytes 200 | tf_op jit(solution)/shard_map/ppermute | solution.py:214
  89.0 2.3 copy-start.8
  89.0 27.7 %copy-start.7 = (bf16[4,576]{1,0:T(4,128)(2,1)S(1)}, bf16[4,576]{1,0:T(4,128)(2,1)}, u32[]{:S(2)}) copy-start(bf16[4,576]{1,0:T(4,128)(2,1)} %param.7) | copy-start | bytes 13828
  89.0 104.5 %copy-start = (bf16[4,576,512]{2,1,0:T(8,128)(2,1)S(1)}, bf16[4,576,512]{2,1,0:T(8,128)(2,1)}, u32[]{:S(2)}) copy-start(bf16[4,576,512]{2,1,0:T(8,128)(2,1)} %own_ref.7) | copy-start | bytes 7077892
  90.7 124.2 %collective-permute-start.15 = (bf16[4,576,512]{2,1,0:T(8,128)(2,1)}, bf16[4,576,512]{2,1,0:T(8,128)(2,1)}, u32[]{:S(2)}, u32[]{:S(2)}) collective-permute-start(bf16[4,576,512]{2,1,0:T(8,128)(2,1)} %pad_maximum_fusion.1), channel_id=1, source_target_pairs={{0,2},{2,0},{4,6},{6,4},{8,10},{10,8},{12,14},{14,12},{1,3},{3,1},... | collective-permute-start | bytes 7077896 | tf_op jit(solution)/shard_map/ppermute | solution.py:214
  91.5 127.9 %collective-permute-start.6 = (bf16[4,576,512]{2,1,0:T(8,128)(2,1)}, bf16[4,576,512]{2,1,0:T(8,128)(2,1)}, u32[]{:S(2)}, u32[]{:S(2)}) collective-permute-start(bf16[4,576,512]{2,1,0:T(8,128)(2,1)} %collective-permute-done.5), channel_id=1, source_target_pairs={{8,12},{10,14},{9,13},{11,15},{24,28},{26,30},{25,29},{27,31}} | collective-permute-start | bytes 7077896 | tf_op jit(solution)/shard_map/ppermute | solution.py:214
  115.4 104.0 %collective-permute-start.3 = (bf16[4,576,512]{2,1,0:T(8,128)(2,1)}, bf16[4,576,512]{2,1,0:T(8,128)(2,1)}, u32[]{:S(2)}, u32[]{:S(2)}) collective-permute-start(bf16[4,576,512]{2,1,0:T(8,128)(2,1)} %collective-permute-done.2), channel_id=1, source_target_pairs={{4,0},{6,2},{5,1},{7,3},{20,16},{22,18},{21,17},{23,19}} | collective-permute-start | bytes 7077896 | tf_op jit(solution)/shard_map/ppermute | solution.py:214
  193.6 2.7 copy-start.6
  194.7 20.1 %collective-permute-start.17 = (bf16[2,576,512]{2,1,0:T(8,128)(2,1)}, bf16[2,576,512]{2,1,0:T(8,128)(2,1)}, u32[]{:S(2)}, u32[]{:S(2)}) collective-permute-start(bf16[2,576,512]{2,1,0:T(8,128)(2,1)} %pad_maximum_fusion.2), channel_id=1, source_target_pairs={{0,2},{2,0},{4,6},{6,4},{8,10},{10,8},{12,14},{14,12},{1,3},{3,1},... | collective-permute-start | bytes 3538952 | tf_op jit(solution)/shard_map/ppermute | solution.py:214
  214.9 44.1 %collective-permute-start.14 = (bf16[4,576,512]{2,1,0:T(8,128)(2,1)S(1)}, bf16[4,576,512]{2,1,0:T(8,128)(2,1)}, u32[]{:S(2)}, u32[]{:S(2)}) collective-permute-start(bf16[4,576,512]{2,1,0:T(8,128)(2,1)S(1)} %pad_maximum_fusion.a_own), channel_id=1, source_target_pairs={{0,1},{1,0},{2,3},{3,2},{4,5},{5,4},{6,7},{7,6},{8,9},{9,8},{10,11... | collective-permute-start | bytes 7077896 | tf_op jit(solution)/shard_map/ppermute | solution.py:214
  214.9 58.5 %collective-permute-start.16 = (bf16[4,576,512]{2,1,0:T(8,128)(2,1)}, bf16[4,576,512]{2,1,0:T(8,128)(2,1)}, u32[]{:S(2)}, u32[]{:S(2)}) collective-permute-start(bf16[4,576,512]{2,1,0:T(8,128)(2,1)} %collective-permute-done.15.b_own), channel_id=1, source_target_pairs={{0,1},{1,0},{2,3},{3,2},{4,5},{5,4},{6,7},{7,6},{8,9},{9,8},{10,11... | collective-permute-start | bytes 7077896 | tf_op jit(solution)/shard_map/ppermute | solution.py:214
  219.4 15.4 %collective-permute-start.18 = (bf16[2,576,512]{2,1,0:T(8,128)(2,1)}, bf16[2,576,512]{2,1,0:T(8,128)(2,1)}, u32[]{:S(2)}, u32[]{:S(2)}) collective-permute-start(bf16[2,576,512]{2,1,0:T(8,128)(2,1)} %collective-permute-done.17.b_own), channel_id=1, source_target_pairs={{0,1},{1,0},{2,3},{3,2},{4,5},{5,4},{6,7},{7,6},{8,9},{9,8},{10,11... | collective-permute-start | bytes 3538952 | tf_op jit(solution)/shard_map/ppermute | solution.py:214
  219.4 29.2 %collective-permute-start.12 = (bf16[2,576,512]{2,1,0:T(8,128)(2,1)}, bf16[2,576,512]{2,1,0:T(8,128)(2,1)}, u32[]{:S(2)}, u32[]{:S(2)}) collective-permute-start(bf16[2,576,512]{2,1,0:T(8,128)(2,1)} %maximum_select_fusion.3), channel_id=1, source_target_pairs={{0,2},{2,0},{4,6},{6,4},{8,10},{10,8},{12,14},{14,12},{1,3},{3,1},... | collective-permute-start | bytes 3538952 | tf_op jit(solution)/shard_map/ppermute | solution.py:214
  231.9 41.5 %collective-permute-start.9 = (bf16[2,576,512]{2,1,0:T(8,128)(2,1)}, bf16[2,576,512]{2,1,0:T(8,128)(2,1)}, u32[]{:S(2)}, u32[]{:S(2)}) collective-permute-start(bf16[2,576,512]{2,1,0:T(8,128)(2,1)} %maximum_select_fusion.1), channel_id=1, source_target_pairs={{0,2},{2,0},{4,6},{6,4},{8,10},{10,8},{12,14},{14,12},{1,3},{3,1},... | collective-permute-start | bytes 3538952 | tf_op jit(solution)/shard_map/ppermute | solution.py:214
  232.8 15.8 %copy-start.1 = (bf16[4,576,512]{2,1,0:T(8,128)(2,1)S(1)}, bf16[4,576,512]{2,1,0:T(8,128)(2,1)}, u32[]{:S(2)}) copy-start(bf16[4,576,512]{2,1,0:T(8,128)(2,1)} %own_ref.7) | copy-start | bytes 7077892
  234.8 24.0 %copy-start.2 = (bf16[1,576,512]{2,1,0:T(8,128)(2,1)S(1)}, bf16[1,576,512]{2,1,0:T(8,128)(2,1)}, u32[]{:S(2)}) copy-start(bf16[1,576,512]{2,1,0:T(8,128)(2,1)} %get-tuple-element.34) | copy-start | bytes 1769476
  234.8 24.0 %copy-start.3 = (bf16[1,576,512]{2,1,0:T(8,128)(2,1)S(1)}, bf16[1,576,512]{2,1,0:T(8,128)(2,1)}, u32[]{:S(2)}) copy-start(bf16[1,576,512]{2,1,0:T(8,128)(2,1)} %get-tuple-element.35) | copy-start | bytes 1769476
  234.8 24.0 %copy-start.4 = (bf16[1,576,512]{2,1,0:T(8,128)(2,1)S(1)}, bf16[1,576,512]{2,1,0:T(8,128)(2,1)}, u32[]{:S(2)}) copy-start(bf16[1,576,512]{2,1,0:T(8,128)(2,1)} %get-tuple-element.38) | copy-start | bytes 1769476
  234.8 24.0 %copy-start.5 = (bf16[1,576,512]{2,1,0:T(8,128)(2,1)S(1)}, bf16[1,576,512]{2,1,0:T(8,128)(2,1)}, u32[]{:S(2)}) copy-start(bf16[1,576,512]{2,1,0:T(8,128)(2,1)} %get-tuple-element.39) | copy-start | bytes 1769476
  234.8 48.7 %collective-permute-start.11 = (bf16[2,576,512]{2,1,0:T(8,128)(2,1)S(1)}, bf16[2,576,512]{2,1,0:T(8,128)(2,1)S(1)}, u32[]{:S(2)}, u32[]{:S(2)}) collective-permute-start(bf16[2,576,512]{2,1,0:T(8,128)(2,1)S(1)} %maximum_select_fusion.2.a_own), channel_id=1, source_target_pairs={{0,1},{1,0},{2,3},{3,2},{4,5},{5,4},{6,7},{7,6},{8,9},{9,8},{10,11... | collective-permute-start | bytes 3538952 | tf_op jit(solution)/shard_map/ppermute | solution.py:214
  248.6 35.0 %collective-permute-start.13 = (bf16[2,576,512]{2,1,0:T(8,128)(2,1)}, bf16[2,576,512]{2,1,0:T(8,128)(2,1)S(1)}, u32[]{:S(2)}, u32[]{:S(2)}) collective-permute-start(bf16[2,576,512]{2,1,0:T(8,128)(2,1)} %collective-permute-done.12.b_own), channel_id=1, source_target_pairs={{0,1},{1,0},{2,3},{3,2},{4,5},{5,4},{6,7},{7,6},{8,9},{9,8},{10,11... | collective-permute-start | bytes 3538952 | tf_op jit(solution)/shard_map/ppermute | solution.py:214
  259.0 31.2 %collective-permute-start.7 = (bf16[2,576,512]{2,1,0:T(8,128)(2,1)S(1)}, bf16[2,576,512]{2,1,0:T(8,128)(2,1)S(1)}, u32[]{:S(2)}, u32[]{:S(2)}) collective-permute-start(bf16[2,576,512]{2,1,0:T(8,128)(2,1)S(1)} %maximum_select_fusion.a_own), channel_id=1, source_target_pairs={{0,1},{1,0},{2,3},{3,2},{4,5},{5,4},{6,7},{7,6},{8,9},{9,8},{10,11... | collective-permute-start | bytes 3538952 | tf_op jit(solution)/shard_map/ppermute | solution.py:214
  273.4 16.8 %collective-permute-start.10 = (bf16[2,576,512]{2,1,0:T(8,128)(2,1)}, bf16[2,576,512]{2,1,0:T(8,128)(2,1)S(1)}, u32[]{:S(2)}, u32[]{:S(2)}) collective-permute-start(bf16[2,576,512]{2,1,0:T(8,128)(2,1)} %collective-permute-done.9.b_own), channel_id=1, source_target_pairs={{0,1},{1,0},{2,3},{3,2},{4,5},{5,4},{6,7},{7,6},{8,9},{9,8},{10,11... | collective-permute-start | bytes 3538952 | tf_op jit(solution)/shard_map/ppermute | solution.py:214

commit v2 on v1

v2 whole, which is shorter than its diff:
```python
import functools

import jax
import jax.numpy as jnp
from jax import lax
from jax.experimental import pallas as pl
from jax.experimental.pallas import tpu as pltpu
from jax.sharding import PartitionSpec as P

NT = (((1,), (1,)), ((), ()))


def windows(full, kept):
    slack = full - kept
    tile = 256 - slack if 0 <= slack <= 128 else kept
    found = []
    base = 0
    while base < kept:
        rows = min(tile, kept - base)
        found.append((base, rows, rows + slack))
        base += rows
    return found


def pair_kernel(call, wins, n_sets, has_prev, meta_ref, shift_ref, ve1_ref, ve2_ref, pick_ref, own_ref, other_ref, *rest):
    sets = [(rest[2 * k], rest[2 * k + 1]) for k in range(n_sets)]
    rest = rest[2 * n_sets + (1 if has_prev else 0):]
    (out_ref, first, second, pick, side_a, side_b, e1_buf, out_buf,
     first_sem, second_sem, pick_sem, out_sem) = rest
    pairs_here = out_ref.shape[0]
    kept = out_ref.shape[1]
    half = own_ref.shape[2]
    n_first = first.shape[0]
    lo = meta_ref[0, call]
    hi = meta_ref[0, call + 1]
    base_first = meta_ref[1, 0]

    def first_copies():
        out = []
        for k in range(n_first):
            out.append(pltpu.make_async_copy(
                own_ref.at[base_first + k], first.at[k, :, pl.ds(0, half)], first_sem.at[2 * k]))
            out.append(pltpu.make_async_copy(
                other_ref.at[base_first + k], first.at[k, :, pl.ds(half, half)], first_sem.at[2 * k + 1]))
        return out

    def fetch(i, slot):
        p = meta_ref[2, i]
        which = meta_ref[3, p]
        idx = meta_ref[4, p]
        pltpu.make_async_copy(pick_ref.at[p], pick.at[slot], pick_sem.at[slot]).start()
        for k, (x_own, x_other) in enumerate(sets):
            @pl.when(which == k)
            def _():
                pltpu.make_async_copy(
                    x_own.at[idx], second.at[slot, :, pl.ds(0, half)], second_sem.at[slot, 0]).start()
                pltpu.make_async_copy(
                    x_other.at[idx], second.at[slot, :, pl.ds(half, half)], second_sem.at[slot, 1]).start()

    def await_fetch(slot):
        pltpu.make_async_copy(pick_ref.at[0], pick.at[slot], pick_sem.at[slot]).wait()
        for k in range(2):
            pltpu.make_async_copy(
                sets[0][0].at[0], second.at[slot, :, pl.ds(k * half, half)], second_sem.at[slot, k]).wait()

    def out_copy(p, slot):
        return pltpu.make_async_copy(out_buf.at[slot], out_ref.at[p], out_sem.at[slot])

    @pl.when(hi > lo)
    def _():
        for c in first_copies():
            c.start()
        fetch(lo, lax.rem(lo, 2))
        for c in first_copies():
            c.wait()

    def step(i, carry):
        slot = lax.rem(i, 2)
        p = meta_ref[2, i]
        f = p // (pairs_here // n_first)

        @pl.when(i + 1 < hi)
        def _():
            fetch(i + 1, 1 - slot)

        await_fetch(slot)

        @pl.when(i >= lo + 2)
        def _():
            out_copy(p, slot).wait()

        e2_parts = []
        for base, rows, span in wins:
            one = pick[slot, 0, base:base + rows, 0:span]
            got = jnp.dot(one, first[f, base:base + span, :], preferred_element_type=jnp.float32)
            side_a[base:base + rows, :] = got.astype(jnp.bfloat16)
            e1_buf[base:base + rows, :] = jnp.dot(
                one, ve1_ref[f, base:base + span, :], preferred_element_type=jnp.float32)
            two = pick[slot, 1, base:base + rows, 0:span]
            got = jnp.dot(two, second[slot, base:base + span, :], preferred_element_type=jnp.float32)
            side_b[base:base + rows, :] = got.astype(jnp.bfloat16)
            ve = jnp.broadcast_to(ve2_ref[p, :, base:base + span], (8, span)).astype(jnp.bfloat16)
            e2_parts.append(
                lax.dot_general(ve, two, NT, preferred_element_type=jnp.float32)[0:1])
        e2 = jnp.concatenate(e2_parts, axis=1)
        shift = shift_ref[p]
        c = lax.dot_general(side_a[...], side_b[...], NT, preferred_element_type=jnp.float32)
        for col in range(0, kept, 128):
            den = e1_buf[...] + e2[:, col:col + 128] - shift
            inv = pl.reciprocal(den, approx=True)
            neg = inv * (den * inv - 2.0)
            out_buf[slot, :, col:col + 128] = (c[:, col:col + 128] * neg).astype(jnp.bfloat16)
        out_copy(p, slot).start()
        return carry

    lax.fori_loop(lo, hi, step, 0)

    @pl.when(hi - lo >= 2)
    def _():
        out_copy(0, lax.rem(hi, 2)).wait()

    @pl.when(hi > lo)
    def _():
        out_copy(0, lax.rem(hi + 1, 2)).wait()


def run_pairs(call, expected, wins, meta, shift, ve1, ve2, pick, own, other, sets, prev):
    pairs_here, _, kept, span = pick.shape
    n_first = ve1.shape[0]
    full, half = own.shape[1], own.shape[2]
    any_spec = pl.BlockSpec(memory_space=pl.ANY)
    smem = pl.BlockSpec(memory_space=pltpu.SMEM)
    vmem = pl.BlockSpec(memory_space=pltpu.VMEM)
    operands = [meta, shift, ve1, ve2, pick, own, other]
    for pair in sets:
        operands += list(pair)
    in_specs = [smem, smem, vmem, vmem] + [any_spec] * (len(operands) - 4)
    aliases = {}
    if prev is not None:
        aliases = {len(operands): 0}
        operands.append(prev)
        in_specs.append(any_spec)
    bf = jnp.bfloat16
    return pl.pallas_call(
        functools.partial(pair_kernel, call, wins, len(sets), prev is not None),
        out_shape=jax.ShapeDtypeStruct((pairs_here, kept, kept), bf),
        in_specs=in_specs,
        out_specs=any_spec,
        scratch_shapes=[
            pltpu.VMEM((n_first, full, 2 * half), bf),
            pltpu.VMEM((2, full, 2 * half), bf),
            pltpu.VMEM((2, 2, kept, span), bf),
            pltpu.VMEM((kept, 2 * half), bf),
            pltpu.VMEM((kept, 2 * half), bf),
            pltpu.VMEM((kept, 128), jnp.float32),
            pltpu.VMEM((2, kept, kept), bf),
            pltpu.SemaphoreType.DMA((2 * n_first,)),
            pltpu.SemaphoreType.DMA((2, 2)),
            pltpu.SemaphoreType.DMA((2,)),
            pltpu.SemaphoreType.DMA((2,)),
        ],
        input_output_aliases=aliases,
        compiler_params=pltpu.CompilerParams(vmem_limit_bytes=40 * 1024 * 1024),
        cost_estimate=pl.CostEstimate(
            flops=int(expected * 4 * kept * kept * 2 * half * 2),
            bytes_accessed=int(expected * (full * half * 4 + kept * kept * 2)),
            transcendentals=0),
        name=f"pairs_{call}",
    )(*operands)


def picks(source, i0, i1):
    return [lax.dynamic_slice_in_dim(source, i0, 1, 0), lax.dynamic_slice_in_dim(source, i1, 1, 0)]


def per_device(blocks, virt_energy, occ_energy, owner_slot, pairs, domains):
    orb_count = lax.axis_size("orb")
    aux_count = lax.axis_size("aux")
    occ_dev, full, half = blocks.shape
    pair_dev = pairs.shape[0]
    kept = domains.shape[2]
    own_rows = pair_dev // aux_count
    n_first = occ_dev // aux_count
    core = lax.axis_index("aux")
    o = lax.axis_index("orb")
    z, y = o // 2, o % 2
    chain = orb_count // 2
    last = chain - 1
    n_slots = orb_count * occ_dev
    i32 = jnp.int32
    wins = windows(full, kept)

    swap_aux = [(0, 1), (1, 0)]
    swap_y = [(k, k ^ 1) for k in range(orb_count)]

    def across_y(a):
        return lax.ppermute(a, "orb", swap_y)

    def across_aux(a):
        return lax.ppermute(a, "aux", swap_aux)

    def hop_down(a, d):
        return lax.ppermute(a, "orb", [(k, k - 2) for k in range(2, orb_count) if k // 2 <= chain - d])

    def hop_up(a, d):
        return lax.ppermute(a, "orb", [(k, k + 2) for k in range(orb_count - 2) if k // 2 >= d - 1])

    downs, ups = [blocks], [blocks]
    for d in range(1, last):
        downs.append(hop_down(downs[-1], d))
        ups.append(hop_up(ups[-1], d))
    local_other = across_aux(blocks)

    orbitals = jnp.arange(owner_slot.shape[0], dtype=i32)
    hit_second = pairs[:, 1][:, None] == orbitals[None, :]
    slot_second = jnp.sum(jnp.where(hit_second, owner_slot[None, :], 0), axis=1)
    slots = jnp.arange(n_slots, dtype=i32)
    wanted_flat = jnp.any(slot_second[:, None] == slots[None, :], axis=0)
    wanted = wanted_flat.reshape(orb_count, occ_dev)
    info = jnp.concatenate(
        [virt_energy, jnp.pad(wanted_flat.astype(jnp.bfloat16), (0, full - n_slots))[None, :]], axis=0)
    info = jnp.concatenate([info, across_y(info)], axis=0)
    per_info = occ_dev + 1
    info_down, info_up = [info], [info]
    for d in range(1, chain):
        info_down.append(hop_down(info_down[-1], d))
        info_up.append(hop_up(info_up[-1], d))

    def wanted_by_opposite(table):
        return (table[2 * per_info - 1, :n_slots] > 0.5).reshape(orb_count, occ_dev)

    wanted_opp = wanted_by_opposite(info)
    local = jnp.arange(occ_dev, dtype=i32)[None, :]

    def two_of(table):
        return jnp.min(jnp.where(table, local, occ_dev - 1), axis=1), jnp.max(jnp.where(table, local, 0), axis=1)

    want, want_opp = two_of(wanted), two_of(wanted_opp)

    def far_place(rows):
        w = rows.astype(i32)
        earlier = (jnp.arange(occ_dev)[:, None] < jnp.arange(occ_dev)[None, :]).astype(i32)
        ahead = jnp.sum(w[:, :, None] * earlier[None], axis=1)
        ahead_not = jnp.sum((1 - w)[:, :, None] * earlier[None], axis=1)
        return jnp.where(rows, ahead, jnp.sum(w, axis=1, keepdims=True) + ahead_not)

    first_row = core * own_rows
    own_second = lax.dynamic_slice_in_dim(slot_second, first_row, own_rows, 0)
    own_pairs = lax.dynamic_slice_in_dim(pairs, first_row, own_rows, 0)
    src = own_second // occ_dev
    part = own_second % occ_dev
    rank = jnp.any(
        (slot_second[None, :] // occ_dev == src[:, None]) & (slot_second[None, :] < own_second[:, None]),
        axis=1).astype(i32)
    src_z, src_y = src // 2, src % 2
    dist = jnp.abs(src_z - z)
    is_opp = (src_y != y).astype(i32)
    from_up = src_z < z
    place_table = far_place(wanted_opp).reshape(-1)
    far = jnp.sum(jnp.where(own_second[:, None] == slots[None, :], place_table[None, :], 0), axis=1)
    both = 2 * dist <= chain - 1
    is_far = (dist == last) & (is_opp == 0)
    idx = jnp.where(
        dist == 0,
        jnp.where(is_opp == 1, rank, part),
        rank + jnp.where(both & from_up, 2, 0))
    idx = jnp.where(is_far, far % 2, idx)
    which = jnp.where(is_far & (far >= 2), 2, is_opp)
    rows = jnp.arange(own_rows, dtype=i32)
    before = (dist[None, :] < dist[:, None]) | ((dist[None, :] == dist[:, None]) & (rows[None, :] < rows[:, None]))
    place = jnp.sum(before.astype(i32), axis=1)
    order = jnp.sum(jnp.where(place[None, :] == rows[:, None], rows[None, :], 0), axis=1)
    bounds = jnp.sum((dist[None, :] < jnp.arange(chain + 1, dtype=i32)[:, None]).astype(i32), axis=1)
    width = max(own_rows, chain + 1)

    def padded(v):
        v = v.reshape(-1)
        return jnp.pad(v, (0, width - v.shape[0]))

    meta = jnp.stack([padded(bounds), padded(core * n_first), padded(order), padded(which), padded(idx)])

    def occ(col):
        hit = own_pairs[:, col][:, None] == orbitals[None, :]
        return jnp.sum(jnp.where(hit, occ_energy[None, :], 0.0), axis=1)

    shift = occ(0) + occ(1)
    ve1 = lax.dynamic_slice_in_dim(virt_energy, core * n_first, n_first, 0)
    ve1 = jnp.broadcast_to(ve1[:, :, None], (n_first, full, 128))

    def energies(tables, row):
        stacked = jnp.concatenate(tables, axis=0)
        hit = (row[:, None] == jnp.arange(stacked.shape[0], dtype=i32)[None, :]).astype(jnp.bfloat16)
        return jnp.dot(hit, stacked, preferred_element_type=jnp.float32).reshape(own_rows, 1, full)

    row_here = is_opp * per_info + part
    row_away = row_here + jnp.where(from_up, 2 * per_info, 0)

    dom = lax.dynamic_slice_in_dim(domains, first_row, own_rows, 0)
    base = jnp.concatenate([jnp.full((r,), b, i32) for b, r, _ in wins])
    span = max(sp for _, _, sp in wins)
    pick = ((dom - base)[..., None] == jnp.arange(span, dtype=i32)).astype(jnp.bfloat16)

    def idx_of(table, source):
        return lax.dynamic_index_in_dim(table, jnp.clip(source, 0, orb_count - 1), 0, keepdims=False)

    def chosen(arrays, table, sources):
        got = []
        for a, s in zip(arrays, sources):
            got += picks(a, idx_of(table[0], s), idx_of(table[1], s))
        return jnp.concatenate(got, axis=0)

    y_own = across_y(chosen([blocks], want_opp, [o]))
    sets = [(blocks, local_other), (y_own, across_aux(y_own))]
    out = run_pairs(
        0, own_rows / 4, wins, meta, shift, ve1, energies([info], row_here), pick, blocks, local_other, sets, None)
    for d in range(1, chain):
        s_down, s_up = o + 2 * d, o - 2 * d
        if d == last:
            sends_down = z == 1
            w = jnp.where(sends_down, wanted_by_opposite(info_up[1]), wanted_by_opposite(info_down[1]))
            w = idx_of(far_place(w), jnp.where(sends_down, 2 * last + y, y))
            turn = [jnp.sum(jnp.where(w == j, local[0], 0)) for j in range(occ_dev)]
            perm = [(2, 0), (3, 1), (2 * (last - 1), 2 * last), (2 * (last - 1) + 1, 2 * last + 1)]
            sets = []
            for j in range(0, occ_dev, 2):
                load = jnp.where(
                    sends_down,
                    jnp.concatenate(picks(downs[-1], turn[j], turn[j + 1]), axis=0),
                    jnp.concatenate(picks(ups[-1], turn[j], turn[j + 1]), axis=0))
                got = lax.ppermute(load, "orb", perm)
                sets.append((got, across_aux(got)))
                if j == 0:
                    opp_own = across_y(got)
                    sets.append((opp_own, across_aux(opp_own)))
        elif 2 * d <= last:
            mine = chosen([downs[d], ups[d]], want, [s_down, s_up])
            opp_own = across_y(chosen([downs[d], ups[d]], want_opp, [s_down, s_up]))
            sets = [(mine, across_aux(mine)), (opp_own, across_aux(opp_own))]
        else:
            is_down = z + d <= last
            s = jnp.where(is_down, s_down, s_up)
            mine = jnp.where(is_down, chosen([downs[d]], want, [s]), chosen([ups[d]], want, [s]))
            theirs = jnp.where(is_down, chosen([downs[d]], want_opp, [s]), chosen([ups[d]], want_opp, [s]))
            opp_own = across_y(theirs)
            sets = [(mine, across_aux(mine)), (opp_own, across_aux(opp_own))]
        ve2 = energies([info_down[d], info_up[d]], row_away)
        out = run_pairs(d, own_rows / 4, wins, meta, shift, ve1, ve2, pick, blocks, local_other, sets, out)
    return out


def solution(mesh):
    in_specs = (
        P(("groups", "orb"), None, "aux"),
        P(("groups", "orb"), None),
        P("groups"),
        P("groups"),
        P(("groups", "orb"), None),
        P(("groups", "orb"), None, None),
    )
    out_specs = P(("groups", "orb", "aux"), None, None)
    return jax.shard_map(
        per_device, mesh=mesh, in_specs=in_specs, out_specs=out_specs, check_vma=False
    )
```

time: 310 us -> 266 us (0.86)
  the two profiles are of different devices: /device:TPU:0 before, /device:TPU:6 now
where the time goes in v2:
time: 266 us; the launch traced here: 264 us
  waiting for transfers between devices  109 us (41%)
  between operations  34.9 us (13%)
  Pallas kernels  34.7 us (13%)
  other arithmetic  29.7 us (11%)
  starting transfers between devices  27.7 us (10%)
  local copies, waits for them, and re-layouts  25.2 us (9%)
    ppermute x5, waiting for transfers between devices, hop_down(): lax.ppermute(a, 'orb', [(k, k - 2) for k in range(2, orb_count) if k // 2...  61.5 us
    ppermute x2, waiting for transfers between devices, per_device(): got = lax.ppermute(load, 'orb', perm)  40.9 us
    pallas_call x4, Pallas kernels, run_pairs(): pl.pallas_call(functools.partial(pair_kernel, call, wins, len(sets), prev...  34.7 us
    ppermute x5, starting transfers between devices, hop_up(): lax.ppermute(a, 'orb', [(k, k + 2) for k in range(orb_count - 2) if k //...  15.1 us
    dynamic_slice x5, local copies, waits for them, and re-layouts, picks(): lax.dynamic_slice_in_dim(source, i0, 1, 0)  13.1 us
    ppermute x5, starting transfers between devices, hop_down(): lax.ppermute(a, 'orb', [(k, k - 2) for k in range(2, orb_count) if k // 2...  6.43 us
    ppermute x5, waiting for transfers between devices, across_y(): return lax.ppermute(a, 'orb', swap_y)  5.84 us
    concatenate x3, other arithmetic, chosen(): return jnp.concatenate(got, axis=0)  5.76 us
  transfers between devices with their start and end apart: 26, of which 9 were waited for; matrix products, arithmetic and copies ran while one was open for 21% of the time, Pallas kernels for 8%

profile of v2, /device:TPU:6, one launch (start us, length us, event | category | flops | bytes accessed | tf_op | source)
XLA Modules:
  0.0 264.0 jit_solution(9065729224723034209)
XLA Ops:
  0.0 1.3 collective-permute-start.8
  1.3 5.9 %collective-permute-start.10 = (bf16[4,576,512]{2,1,0:T(8,128)(2,1)}, bf16[4,576,512]{2,1,0:T(8,128)(2,1)}, u32[]{:S(2)}, u32[]{:S(2)}) collective-permute-start(bf16[4,576,512]{2,1,0:T(8,128)(2,1)} %own_ref.7), channel_id=1, source_target_pairs={{0,4},{2,6},{4,8},{6,10},{8,12},{10,14},{1,5},{3,7},{5,9},{7,11},{... | collective-permute-start | bytes 7077896 | tf_op jit(solution)/shard_map/ppermute | solution.py:206
  7.9 0.8 select_reduce_fusion
  8.9 0.7 pad_maximum_fusion.4
  10.2 0.7 constant_dynamic-slice_fusion.27
  11.6 0.7 constant_dynamic-slice_fusion.26
  12.5 0.8 select_reduce_fusion.1
  13.4 0.8 and_reduce_fusion
  14.2 0.9 dynamic-slice_add_fusion
  15.0 5.7 %fusion.pick_ref = bf16[16,2,512,256]{3,2,1,0:T(8,128)(2,1)} fusion(s32[16,2,512]{2,1,0:T(2,128)S(1)} %dynamic-slice_add_fusion), kind=kLoop, calls=%fused_computation.1 | loop fusion | flops 8388608 | bytes 8454144 | tf_op jit(solution)/shard_map/convert_element_type | solution.py:301
  33.3 1.3 collective-permute-start.1
  34.6 5.1 %collective-permute-start.4 = (bf16[10,576]{1,0:T(8,128)(2,1)S(1)}, bf16[10,576]{1,0:T(8,128)(2,1)}, u32[]{:S(2)}, u32[]{:S(2)}) collective-permute-start(bf16[10,576]{1,0:T(8,128)(2,1)S(1)} %pad_maximum_fusion.3), channel_id=1, source_target_pairs={{0,4},{2,6},{4,8},{6,10},{8,12},{10,14},{1,5},{3,7},{5,9},{7,11},{... | collective-permute-start | bytes 34568 | tf_op jit(solution)/shard_map/ppermute | solution.py:206
  40.8 15.4 %collective-permute-done.1 = bf16[10,576]{1,0:T(8,128)(2,1)S(1)} collective-permute-done((bf16[10,576]{1,0:T(8,128)(2,1)S(1)}, bf16[10,576]{1,0:T(8,128)(2,1)S(1)}, u32[]{:S(2)}, u32[]{:S(2)}) %collective-permute-start.1) | collective-permute-done | bytes 11552 | tf_op jit(solution)/shard_map/ppermute | solution.py:203
  56.2 1.2 collective-permute-done.4
  57.4 0.7 select_reduce_fusion.9
  58.2 2.1 collective-permute-start.11
  75.4 1.3 collective-permute-start.9
  76.7 1.9 constant_dynamic-slice_fusion.4
  78.6 3.0 %constant_dynamic-slice_fusion.2 = (bf16[1,576,512]{2,1,0:T(8,128)(2,1)S(1)}, bf16[1,576,512]{2,1,0:T(8,128)(2,1)S(1)}, bf16[1,576,512]{2,1,0:T(8,128)(2,1)}, bf16[1,576,512]{2,1,0:T(8,128)(2,1)}) fusion(bf16[4,576,512]{2,1,0:T(8,128)(2,1)} %collective-permute-done.10, s32[]{:T(128)S(6)} %select_n.321, s32[]{:T(128)S(6)} %select_n.322, s32[]{:T(128)S(6)} %select_n.318, ...), kind=kLoop, calls=%fused_computation.50 | loop fusion | bytes 4718608 | tf_op jit(solution)/shard_map/dynamic_slice | solution.py:173
  81.6 1.7 pad_maximum_fusion.1
  85.3 1.3 collective-permute-start.2
  86.6 1.1 pad_maximum_fusion.2
  88.4 45.8 %collective-permute-done.2 = bf16[10,576]{1,0:T(8,128)(2,1)S(1)} collective-permute-done((bf16[10,576]{1,0:T(8,128)(2,1)S(1)}, bf16[10,576]{1,0:T(8,128)(2,1)S(1)}, u32[]{:S(2)}, u32[]{:S(2)}) %collective-permute-start.2) | collective-permute-done | bytes 11552 | tf_op jit(solution)/shard_map/ppermute | solution.py:203
  134.8 1.3 collective-permute-start.5
  136.1 0.7 select_reduce_fusion.10
  145.0 1.2 broadcast_add_fusion
  146.2 0.7 copy.13
  147.5 0.8 copy.11
  152.7 0.9 fusion.9
  153.6 2.9 %pad_maximum_fusion.rest_0_ = bf16[4,576,512]{2,1,0:T(8,128)(2,1)} fusion(bf16[1,576,512]{2,1,0:T(8,128)(2,1)} %get-tuple-element.34, bf16[1,576,512]{2,1,0:T(8,128)(2,1)} %get-tuple-element.35, bf16[1,576,512]{2,1,0:T(8,128)(2,1)S(1)} %get-tuple-element.30, bf16[1,576,512]{2,1,0:T(8,128)(2,1)S(1)} %get-tuple-element.31), kind=kLoop, calls=%fused_computation.2 | loop fusion | flops 3538944 | bytes 4718592 | tf_op jit(solution)/shard_map/concatenate | solution.py:310
  156.6 4.1 %constant_dynamic-slice_fusion.10 = (bf16[1,576,512]{2,1,0:T(8,128)(2,1)S(1)}, bf16[1,576,512]{2,1,0:T(8,128)(2,1)S(1)}, bf16[1,576,512]{2,1,0:T(8,128)(2,1)}, b...) fusion(bf16[4,576,512]{2,1,0:T(8,128)(2,1)} %collective-permute, ...), kind=kLoop, calls=%fused_computation.58 | loop fusion | bytes 9437216 | tf_op jit(solution)/shard_map/dynamic_slice | solution.py:173
  160.7 1.3 collective-permute-start.3
  162.0 4.0 %constant_dynamic-slice_fusion.12 = (bf16[1,576,512]{2,1,0:T(8,128)(2,1)S(1)}, bf16[1,576,512]{2,1,0:T(8,128)(2,1)S(1)}, bf16[1,576,512]{2,1,0:T(8,128)(2,1)}, b...) fusion(bf16[4,576,512]{2,1,0:T(8,128)(2,1)} %collective-permute, ...), kind=kLoop, calls=%fused_computation.60 | loop fusion | bytes 9437216 | tf_op jit(solution)/shard_map/dynamic_slice | solution.py:173
  167.1 1.3 maximum_select_fusion
  168.3 2.9 %collective-permute-done.24.rest_2_ = bf16[2,576,512]{2,1,0:T(8,128)(2,1)} collective-permute-done((bf16[2,576,512]{2,1,0:T(8,128)(2,1)}, bf16[2,576,512]{2,1,0:T(8,128)(2,1)}, u32[]{:S(2)}, u32[]{:S(2)}) %collective-permute-start.24) | collective-permute-done | bytes 1179680 | tf_op jit(solution)/shard_map/ppermute | solution.py:197
  171.2 1.3 collective-permute-start.12
  175.1 1.2 maximum_select_fusion.3
  179.1 2.0 maximum_select_fusion.1
  181.1 1.3 collective-permute-start.16
  182.4 19.7 %collective-permute-done.12.rest_0_ = bf16[2,576,512]{2,1,0:T(8,128)(2,1)S(1)} collective-permute-done((bf16[2,576,512]{2,1,0:T(8,128)(2,1)}, bf16[2,576,512]{2,1,0:T(8,128)(2,1)S(1)}, u32[]{:S(2)}, u32[]{:S(2)}) %collective-permute-start.12) | collective-permute-done | bytes 1179680 | tf_op jit(solution)/shard_map/ppermute | solution.py:330
  202.6 0.9 fusion.5
  204.2 0.7 collective-permute-done.19.rest_2_
  205.1 0.7 pairs_0.1.rest_4_
  205.8 21.1 %collective-permute-done.16.rest_4_ = bf16[2,576,512]{2,1,0:T(8,128)(2,1)S(1)} collective-permute-done((bf16[2,576,512]{2,1,0:T(8,128)(2,1)S(1)}, bf16[2,576,512]{2,1,0:T(8,128)(2,1)S(1)}, u32[]{:S(2)}, u32[]{:S(2)}) %collective-permute-start.16) | collective-permute-done | bytes 1179680 | tf_op jit(solution)/shard_map/ppermute | solution.py:330
  227.5 2.2 collective-permute-done.14.rest_2_
  229.8 12.5 %pairs_1.1.rest_4_ = bf16[16,512,512]{2,1,0:T(8,128)(2,1)} custom-call(s32[5,16]{1,0:T(8,128)S(1)} %stack.23.meta_ref, f32[16]{0:T(128)S(1)} %add.181.shift_ref, bf16[2,576,128]{2,1,0:T(8,128)(2,1)S(1)} %broadcast_in_dim.171.ve1_ref, f32[16,1,576]{2,1,0:T(1,128)S(1)} %copy-done.1, ...), custom_call_target="tpu_custom_call", output_to_operand_aliasing={{}: (11, {})} | custom-call | flops 8589934592 | bytes 6815744 | tf_op jit(solution)/shard_map/pairs_1/pallas_call | solution.py:144
  242.2 7.6 %pairs_2.1.rest_6_ = bf16[16,512,512]{2,1,0:T(8,128)(2,1)} custom-call(s32[5,16]{1,0:T(8,128)S(1)} %stack.23.meta_ref, f32[16]{0:T(128)S(1)} %add.181.shift_ref, bf16[2,576,128]{2,1,0:T(8,128)(2,1)S(1)} %broadcast_in_dim.171.ve1_ref, f32[16,1,576]{2,1,0:T(1,128)S(1)} %reshape.163.ve2_ref, ...), custom_call_target="tpu_custom_call", output_to_operand_aliasing={{}: (11, {})} | custom-call | flops 8589934592 | bytes 6815744 | tf_op jit(solution)/shard_map/pairs_2/pallas_call | solution.py:144
  249.9 13.9 %pairs_3.1 = bf16[16,512,512]{2,1,0:T(8,128)(2,1)} custom-call(s32[5,16]{1,0:T(8,128)S(1)} %stack.23.meta_ref, f32[16]{0:T(128)S(1)} %add.181.shift_ref, bf16[2,576,128]{2,1,0:T(8,128)(2,1)S(1)} %broadcast_in_dim.171.ve1_ref, f32[16,1,576]{2,1,0:T(1,128)S(1)} %reshape.162.ve2_ref, ...), custom_call_target="tpu_custom_call", output_to_operand_aliasing={{}: (13, {})} | custom-call | flops 8589934592 | bytes 6815744 | tf_op jit(solution)/shard_map/pairs_3/pallas_call | solution.py:144
  (141 shorter events, 21.5 us)
Async XLA Ops:
  0.0 176.4 %collective-permute-start.7 = (bf16[4,576,512]{2,1,0:T(8,128)(2,1)}, bf16[4,576,512]{2,1,0:T(8,128)(2,1)}, u32[]{:S(2)}, u32[]{:S(2)}) collective-permute-start(bf16[4,576,512]{2,1,0:T(8,128)(2,1)} %own_ref.7), channel_id=1, source_target_pairs={{0,1},{1,0},{2,3},{3,2},{4,5},{5,4},{6,7},{7,6},{8,9},{9,8},{10,11... | collective-permute-start | bytes 7077896 | tf_op jit(solution)/shard_map/ppermute | solution.py:200
  0.0 75.4 %collective-permute-start.8 = (bf16[4,576,512]{2,1,0:T(8,128)(2,1)}, bf16[4,576,512]{2,1,0:T(8,128)(2,1)}, u32[]{:S(2)}, u32[]{:S(2)}) collective-permute-start(bf16[4,576,512]{2,1,0:T(8,128)(2,1)} %own_ref.7), channel_id=1, source_target_pairs={{4,0},{6,2},{8,4},{10,6},{12,8},{14,10},{5,1},{7,3},{9,5},{11,7},{... | collective-permute-start | bytes 7077896 | tf_op jit(solution)/shard_map/ppermute | solution.py:203
  1.3 56.9 %collective-permute-start.10 = (bf16[4,576,512]{2,1,0:T(8,128)(2,1)}, bf16[4,576,512]{2,1,0:T(8,128)(2,1)}, u32[]{:S(2)}, u32[]{:S(2)}) collective-permute-start(bf16[4,576,512]{2,1,0:T(8,128)(2,1)} %own_ref.7), channel_id=1, source_target_pairs={{0,4},{2,6},{4,8},{6,10},{8,12},{10,14},{1,5},{3,7},{5,9},{7,11},{... | collective-permute-start | bytes 7077896 | tf_op jit(solution)/shard_map/ppermute | solution.py:206
  9.6 23.7 %collective-permute-start = (bf16[5,576]{1,0:T(8,128)(2,1)S(1)}, bf16[5,576]{1,0:T(8,128)(2,1)S(1)}, u32[]{:S(2)}, u32[]{:S(2)}) collective-permute-start(bf16[5,576]{1,0:T(8,128)(2,1)S(1)} %pad_maximum_fusion.4), channel_id=1, source_target_pairs={{0,2},{2,0},{4,6},{6,4},{8,10},{10,8},{12,14},{14,12},{1,3},{3,1},... | collective-permute-start | bytes 17288 | tf_op jit(solution)/shard_map/ppermute | solution.py:197
  11.6 9.2 %copy-start.19 = (s32[16]{0:T(128)}, s32[16]{0:T(128)S(1)}, u32[]{:S(2)}) copy-start(s32[16]{0:T(128)S(1)} %get-tuple-element.25) | copy-start | bytes 196
  15.0 18.3 %copy-start.7 = (bf16[4,576]{1,0:T(4,128)(2,1)S(1)}, bf16[4,576]{1,0:T(4,128)(2,1)}, u32[]{:S(2)}) copy-start(bf16[4,576]{1,0:T(4,128)(2,1)} %param.7) | copy-start | bytes 13828
  33.3 45.3 %copy-start.17 = (bf16[5,576]{1,0:T(8,128)(2,1)}, bf16[5,576]{1,0:T(8,128)(2,1)S(1)}, u32[]{:S(2)}) copy-start(bf16[5,576]{1,0:T(8,128)(2,1)S(1)} %collective-permute-done) | copy-start | bytes 17284
  33.3 22.9 %collective-permute-start.1 = (bf16[10,576]{1,0:T(8,128)(2,1)S(1)}, bf16[10,576]{1,0:T(8,128)(2,1)S(1)}, u32[]{:S(2)}, u32[]{:S(2)}) collective-permute-start(bf16[10,576]{1,0:T(8,128)(2,1)S(1)} %pad_maximum_fusion.3), channel_id=1, source_target_pairs={{4,0},{6,2},{8,4},{10,6},{12,8},{14,10},{5,1},{7,3},{9,5},{11,7},{... | collective-permute-start | bytes 34568 | tf_op jit(solution)/shard_map/ppermute | solution.py:203
  34.6 22.7 %collective-permute-start.4 = (bf16[10,576]{1,0:T(8,128)(2,1)S(1)}, bf16[10,576]{1,0:T(8,128)(2,1)}, u32[]{:S(2)}, u32[]{:S(2)}) collective-permute-start(bf16[10,576]{1,0:T(8,128)(2,1)S(1)} %pad_maximum_fusion.3), channel_id=1, source_target_pairs={{0,4},{2,6},{4,8},{6,10},{8,12},{10,14},{1,5},{3,7},{5,9},{7,11},{... | collective-permute-start | bytes 34568 | tf_op jit(solution)/shard_map/ppermute | solution.py:206
  56.2 22.4 %copy-start.8 = (bf16[10,576]{1,0:T(8,128)(2,1)}, bf16[10,576]{1,0:T(8,128)(2,1)S(1)}, u32[]{:S(2)}) copy-start(bf16[10,576]{1,0:T(8,128)(2,1)S(1)} %collective-permute-done.1) | copy-start | bytes 34564
  58.2 98.4 %collective-permute-start.11 = (bf16[4,576,512]{2,1,0:T(8,128)(2,1)}, bf16[4,576,512]{2,1,0:T(8,128)(2,1)}, u32[]{:S(2)}, u32[]{:S(2)}) collective-permute-start(bf16[4,576,512]{2,1,0:T(8,128)(2,1)} %collective-permute-done.10), channel_id=1, source_target_pairs={{4,8},{6,10},{8,12},{10,14},{5,9},{7,11},{9,13},{11,15},{20,24},{2... | collective-permute-start | bytes 7077896 | tf_op jit(solution)/shard_map/ppermute | solution.py:206
  75.4 85.3 %collective-permute-start.9 = (bf16[4,576,512]{2,1,0:T(8,128)(2,1)}, bf16[4,576,512]{2,1,0:T(8,128)(2,1)}, u32[]{:S(2)}, u32[]{:S(2)}) collective-permute-start(bf16[4,576,512]{2,1,0:T(8,128)(2,1)} %collective-permute-done.8), channel_id=1, source_target_pairs={{4,0},{6,2},{8,4},{10,6},{5,1},{7,3},{9,5},{11,7},{20,16},{22,18},... | collective-permute-start | bytes 7077896 | tf_op jit(solution)/shard_map/ppermute | solution.py:203
  81.6 3.0 %copy-start = (bf16[4,576,512]{2,1,0:T(8,128)(2,1)S(1)}, bf16[4,576,512]{2,1,0:T(8,128)(2,1)}, u32[]{:S(2)}) copy-start(bf16[4,576,512]{2,1,0:T(8,128)(2,1)} %own_ref.7) | copy-start | bytes 7077892
  83.3 89.9 %collective-permute-start.22 = (bf16[4,576,512]{2,1,0:T(8,128)(2,1)}, bf16[4,576,512]{2,1,0:T(8,128)(2,1)}, u32[]{:S(2)}, u32[]{:S(2)}) collective-permute-start(bf16[4,576,512]{2,1,0:T(8,128)(2,1)} %pad_maximum_fusion.1), channel_id=1, source_target_pairs={{0,2},{2,0},{4,6},{6,4},{8,10},{10,8},{12,14},{14,12},{1,3},{3,1},... | collective-permute-start | bytes 7077896 | tf_op jit(solution)/shard_map/ppermute | solution.py:197
  85.3 48.9 %collective-permute-start.2 = (bf16[10,576]{1,0:T(8,128)(2,1)S(1)}, bf16[10,576]{1,0:T(8,128)(2,1)S(1)}, u32[]{:S(2)}, u32[]{:S(2)}) collective-permute-start(bf16[10,576]{1,0:T(8,128)(2,1)S(1)} %copy-done.9), channel_id=1, source_target_pairs={{4,0},{6,2},{8,4},{10,6},{5,1},{7,3},{9,5},{11,7},{20,16},{22,18},... | collective-permute-start | bytes 34568 | tf_op jit(solution)/shard_map/ppermute | solution.py:203
  86.6 58.3 %copy-start.18 = (s32[8,4]{0,1:T(4,128)S(1)}, s32[8,4]{0,1:T(4,128)}, u32[]{:S(2)}) copy-start(s32[8,4]{0,1:T(4,128)} %get-tuple-element.10) | copy-start | bytes 388
  134.8 9.6 %collective-permute-start.5 = (bf16[10,576]{1,0:T(8,128)(2,1)}, bf16[10,576]{1,0:T(8,128)(2,1)}, u32[]{:S(2)}, u32[]{:S(2)}) collective-permute-start(bf16[10,576]{1,0:T(8,128)(2,1)} %collective-permute-done.4), channel_id=1, source_target_pairs={{4,8},{6,10},{8,12},{10,14},{5,9},{7,11},{9,13},{11,15},{20,24},{2... | collective-permute-start | bytes 34568 | tf_op jit(solution)/shard_map/ppermute | solution.py:206
  144.4 26.8 %collective-permute-start.24 = (bf16[2,576,512]{2,1,0:T(8,128)(2,1)}, bf16[2,576,512]{2,1,0:T(8,128)(2,1)}, u32[]{:S(2)}, u32[]{:S(2)}) collective-permute-start(bf16[2,576,512]{2,1,0:T(8,128)(2,1)} %pad_maximum_fusion.2), channel_id=1, source_target_pairs={{0,2},{2,0},{4,6},{6,4},{8,10},{10,8},{12,14},{14,12},{1,3},{3,1},... | collective-permute-start | bytes 3538952 | tf_op jit(solution)/shard_map/ppermute | solution.py:197
  156.6 4.1 %copy-start.11 = (bf16[10,576]{1,0:T(8,128)(2,1)S(1)}, bf16[10,576]{1,0:T(8,128)(2,1)}, u32[]{:S(2)}) copy-start(bf16[10,576]{1,0:T(8,128)(2,1)} %copy-done.10) | copy-start | bytes 34564
  156.6 47.5 %collective-permute-start.21 = (bf16[4,576,512]{2,1,0:T(8,128)(2,1)}, bf16[4,576,512]{2,1,0:T(8,128)(2,1)}, u32[]{:S(2)}, u32[]{:S(2)}) collective-permute-start(bf16[4,576,512]{2,1,0:T(8,128)(2,1)} %pad_maximum_fusion.rest_0_), channel_id=1, source_target_pairs={{0,1},{1,0},{2,3},{3,2},{4,5},{5,4},{6,7},{7,6},{8,9},{9,8},{10,11... | collective-permute-start | bytes 7077896 | tf_op jit(solution)/shard_map/ppermute | solution.py:200
  160.7 5.7 %collective-permute-start.3 = (bf16[10,576]{1,0:T(8,128)(2,1)S(1)}, bf16[10,576]{1,0:T(8,128)(2,1)S(1)}, u32[]{:S(2)}, u32[]{:S(2)}) collective-permute-start(bf16[10,576]{1,0:T(8,128)(2,1)S(1)} %copy-done.11), channel_id=1, source_target_pairs={{4,0},{6,2},{5,1},{7,3},{20,16},{22,18},{21,17},{23,19}} | collective-permute-start | bytes 34568 | tf_op jit(solution)/shard_map/ppermute | solution.py:203
  166.4 4.9 %collective-permute-start.6 = (bf16[10,576]{1,0:T(8,128)(2,1)}, bf16[10,576]{1,0:T(8,128)(2,1)S(1)}, u32[]{:S(2)}, u32[]{:S(2)}) collective-permute-start(bf16[10,576]{1,0:T(8,128)(2,1)} %collective-permute-done.5), channel_id=1, source_target_pairs={{8,12},{10,14},{9,13},{11,15},{24,28},{26,30},{25,29},{27,31}} | collective-permute-start | bytes 34568 | tf_op jit(solution)/shard_map/ppermute | solution.py:206
  167.0 5.5 %copy-start.25 = (s32[1,32]{1,0:T(1,128)S(1)}, s32[1,32]{1,0:T(1,128)}, u32[]{:S(2)}) copy-start(s32[1,32]{1,0:T(1,128)} %add.177) | copy-start | bytes 388
  167.0 5.5 %copy-start.26 = (s32[1,32]{1,0:T(1,128)S(1)}, s32[1,32]{1,0:T(1,128)}, u32[]{:S(2)}) copy-start(s32[1,32]{1,0:T(1,128)} %reduce_sum.160) | copy-start | bytes 388
  167.0 6.7 %copy-start.20 = (s32[16]{0:T(128)S(1)}, s32[16]{0:T(128)}, u32[]{:S(2)}) copy-start(s32[16]{0:T(128)} %copy-done.19) | copy-start | bytes 196
  167.0 7.5 %copy-start.22 = (s32[16]{0:T(128)S(1)}, s32[16]{0:T(128)}, u32[]{:S(2)}) copy-start(s32[16]{0:T(128)} %get-tuple-element.22) | copy-start | bytes 196
  167.1 7.5 %copy-start.23 = (s32[16]{0:T(128)S(1)}, s32[16]{0:T(128)}, u32[]{:S(2)}) copy-start(s32[16]{0:T(128)} %get-tuple-element.23) | copy-start | bytes 196
  167.1 7.5 %copy-start.24 = (pred[16]{0:T(512)(128)(4,1)S(1)}, pred[16]{0:T(512)(128)(4,1)}, u32[]{:S(2)}) copy-start(pred[16]{0:T(512)(128)(4,1)} %and_reduce_fusion) | copy-start | bytes 52
  171.2 9.9 %collective-permute-start.25 = (bf16[2,576,512]{2,1,0:T(8,128)(2,1)}, bf16[2,576,512]{2,1,0:T(8,128)(2,1)}, u32[]{:S(2)}, u32[]{:S(2)}) collective-permute-start(bf16[2,576,512]{2,1,0:T(8,128)(2,1)} %collective-permute-done.24.rest_2_), channel_id=1, source_target_pairs={{0,1},{1,0},{2,3},{3,2},{4,5},{5,4},{6,7},{7,6},{8,9},{9,8},{10,11... | collective-permute-start | bytes 3538952 | tf_op jit(solution)/shard_map/ppermute | solution.py:200
  171.2 5.1 %copy-start.15 = (bf16[10,576]{1,0:T(8,128)(2,1)}, bf16[10,576]{1,0:T(8,128)(2,1)S(1)}, u32[]{:S(2)}) copy-start(bf16[10,576]{1,0:T(8,128)(2,1)S(1)} %collective-permute-done.6) | copy-start | bytes 34564
  171.2 30.9 %collective-permute-start.12 = (bf16[2,576,512]{2,1,0:T(8,128)(2,1)}, bf16[2,576,512]{2,1,0:T(8,128)(2,1)S(1)}, u32[]{:S(2)}, u32[]{:S(2)}) collective-permute-start(bf16[2,576,512]{2,1,0:T(8,128)(2,1)} %maximum_select_fusion), channel_id=1, source_target_pairs={{4,0},{6,2},{8,12},{10,14},{5,1},{7,3},{9,13},{11,15},{20,16},{22,... | collective-permute-start | bytes 3538952 | tf_op jit(solution)/shard_map/ppermute | solution.py:330
  173.2 53.8 %collective-permute-start.23 = (bf16[4,576,512]{2,1,0:T(8,128)(2,1)}, bf16[4,576,512]{2,1,0:T(8,128)(2,1)}, u32[]{:S(2)}, u32[]{:S(2)}) collective-permute-start(bf16[4,576,512]{2,1,0:T(8,128)(2,1)} %collective-permute-done.22.rest_2_), channel_id=1, source_target_pairs={{0,1},{1,0},{2,3},{3,2},{4,5},{5,4},{6,7},{7,6},{8,9},{9,8},{10,11... | collective-permute-start | bytes 7077896 | tf_op jit(solution)/shard_map/ppermute | solution.py:200
  176.4 28.5 %collective-permute-start.19 = (bf16[2,576,512]{2,1,0:T(8,128)(2,1)}, bf16[2,576,512]{2,1,0:T(8,128)(2,1)}, u32[]{:S(2)}, u32[]{:S(2)}) collective-permute-start(bf16[2,576,512]{2,1,0:T(8,128)(2,1)} %maximum_select_fusion.3), channel_id=1, source_target_pairs={{0,2},{2,0},{4,6},{6,4},{8,10},{10,8},{12,14},{14,12},{1,3},{3,1},... | collective-permute-start | bytes 3538952 | tf_op jit(solution)/shard_map/ppermute | solution.py:197
  179.1 23.6 %copy-start.12 = (bf16[10,576]{1,0:T(8,128)(2,1)S(1)}, bf16[10,576]{1,0:T(8,128)(2,1)}, u32[]{:S(2)}) copy-start(bf16[10,576]{1,0:T(8,128)(2,1)} %copy-done.10) | copy-start | bytes 34564
  179.1 24.5 %copy-start.14 = (bf16[10,576]{1,0:T(8,128)(2,1)S(1)}, bf16[10,576]{1,0:T(8,128)(2,1)}, u32[]{:S(2)}) copy-start(bf16[10,576]{1,0:T(8,128)(2,1)} %copy-done.13) | copy-start | bytes 34564
  179.1 24.5 %copy-start.16 = (bf16[10,576]{1,0:T(8,128)(2,1)S(1)}, bf16[10,576]{1,0:T(8,128)(2,1)}, u32[]{:S(2)}) copy-start(bf16[10,576]{1,0:T(8,128)(2,1)} %copy-done.15) | copy-start | bytes 34564
  179.1 24.7 %copy-start.3 = (bf16[1,576,512]{2,1,0:T(8,128)(2,1)S(1)}, bf16[1,576,512]{2,1,0:T(8,128)(2,1)}, u32[]{:S(2)}) copy-start(bf16[1,576,512]{2,1,0:T(8,128)(2,1)} %get-tuple-element.38) | copy-start | bytes 1769476
  179.1 24.7 %copy-start.4 = (bf16[1,576,512]{2,1,0:T(8,128)(2,1)S(1)}, bf16[1,576,512]{2,1,0:T(8,128)(2,1)}, u32[]{:S(2)}) copy-start(bf16[1,576,512]{2,1,0:T(8,128)(2,1)} %get-tuple-element.39) | copy-start | bytes 1769476
  179.1 24.7 %copy-start.5 = (bf16[1,576,512]{2,1,0:T(8,128)(2,1)S(1)}, bf16[1,576,512]{2,1,0:T(8,128)(2,1)}, u32[]{:S(2)}) copy-start(bf16[1,576,512]{2,1,0:T(8,128)(2,1)} %get-tuple-element.46) | copy-start | bytes 1769476
  179.1 24.7 %copy-start.6 = (bf16[1,576,512]{2,1,0:T(8,128)(2,1)S(1)}, bf16[1,576,512]{2,1,0:T(8,128)(2,1)}, u32[]{:S(2)}) copy-start(bf16[1,576,512]{2,1,0:T(8,128)(2,1)} %get-tuple-element.47) | copy-start | bytes 1769476
  181.1 45.9 %collective-permute-start.16 = (bf16[2,576,512]{2,1,0:T(8,128)(2,1)S(1)}, bf16[2,576,512]{2,1,0:T(8,128)(2,1)S(1)}, u32[]{:S(2)}, u32[]{:S(2)}) collective-permute-start(bf16[2,576,512]{2,1,0:T(8,128)(2,1)S(1)} %maximum_select_fusion.1), channel_id=1, source_target_pairs={{4,0},{6,2},{8,12},{10,14},{5,1},{7,3},{9,13},{11,15},{20,16},{22,... | collective-permute-start | bytes 3538952 | tf_op jit(solution)/shard_map/ppermute | solution.py:330
  202.1 27.6 %collective-permute-start.14 = (bf16[2,576,512]{2,1,0:T(8,128)(2,1)S(1)}, bf16[2,576,512]{2,1,0:T(8,128)(2,1)S(1)}, u32[]{:S(2)}, u32[]{:S(2)}) collective-permute-start(bf16[2,576,512]{2,1,0:T(8,128)(2,1)S(1)} %collective-permute-done.12.rest_0_), channel_id=1, source_target_pairs={{0,2},{2,0},{4,6},{6,4},{8,10},{10,8},{12,14},{14,12},{1,3},{3,1},... | collective-permute-start | bytes 3538952 | tf_op jit(solution)/shard_map/ppermute | solution.py:197
  204.1 38.1 %collective-permute-start.18 = (bf16[2,576,512]{2,1,0:T(8,128)(2,1)S(1)}, bf16[2,576,512]{2,1,0:T(8,128)(2,1)S(1)}, u32[]{:S(2)}, u32[]{:S(2)}) collective-permute-start(bf16[2,576,512]{2,1,0:T(8,128)(2,1)S(1)} %maximum_select_fusion.2.rest_0_), channel_id=1, source_target_pairs={{0,1},{1,0},{2,3},{3,2},{4,5},{5,4},{6,7},{7,6},{8,9},{9,8},{10,11... | collective-permute-start | bytes 3538952 | tf_op jit(solution)/shard_map/ppermute | solution.py:200
  204.9 37.4 %collective-permute-start.20 = (bf16[2,576,512]{2,1,0:T(8,128)(2,1)}, bf16[2,576,512]{2,1,0:T(8,128)(2,1)}, u32[]{:S(2)}, u32[]{:S(2)}) collective-permute-start(bf16[2,576,512]{2,1,0:T(8,128)(2,1)} %collective-permute-done.19.rest_2_), channel_id=1, source_target_pairs={{0,1},{1,0},{2,3},{3,2},{4,5},{5,4},{6,7},{7,6},{8,9},{9,8},{10,11... | collective-permute-start | bytes 3538952 | tf_op jit(solution)/shard_map/ppermute | solution.py:200
  205.1 24.7 %copy-start.1 = (f32[16,1,576]{2,1,0:T(1,128)S(1)}, f32[16,1,576]{2,1,0:T(1,128)}, u32[]{:S(2)}) copy-start(f32[16,1,576]{2,1,0:T(1,128)} %reshape.165.ve2_ref) | copy-start | bytes 110596
  227.0 22.9 %collective-permute-start.13 = (bf16[2,576,512]{2,1,0:T(8,128)(2,1)S(1)}, bf16[2,576,512]{2,1,0:T(8,128)(2,1)S(1)}, u32[]{:S(2)}, u32[]{:S(2)}) collective-permute-start(bf16[2,576,512]{2,1,0:T(8,128)(2,1)S(1)} %collective-permute-done.12.rest_0_), channel_id=1, source_target_pairs={{0,1},{1,0},{2,3},{3,2},{4,5},{5,4},{6,7},{7,6},{8,9},{9,8},{10,11... | collective-permute-start | bytes 3538952 | tf_op jit(solution)/shard_map/ppermute | solution.py:200
  227.0 22.9 %collective-permute-start.17 = (bf16[2,576,512]{2,1,0:T(8,128)(2,1)S(1)}, bf16[2,576,512]{2,1,0:T(8,128)(2,1)S(1)}, u32[]{:S(2)}, u32[]{:S(2)}) collective-permute-start(bf16[2,576,512]{2,1,0:T(8,128)(2,1)S(1)} %collective-permute-done.16.rest_4_), channel_id=1, source_target_pairs={{0,1},{1,0},{2,3},{3,2},{4,5},{5,4},{6,7},{7,6},{8,9},{9,8},{10,11... | collective-permute-start | bytes 3538952 | tf_op jit(solution)/shard_map/ppermute | solution.py:200
  229.7 20.1 %collective-permute-start.15 = (bf16[2,576,512]{2,1,0:T(8,128)(2,1)S(1)}, bf16[2,576,512]{2,1,0:T(8,128)(2,1)}, u32[]{:S(2)}, u32[]{:S(2)}) collective-permute-start(bf16[2,576,512]{2,1,0:T(8,128)(2,1)S(1)} %collective-permute-done.14.rest_2_), channel_id=1, source_target_pairs={{0,1},{1,0},{2,3},{3,2},{4,5},{5,4},{6,7},{7,6},{8,9},{9,8},{10,11... | collective-permute-start | bytes 3538952 | tf_op jit(solution)/shard_map/ppermute | solution.py:200
  (6 other events, 8.7 us)

commit v3 on v2

--- a/solution.py
+++ b/solution.py
@@ -8,6 +8,7 @@
 from jax.sharding import PartitionSpec as P
 
 NT = (((1,), (1,)), ((), ()))
+EXTRA = 16
 
 
 def windows(full, kept):
@@ -22,9 +23,9 @@
     return found
 
 
-def pair_kernel(call, wins, n_sets, has_prev, meta_ref, shift_ref, ve1_ref, ve2_ref, pick_ref, own_ref, other_ref, *rest):
+def pair_kernel(call, wins, n_sets, n_skip, meta_ref, shift_ref, ve1_ref, pick_ref, own_ref, other_ref, *rest):
     sets = [(rest[2 * k], rest[2 * k + 1]) for k in range(n_sets)]
-    rest = rest[2 * n_sets + (1 if has_prev else 0):]
+    rest = rest[2 * n_sets + n_skip:]
     (out_ref, first, second, pick, side_a, side_b, e1_buf, out_buf,
      first_sem, second_sem, pick_sem, out_sem) = rest
     pairs_here = out_ref.shape[0]
@@ -90,7 +91,8 @@
             out_copy(p, slot).wait()
 
         e2_parts = []
-        for base, rows, span in wins:
+        full = ve1_ref.shape[1]
+        for t, (base, rows, span) in enumerate(wins):
             one = pick[slot, 0, base:base + rows, 0:span]
             got = jnp.dot(one, first[f, base:base + span, :], preferred_element_type=jnp.float32)
             side_a[base:base + rows, :] = got.astype(jnp.bfloat16)
@@ -99,9 +101,9 @@
             two = pick[slot, 1, base:base + rows, 0:span]
             got = jnp.dot(two, second[slot, base:base + span, :], preferred_element_type=jnp.float32)
             side_b[base:base + rows, :] = got.astype(jnp.bfloat16)
-            ve = jnp.broadcast_to(ve2_ref[p, :, base:base + span], (8, span)).astype(jnp.bfloat16)
+            ve = second[slot, full:full + EXTRA, 0:span]
             e2_parts.append(
-                lax.dot_general(ve, two, NT, preferred_element_type=jnp.float32)[0:1])
+                lax.dot_general(ve, two, NT, preferred_element_type=jnp.float32)[t:t + 1])
         e2 = jnp.concatenate(e2_parts, axis=1)
         shift = shift_ref[p]
         c = lax.dot_general(side_a[...], side_b[...], NT, preferred_element_type=jnp.float32)
@@ -124,17 +126,18 @@
         out_copy(0, lax.rem(hi + 1, 2)).wait()
 
 
-def run_pairs(call, expected, wins, meta, shift, ve1, ve2, pick, own, other, sets, prev):
+def run_pairs(call, expected, wins, meta, shift, ve1, pick, own, other, sets, after, prev):
     pairs_here, _, kept, span = pick.shape
     n_first = ve1.shape[0]
     full, half = own.shape[1], own.shape[2]
     any_spec = pl.BlockSpec(memory_space=pl.ANY)
     smem = pl.BlockSpec(memory_space=pltpu.SMEM)
     vmem = pl.BlockSpec(memory_space=pltpu.VMEM)
-    operands = [meta, shift, ve1, ve2, pick, own, other]
+    operands = [meta, shift, ve1, pick, own, other]
     for pair in sets:
         operands += list(pair)
-    in_specs = [smem, smem, vmem, vmem] + [any_spec] * (len(operands) - 4)
+    operands += after
+    in_specs = [smem, smem, vmem] + [any_spec] * (len(operands) - 3)
     aliases = {}
     if prev is not None:
         aliases = {len(operands): 0}
@@ -142,7 +145,7 @@
         in_specs.append(any_spec)
     bf = jnp.bfloat16
     return pl.pallas_call(
-        functools.partial(pair_kernel, call, wins, len(sets), prev is not None),
+        functools.partial(pair_kernel, call, wins, len(sets), len(after) + (prev is not None)),
         out_shape=jax.ShapeDtypeStruct((pairs_here, kept, kept), bf),
         in_specs=in_specs,
         out_specs=any_spec,
@@ -169,8 +172,33 @@
     )(*operands)
 
 
-def picks(source, i0, i1):
-    return [lax.dynamic_slice_in_dim(source, i0, 1, 0), lax.dynamic_slice_in_dim(source, i1, 1, 0)]
+def set_kernel(n_arrays, table_ref, *rest):
+    arrays = rest[:n_arrays]
+    out_ref, sems = rest[n_arrays:]
+    for j in range(out_ref.shape[0]):
+        for k, a in enumerate(arrays):
+            @pl.when(table_ref[0, j] == k)
+            def _():
+                pltpu.make_async_copy(a.at[table_ref[1, j]], out_ref.at[j], sems.at[j]).start()
+    for j in range(out_ref.shape[0]):
+        pltpu.make_async_copy(arrays[0].at[0], out_ref.at[j], sems.at[j]).wait()
+
+
+def copy_sets(which, index, arrays):
+    n = len(index)
+    table = jnp.stack([jnp.stack([jnp.asarray(w, jnp.int32) for w in which]), jnp.stack(index)])
+    block = arrays[0].shape[1:]
+    any_spec = pl.BlockSpec(memory_space=pl.ANY)
+    size = 2 * n * block[0] * block[1] * 2
+    return pl.pallas_call(
+        functools.partial(set_kernel, len(arrays)),
+        out_shape=jax.ShapeDtypeStruct((n,) + block, arrays[0].dtype),
+        in_specs=[pl.BlockSpec(memory_space=pltpu.SMEM)] + [any_spec] * len(arrays),
+        out_specs=any_spec,
+        scratch_shapes=[pltpu.SemaphoreType.DMA((n,))],
+        cost_estimate=pl.CostEstimate(flops=0, bytes_accessed=size, transcendentals=0),
+        name="copy_sets",
+    )(table, *arrays)
 
 
 def per_device(blocks, virt_energy, occ_energy, owner_slot, pairs, domains):
@@ -205,37 +233,33 @@
     def hop_up(a, d):
         return lax.ppermute(a, "orb", [(k, k + 2) for k in range(orb_count - 2) if k // 2 >= d - 1])
 
-    downs, ups = [blocks], [blocks]
+    extra = [
+        jnp.pad(virt_energy[:, None, b:b + sp], ((0, 0), (0, 0), (0, half - sp))) for b, _, sp in wins]
+    extra.append(jnp.zeros((occ_dev, EXTRA - len(wins), half), blocks.dtype))
+    stored = jnp.concatenate([blocks] + extra, axis=1)
+
+    downs, ups = [stored], [stored]
     for d in range(1, last):
         downs.append(hop_down(downs[-1], d))
         ups.append(hop_up(ups[-1], d))
-    local_other = across_aux(blocks)
+    local_other = across_aux(stored)
 
     orbitals = jnp.arange(owner_slot.shape[0], dtype=i32)
     hit_second = pairs[:, 1][:, None] == orbitals[None, :]
     slot_second = jnp.sum(jnp.where(hit_second, owner_slot[None, :], 0), axis=1)
     slots = jnp.arange(n_slots, dtype=i32)
-    wanted_flat = jnp.any(slot_second[:, None] == slots[None, :], axis=0)
-    wanted = wanted_flat.reshape(orb_count, occ_dev)
-    info = jnp.concatenate(
-        [virt_energy, jnp.pad(wanted_flat.astype(jnp.bfloat16), (0, full - n_slots))[None, :]], axis=0)
-    info = jnp.concatenate([info, across_y(info)], axis=0)
-    per_info = occ_dev + 1
-    info_down, info_up = [info], [info]
-    for d in range(1, chain):
-        info_down.append(hop_down(info_down[-1], d))
-        info_up.append(hop_up(info_up[-1], d))
-
-    def wanted_by_opposite(table):
-        return (table[2 * per_info - 1, :n_slots] > 0.5).reshape(orb_count, occ_dev)
-
-    wanted_opp = wanted_by_opposite(info)
+    wanted_flat = jnp.any(slot_second[:, None] == slots[None, :], axis=0).astype(i32)
+    wanted = wanted_flat.reshape(orb_count, occ_dev) > 0
+    wanted_opp = across_y(wanted_flat).reshape(orb_count, occ_dev) > 0
+    top = orb_count - 1
+    tell = [(0, 3), (1, 2), (top, top - 3), (top - 1, top - 2)]
+    wanted_far = lax.ppermute(wanted_flat, "orb", tell).reshape(orb_count, occ_dev) > 0
     local = jnp.arange(occ_dev, dtype=i32)[None, :]
 
     def two_of(table):
         return jnp.min(jnp.where(table, local, occ_dev - 1), axis=1), jnp.max(jnp.where(table, local, 0), axis=1)
 
-    want, want_opp = two_of(wanted), two_of(wanted_opp)
+    want_opp = two_of(wanted_opp)
 
     def far_place(rows):
         w = rows.astype(i32)
@@ -260,12 +284,10 @@
     far = jnp.sum(jnp.where(own_second[:, None] == slots[None, :], place_table[None, :], 0), axis=1)
     both = 2 * dist <= chain - 1
     is_far = (dist == last) & (is_opp == 0)
-    idx = jnp.where(
-        dist == 0,
-        jnp.where(is_opp == 1, rank, part),
-        rank + jnp.where(both & from_up, 2, 0))
+    idx = jnp.where(is_opp == 1, rank + jnp.where(both & from_up, 2, 0), part)
     idx = jnp.where(is_far, far % 2, idx)
-    which = jnp.where(is_far & (far >= 2), 2, is_opp)
+    which_away = jnp.where(is_opp == 1, 2, jnp.where(is_far, far // 2, from_up.astype(i32)))
+    which = jnp.where(dist == 0, is_opp, which_away)
     rows = jnp.arange(own_rows, dtype=i32)
     before = (dist[None, :] < dist[:, None]) | ((dist[None, :] == dist[:, None]) & (rows[None, :] < rows[:, None]))
     place = jnp.sum(before.astype(i32), axis=1)
@@ -287,14 +309,6 @@
     ve1 = lax.dynamic_slice_in_dim(virt_energy, core * n_first, n_first, 0)
     ve1 = jnp.broadcast_to(ve1[:, :, None], (n_first, full, 128))
 
-    def energies(tables, row):
-        stacked = jnp.concatenate(tables, axis=0)
-        hit = (row[:, None] == jnp.arange(stacked.shape[0], dtype=i32)[None, :]).astype(jnp.bfloat16)
-        return jnp.dot(hit, stacked, preferred_element_type=jnp.float32).reshape(own_rows, 1, full)
-
-    row_here = is_opp * per_info + part
-    row_away = row_here + jnp.where(from_up, 2 * per_info, 0)
-
     dom = lax.dynamic_slice_in_dim(domains, first_row, own_rows, 0)
     base = jnp.concatenate([jnp.full((r,), b, i32) for b, r, _ in wins])
     span = max(sp for _, _, sp in wins)
@@ -303,48 +317,40 @@
     def idx_of(table, source):
         return lax.dynamic_index_in_dim(table, jnp.clip(source, 0, orb_count - 1), 0, keepdims=False)
 
-    def chosen(arrays, table, sources):
-        got = []
-        for a, s in zip(arrays, sources):
-            got += picks(a, idx_of(table[0], s), idx_of(table[1], s))
-        return jnp.concatenate(got, axis=0)
-
-    y_own = across_y(chosen([blocks], want_opp, [o]))
-    sets = [(blocks, local_other), (y_own, across_aux(y_own))]
-    out = run_pairs(
-        0, own_rows / 4, wins, meta, shift, ve1, energies([info], row_here), pick, blocks, local_other, sets, None)
-    for d in range(1, chain):
+    def two_for_opposite(source):
+        return [idx_of(want_opp[0], source), idx_of(want_opp[1], source)]
+
+    y_own = across_y(copy_sets([0, 0], two_for_opposite(o), [stored]))
+    sets = {0: [(stored, local_other), (y_own, across_aux(y_own))]}
+    after = {0: [downs[1], ups[1]]}
+    for d in range(1, last):
         s_down, s_up = o + 2 * d, o - 2 * d
-        if d == last:
-            sends_down = z == 1
-            w = jnp.where(sends_down, wanted_by_opposite(info_up[1]), wanted_by_opposite(info_down[1]))
-            w = idx_of(far_place(w), jnp.where(sends_down, 2 * last + y, y))
-            turn = [jnp.sum(jnp.where(w == j, local[0], 0)) for j in range(occ_dev)]
-            perm = [(2, 0), (3, 1), (2 * (last - 1), 2 * last), (2 * (last - 1) + 1, 2 * last + 1)]
-            sets = []
-            for j in range(0, occ_dev, 2):
-                load = jnp.where(
-                    sends_down,
-                    jnp.concatenate(picks(downs[-1], turn[j], turn[j + 1]), axis=0),
-                    jnp.concatenate(picks(ups[-1], turn[j], turn[j + 1]), axis=0))
-                got = lax.ppermute(load, "orb", perm)
-                sets.append((got, across_aux(got)))
-                if j == 0:
-                    opp_own = across_y(got)
-                    sets.append((opp_own, across_aux(opp_own)))
-        elif 2 * d <= last:
-            mine = chosen([downs[d], ups[d]], want, [s_down, s_up])
-            opp_own = across_y(chosen([downs[d], ups[d]], want_opp, [s_down, s_up]))
-            sets = [(mine, across_aux(mine)), (opp_own, across_aux(opp_own))]
+        if 2 * d <= last:
+            theirs = copy_sets([0, 0, 1, 1], two_for_opposite(s_down) + two_for_opposite(s_up), [downs[d], ups[d]])
         else:
-            is_down = z + d <= last
-            s = jnp.where(is_down, s_down, s_up)
-            mine = jnp.where(is_down, chosen([downs[d]], want, [s]), chosen([ups[d]], want, [s]))
-            theirs = jnp.where(is_down, chosen([downs[d]], want_opp, [s]), chosen([ups[d]], want_opp, [s]))
-            opp_own = across_y(theirs)
-            sets = [(mine, across_aux(mine)), (opp_own, across_aux(opp_own))]
-        ve2 = energies([info_down[d], info_up[d]], row_away)
-        out = run_pairs(d, own_rows / 4, wins, meta, shift, ve1, ve2, pick, blocks, local_other, sets, out)
+            is_up = (z + d > last).astype(i32)
+            s = jnp.where(is_up == 1, s_up, s_down)
+            theirs = copy_sets([is_up, is_up], two_for_opposite(s), [downs[d], ups[d]])
+        opp_own = across_y(theirs)
+        sets[d] = [
+            (downs[d], across_aux(downs[d])), (ups[d], across_aux(ups[d])), (opp_own, across_aux(opp_own))]
+        after[d] = [] if d == last - 1 else [downs[d + 1], ups[d + 1]]
+    sends_down = z == 1
+    turn_of = idx_of(far_place(wanted_far), jnp.where(sends_down, 2 * last + y, y))
+    turn = [jnp.sum(jnp.where(turn_of == j, local[0], 0)) for j in range(occ_dev)]
+    perm = [(2, 0), (3, 1), (2 * (last - 1), 2 * last), (2 * (last - 1) + 1, 2 * last + 1)]
+    is_up = 1 - sends_down.astype(i32)
+    loads = [copy_sets([is_up, is_up], turn[j:j + 2], [downs[-1], ups[-1]]) for j in range(0, occ_dev, 2)]
+    got_a, got_b = [lax.ppermute(load, "orb", perm) for load in loads]
+    opp_own = across_y(got_a)
+    sets[last] = [(got_a, across_aux(got_a)), (got_b, across_aux(got_b)), (opp_own, across_aux(opp_own))]
+    for d in range(1, last):
+        after[d] = after[d] + (loads if d == last - 2 else [got_a] if d == last - 1 else [])
+    after[last] = []
+    out = None
+    for d in range(chain):
+        out = run_pairs(
+            d, own_rows / chain, wins, meta, shift, ve1, pick, stored, local_other, sets[d], after[d], out)
     return out
 
 

time: 266 us -> 426 us (1.60)
  the two profiles are of different devices: /device:TPU:6 before, /device:TPU:0 now
where the time goes in v3:
time: 426 us; the launch traced here: 424 us
  Pallas kernels  267 us (63%)
  waiting for transfers between devices  93.2 us (22%)
  starting transfers between devices  24.9 us (6%)
  other arithmetic  19.9 us (5%)
  local copies, waits for them, and re-layouts  17.9 us (4%)
    pallas_call x5, Pallas kernels, copy_sets(): pl.pallas_call(functools.partial(set_kernel, len(arrays)), out_shape=jax....  230 us
    ppermute x2, waiting for transfers between devices, hop_down(): lax.ppermute(a, 'orb', [(k, k - 2) for k in range(2, orb_count) if k // 2...  44.7 us
    ppermute x5, waiting for transfers between devices, across_y(): return lax.ppermute(a, 'orb', swap_y)  39.6 us
    pallas_call x4, Pallas kernels, run_pairs(): pl.pallas_call(functools.partial(pair_kernel, call, wins, len(sets), len(...  37.8 us
    concatenate x1, local copies, waits for them, and re-layouts, per_device(): stored = jnp.concatenate([blocks] + extra, axis=1)  9.95 us
    another operation x7, other arithmetic, copy_sets(): jnp.stack([jnp.stack([jnp.asarray(w, jnp.int32) for w in which]), jnp.sta...  9.47 us
    ppermute x2, starting transfers between devices, hop_up(): lax.ppermute(a, 'orb', [(k, k + 2) for k in range(orb_count - 2) if k //...  9.02 us
    ppermute x2, waiting for transfers between devices, per_device(): got_a, got_b = [lax.ppermute(load, 'orb', perm) for load in loads]  8.88 us
  transfers between devices with their start and end apart: 23, of which 4 were waited for; matrix products, arithmetic and copies ran while one was open for 5% of the time, Pallas kernels for 61%

profile of v3, /device:TPU:0, one launch (start us, length us, event | category | flops | bytes accessed | tf_op | source)
XLA Modules:
  0.0 424.0 jit_solution(12193900310683016335)
XLA Ops:
  0.0 0.8 slice_bitcast_fusion.1
  0.8 0.7 slice_bitcast_fusion
  1.6 10.0 %concatenate.3.rest_0_.own_ref = bf16[4,592,512]{2,1,0:T(8,128)(2,1)S(1)} concatenate(bf16[4,576,512]{2,1,0:T(8,128)(2,1)} %param.6, bf16[4,1,512]{2,1,0:T(2,128)(2,1)S(1)} %pad.22, bf16[4,1,512]{2,1,0:T(2,128)(2,1)S(1)} %pad.23, bf16[4,1,512]{2,1,0:T(2,128)(2,1)S(1)} %pad.24, bf16[4,13,512]{2,1,0:T(8,128)(2,1)S(1)} %broadcast_in_dim.150), dimensions={1} | concatenate | bytes 4849664 | tf_op jit(solution)/shard_map/concatenate | solution.py:239
  11.6 1.4 collective-permute-start.3
  13.0 7.0 %collective-permute-start.5 = (bf16[4,592,512]{2,1,0:T(8,128)(2,1)S(1)}, bf16[4,592,512]{2,1,0:T(8,128)(2,1)}, u32[]{:S(2)}, u32[]{:S(2)}) collective-permute-start(bf16[4,592,512]{2,1,0:T(8,128)(2,1)S(1)} %concatenate.3.rest_0_.own_ref), channel_id=1, source_target_pairs={{0,4},{2,6},{4,8},{6,10},{8,12},{10,14},{1,5},{3,7},{5,9},{7,11},{... | collective-permute-start | bytes 7274504 | tf_op jit(solution)/shard_map/ppermute | solution.py:234
  20.3 2.0 collective-permute-start
  22.3 2.0 collective-permute-start.2
  24.7 44.7 %collective-permute-done.3.rest_0_.rest_4_ = bf16[4,592,512]{2,1,0:T(8,128)(2,1)} collective-permute-done((bf16[4,592,512]{2,1,0:T(8,128)(2,1)S(1)}, bf16[4,592,512]{2,1,0:T(8,128)(2,1)}, u32[]{:S(2)}, u32[]{:S(2)}) %collective-permute-start.3) | collective-permute-done | bytes 2424864 | tf_op jit(solution)/shard_map/ppermute | solution.py:231
  69.4 1.3 collective-permute-start.4
  71.4 0.7 fusion.11
  72.0 0.7 fusion.12
  73.0 0.7 select_reduce_fusion.8
  73.7 0.7 select_reduce_fusion.7
  74.4 2.5 add_bitcast_fusion.2
  76.9 0.6 stack.137.table_ref
  77.5 38.5 %copy_sets.9 = bf16[2,592,512]{2,1,0:T(8,128)(2,1)} custom-call(s32[2,2]{1,0:T(2,128)} %stack.137.table_ref, bf16[4,592,512]{2,1,0:T(8,128)(2,1)} %copy-done), custom_call_target="tpu_custom_call" | custom-call | bytes 2424832 | tf_op jit(solution)/shard_map/copy_sets/pallas_call | solution.py:193
  116.1 1.7 collective-permute-start.21
  117.8 2.1 collective-permute-start.6
  119.9 2.5 add_bitcast_fusion.5
  122.4 0.5 pad_add_fusion.3.table_ref
  123.0 75.4 %copy_sets.8 = bf16[4,592,512]{2,1,0:T(8,128)(2,1)} custom-call(s32[2,4]{1,0:T(2,128)} %pad_add_fusion.3.table_ref, bf16[4,592,512]{2,1,0:T(8,128)(2,1)} %collective-permute-done.3.rest_0_.rest_4_, bf16[4,592,512]{2,1,0:T(8,128)(2,1)} %collective-permute-done.5.rest_1_.rest_5_.rest_2_), custom_call_target="tpu_custom_call" | custom-call | bytes 4849664 | tf_op jit(solution)/shard_map/copy_sets/pallas_call | solution.py:193
  198.4 0.4 collective-permute-start.19
  199.1 0.3 collective-permute-start.18
  199.4 5.7 %fusion.pick_ref = bf16[16,2,512,256]{3,2,1,0:T(8,128)(2,1)} fusion(s32[16,2,512]{2,1,0:T(2,128)S(1)} %dynamic-slice_add_fusion), kind=kLoop, calls=%fused_computation.1 | loop fusion | flops 8388608 | bytes 8454144 | tf_op jit(solution)/shard_map/convert_element_type | solution.py:315
  205.7 0.6 select_reduce_fusion.10
  206.4 0.7 select_reduce_fusion.9
  207.1 1.3 add_bitcast_fusion
  208.4 0.6 pad_add_fusion
  209.0 38.5 %copy_sets.5.rest_8_ = bf16[2,592,512]{2,1,0:T(8,128)(2,1)} custom-call(s32[2,2]{1,0:T(2,128)} %get-tuple-element.39.table_ref, bf16[4,592,512]{2,1,0:T(8,128)(2,1)} %collective-permute-done.4.rest_0_.rest_6_, bf16[4,592,512]{2,1,0:T(8,128)(2,1)} %collective-permute-done.6.rest_1_.rest_7_.rest_2_), custom_call_target="tpu_custom_call" | custom-call | bytes 2424832 | tf_op jit(solution)/shard_map/copy_sets/pallas_call | solution.py:193
  247.6 1.5 copy-done.2
  249.1 1.3 collective-permute-start.7
  250.4 1.3 add_bitcast_fusion.3
  251.7 0.6 pad_add_fusion.2.table_ref
  252.3 38.5 %copy_sets.6.rest_9_ = bf16[2,592,512]{2,1,0:T(8,128)(2,1)} custom-call(s32[2,2]{1,0:T(2,128)} %get-tuple-element.38.table_ref, bf16[4,592,512]{2,1,0:T(8,128)(2,1)} %collective-permute-done.4.rest_0_.rest_6_, bf16[4,592,512]{2,1,0:T(8,128)(2,1)} %collective-permute-done.6.rest_1_.rest_7_.rest_2_), custom_call_target="tpu_custom_call" | custom-call | bytes 2424832 | tf_op jit(solution)/shard_map/copy_sets/pallas_call | solution.py:193
  290.9 38.7 %copy_sets.7 = bf16[2,592,512]{2,1,0:T(8,128)(2,1)} custom-call(s32[2,2]{1,0:T(2,128)} %pad_add_fusion.2.table_ref, bf16[4,592,512]{2,1,0:T(8,128)(2,1)} %collective-permute-done.4.rest_0_.rest_6_, bf16[4,592,512]{2,1,0:T(8,128)(2,1)} %collective-permute-done.6.rest_1_.rest_7_.rest_2_), custom_call_target="tpu_custom_call" | custom-call | bytes 2424832 | tf_op jit(solution)/shard_map/copy_sets/pallas_call | solution.py:193
  329.6 1.7 collective-permute-start.15
  331.3 1.3 collective-permute-start.9
  333.5 0.6 collective-permute-start.13
  334.2 24.6 %collective-permute-done.15.rest_4_ = bf16[2,592,512]{2,1,0:T(8,128)(2,1)} collective-permute-done((bf16[2,592,512]{2,1,0:T(8,128)(2,1)}, bf16[2,592,512]{2,1,0:T(8,128)(2,1)}, u32[]{:S(2)}, u32[]{:S(2)}) %collective-permute-start.15) | collective-permute-done | bytes 1212448 | tf_op jit(solution)/shard_map/ppermute | solution.py:225
  358.8 8.9 %collective-permute-done.9.rest_2_ = bf16[2,592,512]{2,1,0:T(8,128)(2,1)} collective-permute-done((bf16[2,592,512]{2,1,0:T(8,128)(2,1)}, bf16[2,592,512]{2,1,0:T(8,128)(2,1)}, u32[]{:S(2)}, u32[]{:S(2)}) %collective-permute-start.9) | collective-permute-done | bytes 1212448 | tf_op jit(solution)/shard_map/ppermute | solution.py:344
  367.7 0.5 collective-permute-start.11
  368.9 1.7 copy-done.3
  370.6 9.9 %pairs_0.1.rest_10_ = bf16[16,512,512]{2,1,0:T(8,128)(2,1)} custom-call(s32[5,16]{1,0:T(8,128)S(1)} %stack.112.meta_ref, f32[16]{0:T(128)S(1)} %add.107.shift_ref, bf16[2,576,128]{2,1,0:T(8,128)(2,1)S(1)} %broadcast_in_dim.95.ve1_ref, bf16[16,2,512,256]{3,2,1,0:T(8,128)(2,1)} %fusion.pick_ref, bf16[4,592,512]{2,1,0:T(8,128)(2,1)S(1)} %copy-done.1, ...), custom_call_target="tpu_custom_call" | custom-call | flops 8589934592 | bytes 6946816 | tf_op jit(solution)/shard_map/pairs_0/pallas_call | solution.py:147
  380.6 0.5 collective-permute-start.10
  381.1 14.9 %collective-permute-done.11.rest_4_ = bf16[2,592,512]{2,1,0:T(8,128)(2,1)} collective-permute-done((bf16[2,592,512]{2,1,0:T(8,128)(2,1)}, bf16[2,592,512]{2,1,0:T(8,128)(2,1)}, u32[]{:S(2)}, u32[]{:S(2)}) %collective-permute-start.11) | collective-permute-done | bytes 1212448 | tf_op jit(solution)/shard_map/ppermute | solution.py:225
  396.1 6.2 %pairs_1.1.rest_7_ = bf16[16,512,512]{2,1,0:T(8,128)(2,1)} custom-call(s32[5,16]{1,0:T(8,128)S(1)} %stack.112.meta_ref, f32[16]{0:T(128)S(1)} %add.107.shift_ref, bf16[2,576,128]{2,1,0:T(8,128)(2,1)S(1)} %broadcast_in_dim.95.ve1_ref, bf16[16,2,512,256]{3,2,1,0:T(8,128)(2,1)} %fusion.pick_ref, ...), custom_call_target="tpu_custom_call", output_to_operand_aliasing={{}: (16, {})} | custom-call | flops 8589934592 | bytes 6946816 | tf_op jit(solution)/shard_map/pairs_1/pallas_call | solution.py:147
  402.3 12.4 %pairs_2.1.rest_6_ = bf16[16,512,512]{2,1,0:T(8,128)(2,1)} custom-call(s32[5,16]{1,0:T(8,128)S(1)} %stack.112.meta_ref, f32[16]{0:T(128)S(1)} %add.107.shift_ref, bf16[2,576,128]{2,1,0:T(8,128)(2,1)S(1)} %broadcast_in_dim.95.ve1_ref, bf16[16,2,512,256]{3,2,1,0:T(8,128)(2,1)} %fusion.pick_ref, ...), custom_call_target="tpu_custom_call", output_to_operand_aliasing={{}: (13, {})} | custom-call | flops 8589934592 | bytes 6946816 | tf_op jit(solution)/shard_map/pairs_2/pallas_call | solution.py:147
  414.8 9.2 %pairs_3.1 = bf16[16,512,512]{2,1,0:T(8,128)(2,1)} custom-call(s32[5,16]{1,0:T(8,128)S(1)} %stack.112.meta_ref, f32[16]{0:T(128)S(1)} %add.107.shift_ref, bf16[2,576,128]{2,1,0:T(8,128)(2,1)S(1)} %broadcast_in_dim.95.ve1_ref, bf16[16,2,512,256]{3,2,1,0:T(8,128)(2,1)} %fusion.pick_ref, ...), custom_call_target="tpu_custom_call", output_to_operand_aliasing={{}: (12, {})} | custom-call | flops 8589934592 | bytes 6946816 | tf_op jit(solution)/shard_map/pairs_3/pallas_call | solution.py:147
  (105 shorter events, 4.2 us)
Async XLA Ops:
  1.6 18.4 %copy-start.10 = (s32[32,2]{0,1:T(2,128)S(1)}, s32[32,2]{0,1:T(2,128)}, u32[]{:S(2)}) copy-start(s32[32,2]{0,1:T(2,128)} %param.10) | copy-start | bytes 772
  1.6 18.4 %copy-start.13 = (s32[32]{0:T(128)S(1)}, s32[32]{0:T(128)}, u32[]{:S(2)}) copy-start(s32[32]{0:T(128)} %param.9) | copy-start | bytes 388
  11.6 65.9 %copy-start = (bf16[4,592,512]{2,1,0:T(8,128)(2,1)}, bf16[4,592,512]{2,1,0:T(8,128)(2,1)S(1)}, u32[]{:S(2)}) copy-start(bf16[4,592,512]{2,1,0:T(8,128)(2,1)S(1)} %concatenate.3.rest_0_.own_ref) | copy-start | bytes 7274500
  11.6 110.8 %copy-start.12 = (s32[1,4]{1,0:T(1,128)S(1)}, s32[1,4]{1,0:T(1,128)}, u32[]{:S(2)}) copy-start(s32[1,4]{1,0:T(1,128)} %constant.157.clone.1) | copy-start | bytes 52
  11.6 57.8 %collective-permute-start.3 = (bf16[4,592,512]{2,1,0:T(8,128)(2,1)S(1)}, bf16[4,592,512]{2,1,0:T(8,128)(2,1)}, u32[]{:S(2)}, u32[]{:S(2)}) collective-permute-start(bf16[4,592,512]{2,1,0:T(8,128)(2,1)S(1)} %concatenate.3.rest_0_.own_ref), channel_id=1, source_target_pairs={{4,0},{6,2},{8,4},{10,6},{12,8},{14,10},{5,1},{7,3},{9,5},{11,7},{... | collective-permute-start | bytes 7274504 | tf_op jit(solution)/shard_map/ppermute | solution.py:231
  13.0 104.8 %collective-permute-start.5 = (bf16[4,592,512]{2,1,0:T(8,128)(2,1)S(1)}, bf16[4,592,512]{2,1,0:T(8,128)(2,1)}, u32[]{:S(2)}, u32[]{:S(2)}) collective-permute-start(bf16[4,592,512]{2,1,0:T(8,128)(2,1)S(1)} %concatenate.3.rest_0_.own_ref), channel_id=1, source_target_pairs={{0,4},{2,6},{4,8},{6,10},{8,12},{10,14},{1,5},{3,7},{5,9},{7,11},{... | collective-permute-start | bytes 7274504 | tf_op jit(solution)/shard_map/ppermute | solution.py:234
  20.3 4.1 collective-permute-start
  22.3 48.4 %collective-permute-start.2 = (s32[32]{0:T(128)S(1)}, s32[32]{0:T(128)S(1)}, u32[]{:S(2)}, u32[]{:S(2)}) collective-permute-start(s32[32]{0:T(128)S(1)} %convert_element_type.69), channel_id=1, source_target_pairs={{0,6},{2,4},{14,8},{12,10},{1,7},{3,5},{15,9},{13,11},{16,22},{18,... | collective-permute-start | bytes 392 | tf_op jit(solution)/shard_map/ppermute | solution.py:256
  69.4 129.7 %collective-permute-start.4 = (bf16[4,592,512]{2,1,0:T(8,128)(2,1)}, bf16[4,592,512]{2,1,0:T(8,128)(2,1)}, u32[]{:S(2)}, u32[]{:S(2)}) collective-permute-start(bf16[4,592,512]{2,1,0:T(8,128)(2,1)} %collective-permute-done.3.rest_0_.rest_4_), channel_id=1, source_target_pairs={{4,0},{6,2},{8,4},{10,6},{5,1},{7,3},{9,5},{11,7},{20,16},{22,18},... | collective-permute-start | bytes 7274504 | tf_op jit(solution)/shard_map/ppermute | solution.py:231
  116.1 82.7 %collective-permute-start.21 = (bf16[2,592,512]{2,1,0:T(8,128)(2,1)}, bf16[2,592,512]{2,1,0:T(8,128)(2,1)}, u32[]{:S(2)}, u32[]{:S(2)}) collective-permute-start(bf16[2,592,512]{2,1,0:T(8,128)(2,1)} %copy_sets.9), channel_id=1, source_target_pairs={{0,2},{2,0},{4,6},{6,4},{8,10},{10,8},{12,14},{14,12},{1,3},{3,1},... | collective-permute-start | bytes 3637256 | tf_op jit(solution)/shard_map/ppermute | solution.py:225
  117.8 87.4 %collective-permute-start.6 = (bf16[4,592,512]{2,1,0:T(8,128)(2,1)}, bf16[4,592,512]{2,1,0:T(8,128)(2,1)}, u32[]{:S(2)}, u32[]{:S(2)}) collective-permute-start(bf16[4,592,512]{2,1,0:T(8,128)(2,1)} %collective-permute-done.5.rest_1_.rest_5_.rest_2_), channel_id=1, source_target_pairs={{4,8},{6,10},{8,12},{10,14},{5,9},{7,11},{9,13},{11,15},{20,24},{2... | collective-permute-start | bytes 7274504 | tf_op jit(solution)/shard_map/ppermute | solution.py:234
  119.9 127.7 %collective-permute-start.1 = (bf16[4,592,512]{2,1,0:T(8,128)(2,1)}, bf16[4,592,512]{2,1,0:T(8,128)(2,1)S(1)}, u32[]{:S(2)}, u32[]{:S(2)}) collective-permute-start(bf16[4,592,512]{2,1,0:T(8,128)(2,1)} %copy-done), channel_id=1, source_target_pairs={{0,1},{1,0},{2,3},{3,2},{4,5},{5,4},{6,7},{7,6},{8,9},{9,8},{10,11... | collective-permute-start | bytes 7274504 | tf_op jit(solution)/shard_map/ppermute | solution.py:228
  122.9 76.1 %copy-start.7 = (s32[32,2,512]{2,1,0:T(2,128)S(1)}, s32[32,2,512]{2,1,0:T(2,128)}, u32[]{:S(2)}) copy-start(s32[32,2,512]{2,1,0:T(2,128)} %param.11) | copy-start | bytes 393220
  123.0 76.1 %copy-start.9 = (s32[512]{0:T(512)S(1)}, s32[512]{0:T(512)}, u32[]{:S(2)}) copy-start(s32[512]{0:T(512)} %constant.150.clone.1) | copy-start | bytes 6148
  198.4 132.9 %collective-permute-start.19 = (bf16[4,592,512]{2,1,0:T(8,128)(2,1)}, bf16[4,592,512]{2,1,0:T(8,128)(2,1)}, u32[]{:S(2)}, u32[]{:S(2)}) collective-permute-start(bf16[4,592,512]{2,1,0:T(8,128)(2,1)} %copy_sets.8), channel_id=1, source_target_pairs={{0,2},{2,0},{4,6},{6,4},{8,10},{10,8},{12,14},{14,12},{1,3},{3,1},... | collective-permute-start | bytes 7274504 | tf_op jit(solution)/shard_map/ppermute | solution.py:225
  198.8 133.8 %collective-permute-start.17 = (bf16[4,592,512]{2,1,0:T(8,128)(2,1)}, bf16[4,592,512]{2,1,0:T(8,128)(2,1)}, u32[]{:S(2)}, u32[]{:S(2)}) collective-permute-start(bf16[4,592,512]{2,1,0:T(8,128)(2,1)} %collective-permute-done.3.rest_0_.rest_4_), channel_id=1, source_target_pairs={{0,1},{1,0},{2,3},{3,2},{4,5},{5,4},{6,7},{7,6},{8,9},{9,8},{10,11... | collective-permute-start | bytes 7274504 | tf_op jit(solution)/shard_map/ppermute | solution.py:228
  199.1 6.1 %copy-start.8 = (bf16[4,576]{1,0:T(4,128)(2,1)S(1)}, bf16[4,576]{1,0:T(4,128)(2,1)}, u32[]{:S(2)}) copy-start(bf16[4,576]{1,0:T(4,128)(2,1)} %param.7) | copy-start | bytes 13828
  199.1 6.5 %copy-start.11 = (f32[32]{0:T(128)S(1)}, f32[32]{0:T(128)}, u32[]{:S(2)}) copy-start(f32[32]{0:T(128)} %param.8) | copy-start | bytes 388
  199.1 134.4 %collective-permute-start.18 = (bf16[4,592,512]{2,1,0:T(8,128)(2,1)}, bf16[4,592,512]{2,1,0:T(8,128)(2,1)}, u32[]{:S(2)}, u32[]{:S(2)}) collective-permute-start(bf16[4,592,512]{2,1,0:T(8,128)(2,1)} %collective-permute-done.5.rest_1_.rest_5_.rest_2_), channel_id=1, source_target_pairs={{0,1},{1,0},{2,3},{3,2},{4,5},{5,4},{6,7},{7,6},{8,9},{9,8},{10,11... | collective-permute-start | bytes 7274504 | tf_op jit(solution)/shard_map/ppermute | solution.py:228
  205.2 124.3 %collective-permute-start.22 = (bf16[2,592,512]{2,1,0:T(8,128)(2,1)}, bf16[2,592,512]{2,1,0:T(8,128)(2,1)}, u32[]{:S(2)}, u32[]{:S(2)}) collective-permute-start(bf16[2,592,512]{2,1,0:T(8,128)(2,1)} %collective-permute-done.21.rest_2_), channel_id=1, source_target_pairs={{0,1},{1,0},{2,3},{3,2},{4,5},{5,4},{6,7},{7,6},{8,9},{9,8},{10,11... | collective-permute-start | bytes 3637256 | tf_op jit(solution)/shard_map/ppermute | solution.py:228
  247.6 1.5 copy-start.2
  249.1 84.9 %collective-permute-start.7 = (bf16[2,592,512]{2,1,0:T(8,128)(2,1)}, bf16[2,592,512]{2,1,0:T(8,128)(2,1)}, u32[]{:S(2)}, u32[]{:S(2)}) collective-permute-start(bf16[2,592,512]{2,1,0:T(8,128)(2,1)} %copy_sets.5.rest_8_), channel_id=1, source_target_pairs={{4,0},{6,2},{8,12},{10,14},{5,1},{7,3},{9,13},{11,15},{20,16},{22,... | collective-permute-start | bytes 3637256 | tf_op jit(solution)/shard_map/ppermute | solution.py:344
  290.9 78.0 %copy-start.1 = (bf16[4,592,512]{2,1,0:T(8,128)(2,1)S(1)}, bf16[4,592,512]{2,1,0:T(8,128)(2,1)}, u32[]{:S(2)}) copy-start(bf16[4,592,512]{2,1,0:T(8,128)(2,1)} %copy-done) | copy-start | bytes 7274500
  329.6 29.2 %collective-permute-start.15 = (bf16[2,592,512]{2,1,0:T(8,128)(2,1)}, bf16[2,592,512]{2,1,0:T(8,128)(2,1)}, u32[]{:S(2)}, u32[]{:S(2)}) collective-permute-start(bf16[2,592,512]{2,1,0:T(8,128)(2,1)} %copy_sets.7), channel_id=1, source_target_pairs={{0,2},{2,0},{4,6},{6,4},{8,10},{10,8},{12,14},{14,12},{1,3},{3,1},... | collective-permute-start | bytes 3637256 | tf_op jit(solution)/shard_map/ppermute | solution.py:225
  331.3 36.4 %collective-permute-start.9 = (bf16[2,592,512]{2,1,0:T(8,128)(2,1)}, bf16[2,592,512]{2,1,0:T(8,128)(2,1)}, u32[]{:S(2)}, u32[]{:S(2)}) collective-permute-start(bf16[2,592,512]{2,1,0:T(8,128)(2,1)} %copy_sets.6.rest_9_), channel_id=1, source_target_pairs={{4,0},{6,2},{8,12},{10,14},{5,1},{7,3},{9,13},{11,15},{20,16},{22,... | collective-permute-start | bytes 3637256 | tf_op jit(solution)/shard_map/ppermute | solution.py:344
  332.6 47.9 %collective-permute-start.20 = (bf16[4,592,512]{2,1,0:T(8,128)(2,1)}, bf16[4,592,512]{2,1,0:T(8,128)(2,1)}, u32[]{:S(2)}, u32[]{:S(2)}) collective-permute-start(bf16[4,592,512]{2,1,0:T(8,128)(2,1)} %collective-permute-done.19.rest_4_), channel_id=1, source_target_pairs={{0,1},{1,0},{2,3},{3,2},{4,5},{5,4},{6,7},{7,6},{8,9},{9,8},{10,11... | collective-permute-start | bytes 7274504 | tf_op jit(solution)/shard_map/ppermute | solution.py:228
  333.5 68.8 %collective-permute-start.13 = (bf16[4,592,512]{2,1,0:T(8,128)(2,1)}, bf16[4,592,512]{2,1,0:T(8,128)(2,1)}, u32[]{:S(2)}, u32[]{:S(2)}) collective-permute-start(bf16[4,592,512]{2,1,0:T(8,128)(2,1)} %collective-permute-done.4.rest_0_.rest_6_), channel_id=1, source_target_pairs={{0,1},{1,0},{2,3},{3,2},{4,5},{5,4},{6,7},{7,6},{8,9},{9,8},{10,11... | collective-permute-start | bytes 7274504 | tf_op jit(solution)/shard_map/ppermute | solution.py:228
  334.1 68.3 %collective-permute-start.14 = (bf16[4,592,512]{2,1,0:T(8,128)(2,1)}, bf16[4,592,512]{2,1,0:T(8,128)(2,1)}, u32[]{:S(2)}, u32[]{:S(2)}) collective-permute-start(bf16[4,592,512]{2,1,0:T(8,128)(2,1)} %collective-permute-done.6.rest_1_.rest_7_.rest_2_), channel_id=1, source_target_pairs={{0,1},{1,0},{2,3},{3,2},{4,5},{5,4},{6,7},{7,6},{8,9},{9,8},{10,11... | collective-permute-start | bytes 7274504 | tf_op jit(solution)/shard_map/ppermute | solution.py:228
  358.8 21.8 %collective-permute-start.16 = (bf16[2,592,512]{2,1,0:T(8,128)(2,1)}, bf16[2,592,512]{2,1,0:T(8,128)(2,1)}, u32[]{:S(2)}, u32[]{:S(2)}) collective-permute-start(bf16[2,592,512]{2,1,0:T(8,128)(2,1)} %collective-permute-done.15.rest_4_), channel_id=1, source_target_pairs={{0,1},{1,0},{2,3},{3,2},{4,5},{5,4},{6,7},{7,6},{8,9},{9,8},{10,11... | collective-permute-start | bytes 3637256 | tf_op jit(solution)/shard_map/ppermute | solution.py:228
  367.7 28.4 %collective-permute-start.11 = (bf16[2,592,512]{2,1,0:T(8,128)(2,1)}, bf16[2,592,512]{2,1,0:T(8,128)(2,1)}, u32[]{:S(2)}, u32[]{:S(2)}) collective-permute-start(bf16[2,592,512]{2,1,0:T(8,128)(2,1)} %collective-permute-done.7.rest_6_.rest_0_), channel_id=1, source_target_pairs={{0,2},{2,0},{4,6},{6,4},{8,10},{10,8},{12,14},{14,12},{1,3},{3,1},... | collective-permute-start | bytes 3637256 | tf_op jit(solution)/shard_map/ppermute | solution.py:225
  368.9 1.7 copy-start.3
  370.6 25.5 %copy-start.4 = (bf16[4,592,512]{2,1,0:T(8,128)(2,1)S(1)}, bf16[4,592,512]{2,1,0:T(8,128)(2,1)}, u32[]{:S(2)}) copy-start(bf16[4,592,512]{2,1,0:T(8,128)(2,1)} %copy-done.2) | copy-start | bytes 7274500
  370.6 25.5 %copy-start.5 = (bf16[2,592,512]{2,1,0:T(8,128)(2,1)S(1)}, bf16[2,592,512]{2,1,0:T(8,128)(2,1)}, u32[]{:S(2)}) copy-start(bf16[2,592,512]{2,1,0:T(8,128)(2,1)} %copy_sets.5.rest_8_) | copy-start | bytes 3637252
  370.6 25.5 %copy-start.6 = (bf16[2,592,512]{2,1,0:T(8,128)(2,1)S(1)}, bf16[2,592,512]{2,1,0:T(8,128)(2,1)}, u32[]{:S(2)}) copy-start(bf16[2,592,512]{2,1,0:T(8,128)(2,1)} %copy_sets.6.rest_9_) | copy-start | bytes 3637252
  380.5 34.3 %collective-permute-start.8 = (bf16[2,592,512]{2,1,0:T(8,128)(2,1)}, bf16[2,592,512]{2,1,0:T(8,128)(2,1)S(1)}, u32[]{:S(2)}, u32[]{:S(2)}) collective-permute-start(bf16[2,592,512]{2,1,0:T(8,128)(2,1)} %collective-permute-done.7.rest_6_.rest_0_), channel_id=1, source_target_pairs={{0,1},{1,0},{2,3},{3,2},{4,5},{5,4},{6,7},{7,6},{8,9},{9,8},{10,11... | collective-permute-start | bytes 3637256 | tf_op jit(solution)/shard_map/ppermute | solution.py:228
  380.6 34.2 %collective-permute-start.10 = (bf16[2,592,512]{2,1,0:T(8,128)(2,1)}, bf16[2,592,512]{2,1,0:T(8,128)(2,1)S(1)}, u32[]{:S(2)}, u32[]{:S(2)}) collective-permute-start(bf16[2,592,512]{2,1,0:T(8,128)(2,1)} %collective-permute-done.9.rest_2_), channel_id=1, source_target_pairs={{0,1},{1,0},{2,3},{3,2},{4,5},{5,4},{6,7},{7,6},{8,9},{9,8},{10,11... | collective-permute-start | bytes 3637256 | tf_op jit(solution)/shard_map/ppermute | solution.py:228
  396.0 18.8 %collective-permute-start.12 = (bf16[2,592,512]{2,1,0:T(8,128)(2,1)}, bf16[2,592,512]{2,1,0:T(8,128)(2,1)S(1)}, u32[]{:S(2)}, u32[]{:S(2)}) collective-permute-start(bf16[2,592,512]{2,1,0:T(8,128)(2,1)} %collective-permute-done.11.rest_4_), channel_id=1, source_target_pairs={{0,1},{1,0},{2,3},{3,2},{4,5},{5,4},{6,7},{7,6},{8,9},{9,8},{10,11... | collective-permute-start | bytes 3637256 | tf_op jit(solution)/shard_map/ppermute | solution.py:228

commit v4 on v3

--- a/solution.py
+++ b/solution.py
@@ -8,6 +8,7 @@
 from jax.sharding import PartitionSpec as P
 
 NT = (((1,), (1,)), ((), ()))
+VMEM_LIMIT = 56 * 1024 * 1024
 EXTRA = 16
 
 
@@ -130,7 +131,7 @@
     pairs_here, _, kept, span = pick.shape
     n_first = ve1.shape[0]
     full, half = own.shape[1], own.shape[2]
-    any_spec = pl.BlockSpec(memory_space=pl.ANY)
+    any_spec = ANY_SPEC
     smem = pl.BlockSpec(memory_space=pltpu.SMEM)
     vmem = pl.BlockSpec(memory_space=pltpu.VMEM)
     operands = [meta, shift, ve1, pick, own, other]
@@ -163,7 +164,7 @@
             pltpu.SemaphoreType.DMA((2,)),
         ],
         input_output_aliases=aliases,
-        compiler_params=pltpu.CompilerParams(vmem_limit_bytes=40 * 1024 * 1024),
+        compiler_params=pltpu.CompilerParams(vmem_limit_bytes=VMEM_LIMIT),
         cost_estimate=pl.CostEstimate(
             flops=int(expected * 4 * kept * kept * 2 * half * 2),
             bytes_accessed=int(expected * (full * half * 4 + kept * kept * 2)),
@@ -172,33 +173,84 @@
     )(*operands)
 
 
-def set_kernel(n_arrays, table_ref, *rest):
+def set_kernel(n_arrays, n_skip, table_ref, *rest):
     arrays = rest[:n_arrays]
-    out_ref, sems = rest[n_arrays:]
-    for j in range(out_ref.shape[0]):
+    out_ref, held, in_sems, out_sems = rest[n_arrays + n_skip:]
+    count = out_ref.shape[0]
+    for j in range(count):
         for k, a in enumerate(arrays):
             @pl.when(table_ref[0, j] == k)
             def _():
-                pltpu.make_async_copy(a.at[table_ref[1, j]], out_ref.at[j], sems.at[j]).start()
-    for j in range(out_ref.shape[0]):
-        pltpu.make_async_copy(arrays[0].at[0], out_ref.at[j], sems.at[j]).wait()
-
-
-def copy_sets(which, index, arrays):
+                pltpu.make_async_copy(a.at[table_ref[1, j]], held.at[j], in_sems.at[j]).start()
+    for j in range(count):
+        pltpu.make_async_copy(arrays[0].at[0], held.at[j], in_sems.at[j]).wait()
+        pltpu.make_async_copy(held.at[j], out_ref.at[j], out_sems.at[j]).start()
+    for j in range(count):
+        pltpu.make_async_copy(held.at[j], out_ref.at[j], out_sems.at[j]).wait()
+
+
+ANY_SPEC = pl.BlockSpec(memory_space=pl.ANY)
+
+
+def copy_sets(which, index, arrays, after=()):
     n = len(index)
     table = jnp.stack([jnp.stack([jnp.asarray(w, jnp.int32) for w in which]), jnp.stack(index)])
     block = arrays[0].shape[1:]
-    any_spec = pl.BlockSpec(memory_space=pl.ANY)
     size = 2 * n * block[0] * block[1] * 2
     return pl.pallas_call(
-        functools.partial(set_kernel, len(arrays)),
+        functools.partial(set_kernel, len(arrays), len(after)),
         out_shape=jax.ShapeDtypeStruct((n,) + block, arrays[0].dtype),
-        in_specs=[pl.BlockSpec(memory_space=pltpu.SMEM)] + [any_spec] * len(arrays),
-        out_specs=any_spec,
-        scratch_shapes=[pltpu.SemaphoreType.DMA((n,))],
+        in_specs=[pl.BlockSpec(memory_space=pltpu.SMEM)] + [ANY_SPEC] * (len(arrays) + len(after)),
+        out_specs=ANY_SPEC,
+        scratch_shapes=[
+            pltpu.VMEM((n,) + block, arrays[0].dtype),
+            pltpu.SemaphoreType.DMA((n,)),
+            pltpu.SemaphoreType.DMA((n,))],
         cost_estimate=pl.CostEstimate(flops=0, bytes_accessed=size, transcendentals=0),
+        compiler_params=pltpu.CompilerParams(vmem_limit_bytes=VMEM_LIMIT),
         name="copy_sets",
-    )(table, *arrays)
+    )(table, *arrays, *after)
+
+
+def extend_kernel(blocks_ref, extra_ref, out_ref, held, in_sems, out_sems):
+    count, full, _ = blocks_ref.shape
+    for k in range(count):
+        pltpu.make_async_copy(blocks_ref.at[k], held.at[k, 0:full], in_sems.at[k]).start()
+    for k in range(count):
+        held[k, full:, :] = extra_ref[k]
+    for k in range(count):
+        pltpu.make_async_copy(blocks_ref.at[k], held.at[k, 0:full], in_sems.at[k]).wait()
+        pltpu.make_async_copy(held.at[k], out_ref.at[k], out_sems.at[k]).start()
+    for k in range(count):
+        pltpu.make_async_copy(held.at[k], out_ref.at[k], out_sems.at[k]).wait()
+
+
+def extend(blocks, extra):
+    count, full, half = blocks.shape
+    shape = (count, full + extra.shape[1], half)
+    return pl.pallas_call(
+        extend_kernel,
+        out_shape=jax.ShapeDtypeStruct(shape, blocks.dtype),
+        in_specs=[ANY_SPEC, pl.BlockSpec(memory_space=pltpu.VMEM)],
+        out_specs=ANY_SPEC,
+        scratch_shapes=[
+            pltpu.VMEM(shape, blocks.dtype), pltpu.SemaphoreType.DMA((count,)), pltpu.SemaphoreType.DMA((count,))],
+        compiler_params=pltpu.CompilerParams(vmem_limit_bytes=VMEM_LIMIT),
+        name="extend",
+    )(blocks, extra)
+
+
+def tie(x, deps):
+    return pl.pallas_call(
+        lambda *refs: None,
+        out_shape=jax.ShapeDtypeStruct(x.shape, x.dtype),
+        in_specs=[ANY_SPEC] * (1 + len(deps)),
+        out_specs=ANY_SPEC,
+        input_output_aliases={0: 0},
+        compiler_params=pltpu.CompilerParams(vmem_limit_bytes=VMEM_LIMIT),
+        cost_estimate=pl.CostEstimate(flops=0, bytes_accessed=0, transcendentals=0),
+        name="tie",
+    )(x, *deps)
 
 
 def per_device(blocks, virt_energy, occ_energy, owner_slot, pairs, domains):
@@ -236,12 +288,9 @@
     extra = [
         jnp.pad(virt_energy[:, None, b:b + sp], ((0, 0), (0, 0), (0, half - sp))) for b, _, sp in wins]
     extra.append(jnp.zeros((occ_dev, EXTRA - len(wins), half), blocks.dtype))
-    stored = jnp.concatenate([blocks] + extra, axis=1)
-
-    downs, ups = [stored], [stored]
-    for d in range(1, last):
-        downs.append(hop_down(downs[-1], d))
-        ups.append(hop_up(ups[-1], d))
+    stored = extend(blocks, jnp.concatenate(extra, axis=1))
+
+    downs, ups = [stored, hop_down(stored, 1)], [stored, hop_up(stored, 1)]
     local_other = across_aux(stored)
 
     orbitals = jnp.arange(owner_slot.shape[0], dtype=i32)
@@ -320,38 +369,61 @@
     def two_for_opposite(source):
         return [idx_of(want_opp[0], source), idx_of(want_opp[1], source)]
 
-    y_own = across_y(copy_sets([0, 0], two_for_opposite(o), [stored]))
-    sets = {0: [(stored, local_other), (y_own, across_aux(y_own))]}
-    after = {0: [downs[1], ups[1]]}
+    def pairs_at(d, sets, after, prev):
+        return run_pairs(d, own_rows / chain, wins, meta, shift, ve1, pick, stored, local_other, sets, after, prev)
+
+    def pairs_at(d, after, prev):
+        return run_pairs(d, own_rows / chain, wins, meta, shift, ve1, pick, stored, local_other, sets[d], after, prev)
+
+    y_load = copy_sets([0, 0], two_for_opposite(o), [stored])
+    opp = [across_y(y_load)]
+    early = [y_load, pick, meta]
+    downs[1], ups[1] = tie(downs[1], early), tie(ups[1], early)
+    sets = {}
+    out = None
     for d in range(1, last):
         s_down, s_up = o + 2 * d, o - 2 * d
+        loads = []
+        if d + 1 < last:
+            downs.append(hop_down(downs[d], d + 1))
+            ups.append(hop_up(ups[d], d + 1))
+        else:
+            sends_down = z == 1
+            turn_of = idx_of(far_place(wanted_far), jnp.where(sends_down, 2 * last + y, y))
+            turn = [jnp.sum(jnp.where(turn_of == j, local[0], 0)) for j in range(occ_dev)]
+            perm = [(2, 0), (3, 1), (2 * (last - 1), 2 * last), (2 * (last - 1) + 1, 2 * last + 1)]
+            is_up = 1 - sends_down.astype(i32)
+            load_a = copy_sets([is_up, is_up], turn[:2], [downs[d], ups[d]])
+            load_b = copy_sets([is_up, is_up], turn[2:], [downs[d], ups[d]], [load_a])
+            got_a, got_b = lax.ppermute(load_a, "orb", perm), lax.ppermute(load_b, "orb", perm)
+            loads = [load_b]
+            if d > 1:
+                opp[d - 1] = tie(opp[d - 1], loads)
         if 2 * d <= last:
-            theirs = copy_sets([0, 0, 1, 1], two_for_opposite(s_down) + two_for_opposite(s_up), [downs[d], ups[d]])
+            theirs = copy_sets(
+                [0, 0, 1, 1], two_for_opposite(s_down) + two_for_opposite(s_up), [downs[d], ups[d]], loads)
         else:
             is_up = (z + d > last).astype(i32)
             s = jnp.where(is_up == 1, s_up, s_down)
-            theirs = copy_sets([is_up, is_up], two_for_opposite(s), [downs[d], ups[d]])
-        opp_own = across_y(theirs)
-        sets[d] = [
-            (downs[d], across_aux(downs[d])), (ups[d], across_aux(ups[d])), (opp_own, across_aux(opp_own))]
-        after[d] = [] if d == last - 1 else [downs[d + 1], ups[d + 1]]
-    sends_down = z == 1
-    turn_of = idx_of(far_place(wanted_far), jnp.where(sends_down, 2 * last + y, y))
-    turn = [jnp.sum(jnp.where(turn_of == j, local[0], 0)) for j in range(occ_dev)]
-    perm = [(2, 0), (3, 1), (2 * (last - 1), 2 * last), (2 * (last - 1) + 1, 2 * last + 1)]
-    is_up = 1 - sends_down.astype(i32)
-    loads = [copy_sets([is_up, is_up], turn[j:j + 2], [downs[-1], ups[-1]]) for j in range(0, occ_dev, 2)]
-    got_a, got_b = [lax.ppermute(load, "orb", perm) for load in loads]
-    opp_own = across_y(got_a)
-    sets[last] = [(got_a, across_aux(got_a)), (got_b, across_aux(got_b)), (opp_own, across_aux(opp_own))]
-    for d in range(1, last):
-        after[d] = after[d] + (loads if d == last - 2 else [got_a] if d == last - 1 else [])
-    after[last] = []
-    out = None
-    for d in range(chain):
-        out = run_pairs(
-            d, own_rows / chain, wins, meta, shift, ve1, pick, stored, local_other, sets[d], after[d], out)
-    return out
+            theirs = copy_sets([is_up, is_up], two_for_opposite(s), [downs[d], ups[d]], loads)
+        opp.append(across_y(theirs))
+        if d == 1:
+            sets[0] = [(stored, local_other), (opp[0], across_aux(opp[0]))]
+        else:
+            sets[d - 1] = [
+                (downs[d - 1], across_aux(downs[d - 1])), (ups[d - 1], across_aux(ups[d - 1])),
+                (opp[d - 1], across_aux(opp[d - 1]))]
+            out = pairs_at(d - 2, [theirs] + loads, out)
+    got_a = tie(got_a, [out])
+    opp.append(across_y(got_a))
+    sets[last - 1] = [
+        (downs[last - 1], across_aux(downs[last - 1])), (ups[last - 1], across_aux(ups[last - 1])),
+        (opp[last - 1], across_aux(opp[last - 1]))]
+    out = pairs_at(last - 2, [got_a], out)
+    out = pairs_at(last - 1, [got_a], out)
+    got_b = tie(got_b, [out])
+    sets[last] = [(got_a, across_aux(got_a)), (got_b, across_aux(got_b)), (opp[last], across_aux(opp[last]))]
+    return pairs_at(last, [], out)
 
 
 def solution(mesh):

time: 426 us -> 248 us (0.58)
  Pallas kernels: 267 us -> 58.6 us
  waiting for transfers between devices: 93.2 us -> 125 us
  local copies, waits for them, and re-layouts: 17.9 us -> 12.9 us
    pallas_call x5 -> x11, Pallas kernels: 230 us -> 18.3 us  [the longest x5 14.8 us: copy_sets(): pl.pallas_call(functools.partial(set_kernel, len(arrays), len(after)), ou...]
    ppermute x2, waiting for transfers between devices: 0.01 us -> 31.7 us  [hop_up(): lax.ppermute(a, 'orb', [(k, k + 2) for k in range(orb_count - 2) if k //...]
    ppermute x2, waiting for transfers between devices: 44.7 us -> 26.9 us  [hop_down(): lax.ppermute(a, 'orb', [(k, k - 2) for k in range(2, orb_count) if k // 2...]
    ppermute x5, waiting for transfers between devices: 39.6 us -> 52.5 us  [across_y(): return lax.ppermute(a, 'orb', swap_y)]
    concatenate x1, local copies, waits for them, and re-layouts: 9.95 us -> 0.08 us  [per_device(): stored = extend(blocks, jnp.concatenate(extra, axis=1))]
  transfers between devices with their start and end apart: 23 -> 23, of which waited for: 4 -> 10; matrix products, arithmetic and copies ran while one was open for 5% -> 11% of each run, Pallas kernels for 61% -> 20%
where the time goes in v4:
time: 248 us; the launch traced here: 244 us
  waiting for transfers between devices  125 us (50%)
  Pallas kernels  58.6 us (24%)
  starting transfers between devices  25.4 us (10%)
  other arithmetic  21.7 us (9%)
  local copies, waits for them, and re-layouts  12.9 us (5%)
    ppermute x5, waiting for transfers between devices, across_y(): return lax.ppermute(a, 'orb', swap_y)  52.5 us
    pallas_call x4, Pallas kernels, run_pairs(): pl.pallas_call(functools.partial(pair_kernel, call, wins, len(sets), len(...  40.3 us
    ppermute x2, waiting for transfers between devices, hop_up(): lax.ppermute(a, 'orb', [(k, k + 2) for k in range(orb_count - 2) if k //...  31.7 us
    ppermute x2, waiting for transfers between devices, hop_down(): lax.ppermute(a, 'orb', [(k, k - 2) for k in range(2, orb_count) if k // 2...  26.9 us
    pallas_call x5, Pallas kernels, copy_sets(): pl.pallas_call(functools.partial(set_kernel, len(arrays), len(after)), ou...  14.8 us
    another operation x7, other arithmetic, copy_sets(): jnp.stack([jnp.stack([jnp.asarray(w, jnp.int32) for w in which]), jnp.sta...  9.43 us
    ppermute x5, starting transfers between devices, across_y(): return lax.ppermute(a, 'orb', swap_y)  7.89 us
    ppermute x1, waiting for transfers between devices, per_device(): lax.ppermute(load_b, 'orb', perm)  6.23 us
  transfers between devices with their start and end apart: 23, of which 10 were waited for; matrix products, arithmetic and copies ran while one was open for 11% of the time, Pallas kernels for 20%

profile of v4, /device:TPU:0, one launch (start us, length us, event | category | flops | bytes accessed | tf_op | source)
XLA Modules:
  0.0 244.4 jit_solution(15887090430030711511)
XLA Ops:
  0.0 0.7 slice_bitcast_fusion.5
  0.7 0.8 select_reduce_fusion
  1.6 3.0 %collective-permute-start = (s32[32]{0:T(128)S(1)}, s32[32]{0:T(128)S(1)}, u32[]{:S(2)}, u32[]{:S(2)}) collective-permute-start(s32[32]{0:T(128)S(1)} %convert_element_type.69), channel_id=1, source_target_pairs={{0,2},{2,0},{4,6},{6,4},{8,10},{10,8},{12,14},{14,12},{1,3},{3,1},... | collective-permute-start | bytes 392 | tf_op jit(solution)/shard_map/ppermute | solution.py:277
  4.7 3.4 %collective-permute-start.2 = (s32[32]{0:T(128)S(1)}, s32[32]{0:T(128)S(1)}, u32[]{:S(2)}, u32[]{:S(2)}) collective-permute-start(s32[32]{0:T(128)S(1)} %convert_element_type.69), channel_id=1, source_target_pairs={{0,6},{2,4},{14,8},{12,10},{1,7},{3,5},{15,9},{13,11},{16,22},{18,... | collective-permute-start | bytes 392 | tf_op jit(solution)/shard_map/ppermute | solution.py:305
  8.1 0.8 slice_bitcast_fusion.2
  8.9 0.7 slice_bitcast_fusion
  9.7 0.7 fusion.7.extra_ref
  10.4 3.5 %extend.1.rest_0_.own_ref = bf16[4,592,512]{2,1,0:T(8,128)(2,1)} custom-call(bf16[4,576,512]{2,1,0:T(8,128)(2,1)} %blocks_ref.1, bf16[4,16,512]{2,1,0:T(8,128)(2,1)} %fusion.7.extra_ref), custom_call_target="tpu_custom_call" | custom-call | tf_op jit(solution)/shard_map/extend/pallas_call | solution.py:231
  13.9 2.8 %collective-permute-start.5 = (bf16[4,592,512]{2,1,0:T(8,128)(2,1)}, bf16[4,592,512]{2,1,0:T(8,128)(2,1)}, u32[]{:S(2)}, u32[]{:S(2)}) collective-permute-start(bf16[4,592,512]{2,1,0:T(8,128)(2,1)} %extend.1.rest_0_.own_ref), channel_id=1, source_target_pairs={{0,4},{2,6},{4,8},{6,10},{8,12},{10,14},{1,5},{3,7},{5,9},{7,11},{... | collective-permute-start | bytes 7274504 | tf_op jit(solution)/shard_map/ppermute | solution.py:286
  16.7 1.3 collective-permute-start.3
  18.2 5.7 %fusion.refs_2_.pick_ref = bf16[16,2,512,256]{3,2,1,0:T(8,128)(2,1)} fusion(s32[16,2,512]{2,1,0:T(2,128)S(1)} %dynamic-slice_add_fusion), kind=kLoop, calls=%fused_computation.1 | loop fusion | flops 8388608 | bytes 8454144 | tf_op jit(solution)/shard_map/convert_element_type | solution.py:364
  25.1 0.7 fusion.19
  27.9 2.5 %add_bitcast_fusion.2 = (s32[1,2]{1,0:T(1,128)S(1)}, s32[1,2]{1,0:T(1,128)S(1)}) fusion(s32[1]{0:T(128)} %get-tuple-element.37, s32[1]{0:T(128)} %get-tuple-element.33, s32[1]{0:T(128)} %bitcast.22, s32[1]{0:T(128)} %bitcast.21), kind=kLoop, calls=%fused_computation.94 | loop fusion | flops 4 | bytes 32 | tf_op jit(solution)/shard_map/stack | solution.py:197
  31.1 2.8 %copy_sets.5.refs_1_ = bf16[2,592,512]{2,1,0:T(8,128)(2,1)} custom-call(s32[2,2]{1,0:T(2,128)} %stack.123.table_ref, bf16[4,592,512]{2,1,0:T(8,128)(2,1)} %extend.1.rest_0_.own_ref), custom_call_target="tpu_custom_call" | custom-call | bytes 2424832 | tf_op jit(solution)/shard_map/copy_sets/pallas_call | solution.py:200
  35.5 31.7 %collective-permute-done.5.refs_0_ = bf16[4,592,512]{2,1,0:T(8,128)(2,1)} collective-permute-done((bf16[4,592,512]{2,1,0:T(8,128)(2,1)}, bf16[4,592,512]{2,1,0:T(8,128)(2,1)}, u32[]{:S(2)}, u32[]{:S(2)}) %collective-permute-start.5) | collective-permute-done | bytes 2424864 | tf_op jit(solution)/shard_map/ppermute | solution.py:286
  67.2 2.2 collective-permute-start.6
  69.4 1.5 collective-permute-start.8
  70.9 1.9 collective-permute-done.3.refs_0_
  72.7 1.3 collective-permute-start.4
  74.0 2.5 %add_bitcast_fusion.6 = s32[1,4]{1,0:T(1,128)S(1)} fusion(s32[1]{0:T(128)} %get-tuple-element.35, s32[1]{0:T(128)} %get-tuple-element.31, s32[1]{0:T(128)} %get-tuple-element.34, s32[1]{0:T(128)} %get-tuple-element.30), kind=kLoop, calls=%fused_computation.98 | loop fusion | flops 12 | bytes 32 | tf_op jit(solution)/shard_map/stack | solution.py:197
  77.1 3.4 %copy_sets.9 = bf16[4,592,512]{2,1,0:T(8,128)(2,1)} custom-call(s32[2,4]{1,0:T(2,128)} %pad_add_fusion.3.table_ref, bf16[4,592,512]{2,1,0:T(8,128)(2,1)} %tie.5.rest_0_, bf16[4,592,512]{2,1,0:T(8,128)(2,1)} %tie.6.rest_1_.rest_2_), custom_call_target="tpu_custom_call" | custom-call | bytes 4849664 | tf_op jit(solution)/shard_map/copy_sets/pallas_call | solution.py:200
  80.5 1.5 collective-permute-start.18
  82.0 17.0 %collective-permute-done.8.rest_2_ = bf16[2,592,512]{2,1,0:T(8,128)(2,1)S(1)} collective-permute-done((bf16[2,592,512]{2,1,0:T(8,128)(2,1)S(1)}, bf16[2,592,512]{2,1,0:T(8,128)(2,1)S(1)}, u32[]{:S(2)}, u32[]{:S(2)}) %collective-permute-start.8) | collective-permute-done | bytes 1212448 | tf_op jit(solution)/shard_map/ppermute | solution.py:277
  99.0 1.0 copy-done.15
  101.9 1.3 add_bitcast_fusion
  103.8 25.1 %collective-permute-done.4.rest_0_ = bf16[4,592,512]{2,1,0:T(8,128)(2,1)} collective-permute-done((bf16[4,592,512]{2,1,0:T(8,128)(2,1)}, bf16[4,592,512]{2,1,0:T(8,128)(2,1)}, u32[]{:S(2)}, u32[]{:S(2)}) %collective-permute-start.4) | collective-permute-done | bytes 2424864 | tf_op jit(solution)/shard_map/ppermute | solution.py:283
  128.9 2.8 %copy_sets.6.rest_2_ = bf16[2,592,512]{2,1,0:T(8,128)(2,1)} custom-call(s32[2,2]{1,0:T(2,128)} %get-tuple-element.39.table_ref, bf16[4,592,512]{2,1,0:T(8,128)(2,1)} %collective-permute-done.4.rest_0_, bf16[4,592,512]{2,1,0:T(8,128)(2,1)} %collective-permute-done.6.rest_1_.rest_2_), custom_call_target="tpu_custom_call" | custom-call | bytes 2424832 | tf_op jit(solution)/shard_map/copy_sets/pallas_call | solution.py:200
  131.7 1.3 collective-permute-start.7
  133.0 2.8 %copy_sets.7.rest_2_.rest_5_.refs_1_ = bf16[2,592,512]{2,1,0:T(8,128)(2,1)} custom-call(s32[2,2]{1,0:T(2,128)} %get-tuple-element.38.table_ref, bf16[4,592,512]{2,1,0:T(8,128)(2,1)} %collective-permute-done.4.rest_0_, bf16[4,592,512]{2,1,0:T(8,128)(2,1)} %collective-permute-done.6.rest_1_.rest_2_, bf16[2,592,512]{2,1,0:T(8,128)(2,1)} %copy_sets.6.rest_2_), custom_call_target="tpu_custom_call" | custom-call | bytes 2424832 | tf_op jit(solution)/shard_map/copy_sets/pallas_call | solution.py:200
  135.9 12.8 %collective-permute-done.18.refs_0_ = bf16[4,592,512]{2,1,0:T(8,128)(2,1)} collective-permute-done((bf16[4,592,512]{2,1,0:T(8,128)(2,1)}, bf16[4,592,512]{2,1,0:T(8,128)(2,1)}, u32[]{:S(2)}, u32[]{:S(2)}) %collective-permute-start.18) | collective-permute-done | bytes 2424864 | tf_op jit(solution)/shard_map/ppermute | solution.py:277
  149.2 1.3 add_bitcast_fusion.3
  151.1 2.9 %copy_sets.8.rest_4_ = bf16[2,592,512]{2,1,0:T(8,128)(2,1)} custom-call(s32[2,2]{1,0:T(2,128)} %pad_add_fusion.2.table_ref, bf16[4,592,512]{2,1,0:T(8,128)(2,1)} %collective-permute-done.4.rest_0_, bf16[4,592,512]{2,1,0:T(8,128)(2,1)} %collective-permute-done.6.rest_1_.rest_2_, bf16[2,592,512]{2,1,0:T(8,128)(2,1)} %copy_sets.7.rest_2_.rest_5_.refs_1_), custom_call_target="tpu_custom_call" | custom-call | bytes 2424832 | tf_op jit(solution)/shard_map/copy_sets/pallas_call | solution.py:200
  154.1 1.8 collective-permute-start.14
  155.9 3.7 %collective-permute-done.7.refs_0_ = bf16[2,592,512]{2,1,0:T(8,128)(2,1)} collective-permute-done((bf16[2,592,512]{2,1,0:T(8,128)(2,1)}, bf16[2,592,512]{2,1,0:T(8,128)(2,1)}, u32[]{:S(2)}, u32[]{:S(2)}) %collective-permute-start.7) | collective-permute-done | bytes 1212448 | tf_op jit(solution)/shard_map/ppermute | solution.py:398
  160.5 22.6 %collective-permute-done.14.rest_4_ = bf16[2,592,512]{2,1,0:T(8,128)(2,1)} collective-permute-done((bf16[2,592,512]{2,1,0:T(8,128)(2,1)}, bf16[2,592,512]{2,1,0:T(8,128)(2,1)}, u32[]{:S(2)}, u32[]{:S(2)}) %collective-permute-start.14) | collective-permute-done | bytes 1212448 | tf_op jit(solution)/shard_map/ppermute | solution.py:277
  183.1 0.9 broadcast_in_dim.95.ve1_ref
  184.0 10.1 %pairs_0.1.refs_1_.rest_7_ = bf16[16,512,512]{2,1,0:T(8,128)(2,1)} custom-call(s32[5,16]{1,0:T(8,128)} %stack.112.refs_3_.meta_ref, f32[16]{0:T(128)} %add.107.shift_ref, bf16[2,576,128]{2,1,0:T(8,128)(2,1)} %broadcast_in_dim.95.ve1_ref, bf16[16,2,512,256]{3,2,1,0:T(8,128)(2,1)} %fusion.refs_2_.pick_ref, bf16[4,592,512]{2,1,0:T(8,128)(2,1)} %extend.1.rest_0_.own_ref, ...), custom_call_target="tpu_custom_call" | custom-call | flops 8589934592 | bytes 6946816 | tf_op jit(solution)/shard_map/pairs_0/pallas_call | solution.py:148
  194.1 1.3 copy-done.1
  195.4 1.3 collective-permute-start.11
  196.8 1.3 copy-done.4
  198.1 14.7 %pairs_1.1.rest_7_ = bf16[16,512,512]{2,1,0:T(8,128)(2,1)} custom-call(s32[5,16]{1,0:T(8,128)} %stack.112.refs_3_.meta_ref, f32[16]{0:T(128)} %add.107.shift_ref, bf16[2,576,128]{2,1,0:T(8,128)(2,1)} %broadcast_in_dim.95.ve1_ref, bf16[16,2,512,256]{3,2,1,0:T(8,128)(2,1)} %fusion.refs_2_.pick_ref, ...), custom_call_target="tpu_custom_call", output_to_operand_aliasing={{}: (13, {})} | custom-call | flops 8589934592 | bytes 6946816 | tf_op jit(solution)/shard_map/pairs_1/pallas_call | solution.py:148
  213.0 7.0 %pairs_2.1.refs_1_.rest_6_ = bf16[16,512,512]{2,1,0:T(8,128)(2,1)} custom-call(s32[5,16]{1,0:T(8,128)} %stack.112.refs_3_.meta_ref, f32[16]{0:T(128)} %add.107.shift_ref, bf16[2,576,128]{2,1,0:T(8,128)(2,1)} %broadcast_in_dim.95.ve1_ref, bf16[16,2,512,256]{3,2,1,0:T(8,128)(2,1)} %fusion.refs_2_.pick_ref, ...), custom_call_target="tpu_custom_call", output_to_operand_aliasing={{}: (13, {})} | custom-call | flops 8589934592 | bytes 6946816 | tf_op jit(solution)/shard_map/pairs_2/pallas_call | solution.py:148
  219.9 6.2 %collective-permute-done.11.refs_0_ = bf16[2,592,512]{2,1,0:T(8,128)(2,1)S(1)} collective-permute-done((bf16[2,592,512]{2,1,0:T(8,128)(2,1)S(1)}, bf16[2,592,512]{2,1,0:T(8,128)(2,1)S(1)}, u32[]{:S(2)}, u32[]{:S(2)}) %collective-permute-start.11) | collective-permute-done | bytes 1212448 | tf_op jit(solution)/shard_map/ppermute | solution.py:398
  226.2 1.0 copy-done.3
  227.2 2.8 %collective-permute-start.20 = (bf16[2,592,512]{2,1,0:T(8,128)(2,1)}, bf16[2,592,512]{2,1,0:T(8,128)(2,1)S(1)}, u32[]{:S(2)}, u32[]{:S(2)}) collective-permute-start(bf16[2,592,512]{2,1,0:T(8,128)(2,1)} %tie.9.rest_2_), channel_id=1, source_target_pairs={{0,1},{1,0},{2,3},{3,2},{4,5},{5,4},{6,7},{7,6},{8,9},{9,8},{10,11... | collective-permute-start | bytes 3637256 | tf_op jit(solution)/shard_map/ppermute | solution.py:280
  230.2 3.6 %collective-permute-done.20.rest_3_ = bf16[2,592,512]{2,1,0:T(8,128)(2,1)S(1)} collective-permute-done((bf16[2,592,512]{2,1,0:T(8,128)(2,1)}, bf16[2,592,512]{2,1,0:T(8,128)(2,1)S(1)}, u32[]{:S(2)}, u32[]{:S(2)}) %collective-permute-start.20) | collective-permute-done | bytes 1212448 | tf_op jit(solution)/shard_map/ppermute | solution.py:280
  234.8 1.0 copy-done.8
  235.8 8.5 %pairs_3.1 = bf16[16,512,512]{2,1,0:T(8,128)(2,1)} custom-call(s32[5,16]{1,0:T(8,128)} %stack.112.refs_3_.meta_ref, f32[16]{0:T(128)} %add.107.shift_ref, bf16[2,576,128]{2,1,0:T(8,128)(2,1)} %broadcast_in_dim.95.ve1_ref, bf16[16,2,512,256]{3,2,1,0:T(8,128)(2,1)} %fusion.refs_2_.pick_ref, ...), custom_call_target="tpu_custom_call", output_to_operand_aliasing={{}: (12, {})} | custom-call | flops 8589934592 | bytes 6946816 | tf_op jit(solution)/shard_map/pairs_3/pallas_call | solution.py:148
  (113 shorter events, 12.0 us)
Async XLA Ops:
  1.6 22.5 %collective-permute-start = (s32[32]{0:T(128)S(1)}, s32[32]{0:T(128)S(1)}, u32[]{:S(2)}, u32[]{:S(2)}) collective-permute-start(s32[32]{0:T(128)S(1)} %convert_element_type.69), channel_id=1, source_target_pairs={{0,2},{2,0},{4,6},{6,4},{8,10},{10,8},{12,14},{14,12},{1,3},{3,1},... | collective-permute-start | bytes 392 | tf_op jit(solution)/shard_map/ppermute | solution.py:277
  4.7 19.7 %collective-permute-start.2 = (s32[32]{0:T(128)S(1)}, s32[32]{0:T(128)S(1)}, u32[]{:S(2)}, u32[]{:S(2)}) collective-permute-start(s32[32]{0:T(128)S(1)} %convert_element_type.69), channel_id=1, source_target_pairs={{0,6},{2,4},{14,8},{12,10},{1,7},{3,5},{15,9},{13,11},{16,22},{18,... | collective-permute-start | bytes 392 | tf_op jit(solution)/shard_map/ppermute | solution.py:305
  10.4 7.8 %copy-start.9 = (s32[32,2,512]{2,1,0:T(2,128)S(1)}, s32[32,2,512]{2,1,0:T(2,128)}, u32[]{:S(2)}) copy-start(s32[32,2,512]{2,1,0:T(2,128)} %param.11) | copy-start | bytes 393220
  10.4 7.8 %copy-start.11 = (s32[512]{0:T(512)S(1)}, s32[512]{0:T(512)}, u32[]{:S(2)}) copy-start(s32[512]{0:T(512)} %constant.150.clone.1) | copy-start | bytes 6148
  13.9 53.3 %collective-permute-start.5 = (bf16[4,592,512]{2,1,0:T(8,128)(2,1)}, bf16[4,592,512]{2,1,0:T(8,128)(2,1)}, u32[]{:S(2)}, u32[]{:S(2)}) collective-permute-start(bf16[4,592,512]{2,1,0:T(8,128)(2,1)} %extend.1.rest_0_.own_ref), channel_id=1, source_target_pairs={{0,4},{2,6},{4,8},{6,10},{8,12},{10,14},{1,5},{3,7},{5,9},{7,11},{... | collective-permute-start | bytes 7274504 | tf_op jit(solution)/shard_map/ppermute | solution.py:286
  16.7 56.0 %collective-permute-start.3 = (bf16[4,592,512]{2,1,0:T(8,128)(2,1)}, bf16[4,592,512]{2,1,0:T(8,128)(2,1)}, u32[]{:S(2)}, u32[]{:S(2)}) collective-permute-start(bf16[4,592,512]{2,1,0:T(8,128)(2,1)} %extend.1.rest_0_.own_ref), channel_id=1, source_target_pairs={{4,0},{6,2},{8,4},{10,6},{12,8},{14,10},{5,1},{7,3},{9,5},{11,7},{... | collective-permute-start | bytes 7274504 | tf_op jit(solution)/shard_map/ppermute | solution.py:283
  35.5 33.9 %copy-start.2 = (bf16[2,592,512]{2,1,0:T(8,128)(2,1)S(1)}, bf16[2,592,512]{2,1,0:T(8,128)(2,1)}, u32[]{:S(2)}) copy-start(bf16[2,592,512]{2,1,0:T(8,128)(2,1)} %copy_sets.5.refs_1_) | copy-start | bytes 3637252
  67.2 9.3 %copy-start.14 = (s32[1,4]{1,0:T(1,128)S(1)}, s32[1,4]{1,0:T(1,128)}, u32[]{:S(2)}) copy-start(s32[1,4]{1,0:T(1,128)} %constant.157.clone.1) | copy-start | bytes 52
  67.2 32.8 %collective-permute-start.6 = (bf16[4,592,512]{2,1,0:T(8,128)(2,1)}, bf16[4,592,512]{2,1,0:T(8,128)(2,1)}, u32[]{:S(2)}, u32[]{:S(2)}) collective-permute-start(bf16[4,592,512]{2,1,0:T(8,128)(2,1)} %tie.6.rest_1_.rest_2_), channel_id=1, source_target_pairs={{4,8},{6,10},{8,12},{10,14},{5,9},{7,11},{9,13},{11,15},{20,24},{2... | collective-permute-start | bytes 7274504 | tf_op jit(solution)/shard_map/ppermute | solution.py:286
  69.4 29.6 %collective-permute-start.8 = (bf16[2,592,512]{2,1,0:T(8,128)(2,1)S(1)}, bf16[2,592,512]{2,1,0:T(8,128)(2,1)S(1)}, u32[]{:S(2)}, u32[]{:S(2)}) collective-permute-start(bf16[2,592,512]{2,1,0:T(8,128)(2,1)S(1)} %copy-done.2), channel_id=1, source_target_pairs={{0,2},{2,0},{4,6},{6,4},{8,10},{10,8},{12,14},{14,12},{1,3},{3,1},... | collective-permute-start | bytes 3637256 | tf_op jit(solution)/shard_map/ppermute | solution.py:277
  72.7 56.1 %collective-permute-start.4 = (bf16[4,592,512]{2,1,0:T(8,128)(2,1)}, bf16[4,592,512]{2,1,0:T(8,128)(2,1)}, u32[]{:S(2)}, u32[]{:S(2)}) collective-permute-start(bf16[4,592,512]{2,1,0:T(8,128)(2,1)} %tie.5.rest_0_), channel_id=1, source_target_pairs={{4,0},{6,2},{8,4},{10,6},{5,1},{7,3},{9,5},{11,7},{20,16},{22,18},... | collective-permute-start | bytes 7274504 | tf_op jit(solution)/shard_map/ppermute | solution.py:283
  77.1 4.9 %copy-start = (bf16[4,592,512]{2,1,0:T(8,128)(2,1)S(1)}, bf16[4,592,512]{2,1,0:T(8,128)(2,1)}, u32[]{:S(2)}) copy-start(bf16[4,592,512]{2,1,0:T(8,128)(2,1)} %extend.1.rest_0_.own_ref) | copy-start | bytes 7274500
  80.5 68.2 %collective-permute-start.18 = (bf16[4,592,512]{2,1,0:T(8,128)(2,1)}, bf16[4,592,512]{2,1,0:T(8,128)(2,1)}, u32[]{:S(2)}, u32[]{:S(2)}) collective-permute-start(bf16[4,592,512]{2,1,0:T(8,128)(2,1)} %copy_sets.9), channel_id=1, source_target_pairs={{0,2},{2,0},{4,6},{6,4},{8,10},{10,8},{12,14},{14,12},{1,3},{3,1},... | collective-permute-start | bytes 7274504 | tf_op jit(solution)/shard_map/ppermute | solution.py:277
  82.0 66.7 %collective-permute-start.1 = (bf16[4,592,512]{2,1,0:T(8,128)(2,1)S(1)}, bf16[4,592,512]{2,1,0:T(8,128)(2,1)}, u32[]{:S(2)}, u32[]{:S(2)}) collective-permute-start(bf16[4,592,512]{2,1,0:T(8,128)(2,1)S(1)} %copy-done), channel_id=1, source_target_pairs={{0,1},{1,0},{2,3},{3,2},{4,5},{5,4},{6,7},{7,6},{8,9},{9,8},{10,11... | collective-permute-start | bytes 7274504 | tf_op jit(solution)/shard_map/ppermute | solution.py:280
  99.0 1.0 copy-start.15
  100.0 55.9 %collective-permute-start.17 = (bf16[4,592,512]{2,1,0:T(8,128)(2,1)}, bf16[4,592,512]{2,1,0:T(8,128)(2,1)}, u32[]{:S(2)}, u32[]{:S(2)}) collective-permute-start(bf16[4,592,512]{2,1,0:T(8,128)(2,1)} %tie.6.rest_1_.rest_2_), channel_id=1, source_target_pairs={{0,1},{1,0},{2,3},{3,2},{4,5},{5,4},{6,7},{7,6},{8,9},{9,8},{10,11... | collective-permute-start | bytes 7274504 | tf_op jit(solution)/shard_map/ppermute | solution.py:280
  100.1 54.0 %collective-permute-start.9 = (bf16[2,592,512]{2,1,0:T(8,128)(2,1)}, bf16[2,592,512]{2,1,0:T(8,128)(2,1)}, u32[]{:S(2)}, u32[]{:S(2)}) collective-permute-start(bf16[2,592,512]{2,1,0:T(8,128)(2,1)} %copy-done.15), channel_id=1, source_target_pairs={{0,1},{1,0},{2,3},{3,2},{4,5},{5,4},{6,7},{7,6},{8,9},{9,8},{10,11... | collective-permute-start | bytes 3637256 | tf_op jit(solution)/shard_map/ppermute | solution.py:280
  131.7 27.9 %collective-permute-start.7 = (bf16[2,592,512]{2,1,0:T(8,128)(2,1)}, bf16[2,592,512]{2,1,0:T(8,128)(2,1)}, u32[]{:S(2)}, u32[]{:S(2)}) collective-permute-start(bf16[2,592,512]{2,1,0:T(8,128)(2,1)} %copy_sets.6.rest_2_), channel_id=1, source_target_pairs={{4,0},{6,2},{8,12},{10,14},{5,1},{7,3},{9,13},{11,15},{20,16},{22,... | collective-permute-start | bytes 3637256 | tf_op jit(solution)/shard_map/ppermute | solution.py:398
  148.7 45.4 %collective-permute-start.16 = (bf16[4,592,512]{2,1,0:T(8,128)(2,1)}, bf16[4,592,512]{2,1,0:T(8,128)(2,1)}, u32[]{:S(2)}, u32[]{:S(2)}) collective-permute-start(bf16[4,592,512]{2,1,0:T(8,128)(2,1)} %tie.5.rest_0_), channel_id=1, source_target_pairs={{0,1},{1,0},{2,3},{3,2},{4,5},{5,4},{6,7},{7,6},{8,9},{9,8},{10,11... | collective-permute-start | bytes 7274504 | tf_op jit(solution)/shard_map/ppermute | solution.py:280
  148.7 48.0 %collective-permute-start.19 = (bf16[4,592,512]{2,1,0:T(8,128)(2,1)}, bf16[4,592,512]{2,1,0:T(8,128)(2,1)S(1)}, u32[]{:S(2)}, u32[]{:S(2)}) collective-permute-start(bf16[4,592,512]{2,1,0:T(8,128)(2,1)} %tie.8.rest_4_), channel_id=1, source_target_pairs={{0,1},{1,0},{2,3},{3,2},{4,5},{5,4},{6,7},{7,6},{8,9},{9,8},{10,11... | collective-permute-start | bytes 7274504 | tf_op jit(solution)/shard_map/ppermute | solution.py:280
  151.1 8.5 %copy-start.12 = (s32[32,2]{0,1:T(2,128)S(1)}, s32[32,2]{0,1:T(2,128)}, u32[]{:S(2)}) copy-start(s32[32,2]{0,1:T(2,128)} %param.10) | copy-start | bytes 772
  151.1 8.6 %copy-start.13 = (f32[32]{0:T(128)S(1)}, f32[32]{0:T(128)}, u32[]{:S(2)}) copy-start(f32[32]{0:T(128)} %param.8) | copy-start | bytes 388
  151.1 9.4 %copy-start.10 = (bf16[4,576]{1,0:T(4,128)(2,1)S(1)}, bf16[4,576]{1,0:T(4,128)(2,1)}, u32[]{:S(2)}) copy-start(bf16[4,576]{1,0:T(4,128)(2,1)} %param.7) | copy-start | bytes 13828
  154.1 29.0 %collective-permute-start.14 = (bf16[2,592,512]{2,1,0:T(8,128)(2,1)}, bf16[2,592,512]{2,1,0:T(8,128)(2,1)}, u32[]{:S(2)}, u32[]{:S(2)}) collective-permute-start(bf16[2,592,512]{2,1,0:T(8,128)(2,1)} %copy_sets.8.rest_4_), channel_id=1, source_target_pairs={{0,2},{2,0},{4,6},{6,4},{8,10},{10,8},{12,14},{14,12},{1,3},{3,1},... | collective-permute-start | bytes 3637256 | tf_op jit(solution)/shard_map/ppermute | solution.py:277
  155.9 57.0 %collective-permute-start.13 = (bf16[4,592,512]{2,1,0:T(8,128)(2,1)}, bf16[4,592,512]{2,1,0:T(8,128)(2,1)}, u32[]{:S(2)}, u32[]{:S(2)}) collective-permute-start(bf16[4,592,512]{2,1,0:T(8,128)(2,1)} %collective-permute-done.6.rest_1_.rest_2_), channel_id=1, source_target_pairs={{0,1},{1,0},{2,3},{3,2},{4,5},{5,4},{6,7},{7,6},{8,9},{9,8},{10,11... | collective-permute-start | bytes 7274504 | tf_op jit(solution)/shard_map/ppermute | solution.py:280
  159.6 53.3 %collective-permute-start.12 = (bf16[4,592,512]{2,1,0:T(8,128)(2,1)}, bf16[4,592,512]{2,1,0:T(8,128)(2,1)}, u32[]{:S(2)}, u32[]{:S(2)}) collective-permute-start(bf16[4,592,512]{2,1,0:T(8,128)(2,1)} %collective-permute-done.4.rest_0_), channel_id=1, source_target_pairs={{0,1},{1,0},{2,3},{3,2},{4,5},{5,4},{6,7},{7,6},{8,9},{9,8},{10,11... | collective-permute-start | bytes 7274504 | tf_op jit(solution)/shard_map/ppermute | solution.py:280
  183.1 29.7 %collective-permute-start.15 = (bf16[2,592,512]{2,1,0:T(8,128)(2,1)}, bf16[2,592,512]{2,1,0:T(8,128)(2,1)}, u32[]{:S(2)}, u32[]{:S(2)}) collective-permute-start(bf16[2,592,512]{2,1,0:T(8,128)(2,1)} %collective-permute-done.14.rest_4_), channel_id=1, source_target_pairs={{0,1},{1,0},{2,3},{3,2},{4,5},{5,4},{6,7},{7,6},{8,9},{9,8},{10,11... | collective-permute-start | bytes 3637256 | tf_op jit(solution)/shard_map/ppermute | solution.py:280
  194.1 1.3 copy-start.1
  195.4 30.8 %collective-permute-start.11 = (bf16[2,592,512]{2,1,0:T(8,128)(2,1)S(1)}, bf16[2,592,512]{2,1,0:T(8,128)(2,1)S(1)}, u32[]{:S(2)}, u32[]{:S(2)}) collective-permute-start(bf16[2,592,512]{2,1,0:T(8,128)(2,1)S(1)} %copy-done.1), channel_id=1, source_target_pairs={{4,0},{6,2},{8,12},{10,14},{5,1},{7,3},{9,13},{11,15},{20,16},{22,... | collective-permute-start | bytes 3637256 | tf_op jit(solution)/shard_map/ppermute | solution.py:398
  196.7 1.4 copy-start.4
  196.7 33.4 %collective-permute-start.21 = (bf16[2,592,512]{2,1,0:T(8,128)(2,1)}, bf16[2,592,512]{2,1,0:T(8,128)(2,1)S(1)}, u32[]{:S(2)}, u32[]{:S(2)}) collective-permute-start(bf16[2,592,512]{2,1,0:T(8,128)(2,1)} %tie.7.rest_6_.rest_0_), channel_id=1, source_target_pairs={{0,2},{2,0},{4,6},{6,4},{8,10},{10,8},{12,14},{14,12},{1,3},{3,1},... | collective-permute-start | bytes 3637256 | tf_op jit(solution)/shard_map/ppermute | solution.py:277
  212.9 17.3 %collective-permute-start.10 = (bf16[2,592,512]{2,1,0:T(8,128)(2,1)}, bf16[2,592,512]{2,1,0:T(8,128)(2,1)S(1)}, u32[]{:S(2)}, u32[]{:S(2)}) collective-permute-start(bf16[2,592,512]{2,1,0:T(8,128)(2,1)} %tie.7.rest_6_.rest_0_), channel_id=1, source_target_pairs={{0,1},{1,0},{2,3},{3,2},{4,5},{5,4},{6,7},{7,6},{8,9},{9,8},{10,11... | collective-permute-start | bytes 3637256 | tf_op jit(solution)/shard_map/ppermute | solution.py:280
  226.2 1.1 copy-start.3
  227.2 6.5 %collective-permute-start.20 = (bf16[2,592,512]{2,1,0:T(8,128)(2,1)}, bf16[2,592,512]{2,1,0:T(8,128)(2,1)S(1)}, u32[]{:S(2)}, u32[]{:S(2)}) collective-permute-start(bf16[2,592,512]{2,1,0:T(8,128)(2,1)} %tie.9.rest_2_), channel_id=1, source_target_pairs={{0,1},{1,0},{2,3},{3,2},{4,5},{5,4},{6,7},{7,6},{8,9},{9,8},{10,11... | collective-permute-start | bytes 3637256 | tf_op jit(solution)/shard_map/ppermute | solution.py:280
  230.1 4.3 %copy-start.5 = (bf16[2,592,512]{2,1,0:T(8,128)(2,1)}, bf16[2,592,512]{2,1,0:T(8,128)(2,1)S(1)}, u32[]{:S(2)}) copy-start(bf16[2,592,512]{2,1,0:T(8,128)(2,1)S(1)} %collective-permute-done.21.rest_4_) | copy-start | bytes 3637252
  230.1 4.2 %collective-permute-start.22 = (bf16[2,592,512]{2,1,0:T(8,128)(2,1)S(1)}, bf16[2,592,512]{2,1,0:T(8,128)(2,1)S(1)}, u32[]{:S(2)}, u32[]{:S(2)}) collective-permute-start(bf16[2,592,512]{2,1,0:T(8,128)(2,1)S(1)} %collective-permute-done.21.rest_4_), channel_id=1, source_target_pairs={{0,1},{1,0},{2,3},{3,2},{4,5},{5,4},{6,7},{7,6},{8,9},{9,8},{10,11... | collective-permute-start | bytes 3637256 | tf_op jit(solution)/shard_map/ppermute | solution.py:280
  230.1 4.2 %copy-start.6 = (bf16[2,592,512]{2,1,0:T(8,128)(2,1)}, bf16[2,592,512]{2,1,0:T(8,128)(2,1)S(1)}, u32[]{:S(2)}) copy-start(bf16[2,592,512]{2,1,0:T(8,128)(2,1)S(1)} %collective-permute-done.10.rest_1_) | copy-start | bytes 3637252
  233.8 1.0 copy-start.7
  234.8 1.0 copy-start.8

commit v5 on v4

--- a/solution.py
+++ b/solution.py
@@ -127,7 +127,7 @@
         out_copy(0, lax.rem(hi + 1, 2)).wait()
 
 
-def run_pairs(call, expected, wins, meta, shift, ve1, pick, own, other, sets, after, prev):
+def run_pairs(call, wins, meta, shift, ve1, pick, own, other, sets, after, prev):
     pairs_here, _, kept, span = pick.shape
     n_first = ve1.shape[0]
     full, half = own.shape[1], own.shape[2]
@@ -165,10 +165,7 @@
         ],
         input_output_aliases=aliases,
         compiler_params=pltpu.CompilerParams(vmem_limit_bytes=VMEM_LIMIT),
-        cost_estimate=pl.CostEstimate(
-            flops=int(expected * 4 * kept * kept * 2 * half * 2),
-            bytes_accessed=int(expected * (full * half * 4 + kept * kept * 2)),
-            transcendentals=0),
+        cost_estimate=pl.CostEstimate(flops=0, bytes_accessed=0, transcendentals=0),
         name=f"pairs_{call}",
     )(*operands)
 
@@ -196,7 +193,6 @@
     n = len(index)
     table = jnp.stack([jnp.stack([jnp.asarray(w, jnp.int32) for w in which]), jnp.stack(index)])
     block = arrays[0].shape[1:]
-    size = 2 * n * block[0] * block[1] * 2
     return pl.pallas_call(
         functools.partial(set_kernel, len(arrays), len(after)),
         out_shape=jax.ShapeDtypeStruct((n,) + block, arrays[0].dtype),
@@ -206,18 +202,28 @@
             pltpu.VMEM((n,) + block, arrays[0].dtype),
             pltpu.SemaphoreType.DMA((n,)),
             pltpu.SemaphoreType.DMA((n,))],
-        cost_estimate=pl.CostEstimate(flops=0, bytes_accessed=size, transcendentals=0),
+        cost_estimate=pl.CostEstimate(flops=0, bytes_accessed=0, transcendentals=0),
         compiler_params=pltpu.CompilerParams(vmem_limit_bytes=VMEM_LIMIT),
         name="copy_sets",
     )(table, *arrays, *after)
 
 
-def extend_kernel(blocks_ref, extra_ref, out_ref, held, in_sems, out_sems):
-    count, full, _ = blocks_ref.shape
+def extend_kernel(wins, blocks_ref, energy_ref, out_ref, held, in_sems, out_sems):
+    count, full, half = blocks_ref.shape
     for k in range(count):
         pltpu.make_async_copy(blocks_ref.at[k], held.at[k, 0:full], in_sems.at[k]).start()
+    energy = energy_ref[...].astype(jnp.float32)
+    span = max(sp for _, _, sp in wins)
+    row = lax.broadcasted_iota(jnp.int32, (EXTRA, span), 0)
     for k in range(count):
-        held[k, full:, :] = extra_ref[k]
+        held[k, full:, :] = jnp.zeros((EXTRA, half), held.dtype)
+        rows = jnp.zeros((EXTRA, span), jnp.float32)
+        for t, (base, _, sp) in enumerate(wins):
+            piece = energy[k:k + 1, base:base + sp]
+            if sp < span:
+                piece = jnp.concatenate([piece, jnp.zeros((1, span - sp), jnp.float32)], axis=1)
+            rows = jnp.where(row == t, jnp.broadcast_to(piece, (EXTRA, span)), rows)
+        held[k, full:, 0:span] = rows.astype(held.dtype)
     for k in range(count):
         pltpu.make_async_copy(blocks_ref.at[k], held.at[k, 0:full], in_sems.at[k]).wait()
         pltpu.make_async_copy(held.at[k], out_ref.at[k], out_sems.at[k]).start()
@@ -225,11 +231,11 @@
         pltpu.make_async_copy(held.at[k], out_ref.at[k], out_sems.at[k]).wait()
 
 
-def extend(blocks, extra):
+def extend(blocks, energy, wins):
     count, full, half = blocks.shape
-    shape = (count, full + extra.shape[1], half)
+    shape = (count, full + EXTRA, half)
     return pl.pallas_call(
-        extend_kernel,
+        functools.partial(extend_kernel, wins),
         out_shape=jax.ShapeDtypeStruct(shape, blocks.dtype),
         in_specs=[ANY_SPEC, pl.BlockSpec(memory_space=pltpu.VMEM)],
         out_specs=ANY_SPEC,
@@ -237,7 +243,7 @@
             pltpu.VMEM(shape, blocks.dtype), pltpu.SemaphoreType.DMA((count,)), pltpu.SemaphoreType.DMA((count,))],
         compiler_params=pltpu.CompilerParams(vmem_limit_bytes=VMEM_LIMIT),
         name="extend",
-    )(blocks, extra)
+    )(blocks, energy)
 
 
 def tie(x, deps):
@@ -285,10 +291,7 @@
     def hop_up(a, d):
         return lax.ppermute(a, "orb", [(k, k + 2) for k in range(orb_count - 2) if k // 2 >= d - 1])
 
-    extra = [
-        jnp.pad(virt_energy[:, None, b:b + sp], ((0, 0), (0, 0), (0, half - sp))) for b, _, sp in wins]
-    extra.append(jnp.zeros((occ_dev, EXTRA - len(wins), half), blocks.dtype))
-    stored = extend(blocks, jnp.concatenate(extra, axis=1))
+    stored = extend(blocks, virt_energy, wins)
 
     downs, ups = [stored, hop_down(stored, 1)], [stored, hop_up(stored, 1)]
     local_other = across_aux(stored)
@@ -298,6 +301,7 @@
     slot_second = jnp.sum(jnp.where(hit_second, owner_slot[None, :], 0), axis=1)
     slots = jnp.arange(n_slots, dtype=i32)
     wanted_flat = jnp.any(slot_second[:, None] == slots[None, :], axis=0).astype(i32)
+    wanted_flat = tie(wanted_flat, [stored])
     wanted = wanted_flat.reshape(orb_count, occ_dev) > 0
     wanted_opp = across_y(wanted_flat).reshape(orb_count, occ_dev) > 0
     top = orb_count - 1
@@ -308,7 +312,7 @@
     def two_of(table):
         return jnp.min(jnp.where(table, local, occ_dev - 1), axis=1), jnp.max(jnp.where(table, local, 0), axis=1)
 
-    want_opp = two_of(wanted_opp)
+    want, want_opp = two_of(wanted), two_of(wanted_opp)
 
     def far_place(rows):
         w = rows.astype(i32)
@@ -333,15 +337,15 @@
     far = jnp.sum(jnp.where(own_second[:, None] == slots[None, :], place_table[None, :], 0), axis=1)
     both = 2 * dist <= chain - 1
     is_far = (dist == last) & (is_opp == 0)
-    idx = jnp.where(is_opp == 1, rank + jnp.where(both & from_up, 2, 0), part)
+    idx = jnp.where((dist == 0) & (is_opp == 0), part, rank + jnp.where(both & from_up, 2, 0))
     idx = jnp.where(is_far, far % 2, idx)
-    which_away = jnp.where(is_opp == 1, 2, jnp.where(is_far, far // 2, from_up.astype(i32)))
-    which = jnp.where(dist == 0, is_opp, which_away)
+    which = jnp.where(is_far & (far < 2), 2, is_opp)
+    stage = dist - (is_far & (far < 2)).astype(i32)
     rows = jnp.arange(own_rows, dtype=i32)
-    before = (dist[None, :] < dist[:, None]) | ((dist[None, :] == dist[:, None]) & (rows[None, :] < rows[:, None]))
+    before = (stage[None, :] < stage[:, None]) | ((stage[None, :] == stage[:, None]) & (rows[None, :] < rows[:, None]))
     place = jnp.sum(before.astype(i32), axis=1)
     order = jnp.sum(jnp.where(place[None, :] == rows[:, None], rows[None, :], 0), axis=1)
-    bounds = jnp.sum((dist[None, :] < jnp.arange(chain + 1, dtype=i32)[:, None]).astype(i32), axis=1)
+    bounds = jnp.sum((stage[None, :] < jnp.arange(chain + 1, dtype=i32)[:, None]).astype(i32), axis=1)
     width = max(own_rows, chain + 1)
 
     def padded(v):
@@ -366,24 +370,27 @@
     def idx_of(table, source):
         return lax.dynamic_index_in_dim(table, jnp.clip(source, 0, orb_count - 1), 0, keepdims=False)
 
-    def two_for_opposite(source):
-        return [idx_of(want_opp[0], source), idx_of(want_opp[1], source)]
-
-    def pairs_at(d, sets, after, prev):
-        return run_pairs(d, own_rows / chain, wins, meta, shift, ve1, pick, stored, local_other, sets, after, prev)
+    def two_for(table, source):
+        return [idx_of(table[0], source), idx_of(table[1], source)]
+
+    sets = {}
 
     def pairs_at(d, after, prev):
-        return run_pairs(d, own_rows / chain, wins, meta, shift, ve1, pick, stored, local_other, sets[d], after, prev)
-
-    y_load = copy_sets([0, 0], two_for_opposite(o), [stored])
-    opp = [across_y(y_load)]
-    early = [y_load, pick, meta]
+        return run_pairs(d, wins, meta, shift, ve1, pick, stored, local_other, sets[d], after, prev)
+
+    def with_other(a):
+        return a, across_aux(a)
+
+    y_load = copy_sets([0, 0], two_for(want_opp, o), [stored])
+    y_own, y_other = with_other(across_y(y_load))
+    sets[0] = [(stored, local_other), (y_own, y_other)]
+    early = [y_other, local_other, pick, meta]
     downs[1], ups[1] = tie(downs[1], early), tie(ups[1], early)
-    sets = {}
     out = None
+    opp = None
     for d in range(1, last):
         s_down, s_up = o + 2 * d, o - 2 * d
-        loads = []
+        first = []
         if d + 1 < last:
             downs.append(hop_down(downs[d], d + 1))
             ups.append(hop_up(ups[d], d + 1))
@@ -393,36 +400,34 @@
             turn = [jnp.sum(jnp.where(turn_of == j, local[0], 0)) for j in range(occ_dev)]
             perm = [(2, 0), (3, 1), (2 * (last - 1), 2 * last), (2 * (last - 1) + 1, 2 * last + 1)]
             is_up = 1 - sends_down.astype(i32)
-            load_a = copy_sets([is_up, is_up], turn[:2], [downs[d], ups[d]])
+            load_a = copy_sets([is_up, is_up], turn[:2], [downs[d], ups[d]], [mine_other] if d > 1 else [])
             load_b = copy_sets([is_up, is_up], turn[2:], [downs[d], ups[d]], [load_a])
             got_a, got_b = lax.ppermute(load_a, "orb", perm), lax.ppermute(load_b, "orb", perm)
-            loads = [load_b]
-            if d > 1:
-                opp[d - 1] = tie(opp[d - 1], loads)
+            first = [load_b]
         if 2 * d <= last:
-            theirs = copy_sets(
-                [0, 0, 1, 1], two_for_opposite(s_down) + two_for_opposite(s_up), [downs[d], ups[d]], loads)
+            place_of = [0, 0, 1, 1]
+
+            def both_ways(table):
+                return two_for(table, s_down) + two_for(table, s_up)
         else:
             is_up = (z + d > last).astype(i32)
-            s = jnp.where(is_up == 1, s_up, s_down)
-            theirs = copy_sets([is_up, is_up], two_for_opposite(s), [downs[d], ups[d]], loads)
-        opp.append(across_y(theirs))
-        if d == 1:
-            sets[0] = [(stored, local_other), (opp[0], across_aux(opp[0]))]
-        else:
-            sets[d - 1] = [
-                (downs[d - 1], across_aux(downs[d - 1])), (ups[d - 1], across_aux(ups[d - 1])),
-                (opp[d - 1], across_aux(opp[d - 1]))]
-            out = pairs_at(d - 2, [theirs] + loads, out)
+            place_of = [is_up, is_up]
+
+            def both_ways(table):
+                return two_for(table, jnp.where(is_up == 1, s_up, s_down))
+        theirs = copy_sets(place_of, both_ways(want_opp), [downs[d], ups[d]], first)
+        mine = copy_sets(place_of, both_ways(want), [downs[d], ups[d]], [theirs])
+        if d > 1:
+            sets[d - 1] = [(prev_mine, mine_other), with_other(tie(opp, first) if first else opp)]
+            out = pairs_at(d - 2, [mine] + first, out)
+        opp = across_y(theirs)
+        prev_mine, mine_other = with_other(mine)
     got_a = tie(got_a, [out])
-    opp.append(across_y(got_a))
-    sets[last - 1] = [
-        (downs[last - 1], across_aux(downs[last - 1])), (ups[last - 1], across_aux(ups[last - 1])),
-        (opp[last - 1], across_aux(opp[last - 1]))]
+    far_opp = across_y(got_a)
     out = pairs_at(last - 2, [got_a], out)
-    out = pairs_at(last - 1, [got_a], out)
-    got_b = tie(got_b, [out])
-    sets[last] = [(got_a, across_aux(got_a)), (got_b, across_aux(got_b)), (opp[last], across_aux(opp[last]))]
+    sets[last - 1] = [(prev_mine, mine_other), with_other(tie(opp, [out])), with_other(got_a)]
+    out = pairs_at(last - 1, [], out)
+    sets[last] = [with_other(tie(got_b, [out])), with_other(tie(far_opp, [out]))]
     return pairs_at(last, [], out)
 
 

time: 248 us -> 245 us (0.988)
  waiting for transfers between devices: 125 us -> 116 us
  Pallas kernels: 58.6 us -> 64.9 us
  other arithmetic: 21.7 us -> 26.3 us
  starting transfers between devices: 25.4 us -> 21.1 us
    ppermute x2, waiting for transfers between devices: 26.9 us -> 58.6 us  [hop_down(): lax.ppermute(a, 'orb', [(k, k - 2) for k in range(2, orb_count) if k // 2...]
    ppermute x2, waiting for transfers between devices: 31.7 us -> 1.48 us  [hop_up(): lax.ppermute(a, 'orb', [(k, k + 2) for k in range(orb_count - 2) if k //...]
    ppermute x5, waiting for transfers between devices: 52.5 us -> 36.4 us  [across_y(): return lax.ppermute(a, 'orb', swap_y)]
    pallas_call x5 -> x7, Pallas kernels: 14.8 us -> 21.3 us  [copy_sets(): pl.pallas_call(functools.partial(set_kernel, len(arrays), len(after)), ou...]
    ppermute x1, waiting for transfers between devices: 3.74 us -> 8.78 us  [per_device(): lax.ppermute(load_a, 'orb', perm)]
    another operation x7 -> x8, other arithmetic: 9.43 us -> 13.3 us  [copy_sets(): jnp.stack([jnp.stack([jnp.asarray(w, jnp.int32) for w in which]), jnp.sta...]
    ppermute x11 -> x9, starting transfers between devices: 4.02 us -> 1.14 us  [across_aux(): return lax.ppermute(a, 'aux', swap_aux)]
    unnamed x32 -> x36, local copies, waits for them, and re-layouts: 6.19 us -> 6.81 us
  transfers between devices with their start and end apart: 23 -> 21, of which waited for: 10 -> 9; matrix products, arithmetic and copies ran while one was open for 11% -> 13% of each run, Pallas kernels for 20% -> 20%
where the time goes in v5:
time: 245 us; the launch traced here: 242 us
  waiting for transfers between devices  116 us (47%)
  Pallas kernels  64.9 us (26%)
  other arithmetic  26.3 us (11%)
  starting transfers between devices  21.1 us (9%)
  local copies, waits for them, and re-layouts  13.3 us (5%)
    ppermute x2, waiting for transfers between devices, hop_down(): lax.ppermute(a, 'orb', [(k, k - 2) for k in range(2, orb_count) if k // 2...  58.6 us
    pallas_call x4, Pallas kernels, run_pairs(): pl.pallas_call(functools.partial(pair_kernel, call, wins, len(sets), len(...  40.2 us
    ppermute x5, waiting for transfers between devices, across_y(): return lax.ppermute(a, 'orb', swap_y)  36.4 us
    pallas_call x7, Pallas kernels, copy_sets(): pl.pallas_call(functools.partial(set_kernel, len(arrays), len(after)), ou...  21.3 us
    another operation x8, other arithmetic, copy_sets(): jnp.stack([jnp.stack([jnp.asarray(w, jnp.int32) for w in which]), jnp.sta...  13.3 us
    ppermute x1, waiting for transfers between devices, per_device(): lax.ppermute(load_a, 'orb', perm)  8.78 us
    ppermute x5, starting transfers between devices, across_y(): return lax.ppermute(a, 'orb', swap_y)  7.76 us
    ppermute x1, waiting for transfers between devices, per_device(): lax.ppermute(load_b, 'orb', perm)  7.2 us
  transfers between devices with their start and end apart: 21, of which 9 were waited for; matrix products, arithmetic and copies ran while one was open for 13% of the time, Pallas kernels for 20%

profile of v5, /device:TPU:0, one launch (start us, length us, event | category | flops | bytes accessed | tf_op | source)
XLA Modules:
  0.0 241.7 jit_solution(17275845633430488081)
XLA Ops:
  0.0 0.7 slice_bitcast_fusion.2
  0.7 0.8 select_reduce_fusion
  2.1 3.4 %extend.1.refs_1_.rest_0_.own_ref = bf16[4,592,512]{2,1,0:T(8,128)(2,1)} custom-call(bf16[4,576,512]{2,1,0:T(8,128)(2,1)} %blocks_ref.1, bf16[4,576]{1,0:T(4,128)(2,1)} %energy_ref.1), custom_call_target="tpu_custom_call" | custom-call | tf_op jit(solution)/shard_map/extend/pallas_call | solution.py:237
  5.5 3.0 %collective-permute-start = (s32[32]{0:T(128)}, s32[32]{0:T(128)S(1)}, u32[]{:S(2)}, u32[]{:S(2)}) collective-permute-start(s32[32]{0:T(128)} %tie.8), channel_id=1, source_target_pairs={{0,2},{2,0},{4,6},{6,4},{8,10},{10,8},{12,14},{14,12},{1,3},{3,1},... | collective-permute-start | bytes 392 | tf_op jit(solution)/shard_map/ppermute | solution.py:283
  8.6 3.5 %collective-permute-start.2 = (s32[32]{0:T(128)}, s32[32]{0:T(128)S(1)}, u32[]{:S(2)}, u32[]{:S(2)}) collective-permute-start(s32[32]{0:T(128)} %tie.8), channel_id=1, source_target_pairs={{0,6},{2,4},{14,8},{12,10},{1,7},{3,5},{15,9},{13,11},{16,22},{18,... | collective-permute-start | bytes 392 | tf_op jit(solution)/shard_map/ppermute | solution.py:309
  12.2 2.7 %collective-permute-start.7 = (bf16[4,592,512]{2,1,0:T(8,128)(2,1)S(1)}, bf16[4,592,512]{2,1,0:T(8,128)(2,1)}, u32[]{:S(2)}, u32[]{:S(2)}) collective-permute-start(bf16[4,592,512]{2,1,0:T(8,128)(2,1)S(1)} %copy-done), channel_id=1, source_target_pairs={{0,4},{2,6},{4,8},{6,10},{8,12},{10,14},{1,5},{3,7},{5,9},{7,11},{... | collective-permute-start | bytes 7274504 | tf_op jit(solution)/shard_map/ppermute | solution.py:292
  15.0 1.3 collective-permute-start.3
  19.4 0.7 fusion.10
  21.3 0.7 select_reduce_fusion.10
  22.7 2.5 %add_bitcast_fusion.2 = (s32[1,2]{1,0:T(1,128)S(1)}, s32[1,2]{1,0:T(1,128)S(1)}) fusion(s32[1]{0:T(128)} %get-tuple-element.41, s32[1]{0:T(128)} %get-tuple-element.37, s32[1]{0:T(128)} %bitcast.16, s32[1]{0:T(128)} %bitcast.15), kind=kLoop, calls=%fused_computation.78 | loop fusion | flops 4 | bytes 32 | tf_op jit(solution)/shard_map/stack | solution.py:194
  25.8 2.8 %copy_sets.7 = bf16[2,592,512]{2,1,0:T(8,128)(2,1)} custom-call(s32[2,2]{1,0:T(2,128)} %stack.151.table_ref, bf16[4,592,512]{2,1,0:T(8,128)(2,1)} %extend.1.refs_1_.rest_0_.own_ref), custom_call_target="tpu_custom_call" | custom-call | tf_op jit(solution)/shard_map/copy_sets/pallas_call | solution.py:196
  28.6 1.5 collective-permute-start.4
  30.0 5.7 %fusion.refs_3_.pick_ref = bf16[16,2,512,256]{3,2,1,0:T(8,128)(2,1)} fusion(s32[16,2,512]{2,1,0:T(2,128)S(1)} %dynamic-slice_add_fusion), kind=kLoop, calls=%fused_computation.1 | loop fusion | flops 8388608 | bytes 8454144 | tf_op jit(solution)/shard_map/convert_element_type | solution.py:368
  36.3 21.8 %collective-permute-done.4.rest_2_ = bf16[2,592,512]{2,1,0:T(8,128)(2,1)} collective-permute-done((bf16[2,592,512]{2,1,0:T(8,128)(2,1)}, bf16[2,592,512]{2,1,0:T(8,128)(2,1)}, u32[]{:S(2)}, u32[]{:S(2)}) %collective-permute-start.4) | collective-permute-done | bytes 1212448 | tf_op jit(solution)/shard_map/ppermute | solution.py:283
  59.1 5.1 %add_bitcast_fusion.4 = (s32[1,4]{1,0:T(1,128)S(1)}, s32[1,4]{1,0:T(1,128)S(1)}) fusion(s32[1]{0:T(128)} %get-tuple-element.46, s32[1]{0:T(128)} %get-tuple-element.43, s32[1]{0:T(128)} %get-tuple-element.47, s32[1]{0:T(128)} %get-tuple-element.44, s32[1]{0:T(128)} %get-tuple-element.39, s32[1]{0:T(128)} %get-tuple-element.35, s32[1]{0:T(128)} %get-tuple-element.40, ...), kind=kLoop, calls=%fused_computation.80 | loop fusion | flops 24 | bytes 64 | tf_op jit(solution)/shard_map/stack | solution.py:194
  64.9 1.5 collective-permute-done.7.refs_0_
  66.3 5.6 %collective-permute-done.3.refs_0_ = bf16[4,592,512]{2,1,0:T(8,128)(2,1)} collective-permute-done((bf16[4,592,512]{2,1,0:T(8,128)(2,1)S(1)}, bf16[4,592,512]{2,1,0:T(8,128)(2,1)}, u32[]{:S(2)}, u32[]{:S(2)}) %collective-permute-start.3) | collective-permute-done | bytes 2424864 | tf_op jit(solution)/shard_map/ppermute | solution.py:289
  72.0 3.7 %copy_sets.8.rest_2_ = bf16[4,592,512]{2,1,0:T(8,128)(2,1)} custom-call(s32[2,4]{1,0:T(2,128)} %get-tuple-element.48.table_ref, bf16[4,592,512]{2,1,0:T(8,128)(2,1)} %tie.9.rest_0_, bf16[4,592,512]{2,1,0:T(8,128)(2,1)} %tie.10.rest_1_), custom_call_target="tpu_custom_call" | custom-call | tf_op jit(solution)/shard_map/copy_sets/pallas_call | solution.py:196
  75.7 3.2 %copy_sets.9.rest_0_ = bf16[4,592,512]{2,1,0:T(8,128)(2,1)} custom-call(s32[2,4]{1,0:T(2,128)} %get-tuple-element.49.table_ref, bf16[4,592,512]{2,1,0:T(8,128)(2,1)} %tie.9.rest_0_, bf16[4,592,512]{2,1,0:T(8,128)(2,1)} %tie.10.rest_1_, bf16[4,592,512]{2,1,0:T(8,128)(2,1)} %copy_sets.8.rest_2_), custom_call_target="tpu_custom_call" | custom-call | tf_op jit(solution)/shard_map/copy_sets/pallas_call | solution.py:196
  79.0 0.8 collective-permute-start.8
  79.9 1.3 collective-permute-start.6
  81.2 1.1 collective-permute-start.13
  82.9 0.7 select_reduce_fusion.11
  83.5 1.3 add_bitcast_fusion
  85.5 53.0 %collective-permute-done.6.rest_0_ = bf16[4,592,512]{2,1,0:T(8,128)(2,1)} collective-permute-done((bf16[4,592,512]{2,1,0:T(8,128)(2,1)}, bf16[4,592,512]{2,1,0:T(8,128)(2,1)}, u32[]{:S(2)}, u32[]{:S(2)}) %collective-permute-start.6) | collective-permute-done | bytes 2424864 | tf_op jit(solution)/shard_map/ppermute | solution.py:289
  138.5 2.9 %copy_sets.10.rest_2_ = bf16[2,592,512]{2,1,0:T(8,128)(2,1)} custom-call(s32[2,2]{1,0:T(2,128)} %get-tuple-element.50.table_ref, bf16[4,592,512]{2,1,0:T(8,128)(2,1)} %collective-permute-done.6.rest_0_, bf16[4,592,512]{2,1,0:T(8,128)(2,1)} %copy-done.1, bf16[4,592,512]{2,1,0:T(8,128)(2,1)} %collective-permute-done.9.rest_2_.rest_1_), custom_call_target="tpu_custom_call" | custom-call | tf_op jit(solution)/shard_map/copy_sets/pallas_call | solution.py:196
  141.3 2.8 %copy_sets.11.rest_2_.refs_1_.rest_5_ = bf16[2,592,512]{2,1,0:T(8,128)(2,1)} custom-call(s32[2,2]{1,0:T(2,128)} %get-tuple-element.51.table_ref, bf16[4,592,512]{2,1,0:T(8,128)(2,1)} %collective-permute-done.6.rest_0_, bf16[4,592,512]{2,1,0:T(8,128)(2,1)} %copy-done.1, bf16[2,592,512]{2,1,0:T(8,128)(2,1)} %copy_sets.10.rest_2_), custom_call_target="tpu_custom_call" | custom-call | tf_op jit(solution)/shard_map/copy_sets/pallas_call | solution.py:196
  144.3 1.3 add_bitcast_fusion.6
  145.6 1.3 add_bitcast_fusion.8
  146.8 1.3 collective-permute-start.15
  148.7 3.0 %copy_sets.12.rest_2_ = bf16[2,592,512]{2,1,0:T(8,128)(2,1)} custom-call(s32[2,2]{1,0:T(2,128)} %get-tuple-element.32.table_ref, bf16[4,592,512]{2,1,0:T(8,128)(2,1)} %collective-permute-done.6.rest_0_, bf16[4,592,512]{2,1,0:T(8,128)(2,1)} %copy-done.1, bf16[2,592,512]{2,1,0:T(8,128)(2,1)} %copy_sets.11.rest_2_.refs_1_.rest_5_), custom_call_target="tpu_custom_call" | custom-call | tf_op jit(solution)/shard_map/copy_sets/pallas_call | solution.py:196
  151.8 2.2 collective-permute-start.12
  154.9 2.9 %copy_sets.13.rest_4_.rest_0_ = bf16[2,592,512]{2,1,0:T(8,128)(2,1)} custom-call(s32[2,2]{1,0:T(2,128)} %get-tuple-element.33.table_ref, bf16[4,592,512]{2,1,0:T(8,128)(2,1)} %collective-permute-done.6.rest_0_, bf16[4,592,512]{2,1,0:T(8,128)(2,1)} %copy-done.1, bf16[2,592,512]{2,1,0:T(8,128)(2,1)} %copy_sets.12.rest_2_), custom_call_target="tpu_custom_call" | custom-call | tf_op jit(solution)/shard_map/copy_sets/pallas_call | solution.py:196
  157.9 0.9 broadcast_in_dim.150.ve1_ref
  158.9 10.1 %pairs_0.1.refs_1_.rest_5_ = bf16[16,512,512]{2,1,0:T(8,128)(2,1)} custom-call(s32[5,16]{1,0:T(8,128)} %stack.140.refs_4_.meta_ref, f32[16]{0:T(128)} %add.106.shift_ref, bf16[2,576,128]{2,1,0:T(8,128)(2,1)} %broadcast_in_dim.150.ve1_ref, bf16[16,2,512,256]{3,2,1,0:T(8,128)(2,1)} %fusion.refs_3_.pick_ref, ...), custom_call_target="tpu_custom_call" | custom-call | tf_op jit(solution)/shard_map/pairs_0/pallas_call | solution.py:148
  168.9 8.8 %collective-permute-done.15.refs_0_ = bf16[2,592,512]{2,1,0:T(8,128)(2,1)S(1)} collective-permute-done((bf16[2,592,512]{2,1,0:T(8,128)(2,1)S(1)}, bf16[2,592,512]{2,1,0:T(8,128)(2,1)S(1)}, u32[]{:S(2)}, u32[]{:S(2)}) %collective-permute-start.15) | collective-permute-done | bytes 1212448 | tf_op jit(solution)/shard_map/ppermute | solution.py:405
  177.7 1.0 copy-done.3
  178.8 13.1 %pairs_1.1.refs_1_.rest_6_ = bf16[16,512,512]{2,1,0:T(8,128)(2,1)} custom-call(s32[5,16]{1,0:T(8,128)} %stack.140.refs_4_.meta_ref, f32[16]{0:T(128)} %add.106.shift_ref, bf16[2,576,128]{2,1,0:T(8,128)(2,1)} %broadcast_in_dim.150.ve1_ref, bf16[16,2,512,256]{3,2,1,0:T(8,128)(2,1)} %fusion.refs_3_.pick_ref, ...), custom_call_target="tpu_custom_call", output_to_operand_aliasing={{}: (11, {})} | custom-call | tf_op jit(solution)/shard_map/pairs_1/pallas_call | solution.py:148
  192.0 1.2 copy-done.4
  193.6 1.3 collective-permute-start.10
  196.4 10.1 %pairs_2.1.refs_1_.rest_4_ = bf16[16,512,512]{2,1,0:T(8,128)(2,1)} custom-call(s32[5,16]{1,0:T(8,128)} %stack.140.refs_4_.meta_ref, f32[16]{0:T(128)} %add.106.shift_ref, bf16[2,576,128]{2,1,0:T(8,128)(2,1)} %broadcast_in_dim.150.ve1_ref, bf16[16,2,512,256]{3,2,1,0:T(8,128)(2,1)} %fusion.refs_3_.pick_ref, ...), custom_call_target="tpu_custom_call", output_to_operand_aliasing={{}: (12, {})} | custom-call | tf_op jit(solution)/shard_map/pairs_2/pallas_call | solution.py:148
  206.4 14.7 %collective-permute-done.19.refs_0_ = bf16[2,592,512]{2,1,0:T(8,128)(2,1)S(1)} collective-permute-done((bf16[2,592,512]{2,1,0:T(8,128)(2,1)S(1)}, bf16[2,592,512]{2,1,0:T(8,128)(2,1)S(1)}, u32[]{:S(2)}, u32[]{:S(2)}) %collective-permute-start.19) | collective-permute-done | bytes 1212448 | tf_op jit(solution)/shard_map/ppermute | solution.py:283
  221.1 1.0 copy-done.7
  222.1 7.2 %collective-permute-done.10.refs_0_ = bf16[2,592,512]{2,1,0:T(8,128)(2,1)S(1)} collective-permute-done((bf16[2,592,512]{2,1,0:T(8,128)(2,1)S(1)}, bf16[2,592,512]{2,1,0:T(8,128)(2,1)S(1)}, u32[]{:S(2)}, u32[]{:S(2)}) %collective-permute-start.10) | collective-permute-done | bytes 1212448 | tf_op jit(solution)/shard_map/ppermute | solution.py:405
  229.3 1.0 copy-done.6
  231.0 2.7 %collective-permute-done.18.rest_1_ = bf16[2,592,512]{2,1,0:T(8,128)(2,1)S(1)} collective-permute-done((bf16[2,592,512]{2,1,0:T(8,128)(2,1)}, bf16[2,592,512]{2,1,0:T(8,128)(2,1)S(1)}, u32[]{:S(2)}, u32[]{:S(2)}) %collective-permute-start.18) | collective-permute-done | bytes 1212448 | tf_op jit(solution)/shard_map/ppermute | solution.py:286
  233.7 1.0 copy-done.11
  234.8 7.0 %pairs_3.1 = bf16[16,512,512]{2,1,0:T(8,128)(2,1)} custom-call(s32[5,16]{1,0:T(8,128)} %stack.140.refs_4_.meta_ref, f32[16]{0:T(128)} %add.106.shift_ref, bf16[2,576,128]{2,1,0:T(8,128)(2,1)} %broadcast_in_dim.150.ve1_ref, bf16[16,2,512,256]{3,2,1,0:T(8,128)(2,1)} %fusion.refs_3_.pick_ref, ...), custom_call_target="tpu_custom_call", output_to_operand_aliasing={{}: (10, {})} | custom-call | tf_op jit(solution)/shard_map/pairs_3/pallas_call | solution.py:148
  (117 shorter events, 14.1 us)
Async XLA Ops:
  2.1 16.4 %copy-start.12 = (s32[32,2,512]{2,1,0:T(2,128)S(1)}, s32[32,2,512]{2,1,0:T(2,128)}, u32[]{:S(2)}) copy-start(s32[32,2,512]{2,1,0:T(2,128)} %param.11) | copy-start | bytes 393220
  5.5 6.6 %copy-start = (bf16[4,592,512]{2,1,0:T(8,128)(2,1)S(1)}, bf16[4,592,512]{2,1,0:T(8,128)(2,1)}, u32[]{:S(2)}) copy-start(bf16[4,592,512]{2,1,0:T(8,128)(2,1)} %extend.1.refs_1_.rest_0_.own_ref) | copy-start | bytes 7274500
  5.5 13.0 %copy-start.14 = (s32[512]{0:T(512)S(1)}, s32[512]{0:T(512)}, u32[]{:S(2)}) copy-start(s32[512]{0:T(512)} %constant.152.clone.1) | copy-start | bytes 6148
  5.5 13.2 %collective-permute-start = (s32[32]{0:T(128)}, s32[32]{0:T(128)S(1)}, u32[]{:S(2)}, u32[]{:S(2)}) collective-permute-start(s32[32]{0:T(128)} %tie.8), channel_id=1, source_target_pairs={{0,2},{2,0},{4,6},{6,4},{8,10},{10,8},{12,14},{14,12},{1,3},{3,1},... | collective-permute-start | bytes 392 | tf_op jit(solution)/shard_map/ppermute | solution.py:283
  8.6 10.5 %collective-permute-start.2 = (s32[32]{0:T(128)}, s32[32]{0:T(128)S(1)}, u32[]{:S(2)}, u32[]{:S(2)}) collective-permute-start(s32[32]{0:T(128)} %tie.8), channel_id=1, source_target_pairs={{0,6},{2,4},{14,8},{12,10},{1,7},{3,5},{15,9},{13,11},{16,22},{18,... | collective-permute-start | bytes 392 | tf_op jit(solution)/shard_map/ppermute | solution.py:309
  12.1 52.7 %collective-permute-start.1 = (bf16[4,592,512]{2,1,0:T(8,128)(2,1)S(1)}, bf16[4,592,512]{2,1,0:T(8,128)(2,1)}, u32[]{:S(2)}, u32[]{:S(2)}) collective-permute-start(bf16[4,592,512]{2,1,0:T(8,128)(2,1)S(1)} %copy-done), channel_id=1, source_target_pairs={{0,1},{1,0},{2,3},{3,2},{4,5},{5,4},{6,7},{7,6},{8,9},{9,8},{10,11... | collective-permute-start | bytes 7274504 | tf_op jit(solution)/shard_map/ppermute | solution.py:286
  12.2 54.1 %collective-permute-start.7 = (bf16[4,592,512]{2,1,0:T(8,128)(2,1)S(1)}, bf16[4,592,512]{2,1,0:T(8,128)(2,1)}, u32[]{:S(2)}, u32[]{:S(2)}) collective-permute-start(bf16[4,592,512]{2,1,0:T(8,128)(2,1)S(1)} %copy-done), channel_id=1, source_target_pairs={{0,4},{2,6},{4,8},{6,10},{8,12},{10,14},{1,5},{3,7},{5,9},{7,11},{... | collective-permute-start | bytes 7274504 | tf_op jit(solution)/shard_map/ppermute | solution.py:292
  15.0 57.0 %collective-permute-start.3 = (bf16[4,592,512]{2,1,0:T(8,128)(2,1)S(1)}, bf16[4,592,512]{2,1,0:T(8,128)(2,1)}, u32[]{:S(2)}, u32[]{:S(2)}) collective-permute-start(bf16[4,592,512]{2,1,0:T(8,128)(2,1)S(1)} %copy-done), channel_id=1, source_target_pairs={{4,0},{6,2},{8,4},{10,6},{12,8},{14,10},{5,1},{7,3},{9,5},{11,7},{... | collective-permute-start | bytes 7274504 | tf_op jit(solution)/shard_map/ppermute | solution.py:289
  28.6 35.7 %copy-start.17 = (s32[1,4]{1,0:T(1,128)S(1)}, s32[1,4]{1,0:T(1,128)}, u32[]{:S(2)}) copy-start(s32[1,4]{1,0:T(1,128)} %constant.157.clone.1) | copy-start | bytes 52
  28.6 29.4 %collective-permute-start.4 = (bf16[2,592,512]{2,1,0:T(8,128)(2,1)}, bf16[2,592,512]{2,1,0:T(8,128)(2,1)}, u32[]{:S(2)}, u32[]{:S(2)}) collective-permute-start(bf16[2,592,512]{2,1,0:T(8,128)(2,1)} %copy_sets.7), channel_id=1, source_target_pairs={{0,2},{2,0},{4,6},{6,4},{8,10},{10,8},{12,14},{14,12},{1,3},{3,1},... | collective-permute-start | bytes 3637256 | tf_op jit(solution)/shard_map/ppermute | solution.py:283
  58.0 8.3 %collective-permute-start.5 = (bf16[2,592,512]{2,1,0:T(8,128)(2,1)}, bf16[2,592,512]{2,1,0:T(8,128)(2,1)}, u32[]{:S(2)}, u32[]{:S(2)}) collective-permute-start(bf16[2,592,512]{2,1,0:T(8,128)(2,1)} %collective-permute-done.4.rest_2_), channel_id=1, source_target_pairs={{0,1},{1,0},{2,3},{3,2},{4,5},{5,4},{6,7},{7,6},{8,9},{9,8},{10,11... | collective-permute-start | bytes 3637256 | tf_op jit(solution)/shard_map/ppermute | solution.py:286
  79.0 6.5 %collective-permute-start.9 = (bf16[4,592,512]{2,1,0:T(8,128)(2,1)}, bf16[4,592,512]{2,1,0:T(8,128)(2,1)}, u32[]{:S(2)}, u32[]{:S(2)}) collective-permute-start(bf16[4,592,512]{2,1,0:T(8,128)(2,1)} %copy_sets.9.rest_0_), channel_id=1, source_target_pairs={{0,1},{1,0},{2,3},{3,2},{4,5},{5,4},{6,7},{7,6},{8,9},{9,8},{10,11... | collective-permute-start | bytes 7274504 | tf_op jit(solution)/shard_map/ppermute | solution.py:286
  79.0 6.4 %collective-permute-start.8 = (bf16[4,592,512]{2,1,0:T(8,128)(2,1)}, bf16[4,592,512]{2,1,0:T(8,128)(2,1)S(1)}, u32[]{:S(2)}, u32[]{:S(2)}) collective-permute-start(bf16[4,592,512]{2,1,0:T(8,128)(2,1)} %tie.10.rest_1_), channel_id=1, source_target_pairs={{4,8},{6,10},{8,12},{10,14},{5,9},{7,11},{9,13},{11,15},{20,24},{2... | collective-permute-start | bytes 7274504 | tf_op jit(solution)/shard_map/ppermute | solution.py:292
  79.9 58.6 %collective-permute-start.6 = (bf16[4,592,512]{2,1,0:T(8,128)(2,1)}, bf16[4,592,512]{2,1,0:T(8,128)(2,1)}, u32[]{:S(2)}, u32[]{:S(2)}) collective-permute-start(bf16[4,592,512]{2,1,0:T(8,128)(2,1)} %tie.9.rest_0_), channel_id=1, source_target_pairs={{4,0},{6,2},{8,4},{10,6},{5,1},{7,3},{9,5},{11,7},{20,16},{22,18},... | collective-permute-start | bytes 7274504 | tf_op jit(solution)/shard_map/ppermute | solution.py:289
  81.2 63.0 %collective-permute-start.13 = (bf16[4,592,512]{2,1,0:T(8,128)(2,1)}, bf16[4,592,512]{2,1,0:T(8,128)(2,1)}, u32[]{:S(2)}, u32[]{:S(2)}) collective-permute-start(bf16[4,592,512]{2,1,0:T(8,128)(2,1)} %copy_sets.8.rest_2_), channel_id=1, source_target_pairs={{0,2},{2,0},{4,6},{6,4},{8,10},{10,8},{12,14},{14,12},{1,3},{3,1},... | collective-permute-start | bytes 7274504 | tf_op jit(solution)/shard_map/ppermute | solution.py:283
  85.4 53.0 %copy-start.1 = (bf16[4,592,512]{2,1,0:T(8,128)(2,1)}, bf16[4,592,512]{2,1,0:T(8,128)(2,1)S(1)}, u32[]{:S(2)}) copy-start(bf16[4,592,512]{2,1,0:T(8,128)(2,1)S(1)} %collective-permute-done.8.rest_1_) | copy-start | bytes 7274500
  144.1 2.7 %copy-start.5 = (bf16[2,592,512]{2,1,0:T(8,128)(2,1)S(1)}, bf16[2,592,512]{2,1,0:T(8,128)(2,1)}, u32[]{:S(2)}) copy-start(bf16[2,592,512]{2,1,0:T(8,128)(2,1)} %copy_sets.10.rest_2_) | copy-start | bytes 3637252
  144.2 34.6 %collective-permute-start.14 = (bf16[4,592,512]{2,1,0:T(8,128)(2,1)}, bf16[4,592,512]{2,1,0:T(8,128)(2,1)}, u32[]{:S(2)}, u32[]{:S(2)}) collective-permute-start(bf16[4,592,512]{2,1,0:T(8,128)(2,1)} %tie.11.rest_2_), channel_id=1, source_target_pairs={{0,1},{1,0},{2,3},{3,2},{4,5},{5,4},{6,7},{7,6},{8,9},{9,8},{10,11... | collective-permute-start | bytes 7274504 | tf_op jit(solution)/shard_map/ppermute | solution.py:286
  146.8 30.9 %collective-permute-start.15 = (bf16[2,592,512]{2,1,0:T(8,128)(2,1)S(1)}, bf16[2,592,512]{2,1,0:T(8,128)(2,1)S(1)}, u32[]{:S(2)}, u32[]{:S(2)}) collective-permute-start(bf16[2,592,512]{2,1,0:T(8,128)(2,1)S(1)} %copy-done.5), channel_id=1, source_target_pairs={{4,0},{6,2},{8,12},{10,14},{5,1},{7,3},{9,13},{11,15},{20,16},{22,... | collective-permute-start | bytes 3637256 | tf_op jit(solution)/shard_map/ppermute | solution.py:405
  148.7 5.3 %copy-start.15 = (s32[32,2]{0,1:T(2,128)S(1)}, s32[32,2]{0,1:T(2,128)}, u32[]{:S(2)}) copy-start(s32[32,2]{0,1:T(2,128)} %param.10) | copy-start | bytes 772
  148.7 5.4 %copy-start.16 = (f32[32]{0:T(128)S(1)}, f32[32]{0:T(128)}, u32[]{:S(2)}) copy-start(f32[32]{0:T(128)} %param.8) | copy-start | bytes 388
  148.7 6.1 %copy-start.13 = (bf16[4,576]{1,0:T(4,128)(2,1)S(1)}, bf16[4,576]{1,0:T(4,128)(2,1)}, u32[]{:S(2)}) copy-start(bf16[4,576]{1,0:T(4,128)(2,1)} %energy_ref.1) | copy-start | bytes 13828
  151.8 40.2 %collective-permute-start.12 = (bf16[2,592,512]{2,1,0:T(8,128)(2,1)}, bf16[2,592,512]{2,1,0:T(8,128)(2,1)}, u32[]{:S(2)}, u32[]{:S(2)}) collective-permute-start(bf16[2,592,512]{2,1,0:T(8,128)(2,1)} %copy_sets.12.rest_2_), channel_id=1, source_target_pairs={{0,2},{2,0},{4,6},{6,4},{8,10},{10,8},{12,14},{14,12},{1,3},{3,1},... | collective-permute-start | bytes 3637256 | tf_op jit(solution)/shard_map/ppermute | solution.py:283
  157.7 37.1 %collective-permute-start.11 = (bf16[2,592,512]{2,1,0:T(8,128)(2,1)}, bf16[2,592,512]{2,1,0:T(8,128)(2,1)S(1)}, u32[]{:S(2)}, u32[]{:S(2)}) collective-permute-start(bf16[2,592,512]{2,1,0:T(8,128)(2,1)} %copy_sets.13.rest_4_.rest_0_), channel_id=1, source_target_pairs={{0,1},{1,0},{2,3},{3,2},{4,5},{5,4},{6,7},{7,6},{8,9},{9,8},{10,11... | collective-permute-start | bytes 3637256 | tf_op jit(solution)/shard_map/ppermute | solution.py:286
  177.7 1.0 copy-start.3
  178.8 16.1 %collective-permute-start.17 = (bf16[2,592,512]{2,1,0:T(8,128)(2,1)}, bf16[2,592,512]{2,1,0:T(8,128)(2,1)S(1)}, u32[]{:S(2)}, u32[]{:S(2)}) collective-permute-start(bf16[2,592,512]{2,1,0:T(8,128)(2,1)} %tie.12.rest_4_), channel_id=1, source_target_pairs={{0,1},{1,0},{2,3},{3,2},{4,5},{5,4},{6,7},{7,6},{8,9},{9,8},{10,11... | collective-permute-start | bytes 3637256 | tf_op jit(solution)/shard_map/ppermute | solution.py:286
  191.9 1.3 copy-start.4
  191.9 1.6 copy-start.2
  191.9 3.3 %collective-permute-start.16 = (bf16[2,592,512]{2,1,0:T(8,128)(2,1)}, bf16[2,592,512]{2,1,0:T(8,128)(2,1)}, u32[]{:S(2)}, u32[]{:S(2)}) collective-permute-start(bf16[2,592,512]{2,1,0:T(8,128)(2,1)} %tie.13.rest_2_), channel_id=1, source_target_pairs={{0,1},{1,0},{2,3},{3,2},{4,5},{5,4},{6,7},{7,6},{8,9},{9,8},{10,11... | collective-permute-start | bytes 3637256 | tf_op jit(solution)/shard_map/ppermute | solution.py:286
  193.2 27.9 %collective-permute-start.19 = (bf16[2,592,512]{2,1,0:T(8,128)(2,1)S(1)}, bf16[2,592,512]{2,1,0:T(8,128)(2,1)S(1)}, u32[]{:S(2)}, u32[]{:S(2)}) collective-permute-start(bf16[2,592,512]{2,1,0:T(8,128)(2,1)S(1)} %copy-done.4), channel_id=1, source_target_pairs={{0,2},{2,0},{4,6},{6,4},{8,10},{10,8},{12,14},{14,12},{1,3},{3,1},... | collective-permute-start | bytes 3637256 | tf_op jit(solution)/shard_map/ppermute | solution.py:283
  193.6 35.8 %collective-permute-start.10 = (bf16[2,592,512]{2,1,0:T(8,128)(2,1)S(1)}, bf16[2,592,512]{2,1,0:T(8,128)(2,1)S(1)}, u32[]{:S(2)}, u32[]{:S(2)}) collective-permute-start(bf16[2,592,512]{2,1,0:T(8,128)(2,1)S(1)} %copy-done.2), channel_id=1, source_target_pairs={{4,0},{6,2},{8,12},{10,14},{5,1},{7,3},{9,13},{11,15},{20,16},{22,... | collective-permute-start | bytes 3637256 | tf_op jit(solution)/shard_map/ppermute | solution.py:405
  194.9 1.1 copy-start.8
  194.9 1.5 copy-start.9
  221.1 1.0 copy-start.7
  222.1 8.9 %collective-permute-start.20 = (bf16[2,592,512]{2,1,0:T(8,128)(2,1)}, bf16[2,592,512]{2,1,0:T(8,128)(2,1)S(1)}, u32[]{:S(2)}, u32[]{:S(2)}) collective-permute-start(bf16[2,592,512]{2,1,0:T(8,128)(2,1)} %tie.15.rest_2_), channel_id=1, source_target_pairs={{0,1},{1,0},{2,3},{3,2},{4,5},{5,4},{6,7},{7,6},{8,9},{9,8},{10,11... | collective-permute-start | bytes 3637256 | tf_op jit(solution)/shard_map/ppermute | solution.py:286
  229.3 1.0 copy-start.6
  230.4 3.4 %collective-permute-start.18 = (bf16[2,592,512]{2,1,0:T(8,128)(2,1)}, bf16[2,592,512]{2,1,0:T(8,128)(2,1)S(1)}, u32[]{:S(2)}, u32[]{:S(2)}) collective-permute-start(bf16[2,592,512]{2,1,0:T(8,128)(2,1)} %tie.14.rest_0_), channel_id=1, source_target_pairs={{0,1},{1,0},{2,3},{3,2},{4,5},{5,4},{6,7},{7,6},{8,9},{9,8},{10,11... | collective-permute-start | bytes 3637256 | tf_op jit(solution)/shard_map/ppermute | solution.py:286
  231.0 2.7 %copy-start.10 = (bf16[2,592,512]{2,1,0:T(8,128)(2,1)}, bf16[2,592,512]{2,1,0:T(8,128)(2,1)S(1)}, u32[]{:S(2)}) copy-start(bf16[2,592,512]{2,1,0:T(8,128)(2,1)S(1)} %collective-permute-done.20.rest_3_) | copy-start | bytes 3637252
  233.7 1.0 copy-start.11

commit v6 on v5

--- a/solution.py
+++ b/solution.py
@@ -303,23 +303,14 @@
     wanted_flat = jnp.any(slot_second[:, None] == slots[None, :], axis=0).astype(i32)
     wanted_flat = tie(wanted_flat, [stored])
     wanted = wanted_flat.reshape(orb_count, occ_dev) > 0
-    wanted_opp = across_y(wanted_flat).reshape(orb_count, occ_dev) > 0
-    top = orb_count - 1
-    tell = [(0, 3), (1, 2), (top, top - 3), (top - 1, top - 2)]
-    wanted_far = lax.ppermute(wanted_flat, "orb", tell).reshape(orb_count, occ_dev) > 0
+    wanted_both = jnp.stack([wanted_flat, across_y(wanted_flat)])
+    wanted_opp = wanted_both[1].reshape(orb_count, occ_dev) > 0
     local = jnp.arange(occ_dev, dtype=i32)[None, :]
 
     def two_of(table):
         return jnp.min(jnp.where(table, local, occ_dev - 1), axis=1), jnp.max(jnp.where(table, local, 0), axis=1)
 
     want, want_opp = two_of(wanted), two_of(wanted_opp)
-
-    def far_place(rows):
-        w = rows.astype(i32)
-        earlier = (jnp.arange(occ_dev)[:, None] < jnp.arange(occ_dev)[None, :]).astype(i32)
-        ahead = jnp.sum(w[:, :, None] * earlier[None], axis=1)
-        ahead_not = jnp.sum((1 - w)[:, :, None] * earlier[None], axis=1)
-        return jnp.where(rows, ahead, jnp.sum(w, axis=1, keepdims=True) + ahead_not)
 
     first_row = core * own_rows
     own_second = lax.dynamic_slice_in_dim(slot_second, first_row, own_rows, 0)
@@ -333,14 +324,14 @@
     dist = jnp.abs(src_z - z)
     is_opp = (src_y != y).astype(i32)
     from_up = src_z < z
-    place_table = far_place(wanted_opp).reshape(-1)
-    far = jnp.sum(jnp.where(own_second[:, None] == slots[None, :], place_table[None, :], 0), axis=1)
     both = 2 * dist <= chain - 1
-    is_far = (dist == last) & (is_opp == 0)
-    idx = jnp.where((dist == 0) & (is_opp == 0), part, rank + jnp.where(both & from_up, 2, 0))
-    idx = jnp.where(is_far, far % 2, idx)
-    which = jnp.where(is_far & (far < 2), 2, is_opp)
-    stage = dist - (is_far & (far < 2)).astype(i32)
+    is_far = dist == last
+    at_hand = (dist <= 1) & (is_opp == 0)
+    idx = jnp.where(at_hand, part, rank + jnp.where(both & from_up, 2, 0))
+    which_col = jnp.where(dist == 0, 3, jnp.where((dist == 1) & from_up, 2, jnp.where(is_far, 2, 1)))
+    which = jnp.where(is_opp == 1, is_far.astype(i32), which_col)
+    stage_col = jnp.where(is_far, last - 2, jnp.maximum(dist - 1, 0))
+    stage = jnp.where(is_opp == 1, jnp.minimum(dist, last - 1), stage_col)
     rows = jnp.arange(own_rows, dtype=i32)
     before = (stage[None, :] < stage[:, None]) | ((stage[None, :] == stage[:, None]) & (rows[None, :] < rows[:, None]))
     place = jnp.sum(before.astype(i32), axis=1)
@@ -382,12 +373,14 @@
         return a, across_aux(a)
 
     y_load = copy_sets([0, 0], two_for(want_opp, o), [stored])
-    y_own, y_other = with_other(across_y(y_load))
-    sets[0] = [(stored, local_other), (y_own, y_other)]
-    early = [y_other, local_other, pick, meta]
+    opp = with_other(across_y(y_load))
+    top = orb_count - 1
+    tell = [(0, 2), (1, 3), (top, top - 2), (top - 1, top - 3)]
+    wanted_far = lax.ppermute(tie(wanted_both, [y_load]), "orb", tell).reshape(2, orb_count, occ_dev) > 0
+    far_own, far_opp = two_of(wanted_far[0]), two_of(wanted_far[1])
+    early = [opp[1], local_other, pick, meta]
     downs[1], ups[1] = tie(downs[1], early), tie(ups[1], early)
     out = None
-    opp = None
     for d in range(1, last):
         s_down, s_up = o + 2 * d, o - 2 * d
         first = []
@@ -396,14 +389,14 @@
             ups.append(hop_up(ups[d], d + 1))
         else:
             sends_down = z == 1
-            turn_of = idx_of(far_place(wanted_far), jnp.where(sends_down, 2 * last + y, y))
-            turn = [jnp.sum(jnp.where(turn_of == j, local[0], 0)) for j in range(occ_dev)]
+            source = jnp.where(sends_down, 2 * last + y, y)
+            from_set = [1 - sends_down.astype(i32)] * 2
             perm = [(2, 0), (3, 1), (2 * (last - 1), 2 * last), (2 * (last - 1) + 1, 2 * last + 1)]
-            is_up = 1 - sends_down.astype(i32)
-            load_a = copy_sets([is_up, is_up], turn[:2], [downs[d], ups[d]], [mine_other] if d > 1 else [])
-            load_b = copy_sets([is_up, is_up], turn[2:], [downs[d], ups[d]], [load_a])
-            got_a, got_b = lax.ppermute(load_a, "orb", perm), lax.ppermute(load_b, "orb", perm)
-            first = [load_b]
+            load_over = copy_sets(from_set, two_for(far_opp, source), [downs[d], ups[d]], [out])
+            load_own = copy_sets(from_set, two_for(far_own, source), [downs[d], ups[d]], [load_over])
+            far_b = lax.ppermute(across_y(load_over), "orb", perm)
+            far_a = lax.ppermute(load_own, "orb", perm)
+            first = [load_own]
         if 2 * d <= last:
             place_of = [0, 0, 1, 1]
 
@@ -416,19 +409,18 @@
             def both_ways(table):
                 return two_for(table, jnp.where(is_up == 1, s_up, s_down))
         theirs = copy_sets(place_of, both_ways(want_opp), [downs[d], ups[d]], first)
-        mine = copy_sets(place_of, both_ways(want), [downs[d], ups[d]], [theirs])
-        if d > 1:
-            sets[d - 1] = [(prev_mine, mine_other), with_other(tie(opp, first) if first else opp)]
-            out = pairs_at(d - 2, [mine] + first, out)
+        if d == 1:
+            sets[0] = [opp, with_other(downs[1]), with_other(ups[1]), (stored, local_other)]
+            out = pairs_at(0, [theirs], out)
+        else:
+            mine = copy_sets(place_of, both_ways(want), [downs[d], ups[d]], [theirs])
+            sets[d - 1] = [with_other(tie(opp, first) if first else opp), with_other(mine)]
+            if d + 1 == last:
+                sets[d - 1].append(with_other(far_a))
+            out = pairs_at(d - 1, [mine], out)
         opp = across_y(theirs)
-        prev_mine, mine_other = with_other(mine)
-    got_a = tie(got_a, [out])
-    far_opp = across_y(got_a)
-    out = pairs_at(last - 2, [got_a], out)
-    sets[last - 1] = [(prev_mine, mine_other), with_other(tie(opp, [out])), with_other(got_a)]
-    out = pairs_at(last - 1, [], out)
-    sets[last] = [with_other(tie(got_b, [out])), with_other(tie(far_opp, [out]))]
-    return pairs_at(last, [], out)
+    sets[last - 1] = [with_other(tie(opp, [out])), with_other(tie(far_b, [out]))]
+    return pairs_at(last - 1, [], out)
 
 
 def solution(mesh):

time: 245 us -> 214 us (0.87)
  waiting for transfers between devices: 116 us -> 89.1 us
  Pallas kernels: 64.9 us -> 57.6 us
  starting transfers between devices: 21.1 us -> 27.6 us
  other arithmetic: 26.3 us -> 19.9 us
  local copies, waits for them, and re-layouts: 13.3 us -> 16.6 us
    ppermute x2, waiting for transfers between devices: 58.6 us -> 33.3 us  [hop_down(): lax.ppermute(a, 'orb', [(k, k - 2) for k in range(2, orb_count) if k // 2...]
    ppermute x2, starting transfers between devices: 3.56 us -> 8.41 us  [hop_up(): lax.ppermute(a, 'orb', [(k, k + 2) for k in range(orb_count - 2) if k //...]
    pallas_call x4 -> x3, Pallas kernels: 40.2 us -> 36.4 us  [run_pairs(): pl.pallas_call(functools.partial(pair_kernel, call, wins, len(sets), len(...]
    pallas_call x7 -> x6, Pallas kernels: 21.3 us -> 17.8 us  [copy_sets(): pl.pallas_call(functools.partial(set_kernel, len(arrays), len(after)), ou...]
    reduce_sum x7 -> x0, other arithmetic: 3.04 us -> none  [the longest x4 2.66 us: per_device(): jnp.sum(jnp.where(turn_of == j, local[0], 0))]
    ppermute x3, waiting for transfers between devices: 16 us -> 18.9 us  [the longest x1 16.6 us: per_device(): far_a = lax.ppermute(load_own, 'orb', perm)]
    ppermute x5, waiting for transfers between devices: 36.4 us -> 33.7 us  [across_y(): return lax.ppermute(a, 'orb', swap_y)]
    another operation x8 -> x9, other arithmetic: 13.3 us -> 10.7 us  [copy_sets(): jnp.stack([jnp.stack([jnp.asarray(w, jnp.int32) for w in which]), jnp.sta...]
  transfers between devices with their start and end apart: 21 -> 21, of which waited for: 9 -> 8; matrix products, arithmetic and copies ran while one was open for 13% -> 13% of each run, Pallas kernels for 20% -> 21%
where the time goes in v6:
time: 214 us; the launch traced here: 211 us
  waiting for transfers between devices  89.1 us (42%)
  Pallas kernels  57.6 us (27%)
  starting transfers between devices  27.6 us (13%)
  other arithmetic  19.9 us (9%)
  local copies, waits for them, and re-layouts  16.6 us (8%)
    pallas_call x3, Pallas kernels, run_pairs(): pl.pallas_call(functools.partial(pair_kernel, call, wins, len(sets), len(...  36.4 us
    ppermute x5, waiting for transfers between devices, across_y(): return lax.ppermute(a, 'orb', swap_y)  33.7 us
    ppermute x2, waiting for transfers between devices, hop_down(): lax.ppermute(a, 'orb', [(k, k - 2) for k in range(2, orb_count) if k // 2...  33.3 us
    pallas_call x6, Pallas kernels, copy_sets(): pl.pallas_call(functools.partial(set_kernel, len(arrays), len(after)), ou...  17.8 us
    ppermute x1, waiting for transfers between devices, per_device(): far_a = lax.ppermute(load_own, 'orb', perm)  16.6 us
    another operation x9, other arithmetic, copy_sets(): jnp.stack([jnp.stack([jnp.asarray(w, jnp.int32) for w in which]), jnp.sta...  10.7 us
    unnamed x40, local copies, waits for them, and re-layouts  9.12 us
    ppermute x2, starting transfers between devices, hop_up(): lax.ppermute(a, 'orb', [(k, k + 2) for k in range(orb_count - 2) if k //...  8.41 us
  transfers between devices with their start and end apart: 21, of which 8 were waited for; matrix products, arithmetic and copies ran while one was open for 13% of the time, Pallas kernels for 21%

profile of v6, /device:TPU:0, one launch (start us, length us, event | category | flops | bytes accessed | tf_op | source)
XLA Modules:
  0.0 211.1 jit_solution(16723724102210968781)
XLA Ops:
  0.0 3.3 %extend.1.refs_1_.rest_0_.own_ref.rest_6_ = bf16[4,592,512]{2,1,0:T(8,128)(2,1)} custom-call(bf16[4,576,512]{2,1,0:T(8,128)(2,1)} %blocks_ref.1, bf16[4,576]{1,0:T(4,128)(2,1)} %energy_ref.1), custom_call_target="tpu_custom_call" | custom-call | tf_op jit(solution)/shard_map/extend/pallas_call | solution.py:237
  3.4 6.4 %collective-permute-start.6 = (bf16[4,592,512]{2,1,0:T(8,128)(2,1)}, bf16[4,592,512]{2,1,0:T(8,128)(2,1)}, u32[]{:S(2)}, u32[]{:S(2)}) collective-permute-start(bf16[4,592,512]{2,1,0:T(8,128)(2,1)} %extend.1.refs_1_.rest_0_.own_ref.rest_6_), channel_id=1, source_target_pairs={{0,4},{2,6},{4,8},{6,10},{8,12},{10,14},{1,5},{3,7},{5,9},{7,11},{... | collective-permute-start | bytes 7274504 | tf_op jit(solution)/shard_map/ppermute | solution.py:292
  9.7 1.3 collective-permute-start.2
  12.0 1.5 collective-permute-start.1
  13.6 2.0 collective-permute-done.1
  15.8 0.7 fusion.7
  16.5 0.6 fusion.8
  17.1 1.3 add_bitcast_fusion.2
  19.1 2.8 %copy_sets.6.refs_1_ = bf16[2,592,512]{2,1,0:T(8,128)(2,1)} custom-call(s32[2,2]{1,0:T(2,128)} %stack.137.table_ref, bf16[4,592,512]{2,1,0:T(8,128)(2,1)} %extend.1.refs_1_.rest_0_.own_ref.rest_6_), custom_call_target="tpu_custom_call" | custom-call | tf_op jit(solution)/shard_map/copy_sets/pallas_call | solution.py:196
  21.9 1.8 collective-permute-start.3
  24.9 25.4 %collective-permute-done.3.rest_0_ = bf16[2,592,512]{2,1,0:T(8,128)(2,1)} collective-permute-done((bf16[2,592,512]{2,1,0:T(8,128)(2,1)}, bf16[2,592,512]{2,1,0:T(8,128)(2,1)}, u32[]{:S(2)}, u32[]{:S(2)}) %collective-permute-start.3) | collective-permute-done | bytes 1212448 | tf_op jit(solution)/shard_map/ppermute | solution.py:283
  50.4 5.7 %fusion.refs_3_.pick_ref = bf16[16,2,512,256]{3,2,1,0:T(8,128)(2,1)} fusion(s32[16,2,512]{2,1,0:T(2,128)S(1)} %dynamic-slice_add_fusion), kind=kLoop, calls=%fused_computation.1 | loop fusion | flops 8388608 | bytes 8454144 | tf_op jit(solution)/shard_map/convert_element_type | solution.py:359
  56.6 4.9 %collective-permute-start.8 = (s32[2,32]{1,0:T(2,128)}, s32[2,32]{1,0:T(2,128)S(1)}, u32[]{:S(2)}, u32[]{:S(2)}) collective-permute-start(s32[2,32]{1,0:T(2,128)} %tie.10), channel_id=1, source_target_pairs={{0,4},{2,6},{14,10},{12,8},{1,5},{3,7},{15,11},{13,9},{16,20},{18,... | collective-permute-start | bytes 776 | tf_op jit(solution)/shard_map/ppermute | solution.py:379
  61.6 2.5 %add_bitcast_fusion.6 = s32[1,4]{1,0:T(1,128)S(1)} fusion(s32[1]{0:T(128)} %get-tuple-element.33, s32[1]{0:T(128)} %get-tuple-element.29, s32[1]{0:T(128)} %get-tuple-element.32, s32[1]{0:T(128)} %get-tuple-element.28), kind=kLoop, calls=%fused_computation.67 | loop fusion | flops 12 | bytes 32 | tf_op jit(solution)/shard_map/stack | solution.py:194
  64.0 2.0 collective-permute-done.2.refs_0_
  66.0 1.5 copy-done
  67.5 1.0 copy-done.2
  68.6 1.4 collective-permute-start.5
  70.4 2.1 collective-permute-start.7
  73.1 3.4 %copy_sets.7.rest_8_ = bf16[4,592,512]{2,1,0:T(8,128)(2,1)} custom-call(s32[2,4]{1,0:T(2,128)} %pad_add_fusion.5.table_ref, bf16[4,592,512]{2,1,0:T(8,128)(2,1)} %tie.8.rest_0_.rest_2_, bf16[4,592,512]{2,1,0:T(8,128)(2,1)} %tie.9.rest_1_.rest_4_), custom_call_target="tpu_custom_call" | custom-call | tf_op jit(solution)/shard_map/copy_sets/pallas_call | solution.py:196
  76.5 1.6 collective-permute-start.12
  81.8 1.3 add_bitcast_fusion.5
  83.0 1.3 add_bitcast_fusion.4
  84.9 0.9 broadcast_in_dim.140.ve1_ref
  85.9 8.5 %pairs_0.1.rest_2_.rest_7_ = bf16[16,512,512]{2,1,0:T(8,128)(2,1)} custom-call(s32[5,16]{1,0:T(8,128)} %stack.128.refs_4_.meta_ref, f32[16]{0:T(128)} %add.76.shift_ref, bf16[2,576,128]{2,1,0:T(8,128)(2,1)} %broadcast_in_dim.140.ve1_ref, bf16[16,2,512,256]{3,2,1,0:T(8,128)(2,1)} %fusion.refs_3_.pick_ref, ...), custom_call_target="tpu_custom_call" | custom-call | tf_op jit(solution)/shard_map/pairs_0/pallas_call | solution.py:148
  94.4 31.3 %collective-permute-done.5.rest_0_ = bf16[4,592,512]{2,1,0:T(8,128)(2,1)S(1)} collective-permute-done((bf16[4,592,512]{2,1,0:T(8,128)(2,1)}, bf16[4,592,512]{2,1,0:T(8,128)(2,1)S(1)}, u32[]{:S(2)}, u32[]{:S(2)}) %collective-permute-start.5) | collective-permute-done | bytes 2424864 | tf_op jit(solution)/shard_map/ppermute | solution.py:289
  125.7 1.4 copy-done.1
  127.1 2.8 %copy_sets.8.rest_2_ = bf16[2,592,512]{2,1,0:T(8,128)(2,1)} custom-call(s32[2,2]{1,0:T(2,128)} %get-tuple-element.36.table_ref, bf16[4,592,512]{2,1,0:T(8,128)(2,1)} %copy-done.1, bf16[4,592,512]{2,1,0:T(8,128)(2,1)} %collective-permute-done.7.rest_1_, bf16[16,512,512]{2,1,0:T(8,128)(2,1)} %pairs_0.1.rest_2_.rest_7_), custom_call_target="tpu_custom_call" | custom-call | tf_op jit(solution)/shard_map/copy_sets/pallas_call | solution.py:196
  130.0 2.9 %copy_sets.9.rest_2_.refs_1_ = bf16[2,592,512]{2,1,0:T(8,128)(2,1)} custom-call(s32[2,2]{1,0:T(2,128)} %get-tuple-element.37.table_ref, bf16[4,592,512]{2,1,0:T(8,128)(2,1)} %copy-done.1, bf16[4,592,512]{2,1,0:T(8,128)(2,1)} %collective-permute-done.7.rest_1_, bf16[2,592,512]{2,1,0:T(8,128)(2,1)} %copy_sets.8.rest_2_), custom_call_target="tpu_custom_call" | custom-call | tf_op jit(solution)/shard_map/copy_sets/pallas_call | solution.py:196
  132.9 1.4 collective-permute-start.15
  134.5 1.6 collective-permute-start.18
  137.5 1.3 add_bitcast_fusion.7
  138.7 1.4 add_bitcast_fusion
  140.7 2.8 %copy_sets.10.rest_2_ = bf16[2,592,512]{2,1,0:T(8,128)(2,1)} custom-call(s32[2,2]{1,0:T(2,128)} %get-tuple-element.27.table_ref, bf16[4,592,512]{2,1,0:T(8,128)(2,1)} %copy-done.1, bf16[4,592,512]{2,1,0:T(8,128)(2,1)} %collective-permute-done.7.rest_1_, bf16[2,592,512]{2,1,0:T(8,128)(2,1)} %copy_sets.9.rest_2_.refs_1_), custom_call_target="tpu_custom_call" | custom-call | tf_op jit(solution)/shard_map/copy_sets/pallas_call | solution.py:196
  143.5 3.0 %copy_sets.11.rest_2_.rest_6_ = bf16[2,592,512]{2,1,0:T(8,128)(2,1)} custom-call(s32[2,2]{1,0:T(2,128)} %get-tuple-element.26.table_ref, bf16[4,592,512]{2,1,0:T(8,128)(2,1)} %copy-done.1, bf16[4,592,512]{2,1,0:T(8,128)(2,1)} %collective-permute-done.7.rest_1_, bf16[2,592,512]{2,1,0:T(8,128)(2,1)} %copy_sets.10.rest_2_), custom_call_target="tpu_custom_call" | custom-call | tf_op jit(solution)/shard_map/copy_sets/pallas_call | solution.py:196
  146.7 16.6 %collective-permute-done.15.rest_4_ = bf16[2,592,512]{2,1,0:T(8,128)(2,1)S(1)} collective-permute-done((bf16[2,592,512]{2,1,0:T(8,128)(2,1)}, bf16[2,592,512]{2,1,0:T(8,128)(2,1)S(1)}, u32[]{:S(2)}, u32[]{:S(2)}) %collective-permute-start.15) | collective-permute-done | bytes 1212448 | tf_op jit(solution)/shard_map/ppermute | solution.py:398
  163.4 1.6 collective-permute-start.11
  165.0 1.3 collective-permute-start.19
  166.3 1.0 copy-done.8
  167.3 1.0 copy-done.9
  168.4 17.8 %pairs_1.1.refs_1_.rest_4_ = bf16[16,512,512]{2,1,0:T(8,128)(2,1)} custom-call(s32[5,16]{1,0:T(8,128)} %stack.128.refs_4_.meta_ref, f32[16]{0:T(128)} %add.76.shift_ref, bf16[2,576,128]{2,1,0:T(8,128)(2,1)} %broadcast_in_dim.140.ve1_ref, bf16[16,2,512,256]{3,2,1,0:T(8,128)(2,1)} %fusion.refs_3_.pick_ref, ...), custom_call_target="tpu_custom_call", output_to_operand_aliasing={{}: (13, {})} | custom-call | tf_op jit(solution)/shard_map/pairs_1/pallas_call | solution.py:148
  186.2 6.3 %collective-permute-done.11.refs_0_ = bf16[2,592,512]{2,1,0:T(8,128)(2,1)S(1)} collective-permute-done((bf16[2,592,512]{2,1,0:T(8,128)(2,1)S(1)}, bf16[2,592,512]{2,1,0:T(8,128)(2,1)S(1)}, u32[]{:S(2)}, u32[]{:S(2)}) %collective-permute-start.11) | collective-permute-done | bytes 1212448 | tf_op jit(solution)/shard_map/ppermute | solution.py:283
  192.5 1.0 copy-done.6
  193.5 2.3 %collective-permute-done.19.refs_0_ = bf16[2,592,512]{2,1,0:T(8,128)(2,1)S(1)} collective-permute-done((bf16[2,592,512]{2,1,0:T(8,128)(2,1)}, bf16[2,592,512]{2,1,0:T(8,128)(2,1)S(1)}, u32[]{:S(2)}, u32[]{:S(2)}) %collective-permute-start.19) | collective-permute-done | bytes 1212448 | tf_op jit(solution)/shard_map/ppermute | solution.py:397
  195.8 1.0 copy-done.5
  196.9 3.1 %collective-permute-done.20.rest_3_ = bf16[2,592,512]{2,1,0:T(8,128)(2,1)S(1)} collective-permute-done((bf16[2,592,512]{2,1,0:T(8,128)(2,1)}, bf16[2,592,512]{2,1,0:T(8,128)(2,1)S(1)}, u32[]{:S(2)}, u32[]{:S(2)}) %collective-permute-start.20) | collective-permute-done | bytes 1212448 | tf_op jit(solution)/shard_map/ppermute | solution.py:286
  200.0 1.0 copy-done.11
  201.0 10.1 %pairs_2.1 = bf16[16,512,512]{2,1,0:T(8,128)(2,1)} custom-call(s32[5,16]{1,0:T(8,128)} %stack.128.refs_4_.meta_ref, f32[16]{0:T(128)} %add.76.shift_ref, bf16[2,576,128]{2,1,0:T(8,128)(2,1)} %broadcast_in_dim.140.ve1_ref, bf16[16,2,512,256]{3,2,1,0:T(8,128)(2,1)} %fusion.refs_3_.pick_ref, ...), custom_call_target="tpu_custom_call", output_to_operand_aliasing={{}: (10, {})} | custom-call | tf_op jit(solution)/shard_map/pairs_2/pallas_call | solution.py:148
  (104 shorter events, 11.3 us)
Async XLA Ops:
  0.0 11.1 %copy-start.16 = (s32[32,2]{0,1:T(2,128)S(1)}, s32[32,2]{0,1:T(2,128)}, u32[]{:S(2)}) copy-start(s32[32,2]{0,1:T(2,128)} %param.10) | copy-start | bytes 772
  0.0 11.1 %copy-start.19 = (s32[32]{0:T(128)S(1)}, s32[32]{0:T(128)}, u32[]{:S(2)}) copy-start(s32[32]{0:T(128)} %param.9) | copy-start | bytes 388
  3.4 66.6 %collective-permute-start.6 = (bf16[4,592,512]{2,1,0:T(8,128)(2,1)}, bf16[4,592,512]{2,1,0:T(8,128)(2,1)}, u32[]{:S(2)}, u32[]{:S(2)}) collective-permute-start(bf16[4,592,512]{2,1,0:T(8,128)(2,1)} %extend.1.refs_1_.rest_0_.own_ref.rest_6_), channel_id=1, source_target_pairs={{0,4},{2,6},{4,8},{6,10},{8,12},{10,14},{1,5},{3,7},{5,9},{7,11},{... | collective-permute-start | bytes 7274504 | tf_op jit(solution)/shard_map/ppermute | solution.py:292
  9.7 56.3 %collective-permute-start.2 = (bf16[4,592,512]{2,1,0:T(8,128)(2,1)}, bf16[4,592,512]{2,1,0:T(8,128)(2,1)}, u32[]{:S(2)}, u32[]{:S(2)}) collective-permute-start(bf16[4,592,512]{2,1,0:T(8,128)(2,1)} %extend.1.refs_1_.rest_0_.own_ref.rest_6_), channel_id=1, source_target_pairs={{4,0},{6,2},{8,4},{10,6},{12,8},{14,10},{5,1},{7,3},{9,5},{11,7},{... | collective-permute-start | bytes 7274504 | tf_op jit(solution)/shard_map/ppermute | solution.py:289
  11.0 55.0 %collective-permute-start = (bf16[4,592,512]{2,1,0:T(8,128)(2,1)}, bf16[4,592,512]{2,1,0:T(8,128)(2,1)S(1)}, u32[]{:S(2)}, u32[]{:S(2)}) collective-permute-start(bf16[4,592,512]{2,1,0:T(8,128)(2,1)} %extend.1.refs_1_.rest_0_.own_ref.rest_6_), channel_id=1, source_target_pairs={{0,1},{1,0},{2,3},{3,2},{4,5},{5,4},{6,7},{7,6},{8,9},{9,8},{10,11... | collective-permute-start | bytes 7274504 | tf_op jit(solution)/shard_map/ppermute | solution.py:286
  12.0 38.3 %copy-start.12 = (s32[32,2,512]{2,1,0:T(2,128)S(1)}, s32[32,2,512]{2,1,0:T(2,128)}, u32[]{:S(2)}) copy-start(s32[32,2,512]{2,1,0:T(2,128)} %param.11) | copy-start | bytes 393220
  12.0 38.3 %copy-start.14 = (s32[512]{0:T(512)S(1)}, s32[512]{0:T(512)}, u32[]{:S(2)}) copy-start(s32[512]{0:T(512)} %constant.141.clone.1) | copy-start | bytes 6148
  12.0 3.6 %collective-permute-start.1 = (s32[32]{0:T(128)}, s32[32]{0:T(128)S(1)}, u32[]{:S(2)}, u32[]{:S(2)}) collective-permute-start(s32[32]{0:T(128)} %tie.7), channel_id=1, source_target_pairs={{0,2},{2,0},{4,6},{6,4},{8,10},{10,8},{12,14},{14,12},{1,3},{3,1},... | collective-permute-start | bytes 392 | tf_op jit(solution)/shard_map/ppermute | solution.py:283
  21.9 28.4 %collective-permute-start.3 = (bf16[2,592,512]{2,1,0:T(8,128)(2,1)}, bf16[2,592,512]{2,1,0:T(8,128)(2,1)}, u32[]{:S(2)}, u32[]{:S(2)}) collective-permute-start(bf16[2,592,512]{2,1,0:T(8,128)(2,1)} %copy_sets.6.refs_1_), channel_id=1, source_target_pairs={{0,2},{2,0},{4,6},{6,4},{8,10},{10,8},{12,14},{14,12},{1,3},{3,1},... | collective-permute-start | bytes 3637256 | tf_op jit(solution)/shard_map/ppermute | solution.py:283
  50.3 15.7 %collective-permute-start.4 = (bf16[2,592,512]{2,1,0:T(8,128)(2,1)}, bf16[2,592,512]{2,1,0:T(8,128)(2,1)S(1)}, u32[]{:S(2)}, u32[]{:S(2)}) collective-permute-start(bf16[2,592,512]{2,1,0:T(8,128)(2,1)} %collective-permute-done.3.rest_0_), channel_id=1, source_target_pairs={{0,1},{1,0},{2,3},{3,2},{4,5},{5,4},{6,7},{7,6},{8,9},{9,8},{10,11... | collective-permute-start | bytes 3637256 | tf_op jit(solution)/shard_map/ppermute | solution.py:286
  50.4 5.7 %copy-start.15 = (s32[32]{0:T(128)S(1)}, s32[32]{0:T(128)}, u32[]{:S(2)}) copy-start(s32[32]{0:T(128)} %tie.7) | copy-start | bytes 388
  56.6 19.9 %collective-permute-start.8 = (s32[2,32]{1,0:T(2,128)}, s32[2,32]{1,0:T(2,128)S(1)}, u32[]{:S(2)}, u32[]{:S(2)}) collective-permute-start(s32[2,32]{1,0:T(2,128)} %tie.10), channel_id=1, source_target_pairs={{0,4},{2,6},{14,10},{12,8},{1,5},{3,7},{15,11},{13,9},{16,20},{18,... | collective-permute-start | bytes 776 | tf_op jit(solution)/shard_map/ppermute | solution.py:379
  66.0 1.5 copy-start
  67.5 1.0 copy-start.2
  68.5 4.0 %copy-start.18 = (s32[1,4]{1,0:T(1,128)S(1)}, s32[1,4]{1,0:T(1,128)}, u32[]{:S(2)}) copy-start(s32[1,4]{1,0:T(1,128)} %constant.147.clone.1) | copy-start | bytes 52
  68.6 16.4 %collective-permute-start.9 = (bf16[4,592,512]{2,1,0:T(8,128)(2,1)}, bf16[4,592,512]{2,1,0:T(8,128)(2,1)}, u32[]{:S(2)}, u32[]{:S(2)}) collective-permute-start(bf16[4,592,512]{2,1,0:T(8,128)(2,1)} %tie.8.rest_0_.rest_2_), channel_id=1, source_target_pairs={{0,1},{1,0},{2,3},{3,2},{4,5},{5,4},{6,7},{7,6},{8,9},{9,8},{10,11... | collective-permute-start | bytes 7274504 | tf_op jit(solution)/shard_map/ppermute | solution.py:286
  68.6 57.2 %collective-permute-start.5 = (bf16[4,592,512]{2,1,0:T(8,128)(2,1)}, bf16[4,592,512]{2,1,0:T(8,128)(2,1)S(1)}, u32[]{:S(2)}, u32[]{:S(2)}) collective-permute-start(bf16[4,592,512]{2,1,0:T(8,128)(2,1)} %tie.8.rest_0_.rest_2_), channel_id=1, source_target_pairs={{4,0},{6,2},{8,4},{10,6},{5,1},{7,3},{9,5},{11,7},{20,16},{22,18},... | collective-permute-start | bytes 7274504 | tf_op jit(solution)/shard_map/ppermute | solution.py:289
  70.0 14.9 %collective-permute-start.10 = (bf16[4,592,512]{2,1,0:T(8,128)(2,1)}, bf16[4,592,512]{2,1,0:T(8,128)(2,1)}, u32[]{:S(2)}, u32[]{:S(2)}) collective-permute-start(bf16[4,592,512]{2,1,0:T(8,128)(2,1)} %tie.9.rest_1_.rest_4_), channel_id=1, source_target_pairs={{0,1},{1,0},{2,3},{3,2},{4,5},{5,4},{6,7},{7,6},{8,9},{9,8},{10,11... | collective-permute-start | bytes 7274504 | tf_op jit(solution)/shard_map/ppermute | solution.py:286
  70.4 55.3 %collective-permute-start.7 = (bf16[4,592,512]{2,1,0:T(8,128)(2,1)}, bf16[4,592,512]{2,1,0:T(8,128)(2,1)}, u32[]{:S(2)}, u32[]{:S(2)}) collective-permute-start(bf16[4,592,512]{2,1,0:T(8,128)(2,1)} %tie.9.rest_1_.rest_4_), channel_id=1, source_target_pairs={{4,8},{6,10},{8,12},{10,14},{5,9},{7,11},{9,13},{11,15},{20,24},{2... | collective-permute-start | bytes 7274504 | tf_op jit(solution)/shard_map/ppermute | solution.py:292
  73.1 5.1 %copy-start.17 = (f32[32]{0:T(128)S(1)}, f32[32]{0:T(128)}, u32[]{:S(2)}) copy-start(f32[32]{0:T(128)} %param.8) | copy-start | bytes 388
  73.1 5.8 %copy-start.13 = (bf16[4,576]{1,0:T(4,128)(2,1)S(1)}, bf16[4,576]{1,0:T(4,128)(2,1)}, u32[]{:S(2)}) copy-start(bf16[4,576]{1,0:T(4,128)(2,1)} %energy_ref.1) | copy-start | bytes 13828
  76.5 57.9 %collective-permute-start.12 = (bf16[4,592,512]{2,1,0:T(8,128)(2,1)}, bf16[4,592,512]{2,1,0:T(8,128)(2,1)}, u32[]{:S(2)}, u32[]{:S(2)}) collective-permute-start(bf16[4,592,512]{2,1,0:T(8,128)(2,1)} %copy_sets.7.rest_8_), channel_id=1, source_target_pairs={{0,2},{2,0},{4,6},{6,4},{8,10},{10,8},{12,14},{14,12},{1,3},{3,1},... | collective-permute-start | bytes 7274504 | tf_op jit(solution)/shard_map/ppermute | solution.py:283
  125.7 1.4 copy-start.1
  132.9 1.5 copy-start.3
  132.9 30.5 %collective-permute-start.15 = (bf16[2,592,512]{2,1,0:T(8,128)(2,1)}, bf16[2,592,512]{2,1,0:T(8,128)(2,1)S(1)}, u32[]{:S(2)}, u32[]{:S(2)}) collective-permute-start(bf16[2,592,512]{2,1,0:T(8,128)(2,1)} %copy_sets.9.rest_2_.refs_1_), channel_id=1, source_target_pairs={{4,0},{6,2},{8,12},{10,14},{5,1},{7,3},{9,13},{11,15},{20,16},{22,... | collective-permute-start | bytes 3637256 | tf_op jit(solution)/shard_map/ppermute | solution.py:398
  134.4 34.0 %collective-permute-start.13 = (bf16[4,592,512]{2,1,0:T(8,128)(2,1)}, bf16[4,592,512]{2,1,0:T(8,128)(2,1)}, u32[]{:S(2)}, u32[]{:S(2)}) collective-permute-start(bf16[4,592,512]{2,1,0:T(8,128)(2,1)} %tie.11.rest_0_), channel_id=1, source_target_pairs={{0,1},{1,0},{2,3},{3,2},{4,5},{5,4},{6,7},{7,6},{8,9},{9,8},{10,11... | collective-permute-start | bytes 7274504 | tf_op jit(solution)/shard_map/ppermute | solution.py:286
  134.5 30.5 %collective-permute-start.18 = (bf16[2,592,512]{2,1,0:T(8,128)(2,1)S(1)}, bf16[2,592,512]{2,1,0:T(8,128)(2,1)}, u32[]{:S(2)}, u32[]{:S(2)}) collective-permute-start(bf16[2,592,512]{2,1,0:T(8,128)(2,1)S(1)} %copy-done.3), channel_id=1, source_target_pairs={{0,2},{2,0},{4,6},{6,4},{8,10},{10,8},{12,14},{14,12},{1,3},{3,1},... | collective-permute-start | bytes 3637256 | tf_op jit(solution)/shard_map/ppermute | solution.py:283
  143.5 19.9 %copy-start.4 = (bf16[2,592,512]{2,1,0:T(8,128)(2,1)S(1)}, bf16[2,592,512]{2,1,0:T(8,128)(2,1)}, u32[]{:S(2)}) copy-start(bf16[2,592,512]{2,1,0:T(8,128)(2,1)} %copy_sets.10.rest_2_) | copy-start | bytes 3637252
  146.5 19.8 %collective-permute-start.14 = (bf16[2,592,512]{2,1,0:T(8,128)(2,1)}, bf16[2,592,512]{2,1,0:T(8,128)(2,1)S(1)}, u32[]{:S(2)}, u32[]{:S(2)}) collective-permute-start(bf16[2,592,512]{2,1,0:T(8,128)(2,1)} %copy_sets.11.rest_2_.rest_6_), channel_id=1, source_target_pairs={{0,1},{1,0},{2,3},{3,2},{4,5},{5,4},{6,7},{7,6},{8,9},{9,8},{10,11... | collective-permute-start | bytes 3637256 | tf_op jit(solution)/shard_map/ppermute | solution.py:286
  163.4 5.0 %copy-start.7 = (bf16[2,592,512]{2,1,0:T(8,128)(2,1)}, bf16[2,592,512]{2,1,0:T(8,128)(2,1)S(1)}, u32[]{:S(2)}) copy-start(bf16[2,592,512]{2,1,0:T(8,128)(2,1)S(1)} %collective-permute-done.15.rest_4_) | copy-start | bytes 3637252
  163.4 2.9 %collective-permute-start.16 = (bf16[2,592,512]{2,1,0:T(8,128)(2,1)S(1)}, bf16[2,592,512]{2,1,0:T(8,128)(2,1)S(1)}, u32[]{:S(2)}, u32[]{:S(2)}) collective-permute-start(bf16[2,592,512]{2,1,0:T(8,128)(2,1)S(1)} %collective-permute-done.15.rest_4_), channel_id=1, source_target_pairs={{0,1},{1,0},{2,3},{3,2},{4,5},{5,4},{6,7},{7,6},{8,9},{9,8},{10,11... | collective-permute-start | bytes 3637256 | tf_op jit(solution)/shard_map/ppermute | solution.py:286
  163.4 29.1 %collective-permute-start.11 = (bf16[2,592,512]{2,1,0:T(8,128)(2,1)S(1)}, bf16[2,592,512]{2,1,0:T(8,128)(2,1)S(1)}, u32[]{:S(2)}, u32[]{:S(2)}) collective-permute-start(bf16[2,592,512]{2,1,0:T(8,128)(2,1)S(1)} %copy-done.4), channel_id=1, source_target_pairs={{0,2},{2,0},{4,6},{6,4},{8,10},{10,8},{12,14},{14,12},{1,3},{3,1},... | collective-permute-start | bytes 3637256 | tf_op jit(solution)/shard_map/ppermute | solution.py:283
  165.0 30.8 %collective-permute-start.19 = (bf16[2,592,512]{2,1,0:T(8,128)(2,1)}, bf16[2,592,512]{2,1,0:T(8,128)(2,1)S(1)}, u32[]{:S(2)}, u32[]{:S(2)}) collective-permute-start(bf16[2,592,512]{2,1,0:T(8,128)(2,1)} %collective-permute-done.18), channel_id=1, source_target_pairs={{4,0},{6,2},{8,12},{10,14},{5,1},{7,3},{9,13},{11,15},{20,16},{22,... | collective-permute-start | bytes 3637256 | tf_op jit(solution)/shard_map/ppermute | solution.py:397
  166.3 1.0 copy-start.8
  167.3 1.0 copy-start.9
  192.5 1.0 copy-start.6
  193.5 3.4 %collective-permute-start.17 = (bf16[2,592,512]{2,1,0:T(8,128)(2,1)}, bf16[2,592,512]{2,1,0:T(8,128)(2,1)S(1)}, u32[]{:S(2)}, u32[]{:S(2)}) collective-permute-start(bf16[2,592,512]{2,1,0:T(8,128)(2,1)} %tie.12.rest_0_), channel_id=1, source_target_pairs={{0,1},{1,0},{2,3},{3,2},{4,5},{5,4},{6,7},{7,6},{8,9},{9,8},{10,11... | collective-permute-start | bytes 3637256 | tf_op jit(solution)/shard_map/ppermute | solution.py:286
  195.8 1.0 copy-start.5
  196.9 3.1 %collective-permute-start.20 = (bf16[2,592,512]{2,1,0:T(8,128)(2,1)}, bf16[2,592,512]{2,1,0:T(8,128)(2,1)S(1)}, u32[]{:S(2)}, u32[]{:S(2)}) collective-permute-start(bf16[2,592,512]{2,1,0:T(8,128)(2,1)} %tie.13.rest_2_), channel_id=1, source_target_pairs={{0,1},{1,0},{2,3},{3,2},{4,5},{5,4},{6,7},{7,6},{8,9},{9,8},{10,11... | collective-permute-start | bytes 3637256 | tf_op jit(solution)/shard_map/ppermute | solution.py:286
  196.9 3.1 %copy-start.10 = (bf16[2,592,512]{2,1,0:T(8,128)(2,1)}, bf16[2,592,512]{2,1,0:T(8,128)(2,1)S(1)}, u32[]{:S(2)}) copy-start(bf16[2,592,512]{2,1,0:T(8,128)(2,1)S(1)} %collective-permute-done.17.rest_1_) | copy-start | bytes 3637252
  200.0 1.0 copy-start.11

commit v7 on v6

--- a/solution.py
+++ b/solution.py
@@ -107,12 +107,16 @@
                 lax.dot_general(ve, two, NT, preferred_element_type=jnp.float32)[t:t + 1])
         e2 = jnp.concatenate(e2_parts, axis=1)
         shift = shift_ref[p]
-        c = lax.dot_general(side_a[...], side_b[...], NT, preferred_element_type=jnp.float32)
-        for col in range(0, kept, 128):
-            den = e1_buf[...] + e2[:, col:col + 128] - shift
-            inv = pl.reciprocal(den, approx=True)
-            neg = inv * (den * inv - 2.0)
-            out_buf[slot, :, col:col + 128] = (c[:, col:col + 128] * neg).astype(jnp.bfloat16)
+        chunk = min(kept, 256)
+        for start in range(0, kept, chunk):
+            c = lax.dot_general(
+                side_a[...], side_b[start:start + chunk, :], NT, preferred_element_type=jnp.float32)
+            for col in range(0, chunk, 128):
+                den = e1_buf[...] + e2[:, start + col:start + col + 128] - shift
+                inv = pl.reciprocal(den, approx=True)
+                neg = inv * (den * inv - 2.0)
+                out_buf[slot, :, start + col:start + col + 128] = (
+                    c[:, col:col + 128] * neg).astype(jnp.bfloat16)
         out_copy(p, slot).start()
         return carry
 
@@ -170,34 +174,36 @@
     )(*operands)
 
 
-def set_kernel(n_arrays, n_skip, table_ref, *rest):
+def set_kernel(n_arrays, n_skip, sizes, table_ref, *rest):
     arrays = rest[:n_arrays]
-    out_ref, held, in_sems, out_sems = rest[n_arrays + n_skip:]
-    count = out_ref.shape[0]
-    for j in range(count):
+    outs = rest[n_arrays + n_skip:-3]
+    held, in_sems, out_sems = rest[-3:]
+    places = [(o, k) for o, size in zip(outs, sizes) for k in range(size)]
+    for j in range(len(places)):
         for k, a in enumerate(arrays):
             @pl.when(table_ref[0, j] == k)
             def _():
                 pltpu.make_async_copy(a.at[table_ref[1, j]], held.at[j], in_sems.at[j]).start()
-    for j in range(count):
+    for j, (o, k) in enumerate(places):
         pltpu.make_async_copy(arrays[0].at[0], held.at[j], in_sems.at[j]).wait()
-        pltpu.make_async_copy(held.at[j], out_ref.at[j], out_sems.at[j]).start()
-    for j in range(count):
-        pltpu.make_async_copy(held.at[j], out_ref.at[j], out_sems.at[j]).wait()
+        pltpu.make_async_copy(held.at[j], o.at[k], out_sems.at[j]).start()
+    for j, (o, k) in enumerate(places):
+        pltpu.make_async_copy(held.at[j], o.at[k], out_sems.at[j]).wait()
 
 
 ANY_SPEC = pl.BlockSpec(memory_space=pl.ANY)
 
 
-def copy_sets(which, index, arrays, after=()):
+def copy_sets(which, index, arrays, after=(), sizes=None):
     n = len(index)
+    sizes = sizes or [n]
     table = jnp.stack([jnp.stack([jnp.asarray(w, jnp.int32) for w in which]), jnp.stack(index)])
     block = arrays[0].shape[1:]
-    return pl.pallas_call(
-        functools.partial(set_kernel, len(arrays), len(after)),
-        out_shape=jax.ShapeDtypeStruct((n,) + block, arrays[0].dtype),
+    outs = pl.pallas_call(
+        functools.partial(set_kernel, len(arrays), len(after), sizes),
+        out_shape=[jax.ShapeDtypeStruct((size,) + block, arrays[0].dtype) for size in sizes],
         in_specs=[pl.BlockSpec(memory_space=pltpu.SMEM)] + [ANY_SPEC] * (len(arrays) + len(after)),
-        out_specs=ANY_SPEC,
+        out_specs=[ANY_SPEC] * len(sizes),
         scratch_shapes=[
             pltpu.VMEM((n,) + block, arrays[0].dtype),
             pltpu.SemaphoreType.DMA((n,)),
@@ -206,6 +212,7 @@
         compiler_params=pltpu.CompilerParams(vmem_limit_bytes=VMEM_LIMIT),
         name="copy_sets",
     )(table, *arrays, *after)
+    return outs if len(sizes) > 1 else outs[0]
 
 
 def extend_kernel(wins, blocks_ref, energy_ref, out_ref, held, in_sems, out_sems):
@@ -390,10 +397,10 @@
         else:
             sends_down = z == 1
             source = jnp.where(sends_down, 2 * last + y, y)
-            from_set = [1 - sends_down.astype(i32)] * 2
+            from_set = [1 - sends_down.astype(i32)] * 4
             perm = [(2, 0), (3, 1), (2 * (last - 1), 2 * last), (2 * (last - 1) + 1, 2 * last + 1)]
-            load_over = copy_sets(from_set, two_for(far_opp, source), [downs[d], ups[d]], [out])
-            load_own = copy_sets(from_set, two_for(far_own, source), [downs[d], ups[d]], [load_over])
+            load_over, load_own = copy_sets(
+                from_set, two_for(far_opp, source) + two_for(far_own, source), [downs[d], ups[d]], [out], [2, 2])
             far_b = lax.ppermute(across_y(load_over), "orb", perm)
             far_a = lax.ppermute(load_own, "orb", perm)
             first = [load_own]
@@ -408,12 +415,13 @@
 
             def both_ways(table):
                 return two_for(table, jnp.where(is_up == 1, s_up, s_down))
-        theirs = copy_sets(place_of, both_ways(want_opp), [downs[d], ups[d]], first)
         if d == 1:
+            theirs = copy_sets(place_of, both_ways(want_opp), [downs[d], ups[d]])
             sets[0] = [opp, with_other(downs[1]), with_other(ups[1]), (stored, local_other)]
             out = pairs_at(0, [theirs], out)
         else:
-            mine = copy_sets(place_of, both_ways(want), [downs[d], ups[d]], [theirs])
+            theirs, mine = copy_sets(
+                place_of * 2, both_ways(want_opp) + both_ways(want), [downs[d], ups[d]], first, [len(place_of)] * 2)
             sets[d - 1] = [with_other(tie(opp, first) if first else opp), with_other(mine)]
             if d + 1 == last:
                 sets[d - 1].append(with_other(far_a))

time: 214 us -> 215 us (level)
  waiting for transfers between devices: 89.1 us -> 94.6 us
  Pallas kernels: 57.6 us -> 53.1 us
    ppermute x2, waiting for transfers between devices: 33.3 us -> 25.2 us  [hop_down(): lax.ppermute(a, 'orb', [(k, k - 2) for k in range(2, orb_count) if k // 2...]
    ppermute x5, waiting for transfers between devices: 33.7 us -> 39.8 us  [across_y(): return lax.ppermute(a, 'orb', swap_y)]
    ppermute x1, waiting for transfers between devices: 16.6 us -> 22.4 us  [per_device(): far_a = lax.ppermute(load_own, 'orb', perm)]
    pallas_call x6 -> x4, Pallas kernels: 17.8 us -> 13.4 us  [copy_sets(): pl.pallas_call(functools.partial(set_kernel, len(arrays), len(after), siz...]
    another operation x9 -> x4, other arithmetic: 10.7 us -> 9.22 us  [copy_sets(): jnp.stack([jnp.stack([jnp.asarray(w, jnp.int32) for w in which]), jnp.sta...]
    unnamed x40 -> x38, local copies, waits for them, and re-layouts: 9.12 us -> 9.69 us
  transfers between devices with their start and end apart: 21 -> 21, of which waited for: 8 -> 10; matrix products, arithmetic and copies ran while one was open for 13% -> 13% of each run, Pallas kernels for 21% -> 18%
where the time goes in v7:
time: 215 us; the launch traced here: 212 us
  waiting for transfers between devices  94.6 us (44%)
  Pallas kernels  53.1 us (25%)
  starting transfers between devices  27.4 us (13%)
  other arithmetic  18.4 us (9%)
  local copies, waits for them, and re-layouts  18.1 us (8%)
    ppermute x5, waiting for transfers between devices, across_y(): return lax.ppermute(a, 'orb', swap_y)  39.8 us
    pallas_call x3, Pallas kernels, run_pairs(): pl.pallas_call(functools.partial(pair_kernel, call, wins, len(sets), len(...  36.4 us
    ppermute x2, waiting for transfers between devices, hop_down(): lax.ppermute(a, 'orb', [(k, k - 2) for k in range(2, orb_count) if k // 2...  25.2 us
    ppermute x1, waiting for transfers between devices, per_device(): far_a = lax.ppermute(load_own, 'orb', perm)  22.4 us
    pallas_call x4, Pallas kernels, copy_sets(): pl.pallas_call(functools.partial(set_kernel, len(arrays), len(after), siz...  13.4 us
    unnamed x38, local copies, waits for them, and re-layouts  9.69 us
    another operation x4, other arithmetic, copy_sets(): jnp.stack([jnp.stack([jnp.asarray(w, jnp.int32) for w in which]), jnp.sta...  9.22 us
    ppermute x2, starting transfers between devices, hop_up(): lax.ppermute(a, 'orb', [(k, k + 2) for k in range(orb_count - 2) if k //...  8.42 us
  transfers between devices with their start and end apart: 21, of which 10 were waited for; matrix products, arithmetic and copies ran while one was open for 13% of the time, Pallas kernels for 18%

profile of v7, /device:TPU:0, one launch (start us, length us, event | category | flops | bytes accessed | tf_op | source)
XLA Modules:
  0.0 212.0 jit_solution(10857463724264875879)
XLA Ops:
  0.0 3.4 %extend.1.refs_1_.rest_0_.own_ref.rest_6_ = bf16[4,592,512]{2,1,0:T(8,128)(2,1)} custom-call(bf16[4,576,512]{2,1,0:T(8,128)(2,1)} %blocks_ref.1, bf16[4,576]{1,0:T(4,128)(2,1)} %energy_ref.1), custom_call_target="tpu_custom_call" | custom-call | tf_op jit(solution)/shard_map/extend/pallas_call | solution.py:244
  3.4 6.4 %collective-permute-start.6 = (bf16[4,592,512]{2,1,0:T(8,128)(2,1)}, bf16[4,592,512]{2,1,0:T(8,128)(2,1)}, u32[]{:S(2)}, u32[]{:S(2)}) collective-permute-start(bf16[4,592,512]{2,1,0:T(8,128)(2,1)} %extend.1.refs_1_.rest_0_.own_ref.rest_6_), channel_id=1, source_target_pairs={{0,4},{2,6},{4,8},{6,10},{8,12},{10,14},{1,5},{3,7},{5,9},{7,11},{... | collective-permute-start | bytes 7274504 | tf_op jit(solution)/shard_map/ppermute | solution.py:299
  9.7 1.3 collective-permute-start.2
  11.4 0.6 convert_element_type.33.refs_0_
  12.0 1.5 collective-permute-start.1
  13.6 2.0 collective-permute-done.1
  15.8 0.7 fusion.7
  16.5 0.6 fusion.8
  17.1 1.4 add_bitcast_fusion.1
  18.5 0.6 stack.100.table_ref
  19.1 2.8 %copy_sets.4.refs_1_ = bf16[2,592,512]{2,1,0:T(8,128)(2,1)} custom-call(s32[2,2]{1,0:T(2,128)} %stack.100.table_ref, bf16[4,592,512]{2,1,0:T(8,128)(2,1)} %extend.1.refs_1_.rest_0_.own_ref.rest_6_), custom_call_target="tpu_custom_call" | custom-call | tf_op jit(solution)/shard_map/copy_sets/pallas_call | solution.py:202
  21.9 1.6 collective-permute-start.3
  24.2 0.6 stack.94.refs_4_.meta_ref
  24.8 25.6 %collective-permute-done.3.rest_0_ = bf16[2,592,512]{2,1,0:T(8,128)(2,1)} collective-permute-done((bf16[2,592,512]{2,1,0:T(8,128)(2,1)}, bf16[2,592,512]{2,1,0:T(8,128)(2,1)}, u32[]{:S(2)}, u32[]{:S(2)}) %collective-permute-start.3) | collective-permute-done | bytes 1212448 | tf_op jit(solution)/shard_map/ppermute | solution.py:290
  50.4 5.7 %fusion.refs_3_.pick_ref = bf16[16,2,512,256]{3,2,1,0:T(8,128)(2,1)} fusion(s32[16,2,512]{2,1,0:T(2,128)S(1)} %dynamic-slice_add_fusion), kind=kLoop, calls=%fused_computation.1 | loop fusion | flops 8388608 | bytes 8454144 | tf_op jit(solution)/shard_map/convert_element_type | solution.py:366
  56.6 4.9 %collective-permute-start.8 = (s32[2,32]{1,0:T(2,128)}, s32[2,32]{1,0:T(2,128)S(1)}, u32[]{:S(2)}, u32[]{:S(2)}) collective-permute-start(s32[2,32]{1,0:T(2,128)} %tie.10), channel_id=1, source_target_pairs={{0,4},{2,6},{14,10},{12,8},{1,5},{3,7},{15,11},{13,9},{16,20},{18,... | collective-permute-start | bytes 776 | tf_op jit(solution)/shard_map/ppermute | solution.py:386
  61.6 2.4 %add_bitcast_fusion.3 = s32[1,4]{1,0:T(1,128)S(1)} fusion(s32[1]{0:T(128)} %get-tuple-element.39, s32[1]{0:T(128)} %get-tuple-element.35, s32[1]{0:T(128)} %get-tuple-element.38, s32[1]{0:T(128)} %get-tuple-element.34), kind=kLoop, calls=%fused_computation.60 | loop fusion | flops 12 | bytes 32 | tf_op jit(solution)/shard_map/stack | solution.py:200
  64.0 2.0 collective-permute-done.2.refs_0_
  66.0 1.5 copy-done
  67.5 1.0 copy-done.1
  68.6 1.4 collective-permute-start.5
  70.4 2.1 collective-permute-start.7
  73.1 3.4 %copy_sets.5.rest_8_ = bf16[4,592,512]{2,1,0:T(8,128)(2,1)} custom-call(s32[2,4]{1,0:T(2,128)} %pad_add_fusion.1.table_ref, bf16[4,592,512]{2,1,0:T(8,128)(2,1)} %tie.8.rest_0_.rest_2_, bf16[4,592,512]{2,1,0:T(8,128)(2,1)} %tie.9.rest_1_.rest_4_), custom_call_target="tpu_custom_call" | custom-call | tf_op jit(solution)/shard_map/copy_sets/pallas_call | solution.py:202
  76.5 1.6 collective-permute-start.12
  78.9 0.6 dynamic_slice.61
  82.6 0.6 dynamic_slice.67
  83.2 4.8 %add_bitcast_fusion = (s32[1,4]{1,0:T(1,128)S(1)}, s32[1,4]{1,0:T(1,128)S(1)}) fusion(s32[1]{0:T(128)} %dynamic_slice.62, s32[1]{0:T(128)} %dynamic_slice.61, s32[1]{0:T(128)} %get-tuple-element.41, s32[1]{0:T(128)} %get-tuple-element.37, s32[1]{0:T(128)} %dynamic_slice.68, s32[1]{0:T(128)} %dynamic_slice.67, s32[1]{0:T(128)} %dynamic_slice.66, ...), kind=kLoop, calls=%fused_computation.57 | loop fusion | flops 24 | bytes 64 | tf_op jit(solution)/shard_map/stack | solution.py:200
  88.5 0.9 broadcast_in_dim.140.ve1_ref
  89.5 13.1 %pairs_0.1.rest_2_.rest_7_ = bf16[16,512,512]{2,1,0:T(8,128)(2,1)} custom-call(s32[5,16]{1,0:T(8,128)} %stack.94.refs_4_.meta_ref, f32[16]{0:T(128)} %add.80.shift_ref, bf16[2,576,128]{2,1,0:T(8,128)(2,1)} %broadcast_in_dim.140.ve1_ref, bf16[16,2,512,256]{3,2,1,0:T(8,128)(2,1)} %fusion.refs_3_.pick_ref, ...), custom_call_target="tpu_custom_call" | custom-call | tf_op jit(solution)/shard_map/pairs_0/pallas_call | solution.py:152
  102.6 23.2 %collective-permute-done.5.rest_0_ = bf16[4,592,512]{2,1,0:T(8,128)(2,1)} collective-permute-done((bf16[4,592,512]{2,1,0:T(8,128)(2,1)}, bf16[4,592,512]{2,1,0:T(8,128)(2,1)}, u32[]{:S(2)}, u32[]{:S(2)}) %collective-permute-start.5) | collective-permute-done | bytes 2424864 | tf_op jit(solution)/shard_map/ppermute | solution.py:296
  125.8 3.9 %copy_sets.6 = (bf16[2,592,512]{2,1,0:T(8,128)(2,1)}, bf16[2,592,512]{2,1,0:T(8,128)(2,1)}) custom-call(s32[2,4]{1,0:T(2,128)} %stack.106.table_ref, bf16[4,592,512]{2,1,0:T(8,128)(2,1)} %collective-permute-done.5.rest_0_, bf16[4,592,512]{2,1,0:T(8,128)(2,1)} %collective-permute-done.7.rest_1_, bf16[16,512,512]{2,1,0:T(8,128)(2,1)} %pairs_0.1.rest_2_.rest_7_), custom_call_target="tpu_custom_call" | custom-call | tf_op jit(solution)/shard_map/copy_sets/pallas_call | solution.py:202
  129.8 1.4 collective-permute-start.15
  131.5 1.4 copy-done.2
  132.9 1.5 collective-permute-start.18
  135.0 3.3 %copy_sets.7 = (bf16[2,592,512]{2,1,0:T(8,128)(2,1)}, bf16[2,592,512]{2,1,0:T(8,128)(2,1)}) custom-call(s32[2,4]{1,0:T(2,128)} %stack.97.table_ref, bf16[4,592,512]{2,1,0:T(8,128)(2,1)} %collective-permute-done.5.rest_0_, bf16[4,592,512]{2,1,0:T(8,128)(2,1)} %collective-permute-done.7.rest_1_, bf16[2,592,512]{2,1,0:T(8,128)(2,1)} %get-tuple-element.9.rest_2_.refs_1_), custom_call_target="tpu_custom_call" | custom-call | tf_op jit(solution)/shard_map/copy_sets/pallas_call | solution.py:202
  138.5 22.4 %collective-permute-done.15.rest_4_ = bf16[2,592,512]{2,1,0:T(8,128)(2,1)} collective-permute-done((bf16[2,592,512]{2,1,0:T(8,128)(2,1)}, bf16[2,592,512]{2,1,0:T(8,128)(2,1)}, u32[]{:S(2)}, u32[]{:S(2)}) %collective-permute-start.15) | collective-permute-done | bytes 1212448 | tf_op jit(solution)/shard_map/ppermute | solution.py:405
  161.0 1.6 collective-permute-start.11
  162.6 1.3 collective-permute-start.19
  164.1 0.8 copy-done.6
  165.3 1.4 copy-done.5
  166.7 11.6 %pairs_1.1.refs_1_.rest_4_ = bf16[16,512,512]{2,1,0:T(8,128)(2,1)} custom-call(s32[5,16]{1,0:T(8,128)} %stack.94.refs_4_.meta_ref, f32[16]{0:T(128)} %add.80.shift_ref, bf16[2,576,128]{2,1,0:T(8,128)(2,1)} %broadcast_in_dim.140.ve1_ref, bf16[16,2,512,256]{3,2,1,0:T(8,128)(2,1)} %fusion.refs_3_.pick_ref, ...), custom_call_target="tpu_custom_call", output_to_operand_aliasing={{}: (13, {})} | custom-call | tf_op jit(solution)/shard_map/pairs_1/pallas_call | solution.py:152
  178.4 11.9 %collective-permute-done.11.refs_0_ = bf16[2,592,512]{2,1,0:T(8,128)(2,1)S(1)} collective-permute-done((bf16[2,592,512]{2,1,0:T(8,128)(2,1)}, bf16[2,592,512]{2,1,0:T(8,128)(2,1)S(1)}, u32[]{:S(2)}, u32[]{:S(2)}) %collective-permute-start.11) | collective-permute-done | bytes 1212448 | tf_op jit(solution)/shard_map/ppermute | solution.py:290
  190.3 1.0 copy-done.4
  191.3 3.9 %collective-permute-done.19.refs_0_ = bf16[2,592,512]{2,1,0:T(8,128)(2,1)S(1)} collective-permute-done((bf16[2,592,512]{2,1,0:T(8,128)(2,1)}, bf16[2,592,512]{2,1,0:T(8,128)(2,1)S(1)}, u32[]{:S(2)}, u32[]{:S(2)}) %collective-permute-start.19) | collective-permute-done | bytes 1212448 | tf_op jit(solution)/shard_map/ppermute | solution.py:404
  195.3 1.0 copy-done.3
  196.3 3.1 %collective-permute-done.20.rest_3_ = bf16[2,592,512]{2,1,0:T(8,128)(2,1)S(1)} collective-permute-done((bf16[2,592,512]{2,1,0:T(8,128)(2,1)}, bf16[2,592,512]{2,1,0:T(8,128)(2,1)S(1)}, u32[]{:S(2)}, u32[]{:S(2)}) %collective-permute-start.20) | collective-permute-done | bytes 1212448 | tf_op jit(solution)/shard_map/ppermute | solution.py:293
  199.4 1.0 copy-done.9
  200.4 11.6 %pairs_2.1 = bf16[16,512,512]{2,1,0:T(8,128)(2,1)} custom-call(s32[5,16]{1,0:T(8,128)} %stack.94.refs_4_.meta_ref, f32[16]{0:T(128)} %add.80.shift_ref, bf16[2,576,128]{2,1,0:T(8,128)(2,1)} %broadcast_in_dim.140.ve1_ref, bf16[16,2,512,256]{3,2,1,0:T(8,128)(2,1)} %fusion.refs_3_.pick_ref, ...), custom_call_target="tpu_custom_call", output_to_operand_aliasing={{}: (10, {})} | custom-call | tf_op jit(solution)/shard_map/pairs_2/pallas_call | solution.py:152
  (97 shorter events, 9.1 us)
Async XLA Ops:
  0.0 11.1 %copy-start.14 = (s32[32,2]{0,1:T(2,128)S(1)}, s32[32,2]{0,1:T(2,128)}, u32[]{:S(2)}) copy-start(s32[32,2]{0,1:T(2,128)} %param.10) | copy-start | bytes 772
  0.0 11.1 %copy-start.18 = (s32[32]{0:T(128)S(1)}, s32[32]{0:T(128)}, u32[]{:S(2)}) copy-start(s32[32]{0:T(128)} %param.9) | copy-start | bytes 388
  3.4 66.6 %collective-permute-start.6 = (bf16[4,592,512]{2,1,0:T(8,128)(2,1)}, bf16[4,592,512]{2,1,0:T(8,128)(2,1)}, u32[]{:S(2)}, u32[]{:S(2)}) collective-permute-start(bf16[4,592,512]{2,1,0:T(8,128)(2,1)} %extend.1.refs_1_.rest_0_.own_ref.rest_6_), channel_id=1, source_target_pairs={{0,4},{2,6},{4,8},{6,10},{8,12},{10,14},{1,5},{3,7},{5,9},{7,11},{... | collective-permute-start | bytes 7274504 | tf_op jit(solution)/shard_map/ppermute | solution.py:299
  9.7 56.3 %collective-permute-start.2 = (bf16[4,592,512]{2,1,0:T(8,128)(2,1)}, bf16[4,592,512]{2,1,0:T(8,128)(2,1)}, u32[]{:S(2)}, u32[]{:S(2)}) collective-permute-start(bf16[4,592,512]{2,1,0:T(8,128)(2,1)} %extend.1.refs_1_.rest_0_.own_ref.rest_6_), channel_id=1, source_target_pairs={{4,0},{6,2},{8,4},{10,6},{12,8},{14,10},{5,1},{7,3},{9,5},{11,7},{... | collective-permute-start | bytes 7274504 | tf_op jit(solution)/shard_map/ppermute | solution.py:296
  11.0 55.0 %collective-permute-start = (bf16[4,592,512]{2,1,0:T(8,128)(2,1)}, bf16[4,592,512]{2,1,0:T(8,128)(2,1)S(1)}, u32[]{:S(2)}, u32[]{:S(2)}) collective-permute-start(bf16[4,592,512]{2,1,0:T(8,128)(2,1)} %extend.1.refs_1_.rest_0_.own_ref.rest_6_), channel_id=1, source_target_pairs={{0,1},{1,0},{2,3},{3,2},{4,5},{5,4},{6,7},{7,6},{8,9},{9,8},{10,11... | collective-permute-start | bytes 7274504 | tf_op jit(solution)/shard_map/ppermute | solution.py:293
  12.0 38.4 %copy-start.10 = (s32[32,2,512]{2,1,0:T(2,128)S(1)}, s32[32,2,512]{2,1,0:T(2,128)}, u32[]{:S(2)}) copy-start(s32[32,2,512]{2,1,0:T(2,128)} %param.11) | copy-start | bytes 393220
  12.0 38.4 %copy-start.12 = (s32[512]{0:T(512)S(1)}, s32[512]{0:T(512)}, u32[]{:S(2)}) copy-start(s32[512]{0:T(512)} %constant.141.clone.1) | copy-start | bytes 6148
  12.0 3.6 %collective-permute-start.1 = (s32[32]{0:T(128)}, s32[32]{0:T(128)S(1)}, u32[]{:S(2)}, u32[]{:S(2)}) collective-permute-start(s32[32]{0:T(128)} %tie.7), channel_id=1, source_target_pairs={{0,2},{2,0},{4,6},{6,4},{8,10},{10,8},{12,14},{14,12},{1,3},{3,1},... | collective-permute-start | bytes 392 | tf_op jit(solution)/shard_map/ppermute | solution.py:290
  21.9 28.4 %collective-permute-start.3 = (bf16[2,592,512]{2,1,0:T(8,128)(2,1)}, bf16[2,592,512]{2,1,0:T(8,128)(2,1)}, u32[]{:S(2)}, u32[]{:S(2)}) collective-permute-start(bf16[2,592,512]{2,1,0:T(8,128)(2,1)} %copy_sets.4.refs_1_), channel_id=1, source_target_pairs={{0,2},{2,0},{4,6},{6,4},{8,10},{10,8},{12,14},{14,12},{1,3},{3,1},... | collective-permute-start | bytes 3637256 | tf_op jit(solution)/shard_map/ppermute | solution.py:290
  50.4 15.7 %collective-permute-start.4 = (bf16[2,592,512]{2,1,0:T(8,128)(2,1)}, bf16[2,592,512]{2,1,0:T(8,128)(2,1)S(1)}, u32[]{:S(2)}, u32[]{:S(2)}) collective-permute-start(bf16[2,592,512]{2,1,0:T(8,128)(2,1)} %collective-permute-done.3.rest_0_), channel_id=1, source_target_pairs={{0,1},{1,0},{2,3},{3,2},{4,5},{5,4},{6,7},{7,6},{8,9},{9,8},{10,11... | collective-permute-start | bytes 3637256 | tf_op jit(solution)/shard_map/ppermute | solution.py:293
  50.4 5.7 %copy-start.13 = (s32[32]{0:T(128)S(1)}, s32[32]{0:T(128)}, u32[]{:S(2)}) copy-start(s32[32]{0:T(128)} %tie.7) | copy-start | bytes 388
  56.6 19.9 %collective-permute-start.8 = (s32[2,32]{1,0:T(2,128)}, s32[2,32]{1,0:T(2,128)S(1)}, u32[]{:S(2)}, u32[]{:S(2)}) collective-permute-start(s32[2,32]{1,0:T(2,128)} %tie.10), channel_id=1, source_target_pairs={{0,4},{2,6},{14,10},{12,8},{1,5},{3,7},{15,11},{13,9},{16,20},{18,... | collective-permute-start | bytes 776 | tf_op jit(solution)/shard_map/ppermute | solution.py:386
  66.0 1.5 copy-start
  67.5 1.0 copy-start.1
  68.6 4.0 %copy-start.16 = (s32[1,4]{1,0:T(1,128)S(1)}, s32[1,4]{1,0:T(1,128)}, u32[]{:S(2)}) copy-start(s32[1,4]{1,0:T(1,128)} %constant.147.clone.1) | copy-start | bytes 52
  68.6 20.0 %collective-permute-start.9 = (bf16[4,592,512]{2,1,0:T(8,128)(2,1)}, bf16[4,592,512]{2,1,0:T(8,128)(2,1)}, u32[]{:S(2)}, u32[]{:S(2)}) collective-permute-start(bf16[4,592,512]{2,1,0:T(8,128)(2,1)} %tie.8.rest_0_.rest_2_), channel_id=1, source_target_pairs={{0,1},{1,0},{2,3},{3,2},{4,5},{5,4},{6,7},{7,6},{8,9},{9,8},{10,11... | collective-permute-start | bytes 7274504 | tf_op jit(solution)/shard_map/ppermute | solution.py:293
  68.6 57.3 %collective-permute-start.5 = (bf16[4,592,512]{2,1,0:T(8,128)(2,1)}, bf16[4,592,512]{2,1,0:T(8,128)(2,1)}, u32[]{:S(2)}, u32[]{:S(2)}) collective-permute-start(bf16[4,592,512]{2,1,0:T(8,128)(2,1)} %tie.8.rest_0_.rest_2_), channel_id=1, source_target_pairs={{4,0},{6,2},{8,4},{10,6},{5,1},{7,3},{9,5},{11,7},{20,16},{22,18},... | collective-permute-start | bytes 7274504 | tf_op jit(solution)/shard_map/ppermute | solution.py:296
  70.0 18.5 %collective-permute-start.10 = (bf16[4,592,512]{2,1,0:T(8,128)(2,1)}, bf16[4,592,512]{2,1,0:T(8,128)(2,1)}, u32[]{:S(2)}, u32[]{:S(2)}) collective-permute-start(bf16[4,592,512]{2,1,0:T(8,128)(2,1)} %tie.9.rest_1_.rest_4_), channel_id=1, source_target_pairs={{0,1},{1,0},{2,3},{3,2},{4,5},{5,4},{6,7},{7,6},{8,9},{9,8},{10,11... | collective-permute-start | bytes 7274504 | tf_op jit(solution)/shard_map/ppermute | solution.py:293
  70.4 55.4 %collective-permute-start.7 = (bf16[4,592,512]{2,1,0:T(8,128)(2,1)}, bf16[4,592,512]{2,1,0:T(8,128)(2,1)}, u32[]{:S(2)}, u32[]{:S(2)}) collective-permute-start(bf16[4,592,512]{2,1,0:T(8,128)(2,1)} %tie.9.rest_1_.rest_4_), channel_id=1, source_target_pairs={{4,8},{6,10},{8,12},{10,14},{5,9},{7,11},{9,13},{11,15},{20,24},{2... | collective-permute-start | bytes 7274504 | tf_op jit(solution)/shard_map/ppermute | solution.py:299
  73.1 6.5 %copy-start.15 = (f32[32]{0:T(128)S(1)}, f32[32]{0:T(128)}, u32[]{:S(2)}) copy-start(f32[32]{0:T(128)} %param.8) | copy-start | bytes 388
  73.1 7.2 %copy-start.11 = (bf16[4,576]{1,0:T(4,128)(2,1)S(1)}, bf16[4,576]{1,0:T(4,128)(2,1)}, u32[]{:S(2)}) copy-start(bf16[4,576]{1,0:T(4,128)(2,1)} %energy_ref.1) | copy-start | bytes 13828
  76.5 55.0 %collective-permute-start.12 = (bf16[4,592,512]{2,1,0:T(8,128)(2,1)}, bf16[4,592,512]{2,1,0:T(8,128)(2,1)S(1)}, u32[]{:S(2)}, u32[]{:S(2)}) collective-permute-start(bf16[4,592,512]{2,1,0:T(8,128)(2,1)} %copy_sets.5.rest_8_), channel_id=1, source_target_pairs={{0,2},{2,0},{4,6},{6,4},{8,10},{10,8},{12,14},{14,12},{1,3},{3,1},... | collective-permute-start | bytes 7274504 | tf_op jit(solution)/shard_map/ppermute | solution.py:290
  129.7 3.2 %copy-start.17 = (bf16[2,592,512]{2,1,0:T(8,128)(2,1)S(1)}, bf16[2,592,512]{2,1,0:T(8,128)(2,1)}, u32[]{:S(2)}) copy-start(bf16[2,592,512]{2,1,0:T(8,128)(2,1)} %get-tuple-element.12) | copy-start | bytes 3637252
  129.8 31.2 %collective-permute-start.15 = (bf16[2,592,512]{2,1,0:T(8,128)(2,1)}, bf16[2,592,512]{2,1,0:T(8,128)(2,1)}, u32[]{:S(2)}, u32[]{:S(2)}) collective-permute-start(bf16[2,592,512]{2,1,0:T(8,128)(2,1)} %get-tuple-element.9.rest_2_.refs_1_), channel_id=1, source_target_pairs={{4,0},{6,2},{8,12},{10,14},{5,1},{7,3},{9,13},{11,15},{20,16},{22,... | collective-permute-start | bytes 3637256 | tf_op jit(solution)/shard_map/ppermute | solution.py:405
  131.5 1.4 copy-start.2
  132.9 31.2 %collective-permute-start.13 = (bf16[4,592,512]{2,1,0:T(8,128)(2,1)}, bf16[4,592,512]{2,1,0:T(8,128)(2,1)S(1)}, u32[]{:S(2)}, u32[]{:S(2)}) collective-permute-start(bf16[4,592,512]{2,1,0:T(8,128)(2,1)} %tie.11.rest_0_), channel_id=1, source_target_pairs={{0,1},{1,0},{2,3},{3,2},{4,5},{5,4},{6,7},{7,6},{8,9},{9,8},{10,11... | collective-permute-start | bytes 7274504 | tf_op jit(solution)/shard_map/ppermute | solution.py:293
  132.9 29.7 %collective-permute-start.18 = (bf16[2,592,512]{2,1,0:T(8,128)(2,1)S(1)}, bf16[2,592,512]{2,1,0:T(8,128)(2,1)}, u32[]{:S(2)}, u32[]{:S(2)}) collective-permute-start(bf16[2,592,512]{2,1,0:T(8,128)(2,1)S(1)} %copy-done.17), channel_id=1, source_target_pairs={{0,2},{2,0},{4,6},{6,4},{8,10},{10,8},{12,14},{14,12},{1,3},{3,1},... | collective-permute-start | bytes 3637256 | tf_op jit(solution)/shard_map/ppermute | solution.py:290
  138.2 25.7 %collective-permute-start.14 = (bf16[2,592,512]{2,1,0:T(8,128)(2,1)}, bf16[2,592,512]{2,1,0:T(8,128)(2,1)S(1)}, u32[]{:S(2)}, u32[]{:S(2)}) collective-permute-start(bf16[2,592,512]{2,1,0:T(8,128)(2,1)} %get-tuple-element.11.rest_2_.rest_6_), channel_id=1, source_target_pairs={{0,1},{1,0},{2,3},{3,2},{4,5},{5,4},{6,7},{7,6},{8,9},{9,8},{10,11... | collective-permute-start | bytes 3637256 | tf_op jit(solution)/shard_map/ppermute | solution.py:293
  161.0 3.1 %collective-permute-start.16 = (bf16[2,592,512]{2,1,0:T(8,128)(2,1)}, bf16[2,592,512]{2,1,0:T(8,128)(2,1)S(1)}, u32[]{:S(2)}, u32[]{:S(2)}) collective-permute-start(bf16[2,592,512]{2,1,0:T(8,128)(2,1)} %collective-permute-done.15.rest_4_), channel_id=1, source_target_pairs={{0,1},{1,0},{2,3},{3,2},{4,5},{5,4},{6,7},{7,6},{8,9},{9,8},{10,11... | collective-permute-start | bytes 3637256 | tf_op jit(solution)/shard_map/ppermute | solution.py:293
  161.0 29.3 %collective-permute-start.11 = (bf16[2,592,512]{2,1,0:T(8,128)(2,1)}, bf16[2,592,512]{2,1,0:T(8,128)(2,1)S(1)}, u32[]{:S(2)}, u32[]{:S(2)}) collective-permute-start(bf16[2,592,512]{2,1,0:T(8,128)(2,1)} %get-tuple-element.10), channel_id=1, source_target_pairs={{0,2},{2,0},{4,6},{6,4},{8,10},{10,8},{12,14},{14,12},{1,3},{3,1},... | collective-permute-start | bytes 3637256 | tf_op jit(solution)/shard_map/ppermute | solution.py:290
  162.6 32.6 %collective-permute-start.19 = (bf16[2,592,512]{2,1,0:T(8,128)(2,1)}, bf16[2,592,512]{2,1,0:T(8,128)(2,1)S(1)}, u32[]{:S(2)}, u32[]{:S(2)}) collective-permute-start(bf16[2,592,512]{2,1,0:T(8,128)(2,1)} %collective-permute-done.18), channel_id=1, source_target_pairs={{4,0},{6,2},{8,12},{10,14},{5,1},{7,3},{9,13},{11,15},{20,16},{22,... | collective-permute-start | bytes 3637256 | tf_op jit(solution)/shard_map/ppermute | solution.py:404
  163.9 1.0 copy-start.6
  164.1 1.2 copy-start.7
  165.3 1.4 copy-start.5
  190.3 1.0 copy-start.4
  191.3 5.0 %collective-permute-start.17 = (bf16[2,592,512]{2,1,0:T(8,128)(2,1)}, bf16[2,592,512]{2,1,0:T(8,128)(2,1)S(1)}, u32[]{:S(2)}, u32[]{:S(2)}) collective-permute-start(bf16[2,592,512]{2,1,0:T(8,128)(2,1)} %tie.12.rest_0_), channel_id=1, source_target_pairs={{0,1},{1,0},{2,3},{3,2},{4,5},{5,4},{6,7},{7,6},{8,9},{9,8},{10,11... | collective-permute-start | bytes 3637256 | tf_op jit(solution)/shard_map/ppermute | solution.py:293
  195.2 1.0 copy-start.3
  196.3 3.1 %collective-permute-start.20 = (bf16[2,592,512]{2,1,0:T(8,128)(2,1)}, bf16[2,592,512]{2,1,0:T(8,128)(2,1)S(1)}, u32[]{:S(2)}, u32[]{:S(2)}) collective-permute-start(bf16[2,592,512]{2,1,0:T(8,128)(2,1)} %tie.13.rest_2_), channel_id=1, source_target_pairs={{0,1},{1,0},{2,3},{3,2},{4,5},{5,4},{6,7},{7,6},{8,9},{9,8},{10,11... | collective-permute-start | bytes 3637256 | tf_op jit(solution)/shard_map/ppermute | solution.py:293
  196.3 3.1 %copy-start.8 = (bf16[2,592,512]{2,1,0:T(8,128)(2,1)}, bf16[2,592,512]{2,1,0:T(8,128)(2,1)S(1)}, u32[]{:S(2)}) copy-start(bf16[2,592,512]{2,1,0:T(8,128)(2,1)S(1)} %collective-permute-done.17.rest_1_) | copy-start | bytes 3637252
  199.4 1.0 copy-start.9

commit v8 on v7

--- a/solution.py
+++ b/solution.py
@@ -381,13 +381,24 @@
 
     y_load = copy_sets([0, 0], two_for(want_opp, o), [stored])
     opp = with_other(across_y(y_load))
-    top = orb_count - 1
-    tell = [(0, 2), (1, 3), (top, top - 2), (top - 1, top - 3)]
-    wanted_far = lax.ppermute(tie(wanted_both, [y_load]), "orb", tell).reshape(2, orb_count, occ_dev) > 0
-    far_own, far_opp = two_of(wanted_far[0]), two_of(wanted_far[1])
-    early = [opp[1], local_other, pick, meta]
+    told = tie(wanted_both, [y_load])
+
+    def tell(at_first_end, at_last_end):
+        perm = [(c, 2 * at_first_end + c) for c in range(2)]
+        perm += [(2 * last + c, 2 * at_last_end + c) for c in range(2)]
+        return lax.ppermute(told, "orb", perm).reshape(2, orb_count, occ_dev) > 0
+
+    far_opp = two_of(tell(last - 1, 1)[1])
+    far_own = two_of(tell(1, last - 1)[0])
+    over = None
+    early = [opp[1], local_other, pick, meta, far_own[0], far_opp[0]]
     downs[1], ups[1] = tie(downs[1], early), tie(ups[1], early)
     out = None
+
+    def far_perm(left):
+        down = [(2 * (left + 1) + c, 2 * left + c) for c in range(2)]
+        return down + [(2 * (last - left - 1) + c, 2 * (last - left) + c) for c in range(2)]
+
     for d in range(1, last):
         s_down, s_up = o + 2 * d, o - 2 * d
         first = []
@@ -397,13 +408,10 @@
         else:
             sends_down = z == 1
             source = jnp.where(sends_down, 2 * last + y, y)
-            from_set = [1 - sends_down.astype(i32)] * 4
-            perm = [(2, 0), (3, 1), (2 * (last - 1), 2 * last), (2 * (last - 1) + 1, 2 * last + 1)]
-            load_over, load_own = copy_sets(
-                from_set, two_for(far_opp, source) + two_for(far_own, source), [downs[d], ups[d]], [out], [2, 2])
-            far_b = lax.ppermute(across_y(load_over), "orb", perm)
-            far_a = lax.ppermute(load_own, "orb", perm)
-            first = [load_own]
+            from_set = [1 - sends_down.astype(i32)] * 2
+            load_own = copy_sets(from_set, two_for(far_own, source), [downs[d], ups[d]])
+            far_a = lax.ppermute(load_own, "orb", far_perm(0))
+            first = [load_own, out]
         if 2 * d <= last:
             place_of = [0, 0, 1, 1]
 
@@ -415,18 +423,26 @@
 
             def both_ways(table):
                 return two_for(table, jnp.where(is_up == 1, s_up, s_down))
+        if d > 1:
+            over = lax.ppermute(tie(over, [downs[d], ups[d]]), "orb", far_perm(last - d))
         if d == 1:
-            theirs = copy_sets(place_of, both_ways(want_opp), [downs[d], ups[d]])
+            is_up = (z == 1).astype(i32)
+            load_over = copy_sets(
+                [is_up] * 2, two_for(far_opp, jnp.where(is_up == 1, y, 2 * last + y)), [downs[d], ups[d]])
+            over = across_y(load_over)
             sets[0] = [opp, with_other(downs[1]), with_other(ups[1]), (stored, local_other)]
-            out = pairs_at(0, [theirs], out)
+            theirs = copy_sets(place_of, both_ways(want_opp), [downs[d], ups[d]], [over])
+            out = pairs_at(0, [theirs] + downs[2:] + ups[2:], out)
         else:
             theirs, mine = copy_sets(
                 place_of * 2, both_ways(want_opp) + both_ways(want), [downs[d], ups[d]], first, [len(place_of)] * 2)
-            sets[d - 1] = [with_other(tie(opp, first) if first else opp), with_other(mine)]
+            sets[d - 1] = [with_other(tie(opp, [mine] + ([over] if d + 1 == last else []))), with_other(mine)]
             if d + 1 == last:
                 sets[d - 1].append(with_other(far_a))
             out = pairs_at(d - 1, [mine], out)
         opp = across_y(theirs)
+        if d + 1 == last:
+            far_b = lax.ppermute(over, "orb", far_perm(0))
     sets[last - 1] = [with_other(tie(opp, [out])), with_other(tie(far_b, [out]))]
     return pairs_at(last - 1, [], out)
 

time: 215 us -> 224 us (1.042)
  starting transfers between devices: 27.4 us -> 35 us
  waiting for transfers between devices: 94.6 us -> 89.1 us
  other arithmetic: 18.4 us -> 21.1 us
    ppermute x2, waiting for transfers between devices: 25.2 us -> 15.9 us  [hop_down(): lax.ppermute(a, 'orb', [(k, k - 2) for k in range(2, orb_count) if k // 2...]
    ppermute x3 -> x5, starting transfers between devices: 7.64 us -> 16.1 us  [the longest x2 12.8 us: tell(): return lax.ppermute(told, 'orb', perm).reshape(2, orb_count, occ_dev) > 0]
    ppermute x5, waiting for transfers between devices: 39.8 us -> 48.1 us  [across_y(): return lax.ppermute(a, 'orb', swap_y)]
    ppermute x3 -> x5, waiting for transfers between devices: 26.4 us -> 21.8 us  [the longest x1 10.1 us: per_device(): far_b = lax.ppermute(over, 'orb', far_perm(0))]
    unnamed x38 -> x48, local copies, waits for them, and re-layouts: 9.69 us -> 12 us
    pallas_call x4 -> x5, Pallas kernels: 13.4 us -> 15.5 us  [copy_sets(): pl.pallas_call(functools.partial(set_kernel, len(arrays), len(after), siz...]
    another operation x4 -> x10, other arithmetic: 9.22 us -> 11.3 us  [copy_sets(): jnp.stack([jnp.stack([jnp.asarray(w, jnp.int32) for w in which]), jnp.sta...]
    dynamic_slice x8 -> x7, local copies, waits for them, and re-layouts: 4.73 us -> 4.41 us  [idx_of(): lax.dynamic_index_in_dim(table, jnp.clip(source, 0, orb_count - 1), 0, ke...]
  transfers between devices with their start and end apart: 21 -> 23, of which waited for: 10 -> 10; matrix products, arithmetic and copies ran while one was open for 13% -> 13% of each run, Pallas kernels for 18% -> 19%
where the time goes in v8:
time: 224 us; the launch traced here: 220 us
  waiting for transfers between devices  89.1 us (40%)
  Pallas kernels  55.2 us (25%)
  starting transfers between devices  35 us (16%)
  other arithmetic  21.1 us (9%)
  local copies, waits for them, and re-layouts  19.6 us (9%)
    ppermute x5, waiting for transfers between devices, across_y(): return lax.ppermute(a, 'orb', swap_y)  48.1 us
    pallas_call x3, Pallas kernels, run_pairs(): pl.pallas_call(functools.partial(pair_kernel, call, wins, len(sets), len(...  36.4 us
    ppermute x2, waiting for transfers between devices, hop_down(): lax.ppermute(a, 'orb', [(k, k - 2) for k in range(2, orb_count) if k // 2...  15.9 us
    pallas_call x5, Pallas kernels, copy_sets(): pl.pallas_call(functools.partial(set_kernel, len(arrays), len(after), siz...  15.5 us
    ppermute x2, starting transfers between devices, tell(): return lax.ppermute(told, 'orb', perm).reshape(2, orb_count, occ_dev) > 0  12.8 us
    unnamed x48, local copies, waits for them, and re-layouts  12 us
    another operation x10, other arithmetic, copy_sets(): jnp.stack([jnp.stack([jnp.asarray(w, jnp.int32) for w in which]), jnp.sta...  11.3 us
    ppermute x1, waiting for transfers between devices, per_device(): far_b = lax.ppermute(over, 'orb', far_perm(0))  10.1 us
  transfers between devices with their start and end apart: 23, of which 10 were waited for; matrix products, arithmetic and copies ran while one was open for 13% of the time, Pallas kernels for 19%

profile of v8, /device:TPU:0, one launch (start us, length us, event | category | flops | bytes accessed | tf_op | source)
XLA Modules:
  0.0 220.4 jit_solution(3161908498126512596)
XLA Ops:
  0.0 3.4 %extend.1.refs_1_.rest_0_.own_ref.rest_6_ = bf16[4,592,512]{2,1,0:T(8,128)(2,1)} custom-call(bf16[4,576,512]{2,1,0:T(8,128)(2,1)} %blocks_ref.1, bf16[4,576]{1,0:T(4,128)(2,1)} %energy_ref.1), custom_call_target="tpu_custom_call" | custom-call | tf_op jit(solution)/shard_map/extend/pallas_call | solution.py:244
  3.9 5.9 %collective-permute-start.8 = (bf16[4,592,512]{2,1,0:T(8,128)(2,1)}, bf16[4,592,512]{2,1,0:T(8,128)(2,1)}, u32[]{:S(2)}, u32[]{:S(2)}) collective-permute-start(bf16[4,592,512]{2,1,0:T(8,128)(2,1)} %extend.1.refs_1_.rest_0_.own_ref.rest_6_), channel_id=1, source_target_pairs={{0,4},{2,6},{4,8},{6,10},{8,12},{10,14},{1,5},{3,7},{5,9},{7,11},{... | collective-permute-start | bytes 7274504 | tf_op jit(solution)/shard_map/ppermute | solution.py:299
  9.8 1.3 collective-permute-start.2
  12.0 1.5 collective-permute-start.1
  14.0 1.6 collective-permute-done.1
  16.6 1.3 add_bitcast_fusion.1
  18.5 2.8 %copy_sets.5.refs_1_ = bf16[2,592,512]{2,1,0:T(8,128)(2,1)} custom-call(s32[2,2]{1,0:T(2,128)} %stack.123.table_ref, bf16[4,592,512]{2,1,0:T(8,128)(2,1)} %extend.1.refs_1_.rest_0_.own_ref.rest_6_), custom_call_target="tpu_custom_call" | custom-call | tf_op jit(solution)/shard_map/copy_sets/pallas_call | solution.py:202
  21.3 1.8 collective-permute-start.3
  23.4 5.7 %fusion.refs_3_.pick_ref = bf16[16,2,512,256]{3,2,1,0:T(8,128)(2,1)} fusion(s32[16,2,512]{2,1,0:T(2,128)S(1)} %dynamic-slice_add_fusion), kind=kLoop, calls=%fused_computation.1 | loop fusion | flops 8388608 | bytes 8454144 | tf_op jit(solution)/shard_map/convert_element_type | solution.py:366
  29.1 20.4 %collective-permute-done.3.rest_0_ = bf16[2,592,512]{2,1,0:T(8,128)(2,1)} collective-permute-done((bf16[2,592,512]{2,1,0:T(8,128)(2,1)}, bf16[2,592,512]{2,1,0:T(8,128)(2,1)}, u32[]{:S(2)}, u32[]{:S(2)}) %collective-permute-start.3) | collective-permute-done | bytes 1212448 | tf_op jit(solution)/shard_map/ppermute | solution.py:290
  50.2 4.3 %collective-permute-start.6 = (s32[2,32]{1,0:T(2,128)}, s32[2,32]{1,0:T(2,128)S(1)}, u32[]{:S(2)}, u32[]{:S(2)}) collective-permute-start(s32[2,32]{1,0:T(2,128)} %tie.9), channel_id=1, source_target_pairs={{0,8},{2,10},{12,4},{14,6},{1,9},{3,11},{13,5},{15,7},{16,24},{18,... | collective-permute-start | bytes 776 | tf_op jit(solution)/shard_map/ppermute | solution.py:389
  55.1 6.2 %collective-permute-done.6 = s32[2,32]{1,0:T(2,128)S(1)} collective-permute-done((s32[2,32]{1,0:T(2,128)}, s32[2,32]{1,0:T(2,128)S(1)}, u32[]{:S(2)}, u32[]{:S(2)}) %collective-permute-start.6) | collective-permute-done | bytes 288 | tf_op jit(solution)/shard_map/ppermute | solution.py:389
  61.3 8.5 %collective-permute-start.5 = (s32[2,32]{1,0:T(2,128)}, s32[2,32]{1,0:T(2,128)S(1)}, u32[]{:S(2)}, u32[]{:S(2)}) collective-permute-start(s32[2,32]{1,0:T(2,128)} %tie.9), channel_id=1, source_target_pairs={{0,4},{2,6},{12,8},{14,10},{1,5},{3,7},{13,9},{15,11},{16,20},{18,... | collective-permute-start | bytes 776 | tf_op jit(solution)/shard_map/ppermute | solution.py:389
  72.2 1.5 copy-done
  74.5 1.3 collective-permute-start.7
  75.8 1.3 add_bitcast_fusion.6
  77.6 2.9 %copy_sets.7 = bf16[2,592,512]{2,1,0:T(8,128)(2,1)} custom-call(s32[2,2]{1,0:T(2,128)} %pad_add_fusion.3.table_ref, bf16[4,592,512]{2,1,0:T(8,128)(2,1)} %tie.10.rest_0_.rest_2_, bf16[4,592,512]{2,1,0:T(8,128)(2,1)} %tie.11.rest_1_.rest_4_), custom_call_target="tpu_custom_call" | custom-call | tf_op jit(solution)/shard_map/copy_sets/pallas_call | solution.py:202
  80.6 1.6 collective-permute-start.12
  82.2 2.6 %add_bitcast_fusion.4 = s32[1,4]{1,0:T(1,128)S(1)} fusion(s32[1]{0:T(128)} %get-tuple-element.40, s32[1]{0:T(128)} %get-tuple-element.29, s32[1]{0:T(128)} %get-tuple-element.41, s32[1]{0:T(128)} %get-tuple-element.28), kind=kLoop, calls=%fused_computation.63 | loop fusion | flops 12 | bytes 32 | tf_op jit(solution)/shard_map/stack | solution.py:200
  85.9 22.3 %collective-permute-done.12.rest_2_.refs_0_ = bf16[2,592,512]{2,1,0:T(8,128)(2,1)S(1)} collective-permute-done((bf16[2,592,512]{2,1,0:T(8,128)(2,1)}, bf16[2,592,512]{2,1,0:T(8,128)(2,1)S(1)}, u32[]{:S(2)}, u32[]{:S(2)}) %collective-permute-start.12) | collective-permute-done | bytes 1212448 | tf_op jit(solution)/shard_map/ppermute | solution.py:290
  108.2 1.0 copy-done.4
  109.3 3.2 %copy_sets.8.rest_8_ = bf16[4,592,512]{2,1,0:T(8,128)(2,1)} custom-call(s32[2,4]{1,0:T(2,128)} %pad_add_fusion.2.table_ref, bf16[4,592,512]{2,1,0:T(8,128)(2,1)} %tie.10.rest_0_.rest_2_, bf16[4,592,512]{2,1,0:T(8,128)(2,1)} %tie.11.rest_1_.rest_4_, bf16[2,592,512]{2,1,0:T(8,128)(2,1)} %copy-done.4), custom_call_target="tpu_custom_call" | custom-call | tf_op jit(solution)/shard_map/copy_sets/pallas_call | solution.py:202
  112.5 1.6 collective-permute-start.14
  114.1 15.9 %collective-permute-done.7.rest_0_.rest_9_.refs_1_ = bf16[4,592,512]{2,1,0:T(8,128)(2,1)S(1)} collective-permute-done((bf16[4,592,512]{2,1,0:T(8,128)(2,1)}, bf16[4,592,512]{2,1,0:T(8,128)(2,1)S(1)}, u32[]{:S(2)}, u32[]{:S(2)}) %collective-permute-start.7) | collective-permute-done | bytes 2424864 | tf_op jit(solution)/shard_map/ppermute | solution.py:296
  130.0 1.5 copy-done.2
  134.7 2.7 %add_bitcast_fusion = s32[1,4]{1,0:T(1,128)S(1)} fusion(s32[1]{0:T(128)} %dynamic_slice.62, s32[1]{0:T(128)} %dynamic_slice.61, s32[1]{0:T(128)} %get-tuple-element.38, s32[1]{0:T(128)} %get-tuple-element.31), kind=kLoop, calls=%fused_computation.59 | loop fusion | flops 12 | bytes 32 | tf_op jit(solution)/shard_map/stack | solution.py:200
  139.2 1.4 add_bitcast_fusion.3
  141.2 2.8 %copy_sets.6.rest_2_ = bf16[2,592,512]{2,1,0:T(8,128)(2,1)} custom-call(s32[2,2]{1,0:T(2,128)} %pad_add_fusion.1.table_ref, bf16[4,592,512]{2,1,0:T(8,128)(2,1)} %copy-done.2, bf16[4,592,512]{2,1,0:T(8,128)(2,1)} %copy-done.1), custom_call_target="tpu_custom_call" | custom-call | tf_op jit(solution)/shard_map/copy_sets/pallas_call | solution.py:202
  144.0 1.3 collective-permute-start.18
  145.4 0.9 broadcast_in_dim.140.ve1_ref
  146.3 11.6 %pairs_0.1.rest_3_.rest_7_ = bf16[16,512,512]{2,1,0:T(8,128)(2,1)} custom-call(s32[5,16]{1,0:T(8,128)} %stack.117.refs_4_.meta_ref, f32[16]{0:T(128)} %add.82.shift_ref, bf16[2,576,128]{2,1,0:T(8,128)(2,1)} %broadcast_in_dim.140.ve1_ref, bf16[16,2,512,256]{3,2,1,0:T(8,128)(2,1)} %fusion.refs_3_.pick_ref, ...), custom_call_target="tpu_custom_call" | custom-call | tf_op jit(solution)/shard_map/pairs_0/pallas_call | solution.py:152
  157.9 3.7 %copy_sets.9 = (bf16[2,592,512]{2,1,0:T(8,128)(2,1)}, bf16[2,592,512]{2,1,0:T(8,128)(2,1)}) custom-call(s32[2,4]{1,0:T(2,128)} %stack.120.table_ref, bf16[4,592,512]{2,1,0:T(8,128)(2,1)} %copy-done.2, bf16[4,592,512]{2,1,0:T(8,128)(2,1)} %copy-done.1, bf16[2,592,512]{2,1,0:T(8,128)(2,1)} %copy_sets.6.rest_2_, bf16[16,512,512]{2,1,0:T(8,128)(2,1)} %pairs_0.1.rest_3_.rest_7_), custom_call_target="tpu_custom_call" | custom-call | tf_op jit(solution)/shard_map/copy_sets/pallas_call | solution.py:202
  161.6 3.7 %collective-permute-done.14.refs_0_ = bf16[4,592,512]{2,1,0:T(8,128)(2,1)} collective-permute-done((bf16[4,592,512]{2,1,0:T(8,128)(2,1)}, bf16[4,592,512]{2,1,0:T(8,128)(2,1)}, u32[]{:S(2)}, u32[]{:S(2)}) %collective-permute-start.14) | collective-permute-done | bytes 2424864 | tf_op jit(solution)/shard_map/ppermute | solution.py:290
  165.4 1.3 copy-done.3
  166.7 5.6 %collective-permute-done.18.rest_4_ = bf16[2,592,512]{2,1,0:T(8,128)(2,1)S(1)} collective-permute-done((bf16[2,592,512]{2,1,0:T(8,128)(2,1)}, bf16[2,592,512]{2,1,0:T(8,128)(2,1)S(1)}, u32[]{:S(2)}, u32[]{:S(2)}) %collective-permute-start.18) | collective-permute-done | bytes 1212448 | tf_op jit(solution)/shard_map/ppermute | solution.py:413
  172.2 1.3 collective-permute-start.21
  173.5 1.6 collective-permute-start.13
  175.1 1.0 copy-done.10
  176.2 1.1 copy-done.11
  177.2 1.4 copy-done.7
  178.6 14.7 %pairs_1.1.refs_1_.rest_4_ = bf16[16,512,512]{2,1,0:T(8,128)(2,1)} custom-call(s32[5,16]{1,0:T(8,128)} %stack.117.refs_4_.meta_ref, f32[16]{0:T(128)} %add.82.shift_ref, bf16[2,576,128]{2,1,0:T(8,128)(2,1)} %broadcast_in_dim.140.ve1_ref, bf16[16,2,512,256]{3,2,1,0:T(8,128)(2,1)} %fusion.refs_3_.pick_ref, ...), custom_call_target="tpu_custom_call", output_to_operand_aliasing={{}: (13, {})} | custom-call | tf_op jit(solution)/shard_map/pairs_1/pallas_call | solution.py:152
  193.4 10.1 %collective-permute-done.21.refs_0_ = bf16[2,592,512]{2,1,0:T(8,128)(2,1)S(1)} collective-permute-done((bf16[2,592,512]{2,1,0:T(8,128)(2,1)}, bf16[2,592,512]{2,1,0:T(8,128)(2,1)S(1)}, u32[]{:S(2)}, u32[]{:S(2)}) %collective-permute-start.21) | collective-permute-done | bytes 1212448 | tf_op jit(solution)/shard_map/ppermute | solution.py:445
  203.4 1.0 copy-done.6
  204.5 1.0 copy-done.5
  206.0 1.6 collective-permute-done.22.rest_3_
  207.6 1.7 collective-permute-done.20.rest_1_
  209.3 1.0 copy-done.13
  210.3 10.0 %pairs_2.1 = bf16[16,512,512]{2,1,0:T(8,128)(2,1)} custom-call(s32[5,16]{1,0:T(8,128)} %stack.117.refs_4_.meta_ref, f32[16]{0:T(128)} %add.82.shift_ref, bf16[2,576,128]{2,1,0:T(8,128)(2,1)} %broadcast_in_dim.140.ve1_ref, bf16[16,2,512,256]{3,2,1,0:T(8,128)(2,1)} %fusion.refs_3_.pick_ref, ...), custom_call_target="tpu_custom_call", output_to_operand_aliasing={{}: (10, {})} | custom-call | tf_op jit(solution)/shard_map/pairs_2/pallas_call | solution.py:152
  (119 shorter events, 15.8 us)
Async XLA Ops:
  0.0 11.1 %copy-start.20 = (s32[32,2]{0,1:T(2,128)S(1)}, s32[32,2]{0,1:T(2,128)}, u32[]{:S(2)}) copy-start(s32[32,2]{0,1:T(2,128)} %param.10) | copy-start | bytes 772
  0.0 11.1 %copy-start.23 = (s32[32]{0:T(128)S(1)}, s32[32]{0:T(128)}, u32[]{:S(2)}) copy-start(s32[32]{0:T(128)} %param.9) | copy-start | bytes 388
  3.4 68.8 %collective-permute-start = (bf16[4,592,512]{2,1,0:T(8,128)(2,1)}, bf16[4,592,512]{2,1,0:T(8,128)(2,1)S(1)}, u32[]{:S(2)}, u32[]{:S(2)}) collective-permute-start(bf16[4,592,512]{2,1,0:T(8,128)(2,1)} %extend.1.refs_1_.rest_0_.own_ref.rest_6_), channel_id=1, source_target_pairs={{0,1},{1,0},{2,3},{3,2},{4,5},{5,4},{6,7},{7,6},{8,9},{9,8},{10,11... | collective-permute-start | bytes 7274504 | tf_op jit(solution)/shard_map/ppermute | solution.py:293
  3.9 68.2 %collective-permute-start.8 = (bf16[4,592,512]{2,1,0:T(8,128)(2,1)}, bf16[4,592,512]{2,1,0:T(8,128)(2,1)}, u32[]{:S(2)}, u32[]{:S(2)}) collective-permute-start(bf16[4,592,512]{2,1,0:T(8,128)(2,1)} %extend.1.refs_1_.rest_0_.own_ref.rest_6_), channel_id=1, source_target_pairs={{0,4},{2,6},{4,8},{6,10},{8,12},{10,14},{1,5},{3,7},{5,9},{7,11},{... | collective-permute-start | bytes 7274504 | tf_op jit(solution)/shard_map/ppermute | solution.py:299
  9.8 64.6 %collective-permute-start.2 = (bf16[4,592,512]{2,1,0:T(8,128)(2,1)}, bf16[4,592,512]{2,1,0:T(8,128)(2,1)}, u32[]{:S(2)}, u32[]{:S(2)}) collective-permute-start(bf16[4,592,512]{2,1,0:T(8,128)(2,1)} %extend.1.refs_1_.rest_0_.own_ref.rest_6_), channel_id=1, source_target_pairs={{4,0},{6,2},{8,4},{10,6},{12,8},{14,10},{5,1},{7,3},{9,5},{11,7},{... | collective-permute-start | bytes 7274504 | tf_op jit(solution)/shard_map/ppermute | solution.py:296
  12.0 11.3 %copy-start.14 = (s32[32,2,512]{2,1,0:T(2,128)S(1)}, s32[32,2,512]{2,1,0:T(2,128)}, u32[]{:S(2)}) copy-start(s32[32,2,512]{2,1,0:T(2,128)} %param.11) | copy-start | bytes 393220
  12.0 11.3 %copy-start.18 = (s32[512]{0:T(512)S(1)}, s32[512]{0:T(512)}, u32[]{:S(2)}) copy-start(s32[512]{0:T(512)} %constant.142.clone.1) | copy-start | bytes 6148
  12.0 3.6 %collective-permute-start.1 = (s32[32]{0:T(128)}, s32[32]{0:T(128)S(1)}, u32[]{:S(2)}, u32[]{:S(2)}) collective-permute-start(s32[32]{0:T(128)} %tie.8), channel_id=1, source_target_pairs={{0,2},{2,0},{4,6},{6,4},{8,10},{10,8},{12,14},{14,12},{1,3},{3,1},... | collective-permute-start | bytes 392 | tf_op jit(solution)/shard_map/ppermute | solution.py:290
  21.3 28.2 %collective-permute-start.3 = (bf16[2,592,512]{2,1,0:T(8,128)(2,1)}, bf16[2,592,512]{2,1,0:T(8,128)(2,1)}, u32[]{:S(2)}, u32[]{:S(2)}) collective-permute-start(bf16[2,592,512]{2,1,0:T(8,128)(2,1)} %copy_sets.5.refs_1_), channel_id=1, source_target_pairs={{0,2},{2,0},{4,6},{6,4},{8,10},{10,8},{12,14},{14,12},{1,3},{3,1},... | collective-permute-start | bytes 3637256 | tf_op jit(solution)/shard_map/ppermute | solution.py:290
  23.4 26.3 %copy-start.19 = (s32[32]{0:T(128)S(1)}, s32[32]{0:T(128)}, u32[]{:S(2)}) copy-start(s32[32]{0:T(128)} %tie.8) | copy-start | bytes 388
  49.5 22.7 %collective-permute-start.4 = (bf16[2,592,512]{2,1,0:T(8,128)(2,1)}, bf16[2,592,512]{2,1,0:T(8,128)(2,1)}, u32[]{:S(2)}, u32[]{:S(2)}) collective-permute-start(bf16[2,592,512]{2,1,0:T(8,128)(2,1)} %collective-permute-done.3.rest_0_), channel_id=1, source_target_pairs={{0,1},{1,0},{2,3},{3,2},{4,5},{5,4},{6,7},{7,6},{8,9},{9,8},{10,11... | collective-permute-start | bytes 3637256 | tf_op jit(solution)/shard_map/ppermute | solution.py:293
  50.2 11.0 %collective-permute-start.6 = (s32[2,32]{1,0:T(2,128)}, s32[2,32]{1,0:T(2,128)S(1)}, u32[]{:S(2)}, u32[]{:S(2)}) collective-permute-start(s32[2,32]{1,0:T(2,128)} %tie.9), channel_id=1, source_target_pairs={{0,8},{2,10},{12,4},{14,6},{1,9},{3,11},{13,5},{15,7},{16,24},{18,... | collective-permute-start | bytes 776 | tf_op jit(solution)/shard_map/ppermute | solution.py:389
  61.3 10.1 %collective-permute-start.5 = (s32[2,32]{1,0:T(2,128)}, s32[2,32]{1,0:T(2,128)S(1)}, u32[]{:S(2)}, u32[]{:S(2)}) collective-permute-start(s32[2,32]{1,0:T(2,128)} %tie.9), channel_id=1, source_target_pairs={{0,4},{2,6},{12,8},{14,10},{1,5},{3,7},{13,9},{15,11},{16,20},{18,... | collective-permute-start | bytes 776 | tf_op jit(solution)/shard_map/ppermute | solution.py:389
  70.0 2.1 copy-start.17
  72.1 1.5 copy-start
  73.6 40.5 %collective-permute-start.9 = (bf16[4,592,512]{2,1,0:T(8,128)(2,1)}, bf16[4,592,512]{2,1,0:T(8,128)(2,1)S(1)}, u32[]{:S(2)}, u32[]{:S(2)}) collective-permute-start(bf16[4,592,512]{2,1,0:T(8,128)(2,1)} %tie.11.rest_1_.rest_4_), channel_id=1, source_target_pairs={{4,8},{6,10},{8,12},{10,14},{5,9},{7,11},{9,13},{11,15},{20,24},{2... | collective-permute-start | bytes 7274504 | tf_op jit(solution)/shard_map/ppermute | solution.py:299
  74.5 55.6 %collective-permute-start.7 = (bf16[4,592,512]{2,1,0:T(8,128)(2,1)}, bf16[4,592,512]{2,1,0:T(8,128)(2,1)S(1)}, u32[]{:S(2)}, u32[]{:S(2)}) collective-permute-start(bf16[4,592,512]{2,1,0:T(8,128)(2,1)} %tie.10.rest_0_.rest_2_), channel_id=1, source_target_pairs={{4,0},{6,2},{8,4},{10,6},{5,1},{7,3},{9,5},{11,7},{20,16},{22,18},... | collective-permute-start | bytes 7274504 | tf_op jit(solution)/shard_map/ppermute | solution.py:296
  77.6 7.7 %copy-start.22 = (s32[1,4]{1,0:T(1,128)S(1)}, s32[1,4]{1,0:T(1,128)}, u32[]{:S(2)}) copy-start(s32[1,4]{1,0:T(1,128)} %constant.148.clone.1) | copy-start | bytes 52
  80.6 27.7 %collective-permute-start.12 = (bf16[2,592,512]{2,1,0:T(8,128)(2,1)}, bf16[2,592,512]{2,1,0:T(8,128)(2,1)S(1)}, u32[]{:S(2)}, u32[]{:S(2)}) collective-permute-start(bf16[2,592,512]{2,1,0:T(8,128)(2,1)} %copy_sets.7), channel_id=1, source_target_pairs={{0,2},{2,0},{4,6},{6,4},{8,10},{10,8},{12,14},{14,12},{1,3},{3,1},... | collective-permute-start | bytes 3637256 | tf_op jit(solution)/shard_map/ppermute | solution.py:290
  84.8 60.5 %collective-permute-start.11 = (bf16[4,592,512]{2,1,0:T(8,128)(2,1)}, bf16[4,592,512]{2,1,0:T(8,128)(2,1)}, u32[]{:S(2)}, u32[]{:S(2)}) collective-permute-start(bf16[4,592,512]{2,1,0:T(8,128)(2,1)} %tie.11.rest_1_.rest_4_), channel_id=1, source_target_pairs={{0,1},{1,0},{2,3},{3,2},{4,5},{5,4},{6,7},{7,6},{8,9},{9,8},{10,11... | collective-permute-start | bytes 7274504 | tf_op jit(solution)/shard_map/ppermute | solution.py:293
  84.8 60.5 %collective-permute-start.10 = (bf16[4,592,512]{2,1,0:T(8,128)(2,1)}, bf16[4,592,512]{2,1,0:T(8,128)(2,1)}, u32[]{:S(2)}, u32[]{:S(2)}) collective-permute-start(bf16[4,592,512]{2,1,0:T(8,128)(2,1)} %tie.10.rest_0_.rest_2_), channel_id=1, source_target_pairs={{0,1},{1,0},{2,3},{3,2},{4,5},{5,4},{6,7},{7,6},{8,9},{9,8},{10,11... | collective-permute-start | bytes 7274504 | tf_op jit(solution)/shard_map/ppermute | solution.py:293
  108.2 1.0 copy-start.4
  112.5 21.3 %copy-start.21 = (f32[32]{0:T(128)S(1)}, f32[32]{0:T(128)}, u32[]{:S(2)}) copy-start(f32[32]{0:T(128)} %param.8) | copy-start | bytes 388
  112.5 22.2 %copy-start.15 = (bf16[4,576]{1,0:T(4,128)(2,1)S(1)}, bf16[4,576]{1,0:T(4,128)(2,1)}, u32[]{:S(2)}) copy-start(bf16[4,576]{1,0:T(4,128)(2,1)} %energy_ref.1) | copy-start | bytes 13828
  112.5 25.5 %copy-start.16 = (s32[8]{0:T(128)S(1)}, s32[8]{0:T(128)}, u32[]{:S(2)}) copy-start(s32[8]{0:T(128)} %get-tuple-element.12.refs_5_) | copy-start | bytes 100
  112.5 52.8 %collective-permute-start.14 = (bf16[4,592,512]{2,1,0:T(8,128)(2,1)}, bf16[4,592,512]{2,1,0:T(8,128)(2,1)}, u32[]{:S(2)}, u32[]{:S(2)}) collective-permute-start(bf16[4,592,512]{2,1,0:T(8,128)(2,1)} %copy_sets.8.rest_8_), channel_id=1, source_target_pairs={{0,2},{2,0},{4,6},{6,4},{8,10},{10,8},{12,14},{14,12},{1,3},{3,1},... | collective-permute-start | bytes 7274504 | tf_op jit(solution)/shard_map/ppermute | solution.py:290
  114.1 15.9 %copy-start.1 = (bf16[4,592,512]{2,1,0:T(8,128)(2,1)}, bf16[4,592,512]{2,1,0:T(8,128)(2,1)S(1)}, u32[]{:S(2)}) copy-start(bf16[4,592,512]{2,1,0:T(8,128)(2,1)S(1)} %collective-permute-done.9.rest_1_.rest_10_.refs_2_) | copy-start | bytes 7274500
  130.0 1.5 copy-start.2
  131.5 30.1 %collective-permute-start.15 = (bf16[2,592,512]{2,1,0:T(8,128)(2,1)}, bf16[2,592,512]{2,1,0:T(8,128)(2,1)S(1)}, u32[]{:S(2)}, u32[]{:S(2)}) collective-permute-start(bf16[2,592,512]{2,1,0:T(8,128)(2,1)} %tie.12), channel_id=1, source_target_pairs={{8,4},{10,6},{4,8},{6,10},{9,5},{11,7},{5,9},{7,11},{24,20},{26,22... | collective-permute-start | bytes 3637256 | tf_op jit(solution)/shard_map/ppermute | solution.py:427
  144.0 28.2 %collective-permute-start.18 = (bf16[2,592,512]{2,1,0:T(8,128)(2,1)}, bf16[2,592,512]{2,1,0:T(8,128)(2,1)S(1)}, u32[]{:S(2)}, u32[]{:S(2)}) collective-permute-start(bf16[2,592,512]{2,1,0:T(8,128)(2,1)} %copy_sets.6.rest_2_), channel_id=1, source_target_pairs={{4,0},{6,2},{8,12},{10,14},{5,1},{7,3},{9,13},{11,15},{20,16},{22,... | collective-permute-start | bytes 3637256 | tf_op jit(solution)/shard_map/ppermute | solution.py:413
  161.6 3.8 %copy-start.8 = (bf16[2,592,512]{2,1,0:T(8,128)(2,1)}, bf16[2,592,512]{2,1,0:T(8,128)(2,1)S(1)}, u32[]{:S(2)}) copy-start(bf16[2,592,512]{2,1,0:T(8,128)(2,1)S(1)} %collective-permute-done.15.refs_2_) | copy-start | bytes 3637252
  165.4 1.3 copy-start.3
  165.4 11.9 %collective-permute-start.16 = (bf16[4,592,512]{2,1,0:T(8,128)(2,1)}, bf16[4,592,512]{2,1,0:T(8,128)(2,1)S(1)}, u32[]{:S(2)}, u32[]{:S(2)}) collective-permute-start(bf16[4,592,512]{2,1,0:T(8,128)(2,1)} %tie.13.rest_0_), channel_id=1, source_target_pairs={{0,1},{1,0},{2,3},{3,2},{4,5},{5,4},{6,7},{7,6},{8,9},{9,8},{10,11... | collective-permute-start | bytes 7274504 | tf_op jit(solution)/shard_map/ppermute | solution.py:293
  166.7 8.5 %collective-permute-start.17 = (bf16[2,592,512]{2,1,0:T(8,128)(2,1)S(1)}, bf16[2,592,512]{2,1,0:T(8,128)(2,1)S(1)}, u32[]{:S(2)}, u32[]{:S(2)}) collective-permute-start(bf16[2,592,512]{2,1,0:T(8,128)(2,1)S(1)} %copy-done.3), channel_id=1, source_target_pairs={{0,1},{1,0},{2,3},{3,2},{4,5},{5,4},{6,7},{7,6},{8,9},{9,8},{10,11... | collective-permute-start | bytes 3637256 | tf_op jit(solution)/shard_map/ppermute | solution.py:293
  172.2 5.0 %copy-start.9 = (bf16[2,592,512]{2,1,0:T(8,128)(2,1)}, bf16[2,592,512]{2,1,0:T(8,128)(2,1)S(1)}, u32[]{:S(2)}) copy-start(bf16[2,592,512]{2,1,0:T(8,128)(2,1)S(1)} %collective-permute-done.18.rest_4_) | copy-start | bytes 3637252
  172.2 2.9 %collective-permute-start.19 = (bf16[2,592,512]{2,1,0:T(8,128)(2,1)S(1)}, bf16[2,592,512]{2,1,0:T(8,128)(2,1)S(1)}, u32[]{:S(2)}, u32[]{:S(2)}) collective-permute-start(bf16[2,592,512]{2,1,0:T(8,128)(2,1)S(1)} %collective-permute-done.18.rest_4_), channel_id=1, source_target_pairs={{0,1},{1,0},{2,3},{3,2},{4,5},{5,4},{6,7},{7,6},{8,9},{9,8},{10,11... | collective-permute-start | bytes 3637256 | tf_op jit(solution)/shard_map/ppermute | solution.py:293
  172.2 31.2 %collective-permute-start.21 = (bf16[2,592,512]{2,1,0:T(8,128)(2,1)}, bf16[2,592,512]{2,1,0:T(8,128)(2,1)S(1)}, u32[]{:S(2)}, u32[]{:S(2)}) collective-permute-start(bf16[2,592,512]{2,1,0:T(8,128)(2,1)} %copy-done.8), channel_id=1, source_target_pairs={{4,0},{6,2},{8,12},{10,14},{5,1},{7,3},{9,13},{11,15},{20,16},{22,... | collective-permute-start | bytes 3637256 | tf_op jit(solution)/shard_map/ppermute | solution.py:445
  173.5 30.9 %collective-permute-start.13 = (bf16[2,592,512]{2,1,0:T(8,128)(2,1)}, bf16[2,592,512]{2,1,0:T(8,128)(2,1)S(1)}, u32[]{:S(2)}, u32[]{:S(2)}) collective-permute-start(bf16[2,592,512]{2,1,0:T(8,128)(2,1)} %get-tuple-element.7), channel_id=1, source_target_pairs={{0,2},{2,0},{4,6},{6,4},{8,10},{10,8},{12,14},{14,12},{1,3},{3,1},... | collective-permute-start | bytes 3637256 | tf_op jit(solution)/shard_map/ppermute | solution.py:290
  175.1 1.1 copy-start.10
  176.2 1.1 copy-start.11
  177.2 1.4 copy-start.7
  203.4 1.0 copy-start.6
  204.4 3.1 %collective-permute-start.22 = (bf16[2,592,512]{2,1,0:T(8,128)(2,1)}, bf16[2,592,512]{2,1,0:T(8,128)(2,1)S(1)}, u32[]{:S(2)}, u32[]{:S(2)}) collective-permute-start(bf16[2,592,512]{2,1,0:T(8,128)(2,1)} %tie.15.rest_2_), channel_id=1, source_target_pairs={{0,1},{1,0},{2,3},{3,2},{4,5},{5,4},{6,7},{7,6},{8,9},{9,8},{10,11... | collective-permute-start | bytes 3637256 | tf_op jit(solution)/shard_map/ppermute | solution.py:293
  204.5 1.0 copy-start.5
  205.5 3.8 %collective-permute-start.20 = (bf16[2,592,512]{2,1,0:T(8,128)(2,1)}, bf16[2,592,512]{2,1,0:T(8,128)(2,1)S(1)}, u32[]{:S(2)}, u32[]{:S(2)}) collective-permute-start(bf16[2,592,512]{2,1,0:T(8,128)(2,1)} %tie.14.rest_0_), channel_id=1, source_target_pairs={{0,1},{1,0},{2,3},{3,2},{4,5},{5,4},{6,7},{7,6},{8,9},{9,8},{10,11... | collective-permute-start | bytes 3637256 | tf_op jit(solution)/shard_map/ppermute | solution.py:293
  207.6 1.7 copy-start.12
  209.3 1.0 copy-start.13

commit v9 on v7

--- a/solution.py
+++ b/solution.py
@@ -8,7 +8,7 @@
 from jax.sharding import PartitionSpec as P
 
 NT = (((1,), (1,)), ((), ()))
-VMEM_LIMIT = 56 * 1024 * 1024
+VMEM_LIMIT = 63 * 1024 * 1024
 EXTRA = 16
 
 

time: 215 us -> 208 us (0.967)
  local copies, waits for them, and re-layouts: 18.1 us -> 8.78 us
  waiting for transfers between devices: 94.6 us -> 97.6 us
    unnamed x38 -> x16, local copies, waits for them, and re-layouts: 9.69 us -> 0.03 us
  transfers between devices with their start and end apart: 21 -> 21, of which waited for: 10 -> 10; matrix products, arithmetic and copies ran while one was open for 13% -> 13% of each run, Pallas kernels for 18% -> 20%
where the time goes in v9:
time: 208 us; the launch traced here: 205 us
  waiting for transfers between devices  97.6 us (47%)
  Pallas kernels  53.8 us (26%)
  starting transfers between devices  25.7 us (12%)
  other arithmetic  18.8 us (9%)
  local copies, waits for them, and re-layouts  8.78 us (4%)
    ppermute x5, waiting for transfers between devices, across_y(): return lax.ppermute(a, 'orb', swap_y)  40.2 us
    pallas_call x3, Pallas kernels, run_pairs(): pl.pallas_call(functools.partial(pair_kernel, call, wins, len(sets), len(...  36.4 us
    ppermute x2, waiting for transfers between devices, hop_down(): lax.ppermute(a, 'orb', [(k, k - 2) for k in range(2, orb_count) if k // 2...  26.1 us
    ppermute x1, waiting for transfers between devices, per_device(): far_a = lax.ppermute(load_own, 'orb', perm)  23.5 us
    pallas_call x4, Pallas kernels, copy_sets(): pl.pallas_call(functools.partial(set_kernel, len(arrays), len(after), siz...  14 us
    another operation x4, other arithmetic, copy_sets(): jnp.stack([jnp.stack([jnp.asarray(w, jnp.int32) for w in which]), jnp.sta...  9.43 us
    ppermute x2, starting transfers between devices, hop_up(): lax.ppermute(a, 'orb', [(k, k + 2) for k in range(orb_count - 2) if k //...  8.41 us
    ppermute x5, starting transfers between devices, across_y(): return lax.ppermute(a, 'orb', swap_y)  6.46 us
  transfers between devices with their start and end apart: 21, of which 10 were waited for; matrix products, arithmetic and copies ran while one was open for 13% of the time, Pallas kernels for 20%

profile of v9, /device:TPU:0, one launch (start us, length us, event | category | flops | bytes accessed | tf_op | source)
XLA Modules:
  0.0 204.9 jit_solution(4694915756486783913)
XLA Ops:
  0.0 3.4 %extend.1.refs_1_.rest_0_.own_ref.rest_6_ = bf16[4,592,512]{2,1,0:T(8,128)(2,1)} custom-call(bf16[4,576,512]{2,1,0:T(8,128)(2,1)} %blocks_ref.1, bf16[4,576]{1,0:T(4,128)(2,1)} %energy_ref.1), custom_call_target="tpu_custom_call" | custom-call | tf_op jit(solution)/shard_map/extend/pallas_call | solution.py:244
  3.4 6.3 %collective-permute-start.6 = (bf16[4,592,512]{2,1,0:T(8,128)(2,1)}, bf16[4,592,512]{2,1,0:T(8,128)(2,1)}, u32[]{:S(2)}, u32[]{:S(2)}) collective-permute-start(bf16[4,592,512]{2,1,0:T(8,128)(2,1)} %extend.1.refs_1_.rest_0_.own_ref.rest_6_), channel_id=1, source_target_pairs={{0,4},{2,6},{4,8},{6,10},{8,12},{10,14},{1,5},{3,7},{5,9},{7,11},{... | collective-permute-start | bytes 7274504 | tf_op jit(solution)/shard_map/ppermute | solution.py:299
  9.7 1.3 collective-permute-start.2
  11.4 0.6 convert_element_type.33.refs_0_
  12.0 1.5 collective-permute-start.1
  13.6 2.0 collective-permute-done.1
  15.8 0.7 fusion.7
  16.5 0.7 fusion.8
  17.2 1.4 add_bitcast_fusion.1
  18.6 0.6 stack.100.table_ref
  19.1 3.0 %copy_sets.4.refs_1_ = bf16[2,592,512]{2,1,0:T(8,128)(2,1)} custom-call(s32[2,2]{1,0:T(2,128)} %stack.100.table_ref, bf16[4,592,512]{2,1,0:T(8,128)(2,1)} %extend.1.refs_1_.rest_0_.own_ref.rest_6_), custom_call_target="tpu_custom_call" | custom-call | tf_op jit(solution)/shard_map/copy_sets/pallas_call | solution.py:202
  22.2 1.4 collective-permute-start.3
  24.2 0.6 stack.94.refs_4_.meta_ref
  24.8 25.8 %collective-permute-done.3.rest_0_ = bf16[2,592,512]{2,1,0:T(8,128)(2,1)} collective-permute-done((bf16[2,592,512]{2,1,0:T(8,128)(2,1)}, bf16[2,592,512]{2,1,0:T(8,128)(2,1)}, u32[]{:S(2)}, u32[]{:S(2)}) %collective-permute-start.3) | collective-permute-done | bytes 1212448 | tf_op jit(solution)/shard_map/ppermute | solution.py:290
  50.7 5.7 %fusion.refs_3_.pick_ref = bf16[16,2,512,256]{3,2,1,0:T(8,128)(2,1)} fusion(s32[16,2,512]{2,1,0:T(2,128)S(1)} %dynamic-slice_add_fusion), kind=kLoop, calls=%fused_computation.1 | loop fusion | flops 8388608 | bytes 8454144 | tf_op jit(solution)/shard_map/convert_element_type | solution.py:366
  56.4 0.6 pad_add_fusion.refs_0_
  57.0 4.7 %collective-permute-start.8 = (s32[2,32]{1,0:T(2,128)}, s32[2,32]{1,0:T(2,128)S(1)}, u32[]{:S(2)}, u32[]{:S(2)}) collective-permute-start(s32[2,32]{1,0:T(2,128)} %tie.10), channel_id=1, source_target_pairs={{0,4},{2,6},{14,10},{12,8},{1,5},{3,7},{15,11},{13,9},{16,20},{18,... | collective-permute-start | bytes 776 | tf_op jit(solution)/shard_map/ppermute | solution.py:386
  61.7 2.6 %add_bitcast_fusion.3 = s32[1,4]{1,0:T(1,128)S(1)} fusion(s32[1]{0:T(128)} %get-tuple-element.39, s32[1]{0:T(128)} %get-tuple-element.35, s32[1]{0:T(128)} %get-tuple-element.38, s32[1]{0:T(128)} %get-tuple-element.34), kind=kLoop, calls=%fused_computation.60 | loop fusion | flops 12 | bytes 32 | tf_op jit(solution)/shard_map/stack | solution.py:200
  64.3 1.7 collective-permute-done.2.refs_0_
  66.1 1.3 collective-permute-start.5
  68.0 2.1 %collective-permute-start.7 = (bf16[4,592,512]{2,1,0:T(8,128)(2,1)}, bf16[4,592,512]{2,1,0:T(8,128)(2,1)}, u32[]{:S(2)}, u32[]{:S(2)}) collective-permute-start(bf16[4,592,512]{2,1,0:T(8,128)(2,1)} %tie.9.rest_1_.rest_4_), channel_id=1, source_target_pairs={{4,8},{6,10},{8,12},{10,14},{5,9},{7,11},{9,13},{11,15},{20,24},{2... | collective-permute-start | bytes 7274504 | tf_op jit(solution)/shard_map/ppermute | solution.py:299
  70.1 0.6 pad_add_fusion.1.table_ref
  70.6 3.9 %copy_sets.5.rest_8_ = bf16[4,592,512]{2,1,0:T(8,128)(2,1)} custom-call(s32[2,4]{1,0:T(2,128)} %pad_add_fusion.1.table_ref, bf16[4,592,512]{2,1,0:T(8,128)(2,1)} %tie.8.rest_0_.rest_2_, bf16[4,592,512]{2,1,0:T(8,128)(2,1)} %tie.9.rest_1_.rest_4_), custom_call_target="tpu_custom_call" | custom-call | tf_op jit(solution)/shard_map/copy_sets/pallas_call | solution.py:202
  74.6 1.1 collective-permute-start.12
  75.9 0.6 dynamic_slice.62
  76.5 0.6 dynamic_slice.61
  77.4 0.6 add.80.shift_ref
  78.3 0.7 dynamic_slice.66
  78.9 0.6 dynamic_slice.65
  79.8 0.6 dynamic_slice.68
  81.0 4.9 %add_bitcast_fusion = (s32[1,4]{1,0:T(1,128)S(1)}, s32[1,4]{1,0:T(1,128)S(1)}) fusion(s32[1]{0:T(128)} %dynamic_slice.62, s32[1]{0:T(128)} %dynamic_slice.61, s32[1]{0:T(128)} %get-tuple-element.41, s32[1]{0:T(128)} %get-tuple-element.37, s32[1]{0:T(128)} %dynamic_slice.68, s32[1]{0:T(128)} %dynamic_slice.67, s32[1]{0:T(128)} %dynamic_slice.66, ...), kind=kLoop, calls=%fused_computation.57 | loop fusion | flops 24 | bytes 64 | tf_op jit(solution)/shard_map/stack | solution.py:200
  86.4 0.9 broadcast_in_dim.140.ve1_ref
  87.4 11.6 %pairs_0.1.rest_2_.rest_7_ = bf16[16,512,512]{2,1,0:T(8,128)(2,1)} custom-call(s32[5,16]{1,0:T(8,128)} %stack.94.refs_4_.meta_ref, f32[16]{0:T(128)} %add.80.shift_ref, bf16[2,576,128]{2,1,0:T(8,128)(2,1)} %broadcast_in_dim.140.ve1_ref, bf16[16,2,512,256]{3,2,1,0:T(8,128)(2,1)} %fusion.refs_3_.pick_ref, ...), custom_call_target="tpu_custom_call" | custom-call | tf_op jit(solution)/shard_map/pairs_0/pallas_call | solution.py:152
  99.0 24.4 %collective-permute-done.5.rest_0_ = bf16[4,592,512]{2,1,0:T(8,128)(2,1)} collective-permute-done((bf16[4,592,512]{2,1,0:T(8,128)(2,1)}, bf16[4,592,512]{2,1,0:T(8,128)(2,1)}, u32[]{:S(2)}, u32[]{:S(2)}) %collective-permute-start.5) | collective-permute-done | bytes 2424864 | tf_op jit(solution)/shard_map/ppermute | solution.py:296
  123.4 3.8 %copy_sets.6 = (bf16[2,592,512]{2,1,0:T(8,128)(2,1)}, bf16[2,592,512]{2,1,0:T(8,128)(2,1)}) custom-call(s32[2,4]{1,0:T(2,128)} %stack.106.table_ref, bf16[4,592,512]{2,1,0:T(8,128)(2,1)} %collective-permute-done.5.rest_0_, bf16[4,592,512]{2,1,0:T(8,128)(2,1)} %collective-permute-done.7.rest_1_, bf16[16,512,512]{2,1,0:T(8,128)(2,1)} %pairs_0.1.rest_2_.rest_7_), custom_call_target="tpu_custom_call" | custom-call | tf_op jit(solution)/shard_map/copy_sets/pallas_call | solution.py:202
  127.2 1.3 collective-permute-start.15
  128.5 1.0 collective-permute-done.12.refs_0_
  129.5 1.0 collective-permute-start.18
  130.5 0.6 stack.97.table_ref
  131.1 3.3 %copy_sets.7 = (bf16[2,592,512]{2,1,0:T(8,128)(2,1)}, bf16[2,592,512]{2,1,0:T(8,128)(2,1)}) custom-call(s32[2,4]{1,0:T(2,128)} %stack.97.table_ref, bf16[4,592,512]{2,1,0:T(8,128)(2,1)} %collective-permute-done.5.rest_0_, bf16[4,592,512]{2,1,0:T(8,128)(2,1)} %collective-permute-done.7.rest_1_, bf16[2,592,512]{2,1,0:T(8,128)(2,1)} %get-tuple-element.9.rest_2_.refs_1_), custom_call_target="tpu_custom_call" | custom-call | tf_op jit(solution)/shard_map/copy_sets/pallas_call | solution.py:202
  134.7 23.5 %collective-permute-done.15.rest_4_ = bf16[2,592,512]{2,1,0:T(8,128)(2,1)} collective-permute-done((bf16[2,592,512]{2,1,0:T(8,128)(2,1)}, bf16[2,592,512]{2,1,0:T(8,128)(2,1)}, u32[]{:S(2)}, u32[]{:S(2)}) %collective-permute-start.15) | collective-permute-done | bytes 1212448 | tf_op jit(solution)/shard_map/ppermute | solution.py:405
  158.2 1.5 collective-permute-start.11
  159.7 1.3 collective-permute-start.19
  161.4 14.7 %pairs_1.1.refs_1_.rest_4_ = bf16[16,512,512]{2,1,0:T(8,128)(2,1)} custom-call(s32[5,16]{1,0:T(8,128)} %stack.94.refs_4_.meta_ref, f32[16]{0:T(128)} %add.80.shift_ref, bf16[2,576,128]{2,1,0:T(8,128)(2,1)} %broadcast_in_dim.140.ve1_ref, bf16[16,2,512,256]{3,2,1,0:T(8,128)(2,1)} %fusion.refs_3_.pick_ref, ...), custom_call_target="tpu_custom_call", output_to_operand_aliasing={{}: (13, {})} | custom-call | tf_op jit(solution)/shard_map/pairs_1/pallas_call | solution.py:152
  176.1 11.4 %collective-permute-done.11.refs_0_ = bf16[2,592,512]{2,1,0:T(8,128)(2,1)} collective-permute-done((bf16[2,592,512]{2,1,0:T(8,128)(2,1)}, bf16[2,592,512]{2,1,0:T(8,128)(2,1)}, u32[]{:S(2)}, u32[]{:S(2)}) %collective-permute-start.11) | collective-permute-done | bytes 1212448 | tf_op jit(solution)/shard_map/ppermute | solution.py:290
  187.6 4.1 %collective-permute-done.19.refs_0_ = bf16[2,592,512]{2,1,0:T(8,128)(2,1)} collective-permute-done((bf16[2,592,512]{2,1,0:T(8,128)(2,1)}, bf16[2,592,512]{2,1,0:T(8,128)(2,1)}, u32[]{:S(2)}, u32[]{:S(2)}) %collective-permute-start.19) | collective-permute-done | bytes 1212448 | tf_op jit(solution)/shard_map/ppermute | solution.py:404
  191.7 3.2 %collective-permute-done.20.rest_3_ = bf16[2,592,512]{2,1,0:T(8,128)(2,1)} collective-permute-done((bf16[2,592,512]{2,1,0:T(8,128)(2,1)}, bf16[2,592,512]{2,1,0:T(8,128)(2,1)}, u32[]{:S(2)}, u32[]{:S(2)}) %collective-permute-start.20) | collective-permute-done | bytes 1212448 | tf_op jit(solution)/shard_map/ppermute | solution.py:293
  194.9 10.0 %pairs_2.1 = bf16[16,512,512]{2,1,0:T(8,128)(2,1)} custom-call(s32[5,16]{1,0:T(8,128)} %stack.94.refs_4_.meta_ref, f32[16]{0:T(128)} %add.80.shift_ref, bf16[2,576,128]{2,1,0:T(8,128)(2,1)} %broadcast_in_dim.140.ve1_ref, bf16[16,2,512,256]{3,2,1,0:T(8,128)(2,1)} %fusion.refs_3_.pick_ref, ...), custom_call_target="tpu_custom_call", output_to_operand_aliasing={{}: (10, {})} | custom-call | tf_op jit(solution)/shard_map/pairs_2/pallas_call | solution.py:152
  (75 shorter events, 4.9 us)
Async XLA Ops:
  0.0 11.1 %copy-start.4 = (s32[32,2]{0,1:T(2,128)S(1)}, s32[32,2]{0,1:T(2,128)}, u32[]{:S(2)}) copy-start(s32[32,2]{0,1:T(2,128)} %param.10) | copy-start | bytes 772
  0.0 11.1 %copy-start.7 = (s32[32]{0:T(128)S(1)}, s32[32]{0:T(128)}, u32[]{:S(2)}) copy-start(s32[32]{0:T(128)} %param.9) | copy-start | bytes 388
  3.4 64.1 %collective-permute-start.6 = (bf16[4,592,512]{2,1,0:T(8,128)(2,1)}, bf16[4,592,512]{2,1,0:T(8,128)(2,1)}, u32[]{:S(2)}, u32[]{:S(2)}) collective-permute-start(bf16[4,592,512]{2,1,0:T(8,128)(2,1)} %extend.1.refs_1_.rest_0_.own_ref.rest_6_), channel_id=1, source_target_pairs={{0,4},{2,6},{4,8},{6,10},{8,12},{10,14},{1,5},{3,7},{5,9},{7,11},{... | collective-permute-start | bytes 7274504 | tf_op jit(solution)/shard_map/ppermute | solution.py:299
  9.7 56.3 %collective-permute-start.2 = (bf16[4,592,512]{2,1,0:T(8,128)(2,1)}, bf16[4,592,512]{2,1,0:T(8,128)(2,1)}, u32[]{:S(2)}, u32[]{:S(2)}) collective-permute-start(bf16[4,592,512]{2,1,0:T(8,128)(2,1)} %extend.1.refs_1_.rest_0_.own_ref.rest_6_), channel_id=1, source_target_pairs={{4,0},{6,2},{8,4},{10,6},{12,8},{14,10},{5,1},{7,3},{9,5},{11,7},{... | collective-permute-start | bytes 7274504 | tf_op jit(solution)/shard_map/ppermute | solution.py:296
  11.0 55.0 %collective-permute-start = (bf16[4,592,512]{2,1,0:T(8,128)(2,1)}, bf16[4,592,512]{2,1,0:T(8,128)(2,1)}, u32[]{:S(2)}, u32[]{:S(2)}) collective-permute-start(bf16[4,592,512]{2,1,0:T(8,128)(2,1)} %extend.1.refs_1_.rest_0_.own_ref.rest_6_), channel_id=1, source_target_pairs={{0,1},{1,0},{2,3},{3,2},{4,5},{5,4},{6,7},{7,6},{8,9},{9,8},{10,11... | collective-permute-start | bytes 7274504 | tf_op jit(solution)/shard_map/ppermute | solution.py:293
  12.0 38.6 %copy-start = (s32[32,2,512]{2,1,0:T(2,128)S(1)}, s32[32,2,512]{2,1,0:T(2,128)}, u32[]{:S(2)}) copy-start(s32[32,2,512]{2,1,0:T(2,128)} %param.11) | copy-start | bytes 393220
  12.0 38.6 %copy-start.2 = (s32[512]{0:T(512)S(1)}, s32[512]{0:T(512)}, u32[]{:S(2)}) copy-start(s32[512]{0:T(512)} %constant.141.clone.1) | copy-start | bytes 6148
  12.0 3.6 %collective-permute-start.1 = (s32[32]{0:T(128)}, s32[32]{0:T(128)S(1)}, u32[]{:S(2)}, u32[]{:S(2)}) collective-permute-start(s32[32]{0:T(128)} %tie.7), channel_id=1, source_target_pairs={{0,2},{2,0},{4,6},{6,4},{8,10},{10,8},{12,14},{14,12},{1,3},{3,1},... | collective-permute-start | bytes 392 | tf_op jit(solution)/shard_map/ppermute | solution.py:290
  22.2 28.4 %collective-permute-start.3 = (bf16[2,592,512]{2,1,0:T(8,128)(2,1)}, bf16[2,592,512]{2,1,0:T(8,128)(2,1)}, u32[]{:S(2)}, u32[]{:S(2)}) collective-permute-start(bf16[2,592,512]{2,1,0:T(8,128)(2,1)} %copy_sets.4.refs_1_), channel_id=1, source_target_pairs={{0,2},{2,0},{4,6},{6,4},{8,10},{10,8},{12,14},{14,12},{1,3},{3,1},... | collective-permute-start | bytes 3637256 | tf_op jit(solution)/shard_map/ppermute | solution.py:290
  50.6 15.4 %collective-permute-start.4 = (bf16[2,592,512]{2,1,0:T(8,128)(2,1)}, bf16[2,592,512]{2,1,0:T(8,128)(2,1)}, u32[]{:S(2)}, u32[]{:S(2)}) collective-permute-start(bf16[2,592,512]{2,1,0:T(8,128)(2,1)} %collective-permute-done.3.rest_0_), channel_id=1, source_target_pairs={{0,1},{1,0},{2,3},{3,2},{4,5},{5,4},{6,7},{7,6},{8,9},{9,8},{10,11... | collective-permute-start | bytes 3637256 | tf_op jit(solution)/shard_map/ppermute | solution.py:293
  50.7 5.7 %copy-start.3 = (s32[32]{0:T(128)S(1)}, s32[32]{0:T(128)}, u32[]{:S(2)}) copy-start(s32[32]{0:T(128)} %tie.7) | copy-start | bytes 388
  57.0 17.6 %collective-permute-start.8 = (s32[2,32]{1,0:T(2,128)}, s32[2,32]{1,0:T(2,128)S(1)}, u32[]{:S(2)}, u32[]{:S(2)}) collective-permute-start(s32[2,32]{1,0:T(2,128)} %tie.10), channel_id=1, source_target_pairs={{0,4},{2,6},{14,10},{12,8},{1,5},{3,7},{15,11},{13,9},{16,20},{18,... | collective-permute-start | bytes 776 | tf_op jit(solution)/shard_map/ppermute | solution.py:386
  66.0 4.0 %copy-start.6 = (s32[1,4]{1,0:T(1,128)S(1)}, s32[1,4]{1,0:T(1,128)}, u32[]{:S(2)}) copy-start(s32[1,4]{1,0:T(1,128)} %constant.147.clone.1) | copy-start | bytes 52
  66.0 20.4 %collective-permute-start.9 = (bf16[4,592,512]{2,1,0:T(8,128)(2,1)}, bf16[4,592,512]{2,1,0:T(8,128)(2,1)}, u32[]{:S(2)}, u32[]{:S(2)}) collective-permute-start(bf16[4,592,512]{2,1,0:T(8,128)(2,1)} %tie.8.rest_0_.rest_2_), channel_id=1, source_target_pairs={{0,1},{1,0},{2,3},{3,2},{4,5},{5,4},{6,7},{7,6},{8,9},{9,8},{10,11... | collective-permute-start | bytes 7274504 | tf_op jit(solution)/shard_map/ppermute | solution.py:293
  66.1 57.3 %collective-permute-start.5 = (bf16[4,592,512]{2,1,0:T(8,128)(2,1)}, bf16[4,592,512]{2,1,0:T(8,128)(2,1)}, u32[]{:S(2)}, u32[]{:S(2)}) collective-permute-start(bf16[4,592,512]{2,1,0:T(8,128)(2,1)} %tie.8.rest_0_.rest_2_), channel_id=1, source_target_pairs={{4,0},{6,2},{8,4},{10,6},{5,1},{7,3},{9,5},{11,7},{20,16},{22,18},... | collective-permute-start | bytes 7274504 | tf_op jit(solution)/shard_map/ppermute | solution.py:296
  67.4 19.0 %collective-permute-start.10 = (bf16[4,592,512]{2,1,0:T(8,128)(2,1)}, bf16[4,592,512]{2,1,0:T(8,128)(2,1)}, u32[]{:S(2)}, u32[]{:S(2)}) collective-permute-start(bf16[4,592,512]{2,1,0:T(8,128)(2,1)} %tie.9.rest_1_.rest_4_), channel_id=1, source_target_pairs={{0,1},{1,0},{2,3},{3,2},{4,5},{5,4},{6,7},{7,6},{8,9},{9,8},{10,11... | collective-permute-start | bytes 7274504 | tf_op jit(solution)/shard_map/ppermute | solution.py:293
  68.0 55.4 %collective-permute-start.7 = (bf16[4,592,512]{2,1,0:T(8,128)(2,1)}, bf16[4,592,512]{2,1,0:T(8,128)(2,1)}, u32[]{:S(2)}, u32[]{:S(2)}) collective-permute-start(bf16[4,592,512]{2,1,0:T(8,128)(2,1)} %tie.9.rest_1_.rest_4_), channel_id=1, source_target_pairs={{4,8},{6,10},{8,12},{10,14},{5,9},{7,11},{9,13},{11,15},{20,24},{2... | collective-permute-start | bytes 7274504 | tf_op jit(solution)/shard_map/ppermute | solution.py:299
  70.6 6.6 %copy-start.5 = (f32[32]{0:T(128)S(1)}, f32[32]{0:T(128)}, u32[]{:S(2)}) copy-start(f32[32]{0:T(128)} %param.8) | copy-start | bytes 388
  70.6 7.3 %copy-start.1 = (bf16[4,576]{1,0:T(4,128)(2,1)S(1)}, bf16[4,576]{1,0:T(4,128)(2,1)}, u32[]{:S(2)}) copy-start(bf16[4,576]{1,0:T(4,128)(2,1)} %energy_ref.1) | copy-start | bytes 13828
  74.6 55.0 %collective-permute-start.12 = (bf16[4,592,512]{2,1,0:T(8,128)(2,1)}, bf16[4,592,512]{2,1,0:T(8,128)(2,1)}, u32[]{:S(2)}, u32[]{:S(2)}) collective-permute-start(bf16[4,592,512]{2,1,0:T(8,128)(2,1)} %copy_sets.5.rest_8_), channel_id=1, source_target_pairs={{0,2},{2,0},{4,6},{6,4},{8,10},{10,8},{12,14},{14,12},{1,3},{3,1},... | collective-permute-start | bytes 7274504 | tf_op jit(solution)/shard_map/ppermute | solution.py:290
  127.2 31.0 %collective-permute-start.15 = (bf16[2,592,512]{2,1,0:T(8,128)(2,1)}, bf16[2,592,512]{2,1,0:T(8,128)(2,1)}, u32[]{:S(2)}, u32[]{:S(2)}) collective-permute-start(bf16[2,592,512]{2,1,0:T(8,128)(2,1)} %get-tuple-element.9.rest_2_.refs_1_), channel_id=1, source_target_pairs={{4,0},{6,2},{8,12},{10,14},{5,1},{7,3},{9,13},{11,15},{20,16},{22,... | collective-permute-start | bytes 3637256 | tf_op jit(solution)/shard_map/ppermute | solution.py:405
  129.5 31.9 %collective-permute-start.13 = (bf16[4,592,512]{2,1,0:T(8,128)(2,1)}, bf16[4,592,512]{2,1,0:T(8,128)(2,1)}, u32[]{:S(2)}, u32[]{:S(2)}) collective-permute-start(bf16[4,592,512]{2,1,0:T(8,128)(2,1)} %tie.11.rest_0_), channel_id=1, source_target_pairs={{0,1},{1,0},{2,3},{3,2},{4,5},{5,4},{6,7},{7,6},{8,9},{9,8},{10,11... | collective-permute-start | bytes 7274504 | tf_op jit(solution)/shard_map/ppermute | solution.py:293
  129.5 30.2 %collective-permute-start.18 = (bf16[2,592,512]{2,1,0:T(8,128)(2,1)}, bf16[2,592,512]{2,1,0:T(8,128)(2,1)}, u32[]{:S(2)}, u32[]{:S(2)}) collective-permute-start(bf16[2,592,512]{2,1,0:T(8,128)(2,1)} %get-tuple-element.12), channel_id=1, source_target_pairs={{0,2},{2,0},{4,6},{6,4},{8,10},{10,8},{12,14},{14,12},{1,3},{3,1},... | collective-permute-start | bytes 3637256 | tf_op jit(solution)/shard_map/ppermute | solution.py:290
  134.4 26.6 %collective-permute-start.14 = (bf16[2,592,512]{2,1,0:T(8,128)(2,1)}, bf16[2,592,512]{2,1,0:T(8,128)(2,1)}, u32[]{:S(2)}, u32[]{:S(2)}) collective-permute-start(bf16[2,592,512]{2,1,0:T(8,128)(2,1)} %get-tuple-element.11.rest_2_.rest_6_), channel_id=1, source_target_pairs={{0,1},{1,0},{2,3},{3,2},{4,5},{5,4},{6,7},{7,6},{8,9},{9,8},{10,11... | collective-permute-start | bytes 3637256 | tf_op jit(solution)/shard_map/ppermute | solution.py:293
  158.2 3.2 %collective-permute-start.16 = (bf16[2,592,512]{2,1,0:T(8,128)(2,1)}, bf16[2,592,512]{2,1,0:T(8,128)(2,1)}, u32[]{:S(2)}, u32[]{:S(2)}) collective-permute-start(bf16[2,592,512]{2,1,0:T(8,128)(2,1)} %collective-permute-done.15.rest_4_), channel_id=1, source_target_pairs={{0,1},{1,0},{2,3},{3,2},{4,5},{5,4},{6,7},{7,6},{8,9},{9,8},{10,11... | collective-permute-start | bytes 3637256 | tf_op jit(solution)/shard_map/ppermute | solution.py:293
  158.2 29.4 %collective-permute-start.11 = (bf16[2,592,512]{2,1,0:T(8,128)(2,1)}, bf16[2,592,512]{2,1,0:T(8,128)(2,1)}, u32[]{:S(2)}, u32[]{:S(2)}) collective-permute-start(bf16[2,592,512]{2,1,0:T(8,128)(2,1)} %get-tuple-element.10), channel_id=1, source_target_pairs={{0,2},{2,0},{4,6},{6,4},{8,10},{10,8},{12,14},{14,12},{1,3},{3,1},... | collective-permute-start | bytes 3637256 | tf_op jit(solution)/shard_map/ppermute | solution.py:290
  159.7 32.0 %collective-permute-start.19 = (bf16[2,592,512]{2,1,0:T(8,128)(2,1)}, bf16[2,592,512]{2,1,0:T(8,128)(2,1)}, u32[]{:S(2)}, u32[]{:S(2)}) collective-permute-start(bf16[2,592,512]{2,1,0:T(8,128)(2,1)} %collective-permute-done.18), channel_id=1, source_target_pairs={{4,0},{6,2},{8,12},{10,14},{5,1},{7,3},{9,13},{11,15},{20,16},{22,... | collective-permute-start | bytes 3637256 | tf_op jit(solution)/shard_map/ppermute | solution.py:404
  187.6 4.1 %collective-permute-start.17 = (bf16[2,592,512]{2,1,0:T(8,128)(2,1)}, bf16[2,592,512]{2,1,0:T(8,128)(2,1)}, u32[]{:S(2)}, u32[]{:S(2)}) collective-permute-start(bf16[2,592,512]{2,1,0:T(8,128)(2,1)} %tie.12.rest_0_), channel_id=1, source_target_pairs={{0,1},{1,0},{2,3},{3,2},{4,5},{5,4},{6,7},{7,6},{8,9},{9,8},{10,11... | collective-permute-start | bytes 3637256 | tf_op jit(solution)/shard_map/ppermute | solution.py:293
  191.7 3.2 %collective-permute-start.20 = (bf16[2,592,512]{2,1,0:T(8,128)(2,1)}, bf16[2,592,512]{2,1,0:T(8,128)(2,1)}, u32[]{:S(2)}, u32[]{:S(2)}) collective-permute-start(bf16[2,592,512]{2,1,0:T(8,128)(2,1)} %tie.13.rest_2_), channel_id=1, source_target_pairs={{0,1},{1,0},{2,3},{3,2},{4,5},{5,4},{6,7},{7,6},{8,9},{9,8},{10,11... | collective-permute-start | bytes 3637256 | tf_op jit(solution)/shard_map/ppermute | solution.py:293

commit v10 on v9

--- a/solution.py
+++ b/solution.py
@@ -289,6 +289,9 @@
     def across_y(a):
         return lax.ppermute(a, "orb", swap_y)
 
+    def across_y_inside(a):
+        return lax.ppermute(a, "orb", [pair for pair in swap_y if 0 < pair[0] // 2 < last])
+
     def across_aux(a):
         return lax.ppermute(a, "aux", swap_aux)
 
@@ -336,9 +339,11 @@
     at_hand = (dist <= 1) & (is_opp == 0)
     idx = jnp.where(at_hand, part, rank + jnp.where(both & from_up, 2, 0))
     which_col = jnp.where(dist == 0, 3, jnp.where((dist == 1) & from_up, 2, jnp.where(is_far, 2, 1)))
-    which = jnp.where(is_opp == 1, is_far.astype(i32), which_col)
+    at_end = (z == 0) | (z == last)
+    is_early = at_end & (dist == last - 1)
+    which = jnp.where(is_opp == 1, jnp.where(is_early, 3, is_far.astype(i32)), which_col)
     stage_col = jnp.where(is_far, last - 2, jnp.maximum(dist - 1, 0))
-    stage = jnp.where(is_opp == 1, jnp.minimum(dist, last - 1), stage_col)
+    stage = jnp.where(is_opp == 1, jnp.minimum(dist, last - 1) - is_early.astype(i32), stage_col)
     rows = jnp.arange(own_rows, dtype=i32)
     before = (stage[None, :] < stage[:, None]) | ((stage[None, :] == stage[:, None]) & (rows[None, :] < rows[:, None]))
     place = jnp.sum(before.astype(i32), axis=1)
@@ -399,9 +404,14 @@
             source = jnp.where(sends_down, 2 * last + y, y)
             from_set = [1 - sends_down.astype(i32)] * 4
             perm = [(2, 0), (3, 1), (2 * (last - 1), 2 * last), (2 * (last - 1) + 1, 2 * last + 1)]
+            over_set = jnp.where(at_end, (z == last).astype(i32), from_set[0])
+            end_source = jnp.where(z == 0, s_down, s_up)
+            over_pick = [
+                jnp.where(at_end, a, b) for a, b in zip(two_for(want_opp, end_source), two_for(far_opp, source))]
             load_over, load_own = copy_sets(
-                from_set, two_for(far_opp, source) + two_for(far_own, source), [downs[d], ups[d]], [out], [2, 2])
-            far_b = lax.ppermute(across_y(load_over), "orb", perm)
+                [over_set] * 2 + from_set[2:], over_pick + two_for(far_own, source), [downs[d], ups[d]], [out], [2, 2])
+            over = across_y(load_over)
+            far_b = lax.ppermute(over, "orb", perm)
             far_a = lax.ppermute(load_own, "orb", perm)
             first = [load_own]
         if 2 * d <= last:
@@ -424,9 +434,9 @@
                 place_of * 2, both_ways(want_opp) + both_ways(want), [downs[d], ups[d]], first, [len(place_of)] * 2)
             sets[d - 1] = [with_other(tie(opp, first) if first else opp), with_other(mine)]
             if d + 1 == last:
-                sets[d - 1].append(with_other(far_a))
+                sets[d - 1] += [with_other(far_a), with_other(over)]
             out = pairs_at(d - 1, [mine], out)
-        opp = across_y(theirs)
+        opp = across_y(theirs) if d + 1 < last else across_y_inside(theirs)
     sets[last - 1] = [with_other(tie(opp, [out])), with_other(tie(far_b, [out]))]
     return pairs_at(last - 1, [], out)
 

time: 208 us -> 207 us (level)
  between operations: 0.27 us -> 2.59 us
    ppermute x5 -> x4, waiting for transfers between devices: 40.2 us -> 29 us  [across_y(): return lax.ppermute(a, 'orb', swap_y)]
    ppermute x1 -> x2, waiting for transfers between devices: 4.06 us -> 13.6 us  [the longest x1 13.6 us: per_device(): far_b = lax.ppermute(over, 'orb', perm)]
    ppermute x1, starting transfers between devices: 4.73 us -> 2.24 us  [per_device(): lax.ppermute(tie(wanted_both, [y_load]), 'orb', tell)]
    ppermute x9 -> x10, waiting for transfers between devices: 3.68 us -> 4.7 us  [across_aux(): return lax.ppermute(a, 'aux', swap_aux)]
    another operation x4 -> x6, other arithmetic: 9.43 us -> 8.95 us  [copy_sets(): jnp.stack([jnp.stack([jnp.asarray(w, jnp.int32) for w in which]), jnp.sta...]
    ppermute x5 -> x4, starting transfers between devices: 6.46 us -> 6.45 us  [across_y(): return lax.ppermute(a, 'orb', swap_y)]
  transfers between devices with their start and end apart: 21 -> 22, of which waited for: 10 -> 8; matrix products, arithmetic and copies ran while one was open for 13% -> 13% of each run, Pallas kernels for 20% -> 21%
where the time goes in v10:
time: 207 us; the launch traced here: 204 us
  waiting for transfers between devices  95.7 us (46%)
  Pallas kernels  53.1 us (26%)
  starting transfers between devices  26.1 us (13%)
  other arithmetic  18.3 us (9%)
  local copies, waits for them, and re-layouts  8.27 us (4%)
  between operations  2.59 us (1%)
    pallas_call x3, Pallas kernels, run_pairs(): pl.pallas_call(functools.partial(pair_kernel, call, wins, len(sets), len(...  36.3 us
    ppermute x4, waiting for transfers between devices, across_y(): return lax.ppermute(a, 'orb', swap_y)  29 us
    ppermute x1, waiting for transfers between devices, per_device(): far_a = lax.ppermute(load_own, 'orb', perm)  24.3 us
    ppermute x2, waiting for transfers between devices, hop_down(): lax.ppermute(a, 'orb', [(k, k - 2) for k in range(2, orb_count) if k // 2...  24.1 us
    ppermute x1, waiting for transfers between devices, per_device(): far_b = lax.ppermute(over, 'orb', perm)  13.6 us
    pallas_call x4, Pallas kernels, copy_sets(): pl.pallas_call(functools.partial(set_kernel, len(arrays), len(after), siz...  13.4 us
    another operation x6, other arithmetic, copy_sets(): jnp.stack([jnp.stack([jnp.asarray(w, jnp.int32) for w in which]), jnp.sta...  8.95 us
    ppermute x2, starting transfers between devices, hop_up(): lax.ppermute(a, 'orb', [(k, k + 2) for k in range(orb_count - 2) if k //...  8.64 us
  transfers between devices with their start and end apart: 22, of which 8 were waited for; matrix products, arithmetic and copies ran while one was open for 13% of the time, Pallas kernels for 21%

profile of v10, /device:TPU:0, one launch (start us, length us, event | category | flops | bytes accessed | tf_op | source)
XLA Modules:
  0.0 204.1 jit_solution(3549357767806533367)
XLA Ops:
  0.0 3.4 %extend.1.refs_1_.rest_0_.own_ref.rest_6_ = bf16[4,592,512]{2,1,0:T(8,128)(2,1)} custom-call(bf16[4,576,512]{2,1,0:T(8,128)(2,1)} %blocks_ref.1, bf16[4,576]{1,0:T(4,128)(2,1)} %energy_ref.1), custom_call_target="tpu_custom_call" | custom-call | tf_op jit(solution)/shard_map/extend/pallas_call | solution.py:244
  3.9 1.3 collective-permute-start.2
  5.2 6.6 %collective-permute-start.6 = (bf16[4,592,512]{2,1,0:T(8,128)(2,1)}, bf16[4,592,512]{2,1,0:T(8,128)(2,1)}, u32[]{:S(2)}, u32[]{:S(2)}) collective-permute-start(bf16[4,592,512]{2,1,0:T(8,128)(2,1)} %extend.1.refs_1_.rest_0_.own_ref.rest_6_), channel_id=1, source_target_pairs={{0,4},{2,6},{4,8},{6,10},{8,12},{10,14},{1,5},{3,7},{5,9},{7,11},{... | collective-permute-start | bytes 7274504 | tf_op jit(solution)/shard_map/ppermute | solution.py:302
  12.0 0.6 convert_element_type.40.refs_0_
  12.6 2.0 collective-permute-start.1
  14.7 1.6 collective-permute-done.1
  16.5 0.7 fusion.8
  17.2 0.7 fusion.7
  17.8 1.4 add_bitcast_fusion.1
  19.2 0.6 stack.112.table_ref
  19.8 3.0 %copy_sets.4.refs_1_ = bf16[2,592,512]{2,1,0:T(8,128)(2,1)} custom-call(s32[2,2]{1,0:T(2,128)} %stack.112.table_ref, bf16[4,592,512]{2,1,0:T(8,128)(2,1)} %extend.1.refs_1_.rest_0_.own_ref.rest_6_), custom_call_target="tpu_custom_call" | custom-call | tf_op jit(solution)/shard_map/copy_sets/pallas_call | solution.py:202
  22.8 1.8 collective-permute-start.3
  25.3 0.6 stack.106.refs_4_.meta_ref
  25.9 25.4 %collective-permute-done.3.rest_0_ = bf16[2,592,512]{2,1,0:T(8,128)(2,1)} collective-permute-done((bf16[2,592,512]{2,1,0:T(8,128)(2,1)}, bf16[2,592,512]{2,1,0:T(8,128)(2,1)}, u32[]{:S(2)}, u32[]{:S(2)}) %collective-permute-start.3) | collective-permute-done | bytes 1212448 | tf_op jit(solution)/shard_map/ppermute | solution.py:290
  51.4 5.7 %fusion.refs_3_.pick_ref = bf16[16,2,512,256]{3,2,1,0:T(8,128)(2,1)} fusion(s32[16,2,512]{2,1,0:T(2,128)S(1)} %dynamic-slice_add_fusion), kind=kLoop, calls=%fused_computation.1 | loop fusion | flops 8388608 | bytes 8454144 | tf_op jit(solution)/shard_map/convert_element_type | solution.py:371
  57.1 0.6 pad_add_fusion.refs_0_
  57.7 2.2 %collective-permute-start.8 = (s32[2,32]{1,0:T(2,128)}, s32[2,32]{1,0:T(2,128)S(1)}, u32[]{:S(2)}, u32[]{:S(2)}) collective-permute-start(s32[2,32]{1,0:T(2,128)} %tie.10), channel_id=1, source_target_pairs={{0,4},{2,6},{14,10},{12,8},{1,5},{3,7},{15,11},{13,9},{16,20},{18,... | collective-permute-start | bytes 776 | tf_op jit(solution)/shard_map/ppermute | solution.py:391
  60.0 2.6 %add_bitcast_fusion.4 = s32[1,4]{1,0:T(1,128)S(1)} fusion(s32[1]{0:T(128)} %get-tuple-element.40, s32[1]{0:T(128)} %get-tuple-element.35, s32[1]{0:T(128)} %get-tuple-element.39, s32[1]{0:T(128)} %get-tuple-element.34), kind=kLoop, calls=%fused_computation.63 | loop fusion | flops 12 | bytes 32 | tf_op jit(solution)/shard_map/stack | solution.py:200
  62.6 1.3 collective-permute-start.5
  64.2 2.1 %collective-permute-start.7 = (bf16[4,592,512]{2,1,0:T(8,128)(2,1)}, bf16[4,592,512]{2,1,0:T(8,128)(2,1)}, u32[]{:S(2)}, u32[]{:S(2)}) collective-permute-start(bf16[4,592,512]{2,1,0:T(8,128)(2,1)} %tie.9.rest_1_.rest_4_), channel_id=1, source_target_pairs={{4,8},{6,10},{8,12},{10,14},{5,9},{7,11},{9,13},{11,15},{20,24},{2... | collective-permute-start | bytes 7274504 | tf_op jit(solution)/shard_map/ppermute | solution.py:302
  66.5 0.6 pad_add_fusion.2.table_ref
  67.1 3.8 %copy_sets.5.rest_8_ = bf16[4,592,512]{2,1,0:T(8,128)(2,1)} custom-call(s32[2,4]{1,0:T(2,128)} %pad_add_fusion.2.table_ref, bf16[4,592,512]{2,1,0:T(8,128)(2,1)} %tie.8.rest_0_.rest_2_, bf16[4,592,512]{2,1,0:T(8,128)(2,1)} %tie.9.rest_1_.rest_4_), custom_call_target="tpu_custom_call" | custom-call | tf_op jit(solution)/shard_map/copy_sets/pallas_call | solution.py:202
  71.0 1.4 collective-permute-start.12
  72.6 0.6 dynamic_slice.68
  73.2 0.6 dynamic_slice.67
  74.1 0.6 add.80.shift_ref
  74.7 2.6 %add_bitcast_fusion = (s32[1,4]{1,0:T(1,128)S(1)}, s32[1,4]{1,0:T(1,128)S(1)}) fusion(s32[1]{0:T(128)} %dynamic_slice.68, s32[1]{0:T(128)} %dynamic_slice.67, s32[1]{0:T(128)} %get-tuple-element.43, s32[1]{0:T(128)} %get-tuple-element.38, s32[1]{0:T(128)} %bitcast.12, s32[1]{0:T(128)} %bitcast.11), kind=kLoop, calls=%fused_computation.59 | loop fusion | flops 24 | bytes 56 | tf_op jit(solution)/shard_map/stack | solution.py:200
  77.5 0.6 dynamic_slice.76
  78.1 0.6 dynamic_slice.75
  79.0 0.7 dynamic_slice.74
  82.5 1.3 add_bitcast_fusion.3
  84.4 0.9 broadcast_in_dim.141.ve1_ref
  85.4 10.1 %pairs_0.1.rest_2_.rest_9_ = bf16[16,512,512]{2,1,0:T(8,128)(2,1)} custom-call(s32[5,16]{1,0:T(8,128)} %stack.106.refs_4_.meta_ref, f32[16]{0:T(128)} %add.80.shift_ref, bf16[2,576,128]{2,1,0:T(8,128)(2,1)} %broadcast_in_dim.141.ve1_ref, bf16[16,2,512,256]{3,2,1,0:T(8,128)(2,1)} %fusion.refs_3_.pick_ref, ...), custom_call_target="tpu_custom_call" | custom-call | tf_op jit(solution)/shard_map/pairs_0/pallas_call | solution.py:152
  95.5 24.1 %collective-permute-done.5.rest_0_ = bf16[4,592,512]{2,1,0:T(8,128)(2,1)} collective-permute-done((bf16[4,592,512]{2,1,0:T(8,128)(2,1)}, bf16[4,592,512]{2,1,0:T(8,128)(2,1)}, u32[]{:S(2)}, u32[]{:S(2)}) %collective-permute-start.5) | collective-permute-done | bytes 2424864 | tf_op jit(solution)/shard_map/ppermute | solution.py:299
  119.6 3.2 %copy_sets.6 = (bf16[2,592,512]{2,1,0:T(8,128)(2,1)}, bf16[2,592,512]{2,1,0:T(8,128)(2,1)}) custom-call(s32[2,4]{1,0:T(2,128)} %pad_add_fusion.1.table_ref, bf16[4,592,512]{2,1,0:T(8,128)(2,1)} %collective-permute-done.5.rest_0_, bf16[4,592,512]{2,1,0:T(8,128)(2,1)} %collective-permute-done.7.rest_1_, bf16[16,512,512]{2,1,0:T(8,128)(2,1)} %pairs_0.1.rest_2_.rest_9_), custom_call_target="tpu_custom_call" | custom-call | tf_op jit(solution)/shard_map/copy_sets/pallas_call | solution.py:202
  122.8 1.3 collective-permute-start.15
  124.1 2.0 collective-permute-done.12.refs_0_
  126.1 1.3 collective-permute-start.17
  127.4 0.6 stack.109.table_ref
  128.0 3.3 %copy_sets.7 = (bf16[2,592,512]{2,1,0:T(8,128)(2,1)}, bf16[2,592,512]{2,1,0:T(8,128)(2,1)}) custom-call(s32[2,4]{1,0:T(2,128)} %stack.109.table_ref, bf16[4,592,512]{2,1,0:T(8,128)(2,1)} %collective-permute-done.5.rest_0_, bf16[4,592,512]{2,1,0:T(8,128)(2,1)} %collective-permute-done.7.rest_1_, bf16[2,592,512]{2,1,0:T(8,128)(2,1)} %get-tuple-element.9.rest_2_.refs_1_), custom_call_target="tpu_custom_call" | custom-call | tf_op jit(solution)/shard_map/copy_sets/pallas_call | solution.py:202
  131.6 24.3 %collective-permute-done.15.rest_4_ = bf16[2,592,512]{2,1,0:T(8,128)(2,1)} collective-permute-done((bf16[2,592,512]{2,1,0:T(8,128)(2,1)}, bf16[2,592,512]{2,1,0:T(8,128)(2,1)}, u32[]{:S(2)}, u32[]{:S(2)}) %collective-permute-start.15) | collective-permute-done | bytes 1212448 | tf_op jit(solution)/shard_map/ppermute | solution.py:415
  156.4 1.7 collective-permute-start.11
  158.1 1.3 collective-permute-start.20
  159.4 1.5 collective-permute-done.18.rest_7_
  160.9 19.3 %pairs_1.1.refs_1_.rest_4_ = bf16[16,512,512]{2,1,0:T(8,128)(2,1)} custom-call(s32[5,16]{1,0:T(8,128)} %stack.106.refs_4_.meta_ref, f32[16]{0:T(128)} %add.80.shift_ref, bf16[2,576,128]{2,1,0:T(8,128)(2,1)} %broadcast_in_dim.141.ve1_ref, bf16[16,2,512,256]{3,2,1,0:T(8,128)(2,1)} %fusion.refs_3_.pick_ref, ...), custom_call_target="tpu_custom_call", output_to_operand_aliasing={{}: (15, {})} | custom-call | tf_op jit(solution)/shard_map/pairs_1/pallas_call | solution.py:152
  180.3 13.6 %collective-permute-done.20.refs_0_ = bf16[2,592,512]{2,1,0:T(8,128)(2,1)} collective-permute-done((bf16[2,592,512]{2,1,0:T(8,128)(2,1)}, bf16[2,592,512]{2,1,0:T(8,128)(2,1)}, u32[]{:S(2)}, u32[]{:S(2)}) %collective-permute-start.20) | collective-permute-done | bytes 1212448 | tf_op jit(solution)/shard_map/ppermute | solution.py:414
  193.9 3.2 %collective-permute-done.21.rest_3_ = bf16[2,592,512]{2,1,0:T(8,128)(2,1)} collective-permute-done((bf16[2,592,512]{2,1,0:T(8,128)(2,1)}, bf16[2,592,512]{2,1,0:T(8,128)(2,1)}, u32[]{:S(2)}, u32[]{:S(2)}) %collective-permute-start.21) | collective-permute-done | bytes 1212448 | tf_op jit(solution)/shard_map/ppermute | solution.py:296
  197.1 7.0 %pairs_2.1 = bf16[16,512,512]{2,1,0:T(8,128)(2,1)} custom-call(s32[5,16]{1,0:T(8,128)} %stack.106.refs_4_.meta_ref, f32[16]{0:T(128)} %add.80.shift_ref, bf16[2,576,128]{2,1,0:T(8,128)(2,1)} %broadcast_in_dim.141.ve1_ref, bf16[16,2,512,256]{3,2,1,0:T(8,128)(2,1)} %fusion.refs_3_.pick_ref, ...), custom_call_target="tpu_custom_call", output_to_operand_aliasing={{}: (10, {})} | custom-call | tf_op jit(solution)/shard_map/pairs_2/pallas_call | solution.py:152
  (78 shorter events, 5.5 us)
Async XLA Ops:
  0.0 11.8 %copy-start.4 = (s32[32,2]{0,1:T(2,128)S(1)}, s32[32,2]{0,1:T(2,128)}, u32[]{:S(2)}) copy-start(s32[32,2]{0,1:T(2,128)} %param.10) | copy-start | bytes 772
  0.0 11.8 %copy-start.7 = (s32[32]{0:T(128)S(1)}, s32[32]{0:T(128)}, u32[]{:S(2)}) copy-start(s32[32]{0:T(128)} %param.9) | copy-start | bytes 388
  3.4 59.2 %collective-permute-start = (bf16[4,592,512]{2,1,0:T(8,128)(2,1)}, bf16[4,592,512]{2,1,0:T(8,128)(2,1)}, u32[]{:S(2)}, u32[]{:S(2)}) collective-permute-start(bf16[4,592,512]{2,1,0:T(8,128)(2,1)} %extend.1.refs_1_.rest_0_.own_ref.rest_6_), channel_id=1, source_target_pairs={{0,1},{1,0},{2,3},{3,2},{4,5},{5,4},{6,7},{7,6},{8,9},{9,8},{10,11... | collective-permute-start | bytes 7274504 | tf_op jit(solution)/shard_map/ppermute | solution.py:296
  3.9 58.7 %collective-permute-start.2 = (bf16[4,592,512]{2,1,0:T(8,128)(2,1)}, bf16[4,592,512]{2,1,0:T(8,128)(2,1)}, u32[]{:S(2)}, u32[]{:S(2)}) collective-permute-start(bf16[4,592,512]{2,1,0:T(8,128)(2,1)} %extend.1.refs_1_.rest_0_.own_ref.rest_6_), channel_id=1, source_target_pairs={{4,0},{6,2},{8,4},{10,6},{12,8},{14,10},{5,1},{7,3},{9,5},{11,7},{... | collective-permute-start | bytes 7274504 | tf_op jit(solution)/shard_map/ppermute | solution.py:299
  5.2 59.0 %collective-permute-start.6 = (bf16[4,592,512]{2,1,0:T(8,128)(2,1)}, bf16[4,592,512]{2,1,0:T(8,128)(2,1)}, u32[]{:S(2)}, u32[]{:S(2)}) collective-permute-start(bf16[4,592,512]{2,1,0:T(8,128)(2,1)} %extend.1.refs_1_.rest_0_.own_ref.rest_6_), channel_id=1, source_target_pairs={{0,4},{2,6},{4,8},{6,10},{8,12},{10,14},{1,5},{3,7},{5,9},{7,11},{... | collective-permute-start | bytes 7274504 | tf_op jit(solution)/shard_map/ppermute | solution.py:302
  12.6 38.7 %copy-start = (s32[32,2,512]{2,1,0:T(2,128)S(1)}, s32[32,2,512]{2,1,0:T(2,128)}, u32[]{:S(2)}) copy-start(s32[32,2,512]{2,1,0:T(2,128)} %param.11) | copy-start | bytes 393220
  12.6 38.7 %copy-start.2 = (s32[512]{0:T(512)S(1)}, s32[512]{0:T(512)}, u32[]{:S(2)}) copy-start(s32[512]{0:T(512)} %constant.146.clone.1) | copy-start | bytes 6148
  12.6 3.6 %collective-permute-start.1 = (s32[32]{0:T(128)}, s32[32]{0:T(128)S(1)}, u32[]{:S(2)}, u32[]{:S(2)}) collective-permute-start(s32[32]{0:T(128)} %tie.7), channel_id=1, source_target_pairs={{0,2},{2,0},{4,6},{6,4},{8,10},{10,8},{12,14},{14,12},{1,3},{3,1},... | collective-permute-start | bytes 392 | tf_op jit(solution)/shard_map/ppermute | solution.py:290
  22.8 28.6 %collective-permute-start.3 = (bf16[2,592,512]{2,1,0:T(8,128)(2,1)}, bf16[2,592,512]{2,1,0:T(8,128)(2,1)}, u32[]{:S(2)}, u32[]{:S(2)}) collective-permute-start(bf16[2,592,512]{2,1,0:T(8,128)(2,1)} %copy_sets.4.refs_1_), channel_id=1, source_target_pairs={{0,2},{2,0},{4,6},{6,4},{8,10},{10,8},{12,14},{14,12},{1,3},{3,1},... | collective-permute-start | bytes 3637256 | tf_op jit(solution)/shard_map/ppermute | solution.py:290
  51.3 11.2 %collective-permute-start.4 = (bf16[2,592,512]{2,1,0:T(8,128)(2,1)}, bf16[2,592,512]{2,1,0:T(8,128)(2,1)}, u32[]{:S(2)}, u32[]{:S(2)}) collective-permute-start(bf16[2,592,512]{2,1,0:T(8,128)(2,1)} %collective-permute-done.3.rest_0_), channel_id=1, source_target_pairs={{0,1},{1,0},{2,3},{3,2},{4,5},{5,4},{6,7},{7,6},{8,9},{9,8},{10,11... | collective-permute-start | bytes 3637256 | tf_op jit(solution)/shard_map/ppermute | solution.py:296
  51.4 5.7 %copy-start.3 = (s32[32]{0:T(128)S(1)}, s32[32]{0:T(128)}, u32[]{:S(2)}) copy-start(s32[32]{0:T(128)} %tie.7) | copy-start | bytes 388
  57.7 13.2 %collective-permute-start.8 = (s32[2,32]{1,0:T(2,128)}, s32[2,32]{1,0:T(2,128)S(1)}, u32[]{:S(2)}, u32[]{:S(2)}) collective-permute-start(s32[2,32]{1,0:T(2,128)} %tie.10), channel_id=1, source_target_pairs={{0,4},{2,6},{14,10},{12,8},{1,5},{3,7},{15,11},{13,9},{16,20},{18,... | collective-permute-start | bytes 776 | tf_op jit(solution)/shard_map/ppermute | solution.py:391
  62.6 4.0 %copy-start.6 = (s32[1,4]{1,0:T(1,128)S(1)}, s32[1,4]{1,0:T(1,128)}, u32[]{:S(2)}) copy-start(s32[1,4]{1,0:T(1,128)} %constant.152.clone.1) | copy-start | bytes 52
  62.6 57.0 %collective-permute-start.5 = (bf16[4,592,512]{2,1,0:T(8,128)(2,1)}, bf16[4,592,512]{2,1,0:T(8,128)(2,1)}, u32[]{:S(2)}, u32[]{:S(2)}) collective-permute-start(bf16[4,592,512]{2,1,0:T(8,128)(2,1)} %tie.8.rest_0_.rest_2_), channel_id=1, source_target_pairs={{4,0},{6,2},{8,4},{10,6},{5,1},{7,3},{9,5},{11,7},{20,16},{22,18},... | collective-permute-start | bytes 7274504 | tf_op jit(solution)/shard_map/ppermute | solution.py:299
  63.9 20.6 %collective-permute-start.9 = (bf16[4,592,512]{2,1,0:T(8,128)(2,1)}, bf16[4,592,512]{2,1,0:T(8,128)(2,1)}, u32[]{:S(2)}, u32[]{:S(2)}) collective-permute-start(bf16[4,592,512]{2,1,0:T(8,128)(2,1)} %tie.8.rest_0_.rest_2_), channel_id=1, source_target_pairs={{0,1},{1,0},{2,3},{3,2},{4,5},{5,4},{6,7},{7,6},{8,9},{9,8},{10,11... | collective-permute-start | bytes 7274504 | tf_op jit(solution)/shard_map/ppermute | solution.py:296
  64.2 55.4 %collective-permute-start.7 = (bf16[4,592,512]{2,1,0:T(8,128)(2,1)}, bf16[4,592,512]{2,1,0:T(8,128)(2,1)}, u32[]{:S(2)}, u32[]{:S(2)}) collective-permute-start(bf16[4,592,512]{2,1,0:T(8,128)(2,1)} %tie.9.rest_1_.rest_4_), channel_id=1, source_target_pairs={{4,8},{6,10},{8,12},{10,14},{5,9},{7,11},{9,13},{11,15},{20,24},{2... | collective-permute-start | bytes 7274504 | tf_op jit(solution)/shard_map/ppermute | solution.py:302
  66.2 18.2 %collective-permute-start.10 = (bf16[4,592,512]{2,1,0:T(8,128)(2,1)}, bf16[4,592,512]{2,1,0:T(8,128)(2,1)}, u32[]{:S(2)}, u32[]{:S(2)}) collective-permute-start(bf16[4,592,512]{2,1,0:T(8,128)(2,1)} %tie.9.rest_1_.rest_4_), channel_id=1, source_target_pairs={{0,1},{1,0},{2,3},{3,2},{4,5},{5,4},{6,7},{7,6},{8,9},{9,8},{10,11... | collective-permute-start | bytes 7274504 | tf_op jit(solution)/shard_map/ppermute | solution.py:296
  67.1 6.8 %copy-start.5 = (f32[32]{0:T(128)S(1)}, f32[32]{0:T(128)}, u32[]{:S(2)}) copy-start(f32[32]{0:T(128)} %param.8) | copy-start | bytes 388
  67.1 7.6 %copy-start.1 = (bf16[4,576]{1,0:T(4,128)(2,1)S(1)}, bf16[4,576]{1,0:T(4,128)(2,1)}, u32[]{:S(2)}) copy-start(bf16[4,576]{1,0:T(4,128)(2,1)} %energy_ref.1) | copy-start | bytes 13828
  71.0 55.2 %collective-permute-start.12 = (bf16[4,592,512]{2,1,0:T(8,128)(2,1)}, bf16[4,592,512]{2,1,0:T(8,128)(2,1)}, u32[]{:S(2)}, u32[]{:S(2)}) collective-permute-start(bf16[4,592,512]{2,1,0:T(8,128)(2,1)} %copy_sets.5.rest_8_), channel_id=1, source_target_pairs={{0,2},{2,0},{4,6},{6,4},{8,10},{10,8},{12,14},{14,12},{1,3},{3,1},... | collective-permute-start | bytes 7274504 | tf_op jit(solution)/shard_map/ppermute | solution.py:290
  122.8 33.1 %collective-permute-start.15 = (bf16[2,592,512]{2,1,0:T(8,128)(2,1)}, bf16[2,592,512]{2,1,0:T(8,128)(2,1)}, u32[]{:S(2)}, u32[]{:S(2)}) collective-permute-start(bf16[2,592,512]{2,1,0:T(8,128)(2,1)} %get-tuple-element.9.rest_2_.refs_1_), channel_id=1, source_target_pairs={{4,0},{6,2},{8,12},{10,14},{5,1},{7,3},{9,13},{11,15},{20,16},{22,... | collective-permute-start | bytes 3637256 | tf_op jit(solution)/shard_map/ppermute | solution.py:415
  126.1 33.3 %collective-permute-start.13 = (bf16[4,592,512]{2,1,0:T(8,128)(2,1)}, bf16[4,592,512]{2,1,0:T(8,128)(2,1)}, u32[]{:S(2)}, u32[]{:S(2)}) collective-permute-start(bf16[4,592,512]{2,1,0:T(8,128)(2,1)} %tie.11.rest_0_), channel_id=1, source_target_pairs={{0,1},{1,0},{2,3},{3,2},{4,5},{5,4},{6,7},{7,6},{8,9},{9,8},{10,11... | collective-permute-start | bytes 7274504 | tf_op jit(solution)/shard_map/ppermute | solution.py:296
  126.1 29.8 %collective-permute-start.17 = (bf16[2,592,512]{2,1,0:T(8,128)(2,1)}, bf16[2,592,512]{2,1,0:T(8,128)(2,1)}, u32[]{:S(2)}, u32[]{:S(2)}) collective-permute-start(bf16[2,592,512]{2,1,0:T(8,128)(2,1)} %get-tuple-element.12), channel_id=1, source_target_pairs={{0,2},{2,0},{4,6},{6,4},{8,10},{10,8},{12,14},{14,12},{1,3},{3,1},... | collective-permute-start | bytes 3637256 | tf_op jit(solution)/shard_map/ppermute | solution.py:290
  131.3 26.8 %collective-permute-start.14 = (bf16[2,592,512]{2,1,0:T(8,128)(2,1)}, bf16[2,592,512]{2,1,0:T(8,128)(2,1)}, u32[]{:S(2)}, u32[]{:S(2)}) collective-permute-start(bf16[2,592,512]{2,1,0:T(8,128)(2,1)} %get-tuple-element.11.rest_2_.rest_8_), channel_id=1, source_target_pairs={{0,1},{1,0},{2,3},{3,2},{4,5},{5,4},{6,7},{7,6},{8,9},{9,8},{10,11... | collective-permute-start | bytes 3637256 | tf_op jit(solution)/shard_map/ppermute | solution.py:296
  155.9 3.5 %collective-permute-start.16 = (bf16[2,592,512]{2,1,0:T(8,128)(2,1)}, bf16[2,592,512]{2,1,0:T(8,128)(2,1)}, u32[]{:S(2)}, u32[]{:S(2)}) collective-permute-start(bf16[2,592,512]{2,1,0:T(8,128)(2,1)} %collective-permute-done.15.rest_4_), channel_id=1, source_target_pairs={{0,1},{1,0},{2,3},{3,2},{4,5},{5,4},{6,7},{7,6},{8,9},{9,8},{10,11... | collective-permute-start | bytes 3637256 | tf_op jit(solution)/shard_map/ppermute | solution.py:296
  155.9 5.0 %collective-permute-start.18 = (bf16[2,592,512]{2,1,0:T(8,128)(2,1)}, bf16[2,592,512]{2,1,0:T(8,128)(2,1)}, u32[]{:S(2)}, u32[]{:S(2)}) collective-permute-start(bf16[2,592,512]{2,1,0:T(8,128)(2,1)} %collective-permute-done.17.rest_6_), channel_id=1, source_target_pairs={{0,1},{1,0},{2,3},{3,2},{4,5},{5,4},{6,7},{7,6},{8,9},{9,8},{10,11... | collective-permute-start | bytes 3637256 | tf_op jit(solution)/shard_map/ppermute | solution.py:296
  156.4 23.8 %collective-permute-start.11 = (bf16[2,592,512]{2,1,0:T(8,128)(2,1)}, bf16[2,592,512]{2,1,0:T(8,128)(2,1)}, u32[]{:S(2)}, u32[]{:S(2)}) collective-permute-start(bf16[2,592,512]{2,1,0:T(8,128)(2,1)} %get-tuple-element.10), channel_id=1, source_target_pairs={{4,6},{6,4},{8,10},{10,8},{5,7},{7,5},{9,11},{11,9},{20,22},{22,20... | collective-permute-start | bytes 3637256 | tf_op jit(solution)/shard_map/ppermute | solution.py:293
  158.1 35.8 %collective-permute-start.20 = (bf16[2,592,512]{2,1,0:T(8,128)(2,1)}, bf16[2,592,512]{2,1,0:T(8,128)(2,1)}, u32[]{:S(2)}, u32[]{:S(2)}) collective-permute-start(bf16[2,592,512]{2,1,0:T(8,128)(2,1)} %collective-permute-done.17.rest_6_), channel_id=1, source_target_pairs={{4,0},{6,2},{8,12},{10,14},{5,1},{7,3},{9,13},{11,15},{20,16},{22,... | collective-permute-start | bytes 3637256 | tf_op jit(solution)/shard_map/ppermute | solution.py:414
  180.2 13.7 %collective-permute-start.19 = (bf16[2,592,512]{2,1,0:T(8,128)(2,1)}, bf16[2,592,512]{2,1,0:T(8,128)(2,1)}, u32[]{:S(2)}, u32[]{:S(2)}) collective-permute-start(bf16[2,592,512]{2,1,0:T(8,128)(2,1)} %tie.12.rest_0_), channel_id=1, source_target_pairs={{0,1},{1,0},{2,3},{3,2},{4,5},{5,4},{6,7},{7,6},{8,9},{9,8},{10,11... | collective-permute-start | bytes 3637256 | tf_op jit(solution)/shard_map/ppermute | solution.py:296
  193.9 3.2 %collective-permute-start.21 = (bf16[2,592,512]{2,1,0:T(8,128)(2,1)}, bf16[2,592,512]{2,1,0:T(8,128)(2,1)}, u32[]{:S(2)}, u32[]{:S(2)}) collective-permute-start(bf16[2,592,512]{2,1,0:T(8,128)(2,1)} %tie.13.rest_2_), channel_id=1, source_target_pairs={{0,1},{1,0},{2,3},{3,2},{4,5},{5,4},{6,7},{7,6},{8,9},{9,8},{10,11... | collective-permute-start | bytes 3637256 | tf_op jit(solution)/shard_map/ppermute | solution.py:296

commit v11 on v10

--- a/solution.py
+++ b/solution.py
@@ -341,7 +341,7 @@
     which_col = jnp.where(dist == 0, 3, jnp.where((dist == 1) & from_up, 2, jnp.where(is_far, 2, 1)))
     at_end = (z == 0) | (z == last)
     is_early = at_end & (dist == last - 1)
-    which = jnp.where(is_opp == 1, jnp.where(is_early, 3, is_far.astype(i32)), which_col)
+    which = jnp.where(is_opp == 1, jnp.where(is_early, 3, (dist == last - 1).astype(i32)), which_col)
     stage_col = jnp.where(is_far, last - 2, jnp.maximum(dist - 1, 0))
     stage = jnp.where(is_opp == 1, jnp.minimum(dist, last - 1) - is_early.astype(i32), stage_col)
     rows = jnp.arange(own_rows, dtype=i32)
@@ -437,7 +437,7 @@
                 sets[d - 1] += [with_other(far_a), with_other(over)]
             out = pairs_at(d - 1, [mine], out)
         opp = across_y(theirs) if d + 1 < last else across_y_inside(theirs)
-    sets[last - 1] = [with_other(tie(opp, [out])), with_other(tie(far_b, [out]))]
+    sets[last - 1] = [with_other(tie(far_b, [out])), with_other(tie(opp, [out]))]
     return pairs_at(last - 1, [], out)
 
 

time: 207 us -> 207 us (level)
  the two profiles are of different devices: /device:TPU:0 before, /device:TPU:13 now
where the time goes in v11:
time: 207 us; the launch traced here: 204 us
  waiting for transfers between devices  89.7 us (43%)
  Pallas kernels  53.6 us (26%)
  starting transfers between devices  31.5 us (15%)
  other arithmetic  18.3 us (9%)
  local copies, waits for them, and re-layouts  8.31 us (4%)
  between operations  2.66 us (1%)
    pallas_call x3, Pallas kernels, run_pairs(): pl.pallas_call(functools.partial(pair_kernel, call, wins, len(sets), len(...  36.4 us
    ppermute x4, waiting for transfers between devices, across_y(): return lax.ppermute(a, 'orb', swap_y)  32 us
    ppermute x2, waiting for transfers between devices, hop_up(): lax.ppermute(a, 'orb', [(k, k + 2) for k in range(orb_count - 2) if k //...  19 us
    ppermute x1, waiting for transfers between devices, per_device(): far_a = lax.ppermute(load_own, 'orb', perm)  15.8 us
    pallas_call x4, Pallas kernels, copy_sets(): pl.pallas_call(functools.partial(set_kernel, len(arrays), len(after), siz...  13.8 us
    ppermute x1, waiting for transfers between devices, across_y_inside(): lax.ppermute(a, 'orb', [pair for pair in swap_y if 0 < pair[0] // 2 < last])  12.8 us
    another operation x6, other arithmetic, copy_sets(): jnp.stack([jnp.stack([jnp.asarray(w, jnp.int32) for w in which]), jnp.sta...  8.95 us
    ppermute x10, starting transfers between devices, across_aux(): return lax.ppermute(a, 'aux', swap_aux)  8.3 us
  transfers between devices with their start and end apart: 22, of which 9 were waited for; matrix products, arithmetic and copies ran while one was open for 13% of the time, Pallas kernels for 20%

profile of v11, /device:TPU:13, one launch (start us, length us, event | category | flops | bytes accessed | tf_op | source)
XLA Modules:
  0.0 204.0 jit_solution(16697977327041274555)
XLA Ops:
  0.0 3.4 %extend.1.refs_1_.rest_0_.own_ref.rest_6_ = bf16[4,592,512]{2,1,0:T(8,128)(2,1)} custom-call(bf16[4,576,512]{2,1,0:T(8,128)(2,1)} %blocks_ref.1, bf16[4,576]{1,0:T(4,128)(2,1)} %energy_ref.1), custom_call_target="tpu_custom_call" | custom-call | tf_op jit(solution)/shard_map/extend/pallas_call | solution.py:244
  3.4 0.7 collective-permute-start
  4.1 3.2 %collective-permute-start.7 = (bf16[4,592,512]{2,1,0:T(8,128)(2,1)}, bf16[4,592,512]{2,1,0:T(8,128)(2,1)}, u32[]{:S(2)}, u32[]{:S(2)}) collective-permute-start(bf16[4,592,512]{2,1,0:T(8,128)(2,1)} %extend.1.refs_1_.rest_0_.own_ref.rest_6_), channel_id=1, source_target_pairs={{0,4},{2,6},{4,8},{6,10},{8,12},{10,14},{1,5},{3,7},{5,9},{7,11},{... | collective-permute-start | bytes 7274504 | tf_op jit(solution)/shard_map/ppermute | solution.py:302
  7.3 3.6 %collective-permute-start.3 = (bf16[4,592,512]{2,1,0:T(8,128)(2,1)}, bf16[4,592,512]{2,1,0:T(8,128)(2,1)}, u32[]{:S(2)}, u32[]{:S(2)}) collective-permute-start(bf16[4,592,512]{2,1,0:T(8,128)(2,1)} %extend.1.refs_1_.rest_0_.own_ref.rest_6_), channel_id=1, source_target_pairs={{4,0},{6,2},{8,4},{10,6},{12,8},{14,10},{5,1},{7,3},{9,5},{11,7},{... | collective-permute-start | bytes 7274504 | tf_op jit(solution)/shard_map/ppermute | solution.py:299
  12.1 2.7 %collective-permute-done.1 = s32[32]{0:T(128)S(1)} collective-permute-done((s32[32]{0:T(128)}, s32[32]{0:T(128)S(1)}, u32[]{:S(2)}, u32[]{:S(2)}) %collective-permute-start.1) | collective-permute-done | bytes 160 | tf_op jit(solution)/shard_map/ppermute | solution.py:290
  15.1 0.7 fusion.8
  15.7 0.7 fusion.9
  16.4 1.4 add_bitcast_fusion.1
  17.7 0.6 stack.116.table_ref
  18.3 2.8 %copy_sets.4.refs_1_ = bf16[2,592,512]{2,1,0:T(8,128)(2,1)} custom-call(s32[2,2]{1,0:T(2,128)} %stack.116.table_ref, bf16[4,592,512]{2,1,0:T(8,128)(2,1)} %extend.1.refs_1_.rest_0_.own_ref.rest_6_), custom_call_target="tpu_custom_call" | custom-call | tf_op jit(solution)/shard_map/copy_sets/pallas_call | solution.py:202
  22.1 0.6 stack.106.refs_4_.meta_ref
  22.7 25.8 %collective-permute-done.4.rest_0_ = bf16[2,592,512]{2,1,0:T(8,128)(2,1)} collective-permute-done((bf16[2,592,512]{2,1,0:T(8,128)(2,1)}, bf16[2,592,512]{2,1,0:T(8,128)(2,1)}, u32[]{:S(2)}, u32[]{:S(2)}) %collective-permute-start.4) | collective-permute-done | bytes 1212448 | tf_op jit(solution)/shard_map/ppermute | solution.py:290
  48.5 2.1 %collective-permute-start.5 = (bf16[2,592,512]{2,1,0:T(8,128)(2,1)}, bf16[2,592,512]{2,1,0:T(8,128)(2,1)}, u32[]{:S(2)}, u32[]{:S(2)}) collective-permute-start(bf16[2,592,512]{2,1,0:T(8,128)(2,1)} %collective-permute-done.4.rest_0_), channel_id=1, source_target_pairs={{0,1},{1,0},{2,3},{3,2},{4,5},{5,4},{6,7},{7,6},{8,9},{9,8},{10,11... | collective-permute-start | bytes 3637256 | tf_op jit(solution)/shard_map/ppermute | solution.py:296
  50.7 5.7 %fusion.refs_3_.pick_ref = bf16[16,2,512,256]{3,2,1,0:T(8,128)(2,1)} fusion(s32[16,2,512]{2,1,0:T(2,128)S(1)} %dynamic-slice_add_fusion), kind=kLoop, calls=%fused_computation.1 | loop fusion | flops 8388608 | bytes 8454144 | tf_op jit(solution)/shard_map/convert_element_type | solution.py:371
  56.4 0.6 pad_add_fusion.refs_0_
  57.0 1.3 collective-permute-start.2
  58.3 2.6 %add_bitcast_fusion.3 = s32[1,4]{1,0:T(1,128)S(1)} fusion(s32[1]{0:T(128)} %get-tuple-element.40, s32[1]{0:T(128)} %get-tuple-element.35, s32[1]{0:T(128)} %get-tuple-element.41, s32[1]{0:T(128)} %get-tuple-element.36), kind=kLoop, calls=%fused_computation.65 | loop fusion | flops 12 | bytes 32 | tf_op jit(solution)/shard_map/stack | solution.py:200
  61.4 4.6 %collective-permute-start.8 = (bf16[4,592,512]{2,1,0:T(8,128)(2,1)}, bf16[4,592,512]{2,1,0:T(8,128)(2,1)}, u32[]{:S(2)}, u32[]{:S(2)}) collective-permute-start(bf16[4,592,512]{2,1,0:T(8,128)(2,1)} %tie.10.rest_1_.rest_4_), channel_id=1, source_target_pairs={{4,8},{6,10},{8,12},{10,14},{5,9},{7,11},{9,13},{11,15},{20,24},{2... | collective-permute-start | bytes 7274504 | tf_op jit(solution)/shard_map/ppermute | solution.py:302
  66.3 1.9 collective-permute-start.6
  68.8 3.9 %copy_sets.5.rest_8_ = bf16[4,592,512]{2,1,0:T(8,128)(2,1)} custom-call(s32[2,4]{1,0:T(2,128)} %pad_add_fusion.2.table_ref, bf16[4,592,512]{2,1,0:T(8,128)(2,1)} %tie.9.rest_0_.rest_2_, bf16[4,592,512]{2,1,0:T(8,128)(2,1)} %tie.10.rest_1_.rest_4_), custom_call_target="tpu_custom_call" | custom-call | tf_op jit(solution)/shard_map/copy_sets/pallas_call | solution.py:202
  73.0 0.7 dynamic_slice.79
  73.7 0.7 dynamic_slice.80
  75.5 0.6 dynamic_slice.68
  76.1 0.6 dynamic_slice.70
  77.6 0.6 dynamic_slice.72
  80.5 1.2 add_bitcast_fusion
  82.3 0.9 broadcast_in_dim.141.ve1_ref
  83.3 14.7 %pairs_0.1.rest_2_.rest_9_ = bf16[16,512,512]{2,1,0:T(8,128)(2,1)} custom-call(s32[5,16]{1,0:T(8,128)} %stack.106.refs_4_.meta_ref, f32[16]{0:T(128)} %add.80.shift_ref, bf16[2,576,128]{2,1,0:T(8,128)(2,1)} %broadcast_in_dim.141.ve1_ref, bf16[16,2,512,256]{3,2,1,0:T(8,128)(2,1)} %fusion.refs_3_.pick_ref, ...), custom_call_target="tpu_custom_call" | custom-call | tf_op jit(solution)/shard_map/pairs_0/pallas_call | solution.py:152
  98.0 19.0 %collective-permute-done.8.rest_1_ = bf16[4,592,512]{2,1,0:T(8,128)(2,1)} collective-permute-done((bf16[4,592,512]{2,1,0:T(8,128)(2,1)}, bf16[4,592,512]{2,1,0:T(8,128)(2,1)}, u32[]{:S(2)}, u32[]{:S(2)}) %collective-permute-start.8) | collective-permute-done | bytes 2424864 | tf_op jit(solution)/shard_map/ppermute | solution.py:302
  116.9 5.6 %collective-permute-done.6.rest_0_ = bf16[4,592,512]{2,1,0:T(8,128)(2,1)} collective-permute-done((bf16[4,592,512]{2,1,0:T(8,128)(2,1)}, bf16[4,592,512]{2,1,0:T(8,128)(2,1)}, u32[]{:S(2)}, u32[]{:S(2)}) %collective-permute-start.6) | collective-permute-done | bytes 2424864 | tf_op jit(solution)/shard_map/ppermute | solution.py:299
  122.5 3.3 %copy_sets.6 = (bf16[2,592,512]{2,1,0:T(8,128)(2,1)}, bf16[2,592,512]{2,1,0:T(8,128)(2,1)}) custom-call(s32[2,4]{1,0:T(2,128)} %pad_add_fusion.1.table_ref, bf16[4,592,512]{2,1,0:T(8,128)(2,1)} %collective-permute-done.6.rest_0_, bf16[4,592,512]{2,1,0:T(8,128)(2,1)} %collective-permute-done.8.rest_1_, bf16[16,512,512]{2,1,0:T(8,128)(2,1)} %pairs_0.1.rest_2_.rest_9_), custom_call_target="tpu_custom_call" | custom-call | tf_op jit(solution)/shard_map/copy_sets/pallas_call | solution.py:202
  125.9 3.3 %collective-permute-start.16 = (bf16[2,592,512]{2,1,0:T(8,128)(2,1)}, bf16[2,592,512]{2,1,0:T(8,128)(2,1)}, u32[]{:S(2)}, u32[]{:S(2)}) collective-permute-start(bf16[2,592,512]{2,1,0:T(8,128)(2,1)} %get-tuple-element.10.refs_1_.rest_2_), channel_id=1, source_target_pairs={{4,0},{6,2},{8,12},{10,14},{5,1},{7,3},{9,13},{11,15},{20,16},{22,... | collective-permute-start | bytes 3637256 | tf_op jit(solution)/shard_map/ppermute | solution.py:415
  129.1 1.0 collective-permute-start.14
  130.4 2.7 %add_bitcast_fusion.4 = s32[1,4]{1,0:T(1,128)S(1)} fusion(s32[1]{0:T(128)} %dynamic_slice.80, s32[1]{0:T(128)} %dynamic_slice.79, s32[1]{0:T(128)} %get-tuple-element.39, s32[1]{0:T(128)} %get-tuple-element.34), kind=kLoop, calls=%fused_computation.66 | loop fusion | flops 12 | bytes 32 | tf_op jit(solution)/shard_map/stack | solution.py:200
  133.1 0.6 stack.127.table_ref
  133.7 3.8 %copy_sets.7 = (bf16[2,592,512]{2,1,0:T(8,128)(2,1)}, bf16[2,592,512]{2,1,0:T(8,128)(2,1)}) custom-call(s32[2,4]{1,0:T(2,128)} %stack.127.table_ref, bf16[4,592,512]{2,1,0:T(8,128)(2,1)} %collective-permute-done.6.rest_0_, bf16[4,592,512]{2,1,0:T(8,128)(2,1)} %collective-permute-done.8.rest_1_, bf16[2,592,512]{2,1,0:T(8,128)(2,1)} %get-tuple-element.10.refs_1_.rest_2_), custom_call_target="tpu_custom_call" | custom-call | tf_op jit(solution)/shard_map/copy_sets/pallas_call | solution.py:202
  137.8 15.8 %collective-permute-done.16.rest_4_ = bf16[2,592,512]{2,1,0:T(8,128)(2,1)} collective-permute-done((bf16[2,592,512]{2,1,0:T(8,128)(2,1)}, bf16[2,592,512]{2,1,0:T(8,128)(2,1)}, u32[]{:S(2)}, u32[]{:S(2)}) %collective-permute-start.16) | collective-permute-done | bytes 1212448 | tf_op jit(solution)/shard_map/ppermute | solution.py:415
  153.6 1.6 collective-permute-start.17
  155.2 3.5 %collective-permute-done.11.rest_6_ = bf16[2,592,512]{2,1,0:T(8,128)(2,1)} collective-permute-done((bf16[2,592,512]{2,1,0:T(8,128)(2,1)}, bf16[2,592,512]{2,1,0:T(8,128)(2,1)}, u32[]{:S(2)}, u32[]{:S(2)}) %collective-permute-start.11) | collective-permute-done | bytes 1212448 | tf_op jit(solution)/shard_map/ppermute | solution.py:290
  158.8 0.8 collective-permute-start.18
  159.6 2.1 %collective-permute-start.20 = (bf16[2,592,512]{2,1,0:T(8,128)(2,1)}, bf16[2,592,512]{2,1,0:T(8,128)(2,1)}, u32[]{:S(2)}, u32[]{:S(2)}) collective-permute-start(bf16[2,592,512]{2,1,0:T(8,128)(2,1)} %get-tuple-element.12), channel_id=1, source_target_pairs={{4,6},{6,4},{8,10},{10,8},{5,7},{7,5},{9,11},{11,9},{20,22},{22,20... | collective-permute-start | bytes 3637256 | tf_op jit(solution)/shard_map/ppermute | solution.py:293
  161.7 2.4 %collective-permute-start.12 = (bf16[2,592,512]{2,1,0:T(8,128)(2,1)}, bf16[2,592,512]{2,1,0:T(8,128)(2,1)}, u32[]{:S(2)}, u32[]{:S(2)}) collective-permute-start(bf16[2,592,512]{2,1,0:T(8,128)(2,1)} %collective-permute-done.11.rest_6_), channel_id=1, source_target_pairs={{4,0},{6,2},{8,12},{10,14},{5,1},{7,3},{9,13},{11,15},{20,16},{22,... | collective-permute-start | bytes 3637256 | tf_op jit(solution)/shard_map/ppermute | solution.py:414
  164.1 13.2 %pairs_1.1.refs_1_.rest_4_ = bf16[16,512,512]{2,1,0:T(8,128)(2,1)} custom-call(s32[5,16]{1,0:T(8,128)} %stack.106.refs_4_.meta_ref, f32[16]{0:T(128)} %add.80.shift_ref, bf16[2,576,128]{2,1,0:T(8,128)(2,1)} %broadcast_in_dim.141.ve1_ref, bf16[16,2,512,256]{3,2,1,0:T(8,128)(2,1)} %fusion.refs_3_.pick_ref, ...), custom_call_target="tpu_custom_call", output_to_operand_aliasing={{}: (15, {})} | custom-call | tf_op jit(solution)/shard_map/pairs_1/pallas_call | solution.py:152
  177.3 12.8 %collective-permute-done.20.refs_0_ = bf16[2,592,512]{2,1,0:T(8,128)(2,1)} collective-permute-done((bf16[2,592,512]{2,1,0:T(8,128)(2,1)}, bf16[2,592,512]{2,1,0:T(8,128)(2,1)}, u32[]{:S(2)}, u32[]{:S(2)}) %collective-permute-start.20) | collective-permute-done | bytes 1212448 | tf_op jit(solution)/shard_map/ppermute | solution.py:293
  190.1 0.8 collective-permute-start.21
  190.9 2.8 %collective-permute-done.21.rest_3_ = bf16[2,592,512]{2,1,0:T(8,128)(2,1)} collective-permute-done((bf16[2,592,512]{2,1,0:T(8,128)(2,1)}, bf16[2,592,512]{2,1,0:T(8,128)(2,1)}, u32[]{:S(2)}, u32[]{:S(2)}) %collective-permute-start.21) | collective-permute-done | bytes 1212448 | tf_op jit(solution)/shard_map/ppermute | solution.py:296
  193.7 1.7 collective-permute-done.19.rest_1_
  195.4 8.5 %pairs_2.1 = bf16[16,512,512]{2,1,0:T(8,128)(2,1)} custom-call(s32[5,16]{1,0:T(8,128)} %stack.106.refs_4_.meta_ref, f32[16]{0:T(128)} %add.80.shift_ref, bf16[2,576,128]{2,1,0:T(8,128)(2,1)} %broadcast_in_dim.141.ve1_ref, bf16[16,2,512,256]{3,2,1,0:T(8,128)(2,1)} %fusion.refs_3_.pick_ref, ...), custom_call_target="tpu_custom_call", output_to_operand_aliasing={{}: (10, {})} | custom-call | tf_op jit(solution)/shard_map/pairs_2/pallas_call | solution.py:152
  (78 shorter events, 7.3 us)
Async XLA Ops:
  0.0 10.9 %copy-start.4 = (s32[32,2]{0,1:T(2,128)S(1)}, s32[32,2]{0,1:T(2,128)}, u32[]{:S(2)}) copy-start(s32[32,2]{0,1:T(2,128)} %param.10) | copy-start | bytes 772
  0.0 10.9 %copy-start.7 = (s32[32]{0:T(128)S(1)}, s32[32]{0:T(128)}, u32[]{:S(2)}) copy-start(s32[32]{0:T(128)} %param.9) | copy-start | bytes 388
  3.4 57.5 %collective-permute-start = (bf16[4,592,512]{2,1,0:T(8,128)(2,1)}, bf16[4,592,512]{2,1,0:T(8,128)(2,1)}, u32[]{:S(2)}, u32[]{:S(2)}) collective-permute-start(bf16[4,592,512]{2,1,0:T(8,128)(2,1)} %extend.1.refs_1_.rest_0_.own_ref.rest_6_), channel_id=1, source_target_pairs={{0,1},{1,0},{2,3},{3,2},{4,5},{5,4},{6,7},{7,6},{8,9},{9,8},{10,11... | collective-permute-start | bytes 7274504 | tf_op jit(solution)/shard_map/ppermute | solution.py:296
  4.1 56.7 %collective-permute-start.7 = (bf16[4,592,512]{2,1,0:T(8,128)(2,1)}, bf16[4,592,512]{2,1,0:T(8,128)(2,1)}, u32[]{:S(2)}, u32[]{:S(2)}) collective-permute-start(bf16[4,592,512]{2,1,0:T(8,128)(2,1)} %extend.1.refs_1_.rest_0_.own_ref.rest_6_), channel_id=1, source_target_pairs={{0,4},{2,6},{4,8},{6,10},{8,12},{10,14},{1,5},{3,7},{5,9},{7,11},{... | collective-permute-start | bytes 7274504 | tf_op jit(solution)/shard_map/ppermute | solution.py:302
  7.3 58.7 %collective-permute-start.3 = (bf16[4,592,512]{2,1,0:T(8,128)(2,1)}, bf16[4,592,512]{2,1,0:T(8,128)(2,1)}, u32[]{:S(2)}, u32[]{:S(2)}) collective-permute-start(bf16[4,592,512]{2,1,0:T(8,128)(2,1)} %extend.1.refs_1_.rest_0_.own_ref.rest_6_), channel_id=1, source_target_pairs={{4,0},{6,2},{8,4},{10,6},{12,8},{14,10},{5,1},{7,3},{9,5},{11,7},{... | collective-permute-start | bytes 7274504 | tf_op jit(solution)/shard_map/ppermute | solution.py:299
  11.8 38.8 %copy-start = (s32[32,2,512]{2,1,0:T(2,128)S(1)}, s32[32,2,512]{2,1,0:T(2,128)}, u32[]{:S(2)}) copy-start(s32[32,2,512]{2,1,0:T(2,128)} %param.11) | copy-start | bytes 393220
  11.8 38.8 %copy-start.2 = (s32[512]{0:T(512)S(1)}, s32[512]{0:T(512)}, u32[]{:S(2)}) copy-start(s32[512]{0:T(512)} %constant.146.clone.1) | copy-start | bytes 6148
  11.8 3.0 %collective-permute-start.1 = (s32[32]{0:T(128)}, s32[32]{0:T(128)S(1)}, u32[]{:S(2)}, u32[]{:S(2)}) collective-permute-start(s32[32]{0:T(128)} %tie.7), channel_id=1, source_target_pairs={{0,2},{2,0},{4,6},{6,4},{8,10},{10,8},{12,14},{14,12},{1,3},{3,1},... | collective-permute-start | bytes 392 | tf_op jit(solution)/shard_map/ppermute | solution.py:290
  21.1 27.4 %collective-permute-start.4 = (bf16[2,592,512]{2,1,0:T(8,128)(2,1)}, bf16[2,592,512]{2,1,0:T(8,128)(2,1)}, u32[]{:S(2)}, u32[]{:S(2)}) collective-permute-start(bf16[2,592,512]{2,1,0:T(8,128)(2,1)} %copy_sets.4.refs_1_), channel_id=1, source_target_pairs={{0,2},{2,0},{4,6},{6,4},{8,10},{10,8},{12,14},{14,12},{1,3},{3,1},... | collective-permute-start | bytes 3637256 | tf_op jit(solution)/shard_map/ppermute | solution.py:290
  48.5 12.3 %collective-permute-start.5 = (bf16[2,592,512]{2,1,0:T(8,128)(2,1)}, bf16[2,592,512]{2,1,0:T(8,128)(2,1)}, u32[]{:S(2)}, u32[]{:S(2)}) collective-permute-start(bf16[2,592,512]{2,1,0:T(8,128)(2,1)} %collective-permute-done.4.rest_0_), channel_id=1, source_target_pairs={{0,1},{1,0},{2,3},{3,2},{4,5},{5,4},{6,7},{7,6},{8,9},{9,8},{10,11... | collective-permute-start | bytes 3637256 | tf_op jit(solution)/shard_map/ppermute | solution.py:296
  50.7 5.7 %copy-start.3 = (s32[32]{0:T(128)S(1)}, s32[32]{0:T(128)}, u32[]{:S(2)}) copy-start(s32[32]{0:T(128)} %tie.7) | copy-start | bytes 388
  57.0 15.7 %collective-permute-start.2 = (s32[2,32]{1,0:T(2,128)}, s32[2,32]{1,0:T(2,128)S(1)}, u32[]{:S(2)}, u32[]{:S(2)}) collective-permute-start(s32[2,32]{1,0:T(2,128)} %tie.8), channel_id=1, source_target_pairs={{0,4},{2,6},{14,10},{12,8},{1,5},{3,7},{15,11},{13,9},{16,20},{18,... | collective-permute-start | bytes 776 | tf_op jit(solution)/shard_map/ppermute | solution.py:391
  60.9 7.3 %copy-start.6 = (s32[1,4]{1,0:T(1,128)S(1)}, s32[1,4]{1,0:T(1,128)}, u32[]{:S(2)}) copy-start(s32[1,4]{1,0:T(1,128)} %constant.152.clone.1) | copy-start | bytes 52
  60.9 21.4 %collective-permute-start.10 = (bf16[4,592,512]{2,1,0:T(8,128)(2,1)}, bf16[4,592,512]{2,1,0:T(8,128)(2,1)}, u32[]{:S(2)}, u32[]{:S(2)}) collective-permute-start(bf16[4,592,512]{2,1,0:T(8,128)(2,1)} %tie.10.rest_1_.rest_4_), channel_id=1, source_target_pairs={{0,1},{1,0},{2,3},{3,2},{4,5},{5,4},{6,7},{7,6},{8,9},{9,8},{10,11... | collective-permute-start | bytes 7274504 | tf_op jit(solution)/shard_map/ppermute | solution.py:296
  61.4 55.6 %collective-permute-start.8 = (bf16[4,592,512]{2,1,0:T(8,128)(2,1)}, bf16[4,592,512]{2,1,0:T(8,128)(2,1)}, u32[]{:S(2)}, u32[]{:S(2)}) collective-permute-start(bf16[4,592,512]{2,1,0:T(8,128)(2,1)} %tie.10.rest_1_.rest_4_), channel_id=1, source_target_pairs={{4,8},{6,10},{8,12},{10,14},{5,9},{7,11},{9,13},{11,15},{20,24},{2... | collective-permute-start | bytes 7274504 | tf_op jit(solution)/shard_map/ppermute | solution.py:302
  66.0 16.3 %collective-permute-start.9 = (bf16[4,592,512]{2,1,0:T(8,128)(2,1)}, bf16[4,592,512]{2,1,0:T(8,128)(2,1)}, u32[]{:S(2)}, u32[]{:S(2)}) collective-permute-start(bf16[4,592,512]{2,1,0:T(8,128)(2,1)} %tie.9.rest_0_.rest_2_), channel_id=1, source_target_pairs={{0,1},{1,0},{2,3},{3,2},{4,5},{5,4},{6,7},{7,6},{8,9},{9,8},{10,11... | collective-permute-start | bytes 7274504 | tf_op jit(solution)/shard_map/ppermute | solution.py:296
  66.3 56.3 %collective-permute-start.6 = (bf16[4,592,512]{2,1,0:T(8,128)(2,1)}, bf16[4,592,512]{2,1,0:T(8,128)(2,1)}, u32[]{:S(2)}, u32[]{:S(2)}) collective-permute-start(bf16[4,592,512]{2,1,0:T(8,128)(2,1)} %tie.9.rest_0_.rest_2_), channel_id=1, source_target_pairs={{4,0},{6,2},{8,4},{10,6},{5,1},{7,3},{9,5},{11,7},{20,16},{22,18},... | collective-permute-start | bytes 7274504 | tf_op jit(solution)/shard_map/ppermute | solution.py:299
  68.8 5.7 %copy-start.5 = (f32[32]{0:T(128)S(1)}, f32[32]{0:T(128)}, u32[]{:S(2)}) copy-start(f32[32]{0:T(128)} %param.8) | copy-start | bytes 388
  68.8 6.4 %copy-start.1 = (bf16[4,576]{1,0:T(4,128)(2,1)S(1)}, bf16[4,576]{1,0:T(4,128)(2,1)}, u32[]{:S(2)}) copy-start(bf16[4,576]{1,0:T(4,128)(2,1)} %energy_ref.1) | copy-start | bytes 13828
  72.7 56.4 %collective-permute-start.13 = (bf16[4,592,512]{2,1,0:T(8,128)(2,1)}, bf16[4,592,512]{2,1,0:T(8,128)(2,1)}, u32[]{:S(2)}, u32[]{:S(2)}) collective-permute-start(bf16[4,592,512]{2,1,0:T(8,128)(2,1)} %copy_sets.5.rest_8_), channel_id=1, source_target_pairs={{0,2},{2,0},{4,6},{6,4},{8,10},{10,8},{12,14},{14,12},{1,3},{3,1},... | collective-permute-start | bytes 7274504 | tf_op jit(solution)/shard_map/ppermute | solution.py:290
  125.9 27.7 %collective-permute-start.16 = (bf16[2,592,512]{2,1,0:T(8,128)(2,1)}, bf16[2,592,512]{2,1,0:T(8,128)(2,1)}, u32[]{:S(2)}, u32[]{:S(2)}) collective-permute-start(bf16[2,592,512]{2,1,0:T(8,128)(2,1)} %get-tuple-element.10.refs_1_.rest_2_), channel_id=1, source_target_pairs={{4,0},{6,2},{8,12},{10,14},{5,1},{7,3},{9,13},{11,15},{20,16},{22,... | collective-permute-start | bytes 3637256 | tf_op jit(solution)/shard_map/ppermute | solution.py:415
  129.1 35.0 %collective-permute-start.14 = (bf16[4,592,512]{2,1,0:T(8,128)(2,1)}, bf16[4,592,512]{2,1,0:T(8,128)(2,1)}, u32[]{:S(2)}, u32[]{:S(2)}) collective-permute-start(bf16[4,592,512]{2,1,0:T(8,128)(2,1)} %tie.11.rest_0_), channel_id=1, source_target_pairs={{0,1},{1,0},{2,3},{3,2},{4,5},{5,4},{6,7},{7,6},{8,9},{9,8},{10,11... | collective-permute-start | bytes 7274504 | tf_op jit(solution)/shard_map/ppermute | solution.py:296
  130.2 28.6 %collective-permute-start.11 = (bf16[2,592,512]{2,1,0:T(8,128)(2,1)}, bf16[2,592,512]{2,1,0:T(8,128)(2,1)}, u32[]{:S(2)}, u32[]{:S(2)}) collective-permute-start(bf16[2,592,512]{2,1,0:T(8,128)(2,1)} %get-tuple-element.9), channel_id=1, source_target_pairs={{0,2},{2,0},{4,6},{6,4},{8,10},{10,8},{12,14},{14,12},{1,3},{3,1},... | collective-permute-start | bytes 3637256 | tf_op jit(solution)/shard_map/ppermute | solution.py:290
  137.5 24.2 %collective-permute-start.15 = (bf16[2,592,512]{2,1,0:T(8,128)(2,1)}, bf16[2,592,512]{2,1,0:T(8,128)(2,1)}, u32[]{:S(2)}, u32[]{:S(2)}) collective-permute-start(bf16[2,592,512]{2,1,0:T(8,128)(2,1)} %get-tuple-element.11.rest_2_.rest_8_), channel_id=1, source_target_pairs={{0,1},{1,0},{2,3},{3,2},{4,5},{5,4},{6,7},{7,6},{8,9},{9,8},{10,11... | collective-permute-start | bytes 3637256 | tf_op jit(solution)/shard_map/ppermute | solution.py:296
  153.6 10.5 %collective-permute-start.17 = (bf16[2,592,512]{2,1,0:T(8,128)(2,1)}, bf16[2,592,512]{2,1,0:T(8,128)(2,1)}, u32[]{:S(2)}, u32[]{:S(2)}) collective-permute-start(bf16[2,592,512]{2,1,0:T(8,128)(2,1)} %collective-permute-done.16.rest_4_), channel_id=1, source_target_pairs={{0,1},{1,0},{2,3},{3,2},{4,5},{5,4},{6,7},{7,6},{8,9},{9,8},{10,11... | collective-permute-start | bytes 3637256 | tf_op jit(solution)/shard_map/ppermute | solution.py:296
  158.8 5.4 %collective-permute-start.18 = (bf16[2,592,512]{2,1,0:T(8,128)(2,1)}, bf16[2,592,512]{2,1,0:T(8,128)(2,1)}, u32[]{:S(2)}, u32[]{:S(2)}) collective-permute-start(bf16[2,592,512]{2,1,0:T(8,128)(2,1)} %collective-permute-done.11.rest_6_), channel_id=1, source_target_pairs={{0,1},{1,0},{2,3},{3,2},{4,5},{5,4},{6,7},{7,6},{8,9},{9,8},{10,11... | collective-permute-start | bytes 3637256 | tf_op jit(solution)/shard_map/ppermute | solution.py:296
  159.6 30.5 %collective-permute-start.20 = (bf16[2,592,512]{2,1,0:T(8,128)(2,1)}, bf16[2,592,512]{2,1,0:T(8,128)(2,1)}, u32[]{:S(2)}, u32[]{:S(2)}) collective-permute-start(bf16[2,592,512]{2,1,0:T(8,128)(2,1)} %get-tuple-element.12), channel_id=1, source_target_pairs={{4,6},{6,4},{8,10},{10,8},{5,7},{7,5},{9,11},{11,9},{20,22},{22,20... | collective-permute-start | bytes 3637256 | tf_op jit(solution)/shard_map/ppermute | solution.py:293
  161.7 29.1 %collective-permute-start.12 = (bf16[2,592,512]{2,1,0:T(8,128)(2,1)}, bf16[2,592,512]{2,1,0:T(8,128)(2,1)}, u32[]{:S(2)}, u32[]{:S(2)}) collective-permute-start(bf16[2,592,512]{2,1,0:T(8,128)(2,1)} %collective-permute-done.11.rest_6_), channel_id=1, source_target_pairs={{4,0},{6,2},{8,12},{10,14},{5,1},{7,3},{9,13},{11,15},{20,16},{22,... | collective-permute-start | bytes 3637256 | tf_op jit(solution)/shard_map/ppermute | solution.py:414
  190.1 3.6 %collective-permute-start.21 = (bf16[2,592,512]{2,1,0:T(8,128)(2,1)}, bf16[2,592,512]{2,1,0:T(8,128)(2,1)}, u32[]{:S(2)}, u32[]{:S(2)}) collective-permute-start(bf16[2,592,512]{2,1,0:T(8,128)(2,1)} %tie.13.rest_2_), channel_id=1, source_target_pairs={{0,1},{1,0},{2,3},{3,2},{4,5},{5,4},{6,7},{7,6},{8,9},{9,8},{10,11... | collective-permute-start | bytes 3637256 | tf_op jit(solution)/shard_map/ppermute | solution.py:296
  190.8 4.6 %collective-permute-start.19 = (bf16[2,592,512]{2,1,0:T(8,128)(2,1)}, bf16[2,592,512]{2,1,0:T(8,128)(2,1)}, u32[]{:S(2)}, u32[]{:S(2)}) collective-permute-start(bf16[2,592,512]{2,1,0:T(8,128)(2,1)} %tie.12.rest_0_), channel_id=1, source_target_pairs={{0,1},{1,0},{2,3},{3,2},{4,5},{5,4},{6,7},{7,6},{8,9},{9,8},{10,11... | collective-permute-start | bytes 3637256 | tf_op jit(solution)/shard_map/ppermute | solution.py:296

commit v12 on v10

--- a/solution.py
+++ b/solution.py
@@ -174,21 +174,30 @@
     )(*operands)
 
 
+def halves(rows):
+    cut = rows // 32 * 16
+    return [(0, cut), (cut, rows - cut)]
+
+
 def set_kernel(n_arrays, n_skip, sizes, table_ref, *rest):
     arrays = rest[:n_arrays]
     outs = rest[n_arrays + n_skip:-3]
     held, in_sems, out_sems = rest[-3:]
     places = [(o, k) for o, size in zip(outs, sizes) for k in range(size)]
+    cuts = [pl.ds(start, rows) for start, rows in halves(held.shape[1])]
     for j in range(len(places)):
         for k, a in enumerate(arrays):
             @pl.when(table_ref[0, j] == k)
             def _():
-                pltpu.make_async_copy(a.at[table_ref[1, j]], held.at[j], in_sems.at[j]).start()
+                for c, cut in enumerate(cuts):
+                    pltpu.make_async_copy(a.at[table_ref[1, j], cut], held.at[j, cut], in_sems.at[j, c]).start()
     for j, (o, k) in enumerate(places):
-        pltpu.make_async_copy(arrays[0].at[0], held.at[j], in_sems.at[j]).wait()
-        pltpu.make_async_copy(held.at[j], o.at[k], out_sems.at[j]).start()
+        for c, cut in enumerate(cuts):
+            pltpu.make_async_copy(arrays[0].at[0, cut], held.at[j, cut], in_sems.at[j, c]).wait()
+            pltpu.make_async_copy(held.at[j, cut], o.at[k, cut], out_sems.at[j, c]).start()
     for j, (o, k) in enumerate(places):
-        pltpu.make_async_copy(held.at[j], o.at[k], out_sems.at[j]).wait()
+        for c, cut in enumerate(cuts):
+            pltpu.make_async_copy(held.at[j, cut], o.at[k, cut], out_sems.at[j, c]).wait()
 
 
 ANY_SPEC = pl.BlockSpec(memory_space=pl.ANY)
@@ -206,8 +215,8 @@
         out_specs=[ANY_SPEC] * len(sizes),
         scratch_shapes=[
             pltpu.VMEM((n,) + block, arrays[0].dtype),
-            pltpu.SemaphoreType.DMA((n,)),
-            pltpu.SemaphoreType.DMA((n,))],
+            pltpu.SemaphoreType.DMA((n, 2)),
+            pltpu.SemaphoreType.DMA((n, 2))],
         cost_estimate=pl.CostEstimate(flops=0, bytes_accessed=0, transcendentals=0),
         compiler_params=pltpu.CompilerParams(vmem_limit_bytes=VMEM_LIMIT),
         name="copy_sets",
@@ -217,8 +226,19 @@
 
 def extend_kernel(wins, blocks_ref, energy_ref, out_ref, held, in_sems, out_sems):
     count, full, half = blocks_ref.shape
+    cuts = halves(full)
+
+    def arrive(k, c):
+        rows = pl.ds(*cuts[c])
+        return pltpu.make_async_copy(blocks_ref.at[k, rows], held.at[k, rows], in_sems.at[k, c])
+
+    def leave(k, c):
+        rows = pl.ds(cuts[c][0], cuts[c][1] + c * EXTRA)
+        return pltpu.make_async_copy(held.at[k, rows], out_ref.at[k, rows], out_sems.at[k, c])
+
     for k in range(count):
-        pltpu.make_async_copy(blocks_ref.at[k], held.at[k, 0:full], in_sems.at[k]).start()
+        for c in range(2):
+            arrive(k, c).start()
     energy = energy_ref[...].astype(jnp.float32)
     span = max(sp for _, _, sp in wins)
     row = lax.broadcasted_iota(jnp.int32, (EXTRA, span), 0)
@@ -232,10 +252,12 @@
             rows = jnp.where(row == t, jnp.broadcast_to(piece, (EXTRA, span)), rows)
         held[k, full:, 0:span] = rows.astype(held.dtype)
     for k in range(count):
-        pltpu.make_async_copy(blocks_ref.at[k], held.at[k, 0:full], in_sems.at[k]).wait()
-        pltpu.make_async_copy(held.at[k], out_ref.at[k], out_sems.at[k]).start()
+        for c in range(2):
+            arrive(k, c).wait()
+            leave(k, c).start()
     for k in range(count):
-        pltpu.make_async_copy(held.at[k], out_ref.at[k], out_sems.at[k]).wait()
+        for c in range(2):
+            leave(k, c).wait()
 
 
 def extend(blocks, energy, wins):
@@ -247,7 +269,7 @@
         in_specs=[ANY_SPEC, pl.BlockSpec(memory_space=pltpu.VMEM)],
         out_specs=ANY_SPEC,
         scratch_shapes=[
-            pltpu.VMEM(shape, blocks.dtype), pltpu.SemaphoreType.DMA((count,)), pltpu.SemaphoreType.DMA((count,))],
+            pltpu.VMEM(shape, blocks.dtype), pltpu.SemaphoreType.DMA((count, 2)), pltpu.SemaphoreType.DMA((count, 2))],
         compiler_params=pltpu.CompilerParams(vmem_limit_bytes=VMEM_LIMIT),
         name="extend",
     )(blocks, energy)

time: 207 us -> 207 us (level)
    ppermute x2, waiting for transfers between devices: 24.1 us -> 26.5 us  [hop_down(): lax.ppermute(a, 'orb', [(k, k - 2) for k in range(2, orb_count) if k // 2...]
  transfers between devices with their start and end apart: 22 -> 22, of which waited for: 8 -> 8; matrix products, arithmetic and copies ran while one was open for 13% -> 13% of each run, Pallas kernels for 21% -> 20%
where the time goes in v12:
time: 207 us; the launch traced here: 205 us
  waiting for transfers between devices  95.2 us (46%)
  Pallas kernels  53.2 us (26%)
  starting transfers between devices  27.7 us (13%)
  other arithmetic  18.3 us (9%)
  local copies, waits for them, and re-layouts  8.27 us (4%)
  between operations  2.58 us (1%)
    pallas_call x3, Pallas kernels, run_pairs(): pl.pallas_call(functools.partial(pair_kernel, call, wins, len(sets), len(...  36.7 us
    ppermute x4, waiting for transfers between devices, across_y(): return lax.ppermute(a, 'orb', swap_y)  28.8 us
    ppermute x2, waiting for transfers between devices, hop_down(): lax.ppermute(a, 'orb', [(k, k - 2) for k in range(2, orb_count) if k // 2...  26.5 us
    ppermute x1, waiting for transfers between devices, per_device(): far_a = lax.ppermute(load_own, 'orb', perm)  23.2 us
    pallas_call x4, Pallas kernels, copy_sets(): pl.pallas_call(functools.partial(set_kernel, len(arrays), len(after), siz...  13.1 us
    ppermute x1, waiting for transfers between devices, per_device(): far_b = lax.ppermute(over, 'orb', perm)  12 us
    another operation x6, other arithmetic, copy_sets(): jnp.stack([jnp.stack([jnp.asarray(w, jnp.int32) for w in which]), jnp.sta...  8.95 us
    ppermute x2, starting transfers between devices, hop_up(): lax.ppermute(a, 'orb', [(k, k + 2) for k in range(orb_count - 2) if k //...  8.64 us
  transfers between devices with their start and end apart: 22, of which 8 were waited for; matrix products, arithmetic and copies ran while one was open for 13% of the time, Pallas kernels for 20%

profile of v12, /device:TPU:0, one launch (start us, length us, event | category | flops | bytes accessed | tf_op | source)
XLA Modules:
  0.0 205.2 jit_solution(664392208795670858)
XLA Ops:
  0.0 3.3 %extend.1.refs_1_.rest_0_.own_ref.rest_6_ = bf16[4,592,512]{2,1,0:T(8,128)(2,1)} custom-call(bf16[4,576,512]{2,1,0:T(8,128)(2,1)} %blocks_ref.1, bf16[4,576]{1,0:T(4,128)(2,1)} %energy_ref.1), custom_call_target="tpu_custom_call" | custom-call | tf_op jit(solution)/shard_map/extend/pallas_call | solution.py:266
  3.9 1.3 collective-permute-start.2
  5.1 6.6 %collective-permute-start.6 = (bf16[4,592,512]{2,1,0:T(8,128)(2,1)}, bf16[4,592,512]{2,1,0:T(8,128)(2,1)}, u32[]{:S(2)}, u32[]{:S(2)}) collective-permute-start(bf16[4,592,512]{2,1,0:T(8,128)(2,1)} %extend.1.refs_1_.rest_0_.own_ref.rest_6_), channel_id=1, source_target_pairs={{0,4},{2,6},{4,8},{6,10},{8,12},{10,14},{1,5},{3,7},{5,9},{7,11},{... | collective-permute-start | bytes 7274504 | tf_op jit(solution)/shard_map/ppermute | solution.py:324
  12.0 0.6 convert_element_type.40.refs_0_
  12.6 2.0 collective-permute-start.1
  14.6 1.6 collective-permute-done.1
  16.5 0.7 fusion.8
  17.1 0.7 fusion.7
  17.8 1.4 add_bitcast_fusion.1
  19.1 0.6 stack.112.table_ref
  19.7 2.7 %copy_sets.4.refs_1_ = bf16[2,592,512]{2,1,0:T(8,128)(2,1)} custom-call(s32[2,2]{1,0:T(2,128)} %stack.112.table_ref, bf16[4,592,512]{2,1,0:T(8,128)(2,1)} %extend.1.refs_1_.rest_0_.own_ref.rest_6_), custom_call_target="tpu_custom_call" | custom-call | tf_op jit(solution)/shard_map/copy_sets/pallas_call | solution.py:211
  22.5 2.0 collective-permute-start.3
  25.2 0.6 stack.106.refs_4_.meta_ref
  25.8 25.3 %collective-permute-done.3.rest_0_ = bf16[2,592,512]{2,1,0:T(8,128)(2,1)} collective-permute-done((bf16[2,592,512]{2,1,0:T(8,128)(2,1)}, bf16[2,592,512]{2,1,0:T(8,128)(2,1)}, u32[]{:S(2)}, u32[]{:S(2)}) %collective-permute-start.3) | collective-permute-done | bytes 1212448 | tf_op jit(solution)/shard_map/ppermute | solution.py:312
  51.1 5.7 %fusion.refs_3_.pick_ref = bf16[16,2,512,256]{3,2,1,0:T(8,128)(2,1)} fusion(s32[16,2,512]{2,1,0:T(2,128)S(1)} %dynamic-slice_add_fusion), kind=kLoop, calls=%fused_computation.1 | loop fusion | flops 8388608 | bytes 8454144 | tf_op jit(solution)/shard_map/convert_element_type | solution.py:393
  56.8 0.6 pad_add_fusion.refs_0_
  57.4 2.2 %collective-permute-start.8 = (s32[2,32]{1,0:T(2,128)}, s32[2,32]{1,0:T(2,128)S(1)}, u32[]{:S(2)}, u32[]{:S(2)}) collective-permute-start(s32[2,32]{1,0:T(2,128)} %tie.10), channel_id=1, source_target_pairs={{0,4},{2,6},{14,10},{12,8},{1,5},{3,7},{15,11},{13,9},{16,20},{18,... | collective-permute-start | bytes 776 | tf_op jit(solution)/shard_map/ppermute | solution.py:413
  59.7 2.6 %add_bitcast_fusion.4 = s32[1,4]{1,0:T(1,128)S(1)} fusion(s32[1]{0:T(128)} %get-tuple-element.40, s32[1]{0:T(128)} %get-tuple-element.35, s32[1]{0:T(128)} %get-tuple-element.39, s32[1]{0:T(128)} %get-tuple-element.34), kind=kLoop, calls=%fused_computation.63 | loop fusion | flops 12 | bytes 32 | tf_op jit(solution)/shard_map/stack | solution.py:209
  62.3 1.3 collective-permute-start.5
  63.9 2.1 %collective-permute-start.7 = (bf16[4,592,512]{2,1,0:T(8,128)(2,1)}, bf16[4,592,512]{2,1,0:T(8,128)(2,1)}, u32[]{:S(2)}, u32[]{:S(2)}) collective-permute-start(bf16[4,592,512]{2,1,0:T(8,128)(2,1)} %tie.9.rest_1_.rest_4_), channel_id=1, source_target_pairs={{4,8},{6,10},{8,12},{10,14},{5,9},{7,11},{9,13},{11,15},{20,24},{2... | collective-permute-start | bytes 7274504 | tf_op jit(solution)/shard_map/ppermute | solution.py:324
  66.2 0.6 pad_add_fusion.2.table_ref
  66.8 3.3 %copy_sets.5.rest_8_ = bf16[4,592,512]{2,1,0:T(8,128)(2,1)} custom-call(s32[2,4]{1,0:T(2,128)} %pad_add_fusion.2.table_ref, bf16[4,592,512]{2,1,0:T(8,128)(2,1)} %tie.8.rest_0_.rest_2_, bf16[4,592,512]{2,1,0:T(8,128)(2,1)} %tie.9.rest_1_.rest_4_), custom_call_target="tpu_custom_call" | custom-call | tf_op jit(solution)/shard_map/copy_sets/pallas_call | solution.py:211
  70.2 2.2 %collective-permute-start.12 = (bf16[4,592,512]{2,1,0:T(8,128)(2,1)}, bf16[4,592,512]{2,1,0:T(8,128)(2,1)}, u32[]{:S(2)}, u32[]{:S(2)}) collective-permute-start(bf16[4,592,512]{2,1,0:T(8,128)(2,1)} %copy_sets.5.rest_8_), channel_id=1, source_target_pairs={{0,2},{2,0},{4,6},{6,4},{8,10},{10,8},{12,14},{14,12},{1,3},{3,1},... | collective-permute-start | bytes 7274504 | tf_op jit(solution)/shard_map/ppermute | solution.py:312
  72.6 0.6 dynamic_slice.68
  73.2 0.6 dynamic_slice.67
  74.1 0.6 add.80.shift_ref
  74.7 2.6 %add_bitcast_fusion = (s32[1,4]{1,0:T(1,128)S(1)}, s32[1,4]{1,0:T(1,128)S(1)}) fusion(s32[1]{0:T(128)} %dynamic_slice.68, s32[1]{0:T(128)} %dynamic_slice.67, s32[1]{0:T(128)} %get-tuple-element.43, s32[1]{0:T(128)} %get-tuple-element.38, s32[1]{0:T(128)} %bitcast.12, s32[1]{0:T(128)} %bitcast.11), kind=kLoop, calls=%fused_computation.59 | loop fusion | flops 24 | bytes 56 | tf_op jit(solution)/shard_map/stack | solution.py:209
  77.5 0.6 dynamic_slice.76
  78.1 0.6 dynamic_slice.75
  79.0 0.7 dynamic_slice.74
  82.6 1.3 add_bitcast_fusion.3
  84.5 0.9 broadcast_in_dim.141.ve1_ref
  85.4 7.3 %pairs_0.1.rest_2_.rest_9_ = bf16[16,512,512]{2,1,0:T(8,128)(2,1)} custom-call(s32[5,16]{1,0:T(8,128)} %stack.106.refs_4_.meta_ref, f32[16]{0:T(128)} %add.80.shift_ref, bf16[2,576,128]{2,1,0:T(8,128)(2,1)} %broadcast_in_dim.141.ve1_ref, bf16[16,2,512,256]{3,2,1,0:T(8,128)(2,1)} %fusion.refs_3_.pick_ref, ...), custom_call_target="tpu_custom_call" | custom-call | tf_op jit(solution)/shard_map/pairs_0/pallas_call | solution.py:152
  92.7 26.5 %collective-permute-done.5.rest_0_ = bf16[4,592,512]{2,1,0:T(8,128)(2,1)} collective-permute-done((bf16[4,592,512]{2,1,0:T(8,128)(2,1)}, bf16[4,592,512]{2,1,0:T(8,128)(2,1)}, u32[]{:S(2)}, u32[]{:S(2)}) %collective-permute-start.5) | collective-permute-done | bytes 2424864 | tf_op jit(solution)/shard_map/ppermute | solution.py:321
  119.3 3.2 %copy_sets.6 = (bf16[2,592,512]{2,1,0:T(8,128)(2,1)}, bf16[2,592,512]{2,1,0:T(8,128)(2,1)}) custom-call(s32[2,4]{1,0:T(2,128)} %pad_add_fusion.1.table_ref, bf16[4,592,512]{2,1,0:T(8,128)(2,1)} %collective-permute-done.5.rest_0_, bf16[4,592,512]{2,1,0:T(8,128)(2,1)} %collective-permute-done.7.rest_1_, bf16[16,512,512]{2,1,0:T(8,128)(2,1)} %pairs_0.1.rest_2_.rest_9_), custom_call_target="tpu_custom_call" | custom-call | tf_op jit(solution)/shard_map/copy_sets/pallas_call | solution.py:211
  122.5 1.3 collective-permute-start.15
  123.8 1.9 collective-permute-done.12.refs_0_
  125.7 1.7 collective-permute-start.17
  127.4 0.6 stack.109.table_ref
  128.0 3.8 %copy_sets.7 = (bf16[2,592,512]{2,1,0:T(8,128)(2,1)}, bf16[2,592,512]{2,1,0:T(8,128)(2,1)}) custom-call(s32[2,4]{1,0:T(2,128)} %stack.109.table_ref, bf16[4,592,512]{2,1,0:T(8,128)(2,1)} %collective-permute-done.5.rest_0_, bf16[4,592,512]{2,1,0:T(8,128)(2,1)} %collective-permute-done.7.rest_1_, bf16[2,592,512]{2,1,0:T(8,128)(2,1)} %get-tuple-element.9.rest_2_.refs_1_), custom_call_target="tpu_custom_call" | custom-call | tf_op jit(solution)/shard_map/copy_sets/pallas_call | solution.py:211
  132.1 23.2 %collective-permute-done.15.rest_4_ = bf16[2,592,512]{2,1,0:T(8,128)(2,1)} collective-permute-done((bf16[2,592,512]{2,1,0:T(8,128)(2,1)}, bf16[2,592,512]{2,1,0:T(8,128)(2,1)}, u32[]{:S(2)}, u32[]{:S(2)}) %collective-permute-start.15) | collective-permute-done | bytes 1212448 | tf_op jit(solution)/shard_map/ppermute | solution.py:437
  155.8 1.7 collective-permute-start.11
  157.5 1.3 collective-permute-start.20
  158.8 1.5 collective-permute-done.18.rest_7_
  160.3 20.9 %pairs_1.1.refs_1_.rest_4_ = bf16[16,512,512]{2,1,0:T(8,128)(2,1)} custom-call(s32[5,16]{1,0:T(8,128)} %stack.106.refs_4_.meta_ref, f32[16]{0:T(128)} %add.80.shift_ref, bf16[2,576,128]{2,1,0:T(8,128)(2,1)} %broadcast_in_dim.141.ve1_ref, bf16[16,2,512,256]{3,2,1,0:T(8,128)(2,1)} %fusion.refs_3_.pick_ref, ...), custom_call_target="tpu_custom_call", output_to_operand_aliasing={{}: (15, {})} | custom-call | tf_op jit(solution)/shard_map/pairs_1/pallas_call | solution.py:152
  181.4 12.0 %collective-permute-done.20.refs_0_ = bf16[2,592,512]{2,1,0:T(8,128)(2,1)} collective-permute-done((bf16[2,592,512]{2,1,0:T(8,128)(2,1)}, bf16[2,592,512]{2,1,0:T(8,128)(2,1)}, u32[]{:S(2)}, u32[]{:S(2)}) %collective-permute-start.20) | collective-permute-done | bytes 1212448 | tf_op jit(solution)/shard_map/ppermute | solution.py:436
  193.4 3.2 %collective-permute-done.21.rest_3_ = bf16[2,592,512]{2,1,0:T(8,128)(2,1)} collective-permute-done((bf16[2,592,512]{2,1,0:T(8,128)(2,1)}, bf16[2,592,512]{2,1,0:T(8,128)(2,1)}, u32[]{:S(2)}, u32[]{:S(2)}) %collective-permute-start.21) | collective-permute-done | bytes 1212448 | tf_op jit(solution)/shard_map/ppermute | solution.py:318
  196.6 8.6 %pairs_2.1 = bf16[16,512,512]{2,1,0:T(8,128)(2,1)} custom-call(s32[5,16]{1,0:T(8,128)} %stack.106.refs_4_.meta_ref, f32[16]{0:T(128)} %add.80.shift_ref, bf16[2,576,128]{2,1,0:T(8,128)(2,1)} %broadcast_in_dim.141.ve1_ref, bf16[16,2,512,256]{3,2,1,0:T(8,128)(2,1)} %fusion.refs_3_.pick_ref, ...), custom_call_target="tpu_custom_call", output_to_operand_aliasing={{}: (10, {})} | custom-call | tf_op jit(solution)/shard_map/pairs_2/pallas_call | solution.py:152
  (78 shorter events, 5.6 us)
Async XLA Ops:
  0.0 11.7 %copy-start.4 = (s32[32,2]{0,1:T(2,128)S(1)}, s32[32,2]{0,1:T(2,128)}, u32[]{:S(2)}) copy-start(s32[32,2]{0,1:T(2,128)} %param.10) | copy-start | bytes 772
  0.0 11.7 %copy-start.7 = (s32[32]{0:T(128)S(1)}, s32[32]{0:T(128)}, u32[]{:S(2)}) copy-start(s32[32]{0:T(128)} %param.9) | copy-start | bytes 388
  3.3 58.9 %collective-permute-start = (bf16[4,592,512]{2,1,0:T(8,128)(2,1)}, bf16[4,592,512]{2,1,0:T(8,128)(2,1)}, u32[]{:S(2)}, u32[]{:S(2)}) collective-permute-start(bf16[4,592,512]{2,1,0:T(8,128)(2,1)} %extend.1.refs_1_.rest_0_.own_ref.rest_6_), channel_id=1, source_target_pairs={{0,1},{1,0},{2,3},{3,2},{4,5},{5,4},{6,7},{7,6},{8,9},{9,8},{10,11... | collective-permute-start | bytes 7274504 | tf_op jit(solution)/shard_map/ppermute | solution.py:318
  3.9 58.4 %collective-permute-start.2 = (bf16[4,592,512]{2,1,0:T(8,128)(2,1)}, bf16[4,592,512]{2,1,0:T(8,128)(2,1)}, u32[]{:S(2)}, u32[]{:S(2)}) collective-permute-start(bf16[4,592,512]{2,1,0:T(8,128)(2,1)} %extend.1.refs_1_.rest_0_.own_ref.rest_6_), channel_id=1, source_target_pairs={{4,0},{6,2},{8,4},{10,6},{12,8},{14,10},{5,1},{7,3},{9,5},{11,7},{... | collective-permute-start | bytes 7274504 | tf_op jit(solution)/shard_map/ppermute | solution.py:321
  5.1 58.7 %collective-permute-start.6 = (bf16[4,592,512]{2,1,0:T(8,128)(2,1)}, bf16[4,592,512]{2,1,0:T(8,128)(2,1)}, u32[]{:S(2)}, u32[]{:S(2)}) collective-permute-start(bf16[4,592,512]{2,1,0:T(8,128)(2,1)} %extend.1.refs_1_.rest_0_.own_ref.rest_6_), channel_id=1, source_target_pairs={{0,4},{2,6},{4,8},{6,10},{8,12},{10,14},{1,5},{3,7},{5,9},{7,11},{... | collective-permute-start | bytes 7274504 | tf_op jit(solution)/shard_map/ppermute | solution.py:324
  12.6 38.5 %copy-start = (s32[32,2,512]{2,1,0:T(2,128)S(1)}, s32[32,2,512]{2,1,0:T(2,128)}, u32[]{:S(2)}) copy-start(s32[32,2,512]{2,1,0:T(2,128)} %param.11) | copy-start | bytes 393220
  12.6 38.5 %copy-start.2 = (s32[512]{0:T(512)S(1)}, s32[512]{0:T(512)}, u32[]{:S(2)}) copy-start(s32[512]{0:T(512)} %constant.146.clone.1) | copy-start | bytes 6148
  12.6 3.6 %collective-permute-start.1 = (s32[32]{0:T(128)}, s32[32]{0:T(128)S(1)}, u32[]{:S(2)}, u32[]{:S(2)}) collective-permute-start(s32[32]{0:T(128)} %tie.7), channel_id=1, source_target_pairs={{0,2},{2,0},{4,6},{6,4},{8,10},{10,8},{12,14},{14,12},{1,3},{3,1},... | collective-permute-start | bytes 392 | tf_op jit(solution)/shard_map/ppermute | solution.py:312
  22.5 28.6 %collective-permute-start.3 = (bf16[2,592,512]{2,1,0:T(8,128)(2,1)}, bf16[2,592,512]{2,1,0:T(8,128)(2,1)}, u32[]{:S(2)}, u32[]{:S(2)}) collective-permute-start(bf16[2,592,512]{2,1,0:T(8,128)(2,1)} %copy_sets.4.refs_1_), channel_id=1, source_target_pairs={{0,2},{2,0},{4,6},{6,4},{8,10},{10,8},{12,14},{14,12},{1,3},{3,1},... | collective-permute-start | bytes 3637256 | tf_op jit(solution)/shard_map/ppermute | solution.py:312
  51.0 11.2 %collective-permute-start.4 = (bf16[2,592,512]{2,1,0:T(8,128)(2,1)}, bf16[2,592,512]{2,1,0:T(8,128)(2,1)}, u32[]{:S(2)}, u32[]{:S(2)}) collective-permute-start(bf16[2,592,512]{2,1,0:T(8,128)(2,1)} %collective-permute-done.3.rest_0_), channel_id=1, source_target_pairs={{0,1},{1,0},{2,3},{3,2},{4,5},{5,4},{6,7},{7,6},{8,9},{9,8},{10,11... | collective-permute-start | bytes 3637256 | tf_op jit(solution)/shard_map/ppermute | solution.py:318
  51.1 5.7 %copy-start.3 = (s32[32]{0:T(128)S(1)}, s32[32]{0:T(128)}, u32[]{:S(2)}) copy-start(s32[32]{0:T(128)} %tie.7) | copy-start | bytes 388
  57.4 12.7 %collective-permute-start.8 = (s32[2,32]{1,0:T(2,128)}, s32[2,32]{1,0:T(2,128)S(1)}, u32[]{:S(2)}, u32[]{:S(2)}) collective-permute-start(s32[2,32]{1,0:T(2,128)} %tie.10), channel_id=1, source_target_pairs={{0,4},{2,6},{14,10},{12,8},{1,5},{3,7},{15,11},{13,9},{16,20},{18,... | collective-permute-start | bytes 776 | tf_op jit(solution)/shard_map/ppermute | solution.py:413
  62.3 4.0 %copy-start.6 = (s32[1,4]{1,0:T(1,128)S(1)}, s32[1,4]{1,0:T(1,128)}, u32[]{:S(2)}) copy-start(s32[1,4]{1,0:T(1,128)} %constant.152.clone.1) | copy-start | bytes 52
  62.3 57.0 %collective-permute-start.5 = (bf16[4,592,512]{2,1,0:T(8,128)(2,1)}, bf16[4,592,512]{2,1,0:T(8,128)(2,1)}, u32[]{:S(2)}, u32[]{:S(2)}) collective-permute-start(bf16[4,592,512]{2,1,0:T(8,128)(2,1)} %tie.8.rest_0_.rest_2_), channel_id=1, source_target_pairs={{4,0},{6,2},{8,4},{10,6},{5,1},{7,3},{9,5},{11,7},{20,16},{22,18},... | collective-permute-start | bytes 7274504 | tf_op jit(solution)/shard_map/ppermute | solution.py:321
  63.6 20.9 %collective-permute-start.9 = (bf16[4,592,512]{2,1,0:T(8,128)(2,1)}, bf16[4,592,512]{2,1,0:T(8,128)(2,1)}, u32[]{:S(2)}, u32[]{:S(2)}) collective-permute-start(bf16[4,592,512]{2,1,0:T(8,128)(2,1)} %tie.8.rest_0_.rest_2_), channel_id=1, source_target_pairs={{0,1},{1,0},{2,3},{3,2},{4,5},{5,4},{6,7},{7,6},{8,9},{9,8},{10,11... | collective-permute-start | bytes 7274504 | tf_op jit(solution)/shard_map/ppermute | solution.py:318
  63.9 55.4 %collective-permute-start.7 = (bf16[4,592,512]{2,1,0:T(8,128)(2,1)}, bf16[4,592,512]{2,1,0:T(8,128)(2,1)}, u32[]{:S(2)}, u32[]{:S(2)}) collective-permute-start(bf16[4,592,512]{2,1,0:T(8,128)(2,1)} %tie.9.rest_1_.rest_4_), channel_id=1, source_target_pairs={{4,8},{6,10},{8,12},{10,14},{5,9},{7,11},{9,13},{11,15},{20,24},{2... | collective-permute-start | bytes 7274504 | tf_op jit(solution)/shard_map/ppermute | solution.py:324
  65.9 18.6 %collective-permute-start.10 = (bf16[4,592,512]{2,1,0:T(8,128)(2,1)}, bf16[4,592,512]{2,1,0:T(8,128)(2,1)}, u32[]{:S(2)}, u32[]{:S(2)}) collective-permute-start(bf16[4,592,512]{2,1,0:T(8,128)(2,1)} %tie.9.rest_1_.rest_4_), channel_id=1, source_target_pairs={{0,1},{1,0},{2,3},{3,2},{4,5},{5,4},{6,7},{7,6},{8,9},{9,8},{10,11... | collective-permute-start | bytes 7274504 | tf_op jit(solution)/shard_map/ppermute | solution.py:318
  66.8 7.1 %copy-start.5 = (f32[32]{0:T(128)S(1)}, f32[32]{0:T(128)}, u32[]{:S(2)}) copy-start(f32[32]{0:T(128)} %param.8) | copy-start | bytes 388
  66.8 7.9 %copy-start.1 = (bf16[4,576]{1,0:T(4,128)(2,1)S(1)}, bf16[4,576]{1,0:T(4,128)(2,1)}, u32[]{:S(2)}) copy-start(bf16[4,576]{1,0:T(4,128)(2,1)} %energy_ref.1) | copy-start | bytes 13828
  70.2 55.6 %collective-permute-start.12 = (bf16[4,592,512]{2,1,0:T(8,128)(2,1)}, bf16[4,592,512]{2,1,0:T(8,128)(2,1)}, u32[]{:S(2)}, u32[]{:S(2)}) collective-permute-start(bf16[4,592,512]{2,1,0:T(8,128)(2,1)} %copy_sets.5.rest_8_), channel_id=1, source_target_pairs={{0,2},{2,0},{4,6},{6,4},{8,10},{10,8},{12,14},{14,12},{1,3},{3,1},... | collective-permute-start | bytes 7274504 | tf_op jit(solution)/shard_map/ppermute | solution.py:312
  122.5 32.8 %collective-permute-start.15 = (bf16[2,592,512]{2,1,0:T(8,128)(2,1)}, bf16[2,592,512]{2,1,0:T(8,128)(2,1)}, u32[]{:S(2)}, u32[]{:S(2)}) collective-permute-start(bf16[2,592,512]{2,1,0:T(8,128)(2,1)} %get-tuple-element.9.rest_2_.refs_1_), channel_id=1, source_target_pairs={{4,0},{6,2},{8,12},{10,14},{5,1},{7,3},{9,13},{11,15},{20,16},{22,... | collective-permute-start | bytes 3637256 | tf_op jit(solution)/shard_map/ppermute | solution.py:437
  125.7 33.1 %collective-permute-start.13 = (bf16[4,592,512]{2,1,0:T(8,128)(2,1)}, bf16[4,592,512]{2,1,0:T(8,128)(2,1)}, u32[]{:S(2)}, u32[]{:S(2)}) collective-permute-start(bf16[4,592,512]{2,1,0:T(8,128)(2,1)} %tie.11.rest_0_), channel_id=1, source_target_pairs={{0,1},{1,0},{2,3},{3,2},{4,5},{5,4},{6,7},{7,6},{8,9},{9,8},{10,11... | collective-permute-start | bytes 7274504 | tf_op jit(solution)/shard_map/ppermute | solution.py:318
  125.7 29.6 %collective-permute-start.17 = (bf16[2,592,512]{2,1,0:T(8,128)(2,1)}, bf16[2,592,512]{2,1,0:T(8,128)(2,1)}, u32[]{:S(2)}, u32[]{:S(2)}) collective-permute-start(bf16[2,592,512]{2,1,0:T(8,128)(2,1)} %get-tuple-element.12), channel_id=1, source_target_pairs={{0,2},{2,0},{4,6},{6,4},{8,10},{10,8},{12,14},{14,12},{1,3},{3,1},... | collective-permute-start | bytes 3637256 | tf_op jit(solution)/shard_map/ppermute | solution.py:312
  131.8 25.7 %collective-permute-start.14 = (bf16[2,592,512]{2,1,0:T(8,128)(2,1)}, bf16[2,592,512]{2,1,0:T(8,128)(2,1)}, u32[]{:S(2)}, u32[]{:S(2)}) collective-permute-start(bf16[2,592,512]{2,1,0:T(8,128)(2,1)} %get-tuple-element.11.rest_2_.rest_8_), channel_id=1, source_target_pairs={{0,1},{1,0},{2,3},{3,2},{4,5},{5,4},{6,7},{7,6},{8,9},{9,8},{10,11... | collective-permute-start | bytes 3637256 | tf_op jit(solution)/shard_map/ppermute | solution.py:318
  155.3 3.5 %collective-permute-start.16 = (bf16[2,592,512]{2,1,0:T(8,128)(2,1)}, bf16[2,592,512]{2,1,0:T(8,128)(2,1)}, u32[]{:S(2)}, u32[]{:S(2)}) collective-permute-start(bf16[2,592,512]{2,1,0:T(8,128)(2,1)} %collective-permute-done.15.rest_4_), channel_id=1, source_target_pairs={{0,1},{1,0},{2,3},{3,2},{4,5},{5,4},{6,7},{7,6},{8,9},{9,8},{10,11... | collective-permute-start | bytes 3637256 | tf_op jit(solution)/shard_map/ppermute | solution.py:318
  155.3 5.0 %collective-permute-start.18 = (bf16[2,592,512]{2,1,0:T(8,128)(2,1)}, bf16[2,592,512]{2,1,0:T(8,128)(2,1)}, u32[]{:S(2)}, u32[]{:S(2)}) collective-permute-start(bf16[2,592,512]{2,1,0:T(8,128)(2,1)} %collective-permute-done.17.rest_6_), channel_id=1, source_target_pairs={{0,1},{1,0},{2,3},{3,2},{4,5},{5,4},{6,7},{7,6},{8,9},{9,8},{10,11... | collective-permute-start | bytes 3637256 | tf_op jit(solution)/shard_map/ppermute | solution.py:318
  155.8 25.3 %collective-permute-start.11 = (bf16[2,592,512]{2,1,0:T(8,128)(2,1)}, bf16[2,592,512]{2,1,0:T(8,128)(2,1)}, u32[]{:S(2)}, u32[]{:S(2)}) collective-permute-start(bf16[2,592,512]{2,1,0:T(8,128)(2,1)} %get-tuple-element.10), channel_id=1, source_target_pairs={{4,6},{6,4},{8,10},{10,8},{5,7},{7,5},{9,11},{11,9},{20,22},{22,20... | collective-permute-start | bytes 3637256 | tf_op jit(solution)/shard_map/ppermute | solution.py:315
  157.5 35.8 %collective-permute-start.20 = (bf16[2,592,512]{2,1,0:T(8,128)(2,1)}, bf16[2,592,512]{2,1,0:T(8,128)(2,1)}, u32[]{:S(2)}, u32[]{:S(2)}) collective-permute-start(bf16[2,592,512]{2,1,0:T(8,128)(2,1)} %collective-permute-done.17.rest_6_), channel_id=1, source_target_pairs={{4,0},{6,2},{8,12},{10,14},{5,1},{7,3},{9,13},{11,15},{20,16},{22,... | collective-permute-start | bytes 3637256 | tf_op jit(solution)/shard_map/ppermute | solution.py:436
  181.2 12.2 %collective-permute-start.19 = (bf16[2,592,512]{2,1,0:T(8,128)(2,1)}, bf16[2,592,512]{2,1,0:T(8,128)(2,1)}, u32[]{:S(2)}, u32[]{:S(2)}) collective-permute-start(bf16[2,592,512]{2,1,0:T(8,128)(2,1)} %tie.12.rest_0_), channel_id=1, source_target_pairs={{0,1},{1,0},{2,3},{3,2},{4,5},{5,4},{6,7},{7,6},{8,9},{9,8},{10,11... | collective-permute-start | bytes 3637256 | tf_op jit(solution)/shard_map/ppermute | solution.py:318
  193.4 3.2 %collective-permute-start.21 = (bf16[2,592,512]{2,1,0:T(8,128)(2,1)}, bf16[2,592,512]{2,1,0:T(8,128)(2,1)}, u32[]{:S(2)}, u32[]{:S(2)}) collective-permute-start(bf16[2,592,512]{2,1,0:T(8,128)(2,1)} %tie.13.rest_2_), channel_id=1, source_target_pairs={{0,1},{1,0},{2,3},{3,2},{4,5},{5,4},{6,7},{7,6},{8,9},{9,8},{10,11... | collective-permute-start | bytes 3637256 | tf_op jit(solution)/shard_map/ppermute | solution.py:318

commit v13 on v12

--- a/solution.py
+++ b/solution.py
@@ -403,6 +403,10 @@
     def pairs_at(d, after, prev):
         return run_pairs(d, wins, meta, shift, ve1, pick, stored, local_other, sets[d], after, prev)
 
+    def across_aux_at_ends(a):
+        ends = [k for k in range(orb_count) if k // 2 in (0, last)]
+        return lax.ppermute(a, ("orb", "aux"), [(2 * k + c, 2 * k + 1 - c) for k in ends for c in range(2)])
+
     def with_other(a):
         return a, across_aux(a)
 
@@ -456,7 +460,7 @@
                 place_of * 2, both_ways(want_opp) + both_ways(want), [downs[d], ups[d]], first, [len(place_of)] * 2)
             sets[d - 1] = [with_other(tie(opp, first) if first else opp), with_other(mine)]
             if d + 1 == last:
-                sets[d - 1] += [with_other(far_a), with_other(over)]
+                sets[d - 1] += [with_other(far_a), (over, across_aux_at_ends(over))]
             out = pairs_at(d - 1, [mine], out)
         opp = across_y(theirs) if d + 1 < last else across_y_inside(theirs)
     sets[last - 1] = [with_other(tie(opp, [out])), with_other(tie(far_b, [out]))]

time: 207 us -> 209 us (level)
  starting transfers between devices: 27.7 us -> 33.3 us
  waiting for transfers between devices: 95.2 us -> 91.4 us
    ppermute x10 -> x9, starting transfers between devices: 2.1 us -> 6.26 us  [across_aux(): return lax.ppermute(a, 'aux', swap_aux)]
    ppermute x1, waiting for transfers between devices: 12 us -> 9.31 us  [per_device(): far_b = lax.ppermute(over, 'orb', perm)]
    ppermute x0 -> x1, starting transfers between devices: none -> 2.41 us  [across_aux_at_ends(): lax.ppermute(a, ('orb', 'aux'), [(2 * k + c, 2 * k + 1 - c) for k in ends...]
    ppermute x10 -> x9, waiting for transfers between devices: 4.7 us -> 3.25 us  [across_aux(): return lax.ppermute(a, 'aux', swap_aux)]
  transfers between devices with their start and end apart: 22 -> 22, of which waited for: 8 -> 7; matrix products, arithmetic and copies ran while one was open for 13% -> 13% of each run, Pallas kernels for 20% -> 20%
where the time goes in v13:
time: 209 us; the launch traced here: 207 us
  waiting for transfers between devices  91.4 us (44%)
  Pallas kernels  52.9 us (25%)
  starting transfers between devices  33.3 us (16%)
  other arithmetic  18.3 us (9%)
  local copies, waits for them, and re-layouts  8.27 us (4%)
  between operations  2.59 us (1%)
    pallas_call x3, Pallas kernels, run_pairs(): pl.pallas_call(functools.partial(pair_kernel, call, wins, len(sets), len(...  36.4 us
    ppermute x4, waiting for transfers between devices, across_y(): return lax.ppermute(a, 'orb', swap_y)  28.4 us
    ppermute x2, waiting for transfers between devices, hop_down(): lax.ppermute(a, 'orb', [(k, k - 2) for k in range(2, orb_count) if k // 2...  26.1 us
    ppermute x1, waiting for transfers between devices, per_device(): far_a = lax.ppermute(load_own, 'orb', perm)  24.4 us
    pallas_call x4, Pallas kernels, copy_sets(): pl.pallas_call(functools.partial(set_kernel, len(arrays), len(after), siz...  13.1 us
    ppermute x1, waiting for transfers between devices, per_device(): far_b = lax.ppermute(over, 'orb', perm)  9.31 us
    another operation x6, other arithmetic, copy_sets(): jnp.stack([jnp.stack([jnp.asarray(w, jnp.int32) for w in which]), jnp.sta...  8.95 us
    ppermute x2, starting transfers between devices, hop_up(): lax.ppermute(a, 'orb', [(k, k + 2) for k in range(orb_count - 2) if k //...  8.64 us
  transfers between devices with their start and end apart: 22, of which 7 were waited for; matrix products, arithmetic and copies ran while one was open for 13% of the time, Pallas kernels for 20%

profile of v13, /device:TPU:0, one launch (start us, length us, event | category | flops | bytes accessed | tf_op | source)
XLA Modules:
  0.0 206.6 jit_solution(1804263400090121408)
XLA Ops:
  0.0 3.3 %extend.1.refs_1_.rest_0_.own_ref.rest_6_ = bf16[4,592,512]{2,1,0:T(8,128)(2,1)} custom-call(bf16[4,576,512]{2,1,0:T(8,128)(2,1)} %blocks_ref.1, bf16[4,576]{1,0:T(4,128)(2,1)} %energy_ref.1), custom_call_target="tpu_custom_call" | custom-call | tf_op jit(solution)/shard_map/extend/pallas_call | solution.py:266
  3.9 1.3 collective-permute-start.2
  5.1 6.6 %collective-permute-start.6 = (bf16[4,592,512]{2,1,0:T(8,128)(2,1)}, bf16[4,592,512]{2,1,0:T(8,128)(2,1)}, u32[]{:S(2)}, u32[]{:S(2)}) collective-permute-start(bf16[4,592,512]{2,1,0:T(8,128)(2,1)} %extend.1.refs_1_.rest_0_.own_ref.rest_6_), channel_id=1, source_target_pairs={{0,4},{2,6},{4,8},{6,10},{8,12},{10,14},{1,5},{3,7},{5,9},{7,11},{... | collective-permute-start | bytes 7274504 | tf_op jit(solution)/shard_map/ppermute | solution.py:324
  12.0 0.6 convert_element_type.40.refs_0_
  12.6 2.0 collective-permute-start.1
  14.6 1.6 collective-permute-done.1
  16.5 0.7 fusion.8
  17.1 0.7 fusion.7
  17.8 1.4 add_bitcast_fusion.1
  19.1 0.6 stack.112.table_ref
  19.7 2.7 %copy_sets.4.refs_1_ = bf16[2,592,512]{2,1,0:T(8,128)(2,1)} custom-call(s32[2,2]{1,0:T(2,128)} %stack.112.table_ref, bf16[4,592,512]{2,1,0:T(8,128)(2,1)} %extend.1.refs_1_.rest_0_.own_ref.rest_6_), custom_call_target="tpu_custom_call" | custom-call | tf_op jit(solution)/shard_map/copy_sets/pallas_call | solution.py:211
  22.5 2.0 collective-permute-start.3
  25.2 0.6 stack.106.refs_4_.meta_ref
  25.8 25.3 %collective-permute-done.3.rest_0_ = bf16[2,592,512]{2,1,0:T(8,128)(2,1)} collective-permute-done((bf16[2,592,512]{2,1,0:T(8,128)(2,1)}, bf16[2,592,512]{2,1,0:T(8,128)(2,1)}, u32[]{:S(2)}, u32[]{:S(2)}) %collective-permute-start.3) | collective-permute-done | bytes 1212448 | tf_op jit(solution)/shard_map/ppermute | solution.py:312
  51.1 5.7 %fusion.refs_3_.pick_ref = bf16[16,2,512,256]{3,2,1,0:T(8,128)(2,1)} fusion(s32[16,2,512]{2,1,0:T(2,128)S(1)} %dynamic-slice_add_fusion), kind=kLoop, calls=%fused_computation.1 | loop fusion | flops 8388608 | bytes 8454144 | tf_op jit(solution)/shard_map/convert_element_type | solution.py:393
  56.8 0.6 pad_add_fusion.refs_0_
  57.4 2.4 %collective-permute-start.8 = (s32[2,32]{1,0:T(2,128)}, s32[2,32]{1,0:T(2,128)S(1)}, u32[]{:S(2)}, u32[]{:S(2)}) collective-permute-start(s32[2,32]{1,0:T(2,128)} %tie.10), channel_id=1, source_target_pairs={{0,4},{2,6},{14,10},{12,8},{1,5},{3,7},{15,11},{13,9},{16,20},{18,... | collective-permute-start | bytes 776 | tf_op jit(solution)/shard_map/ppermute | solution.py:417
  59.8 2.6 %add_bitcast_fusion.4 = s32[1,4]{1,0:T(1,128)S(1)} fusion(s32[1]{0:T(128)} %get-tuple-element.40, s32[1]{0:T(128)} %get-tuple-element.35, s32[1]{0:T(128)} %get-tuple-element.39, s32[1]{0:T(128)} %get-tuple-element.34), kind=kLoop, calls=%fused_computation.63 | loop fusion | flops 12 | bytes 32 | tf_op jit(solution)/shard_map/stack | solution.py:209
  62.4 1.3 collective-permute-start.5
  64.0 2.1 collective-permute-start.7
  67.0 3.3 %copy_sets.5.rest_8_ = bf16[4,592,512]{2,1,0:T(8,128)(2,1)} custom-call(s32[2,4]{1,0:T(2,128)} %pad_add_fusion.2.table_ref, bf16[4,592,512]{2,1,0:T(8,128)(2,1)} %tie.8.rest_0_.rest_2_, bf16[4,592,512]{2,1,0:T(8,128)(2,1)} %tie.9.rest_1_.rest_4_), custom_call_target="tpu_custom_call" | custom-call | tf_op jit(solution)/shard_map/copy_sets/pallas_call | solution.py:211
  70.3 1.4 collective-permute-start.12
  72.0 0.6 dynamic_slice.68
  72.6 0.6 dynamic_slice.67
  73.5 0.6 add.80.shift_ref
  74.1 2.6 %add_bitcast_fusion = (s32[1,4]{1,0:T(1,128)S(1)}, s32[1,4]{1,0:T(1,128)S(1)}) fusion(s32[1]{0:T(128)} %dynamic_slice.68, s32[1]{0:T(128)} %dynamic_slice.67, s32[1]{0:T(128)} %get-tuple-element.43, s32[1]{0:T(128)} %get-tuple-element.38, s32[1]{0:T(128)} %bitcast.12, s32[1]{0:T(128)} %bitcast.11), kind=kLoop, calls=%fused_computation.59 | loop fusion | flops 24 | bytes 56 | tf_op jit(solution)/shard_map/stack | solution.py:209
  76.9 0.6 dynamic_slice.76
  77.5 0.6 dynamic_slice.75
  78.4 0.7 dynamic_slice.74
  82.0 1.3 add_bitcast_fusion.3
  83.9 0.9 broadcast_in_dim.141.ve1_ref
  84.8 8.6 %pairs_0.1.rest_2_.rest_9_ = bf16[16,512,512]{2,1,0:T(8,128)(2,1)} custom-call(s32[5,16]{1,0:T(8,128)} %stack.106.refs_4_.meta_ref, f32[16]{0:T(128)} %add.80.shift_ref, bf16[2,576,128]{2,1,0:T(8,128)(2,1)} %broadcast_in_dim.141.ve1_ref, bf16[16,2,512,256]{3,2,1,0:T(8,128)(2,1)} %fusion.refs_3_.pick_ref, ...), custom_call_target="tpu_custom_call" | custom-call | tf_op jit(solution)/shard_map/pairs_0/pallas_call | solution.py:152
  93.4 26.1 %collective-permute-done.5.rest_0_ = bf16[4,592,512]{2,1,0:T(8,128)(2,1)} collective-permute-done((bf16[4,592,512]{2,1,0:T(8,128)(2,1)}, bf16[4,592,512]{2,1,0:T(8,128)(2,1)}, u32[]{:S(2)}, u32[]{:S(2)}) %collective-permute-start.5) | collective-permute-done | bytes 2424864 | tf_op jit(solution)/shard_map/ppermute | solution.py:321
  119.4 3.2 %copy_sets.6 = (bf16[2,592,512]{2,1,0:T(8,128)(2,1)}, bf16[2,592,512]{2,1,0:T(8,128)(2,1)}) custom-call(s32[2,4]{1,0:T(2,128)} %pad_add_fusion.1.table_ref, bf16[4,592,512]{2,1,0:T(8,128)(2,1)} %collective-permute-done.5.rest_0_, bf16[4,592,512]{2,1,0:T(8,128)(2,1)} %collective-permute-done.7.rest_1_, bf16[16,512,512]{2,1,0:T(8,128)(2,1)} %pairs_0.1.rest_2_.rest_9_), custom_call_target="tpu_custom_call" | custom-call | tf_op jit(solution)/shard_map/copy_sets/pallas_call | solution.py:211
  122.6 1.3 collective-permute-start.15
  123.9 1.5 collective-permute-done.12.refs_0_
  125.5 1.4 collective-permute-start.17
  126.8 0.6 stack.109.table_ref
  127.4 3.8 %copy_sets.7 = (bf16[2,592,512]{2,1,0:T(8,128)(2,1)}, bf16[2,592,512]{2,1,0:T(8,128)(2,1)}) custom-call(s32[2,4]{1,0:T(2,128)} %stack.109.table_ref, bf16[4,592,512]{2,1,0:T(8,128)(2,1)} %collective-permute-done.5.rest_0_, bf16[4,592,512]{2,1,0:T(8,128)(2,1)} %collective-permute-done.7.rest_1_, bf16[2,592,512]{2,1,0:T(8,128)(2,1)} %get-tuple-element.9.rest_2_.refs_1_), custom_call_target="tpu_custom_call" | custom-call | tf_op jit(solution)/shard_map/copy_sets/pallas_call | solution.py:211
  131.5 24.4 %collective-permute-done.15.rest_4_ = bf16[2,592,512]{2,1,0:T(8,128)(2,1)} collective-permute-done((bf16[2,592,512]{2,1,0:T(8,128)(2,1)}, bf16[2,592,512]{2,1,0:T(8,128)(2,1)}, u32[]{:S(2)}, u32[]{:S(2)}) %collective-permute-start.15) | collective-permute-done | bytes 1212448 | tf_op jit(solution)/shard_map/ppermute | solution.py:441
  155.9 2.4 %collective-permute-start.18 = (bf16[2,592,512]{2,1,0:T(8,128)(2,1)}, bf16[2,592,512]{2,1,0:T(8,128)(2,1)}, u32[]{:S(2)}, u32[]{:S(2)}) collective-permute-start(bf16[2,592,512]{2,1,0:T(8,128)(2,1)} %collective-permute-done.17.rest_6_), channel_id=1, source_target_pairs={{0,1},{1,0},{2,3},{3,2},{12,13},{13,12},{14,15},{15,14},{16,17},{1... | collective-permute-start | bytes 3637256 | tf_op jit(solution)/shard_map/ppermute | solution.py:408
  158.3 1.7 collective-permute-start.11
  160.0 1.3 collective-permute-start.20
  161.3 19.3 %pairs_1.1.refs_1_.rest_4_ = bf16[16,512,512]{2,1,0:T(8,128)(2,1)} custom-call(s32[5,16]{1,0:T(8,128)} %stack.106.refs_4_.meta_ref, f32[16]{0:T(128)} %add.80.shift_ref, bf16[2,576,128]{2,1,0:T(8,128)(2,1)} %broadcast_in_dim.141.ve1_ref, bf16[16,2,512,256]{3,2,1,0:T(8,128)(2,1)} %fusion.refs_3_.pick_ref, ...), custom_call_target="tpu_custom_call", output_to_operand_aliasing={{}: (15, {})} | custom-call | tf_op jit(solution)/shard_map/pairs_1/pallas_call | solution.py:152
  180.7 4.9 %collective-permute-start.19 = (bf16[2,592,512]{2,1,0:T(8,128)(2,1)}, bf16[2,592,512]{2,1,0:T(8,128)(2,1)}, u32[]{:S(2)}, u32[]{:S(2)}) collective-permute-start(bf16[2,592,512]{2,1,0:T(8,128)(2,1)} %tie.12.rest_0_), channel_id=1, source_target_pairs={{0,1},{1,0},{2,3},{3,2},{4,5},{5,4},{6,7},{7,6},{8,9},{9,8},{10,11... | collective-permute-start | bytes 3637256 | tf_op jit(solution)/shard_map/ppermute | solution.py:318
  185.5 9.3 %collective-permute-done.20.refs_0_ = bf16[2,592,512]{2,1,0:T(8,128)(2,1)} collective-permute-done((bf16[2,592,512]{2,1,0:T(8,128)(2,1)}, bf16[2,592,512]{2,1,0:T(8,128)(2,1)}, u32[]{:S(2)}, u32[]{:S(2)}) %collective-permute-start.20) | collective-permute-done | bytes 1212448 | tf_op jit(solution)/shard_map/ppermute | solution.py:440
  194.9 3.2 %collective-permute-done.21.rest_3_ = bf16[2,592,512]{2,1,0:T(8,128)(2,1)} collective-permute-done((bf16[2,592,512]{2,1,0:T(8,128)(2,1)}, bf16[2,592,512]{2,1,0:T(8,128)(2,1)}, u32[]{:S(2)}, u32[]{:S(2)}) %collective-permute-start.21) | collective-permute-done | bytes 1212448 | tf_op jit(solution)/shard_map/ppermute | solution.py:318
  198.1 8.5 %pairs_2.1 = bf16[16,512,512]{2,1,0:T(8,128)(2,1)} custom-call(s32[5,16]{1,0:T(8,128)} %stack.106.refs_4_.meta_ref, f32[16]{0:T(128)} %add.80.shift_ref, bf16[2,576,128]{2,1,0:T(8,128)(2,1)} %broadcast_in_dim.141.ve1_ref, bf16[16,2,512,256]{3,2,1,0:T(8,128)(2,1)} %fusion.refs_3_.pick_ref, ...), custom_call_target="tpu_custom_call", output_to_operand_aliasing={{}: (10, {})} | custom-call | tf_op jit(solution)/shard_map/pairs_2/pallas_call | solution.py:152
  (78 shorter events, 5.5 us)
Async XLA Ops:
  0.0 11.7 %copy-start.4 = (s32[32,2]{0,1:T(2,128)S(1)}, s32[32,2]{0,1:T(2,128)}, u32[]{:S(2)}) copy-start(s32[32,2]{0,1:T(2,128)} %param.10) | copy-start | bytes 772
  0.0 11.7 %copy-start.7 = (s32[32]{0:T(128)S(1)}, s32[32]{0:T(128)}, u32[]{:S(2)}) copy-start(s32[32]{0:T(128)} %param.9) | copy-start | bytes 388
  3.3 59.1 %collective-permute-start = (bf16[4,592,512]{2,1,0:T(8,128)(2,1)}, bf16[4,592,512]{2,1,0:T(8,128)(2,1)}, u32[]{:S(2)}, u32[]{:S(2)}) collective-permute-start(bf16[4,592,512]{2,1,0:T(8,128)(2,1)} %extend.1.refs_1_.rest_0_.own_ref.rest_6_), channel_id=1, source_target_pairs={{0,1},{1,0},{2,3},{3,2},{4,5},{5,4},{6,7},{7,6},{8,9},{9,8},{10,11... | collective-permute-start | bytes 7274504 | tf_op jit(solution)/shard_map/ppermute | solution.py:318
  3.9 58.5 %collective-permute-start.2 = (bf16[4,592,512]{2,1,0:T(8,128)(2,1)}, bf16[4,592,512]{2,1,0:T(8,128)(2,1)}, u32[]{:S(2)}, u32[]{:S(2)}) collective-permute-start(bf16[4,592,512]{2,1,0:T(8,128)(2,1)} %extend.1.refs_1_.rest_0_.own_ref.rest_6_), channel_id=1, source_target_pairs={{4,0},{6,2},{8,4},{10,6},{12,8},{14,10},{5,1},{7,3},{9,5},{11,7},{... | collective-permute-start | bytes 7274504 | tf_op jit(solution)/shard_map/ppermute | solution.py:321
  5.1 58.9 %collective-permute-start.6 = (bf16[4,592,512]{2,1,0:T(8,128)(2,1)}, bf16[4,592,512]{2,1,0:T(8,128)(2,1)}, u32[]{:S(2)}, u32[]{:S(2)}) collective-permute-start(bf16[4,592,512]{2,1,0:T(8,128)(2,1)} %extend.1.refs_1_.rest_0_.own_ref.rest_6_), channel_id=1, source_target_pairs={{0,4},{2,6},{4,8},{6,10},{8,12},{10,14},{1,5},{3,7},{5,9},{7,11},{... | collective-permute-start | bytes 7274504 | tf_op jit(solution)/shard_map/ppermute | solution.py:324
  12.6 38.5 %copy-start = (s32[32,2,512]{2,1,0:T(2,128)S(1)}, s32[32,2,512]{2,1,0:T(2,128)}, u32[]{:S(2)}) copy-start(s32[32,2,512]{2,1,0:T(2,128)} %param.11) | copy-start | bytes 393220
  12.6 38.5 %copy-start.2 = (s32[512]{0:T(512)S(1)}, s32[512]{0:T(512)}, u32[]{:S(2)}) copy-start(s32[512]{0:T(512)} %constant.146.clone.1) | copy-start | bytes 6148
  12.6 3.6 %collective-permute-start.1 = (s32[32]{0:T(128)}, s32[32]{0:T(128)S(1)}, u32[]{:S(2)}, u32[]{:S(2)}) collective-permute-start(s32[32]{0:T(128)} %tie.7), channel_id=1, source_target_pairs={{0,2},{2,0},{4,6},{6,4},{8,10},{10,8},{12,14},{14,12},{1,3},{3,1},... | collective-permute-start | bytes 392 | tf_op jit(solution)/shard_map/ppermute | solution.py:312
  22.5 28.6 %collective-permute-start.3 = (bf16[2,592,512]{2,1,0:T(8,128)(2,1)}, bf16[2,592,512]{2,1,0:T(8,128)(2,1)}, u32[]{:S(2)}, u32[]{:S(2)}) collective-permute-start(bf16[2,592,512]{2,1,0:T(8,128)(2,1)} %copy_sets.4.refs_1_), channel_id=1, source_target_pairs={{0,2},{2,0},{4,6},{6,4},{8,10},{10,8},{12,14},{14,12},{1,3},{3,1},... | collective-permute-start | bytes 3637256 | tf_op jit(solution)/shard_map/ppermute | solution.py:312
  51.0 11.4 %collective-permute-start.4 = (bf16[2,592,512]{2,1,0:T(8,128)(2,1)}, bf16[2,592,512]{2,1,0:T(8,128)(2,1)}, u32[]{:S(2)}, u32[]{:S(2)}) collective-permute-start(bf16[2,592,512]{2,1,0:T(8,128)(2,1)} %collective-permute-done.3.rest_0_), channel_id=1, source_target_pairs={{0,1},{1,0},{2,3},{3,2},{4,5},{5,4},{6,7},{7,6},{8,9},{9,8},{10,11... | collective-permute-start | bytes 3637256 | tf_op jit(solution)/shard_map/ppermute | solution.py:318
  51.1 5.7 %copy-start.3 = (s32[32]{0:T(128)S(1)}, s32[32]{0:T(128)}, u32[]{:S(2)}) copy-start(s32[32]{0:T(128)} %tie.7) | copy-start | bytes 388
  57.4 12.9 %collective-permute-start.8 = (s32[2,32]{1,0:T(2,128)}, s32[2,32]{1,0:T(2,128)S(1)}, u32[]{:S(2)}, u32[]{:S(2)}) collective-permute-start(s32[2,32]{1,0:T(2,128)} %tie.10), channel_id=1, source_target_pairs={{0,4},{2,6},{14,10},{12,8},{1,5},{3,7},{15,11},{13,9},{16,20},{18,... | collective-permute-start | bytes 776 | tf_op jit(solution)/shard_map/ppermute | solution.py:417
  62.4 4.0 %copy-start.6 = (s32[1,4]{1,0:T(1,128)S(1)}, s32[1,4]{1,0:T(1,128)}, u32[]{:S(2)}) copy-start(s32[1,4]{1,0:T(1,128)} %constant.152.clone.1) | copy-start | bytes 52
  62.4 57.0 %collective-permute-start.5 = (bf16[4,592,512]{2,1,0:T(8,128)(2,1)}, bf16[4,592,512]{2,1,0:T(8,128)(2,1)}, u32[]{:S(2)}, u32[]{:S(2)}) collective-permute-start(bf16[4,592,512]{2,1,0:T(8,128)(2,1)} %tie.8.rest_0_.rest_2_), channel_id=1, source_target_pairs={{4,0},{6,2},{8,4},{10,6},{5,1},{7,3},{9,5},{11,7},{20,16},{22,18},... | collective-permute-start | bytes 7274504 | tf_op jit(solution)/shard_map/ppermute | solution.py:321
  63.7 20.1 %collective-permute-start.9 = (bf16[4,592,512]{2,1,0:T(8,128)(2,1)}, bf16[4,592,512]{2,1,0:T(8,128)(2,1)}, u32[]{:S(2)}, u32[]{:S(2)}) collective-permute-start(bf16[4,592,512]{2,1,0:T(8,128)(2,1)} %tie.8.rest_0_.rest_2_), channel_id=1, source_target_pairs={{0,1},{1,0},{2,3},{3,2},{4,5},{5,4},{6,7},{7,6},{8,9},{9,8},{10,11... | collective-permute-start | bytes 7274504 | tf_op jit(solution)/shard_map/ppermute | solution.py:318
  64.0 55.4 %collective-permute-start.7 = (bf16[4,592,512]{2,1,0:T(8,128)(2,1)}, bf16[4,592,512]{2,1,0:T(8,128)(2,1)}, u32[]{:S(2)}, u32[]{:S(2)}) collective-permute-start(bf16[4,592,512]{2,1,0:T(8,128)(2,1)} %tie.9.rest_1_.rest_4_), channel_id=1, source_target_pairs={{4,8},{6,10},{8,12},{10,14},{5,9},{7,11},{9,13},{11,15},{20,24},{2... | collective-permute-start | bytes 7274504 | tf_op jit(solution)/shard_map/ppermute | solution.py:324
  66.1 17.8 %collective-permute-start.10 = (bf16[4,592,512]{2,1,0:T(8,128)(2,1)}, bf16[4,592,512]{2,1,0:T(8,128)(2,1)}, u32[]{:S(2)}, u32[]{:S(2)}) collective-permute-start(bf16[4,592,512]{2,1,0:T(8,128)(2,1)} %tie.9.rest_1_.rest_4_), channel_id=1, source_target_pairs={{0,1},{1,0},{2,3},{3,2},{4,5},{5,4},{6,7},{7,6},{8,9},{9,8},{10,11... | collective-permute-start | bytes 7274504 | tf_op jit(solution)/shard_map/ppermute | solution.py:318
  67.0 6.4 %copy-start.5 = (f32[32]{0:T(128)S(1)}, f32[32]{0:T(128)}, u32[]{:S(2)}) copy-start(f32[32]{0:T(128)} %param.8) | copy-start | bytes 388
  67.0 7.1 %copy-start.1 = (bf16[4,576]{1,0:T(4,128)(2,1)S(1)}, bf16[4,576]{1,0:T(4,128)(2,1)}, u32[]{:S(2)}) copy-start(bf16[4,576]{1,0:T(4,128)(2,1)} %energy_ref.1) | copy-start | bytes 13828
  70.3 55.2 %collective-permute-start.12 = (bf16[4,592,512]{2,1,0:T(8,128)(2,1)}, bf16[4,592,512]{2,1,0:T(8,128)(2,1)}, u32[]{:S(2)}, u32[]{:S(2)}) collective-permute-start(bf16[4,592,512]{2,1,0:T(8,128)(2,1)} %copy_sets.5.rest_8_), channel_id=1, source_target_pairs={{0,2},{2,0},{4,6},{6,4},{8,10},{10,8},{12,14},{14,12},{1,3},{3,1},... | collective-permute-start | bytes 7274504 | tf_op jit(solution)/shard_map/ppermute | solution.py:312
  122.6 33.2 %collective-permute-start.15 = (bf16[2,592,512]{2,1,0:T(8,128)(2,1)}, bf16[2,592,512]{2,1,0:T(8,128)(2,1)}, u32[]{:S(2)}, u32[]{:S(2)}) collective-permute-start(bf16[2,592,512]{2,1,0:T(8,128)(2,1)} %get-tuple-element.9.rest_2_.refs_1_), channel_id=1, source_target_pairs={{4,0},{6,2},{8,12},{10,14},{5,1},{7,3},{9,13},{11,15},{20,16},{22,... | collective-permute-start | bytes 3637256 | tf_op jit(solution)/shard_map/ppermute | solution.py:441
  125.5 35.8 %collective-permute-start.13 = (bf16[4,592,512]{2,1,0:T(8,128)(2,1)}, bf16[4,592,512]{2,1,0:T(8,128)(2,1)}, u32[]{:S(2)}, u32[]{:S(2)}) collective-permute-start(bf16[4,592,512]{2,1,0:T(8,128)(2,1)} %tie.11.rest_0_), channel_id=1, source_target_pairs={{0,1},{1,0},{2,3},{3,2},{4,5},{5,4},{6,7},{7,6},{8,9},{9,8},{10,11... | collective-permute-start | bytes 7274504 | tf_op jit(solution)/shard_map/ppermute | solution.py:318
  125.5 30.4 %collective-permute-start.17 = (bf16[2,592,512]{2,1,0:T(8,128)(2,1)}, bf16[2,592,512]{2,1,0:T(8,128)(2,1)}, u32[]{:S(2)}, u32[]{:S(2)}) collective-permute-start(bf16[2,592,512]{2,1,0:T(8,128)(2,1)} %get-tuple-element.12), channel_id=1, source_target_pairs={{0,2},{2,0},{4,6},{6,4},{8,10},{10,8},{12,14},{14,12},{1,3},{3,1},... | collective-permute-start | bytes 3637256 | tf_op jit(solution)/shard_map/ppermute | solution.py:312
  131.2 28.8 %collective-permute-start.14 = (bf16[2,592,512]{2,1,0:T(8,128)(2,1)}, bf16[2,592,512]{2,1,0:T(8,128)(2,1)}, u32[]{:S(2)}, u32[]{:S(2)}) collective-permute-start(bf16[2,592,512]{2,1,0:T(8,128)(2,1)} %get-tuple-element.11.rest_2_.rest_8_), channel_id=1, source_target_pairs={{0,1},{1,0},{2,3},{3,2},{4,5},{5,4},{6,7},{7,6},{8,9},{9,8},{10,11... | collective-permute-start | bytes 3637256 | tf_op jit(solution)/shard_map/ppermute | solution.py:318
  155.9 5.4 %collective-permute-start.16 = (bf16[2,592,512]{2,1,0:T(8,128)(2,1)}, bf16[2,592,512]{2,1,0:T(8,128)(2,1)}, u32[]{:S(2)}, u32[]{:S(2)}) collective-permute-start(bf16[2,592,512]{2,1,0:T(8,128)(2,1)} %collective-permute-done.15.rest_4_), channel_id=1, source_target_pairs={{0,1},{1,0},{2,3},{3,2},{4,5},{5,4},{6,7},{7,6},{8,9},{9,8},{10,11... | collective-permute-start | bytes 3637256 | tf_op jit(solution)/shard_map/ppermute | solution.py:318
  155.9 5.4 %collective-permute-start.18 = (bf16[2,592,512]{2,1,0:T(8,128)(2,1)}, bf16[2,592,512]{2,1,0:T(8,128)(2,1)}, u32[]{:S(2)}, u32[]{:S(2)}) collective-permute-start(bf16[2,592,512]{2,1,0:T(8,128)(2,1)} %collective-permute-done.17.rest_6_), channel_id=1, source_target_pairs={{0,1},{1,0},{2,3},{3,2},{12,13},{13,12},{14,15},{15,14},{16,17},{1... | collective-permute-start | bytes 3637256 | tf_op jit(solution)/shard_map/ppermute | solution.py:408
  158.3 22.4 %collective-permute-start.11 = (bf16[2,592,512]{2,1,0:T(8,128)(2,1)}, bf16[2,592,512]{2,1,0:T(8,128)(2,1)}, u32[]{:S(2)}, u32[]{:S(2)}) collective-permute-start(bf16[2,592,512]{2,1,0:T(8,128)(2,1)} %get-tuple-element.10), channel_id=1, source_target_pairs={{4,6},{6,4},{8,10},{10,8},{5,7},{7,5},{9,11},{11,9},{20,22},{22,20... | collective-permute-start | bytes 3637256 | tf_op jit(solution)/shard_map/ppermute | solution.py:315
  160.0 34.9 %collective-permute-start.20 = (bf16[2,592,512]{2,1,0:T(8,128)(2,1)}, bf16[2,592,512]{2,1,0:T(8,128)(2,1)}, u32[]{:S(2)}, u32[]{:S(2)}) collective-permute-start(bf16[2,592,512]{2,1,0:T(8,128)(2,1)} %collective-permute-done.17.rest_6_), channel_id=1, source_target_pairs={{4,0},{6,2},{8,12},{10,14},{5,1},{7,3},{9,13},{11,15},{20,16},{22,... | collective-permute-start | bytes 3637256 | tf_op jit(solution)/shard_map/ppermute | solution.py:440
  180.7 14.2 %collective-permute-start.19 = (bf16[2,592,512]{2,1,0:T(8,128)(2,1)}, bf16[2,592,512]{2,1,0:T(8,128)(2,1)}, u32[]{:S(2)}, u32[]{:S(2)}) collective-permute-start(bf16[2,592,512]{2,1,0:T(8,128)(2,1)} %tie.12.rest_0_), channel_id=1, source_target_pairs={{0,1},{1,0},{2,3},{3,2},{4,5},{5,4},{6,7},{7,6},{8,9},{9,8},{10,11... | collective-permute-start | bytes 3637256 | tf_op jit(solution)/shard_map/ppermute | solution.py:318
  194.9 3.2 %collective-permute-start.21 = (bf16[2,592,512]{2,1,0:T(8,128)(2,1)}, bf16[2,592,512]{2,1,0:T(8,128)(2,1)}, u32[]{:S(2)}, u32[]{:S(2)}) collective-permute-start(bf16[2,592,512]{2,1,0:T(8,128)(2,1)} %tie.13.rest_2_), channel_id=1, source_target_pairs={{0,1},{1,0},{2,3},{3,2},{4,5},{5,4},{6,7},{7,6},{8,9},{9,8},{10,11... | collective-permute-start | bytes 3637256 | tf_op jit(solution)/shard_map/ppermute | solution.py:318
